TPU v7x, 32 devices: a whole 2x2x4 slice. The times are simulated.
32 devices in a mesh: section: 2 (over y), dp: 4 (over z), mp: 4 (over x, core).
Axes of the slice: x: 2, y: 2, z: 4, core: 2. Of those that a mesh axis runs over, the one named last changes fastest.
Arguments:
- conv_input: bfloat16 [4, 64, 2, 13, 13, 384], P(None, 'dp', None, None, None, 'mp'), may hold values from -6 to 6
- group_ids: int32 [4], replicated, may hold values from 0 to 1, as said below
- conv_weight: bfloat16 [2, 3456, 256], P(None, 'dp', 'mp'), may hold values from -0.21875 to 0.21875
- conv_bias: float32 [2, 256], P(None, 'mp'), may hold values from -3 to 3
- conv_stitch: float32 [2, 2, 256], P(None, None, 'mp'), may hold values from 0.1 to 1
- fc_weight: bfloat16 [2, 9216, 4096], P(None, 'dp', 'mp'), may hold values from -0.125 to 0.125
- fc_bias: float32 [2, 4096], P(None, 'mp'), may hold values from -3 to 3
- fc_stitch: float32 [2, 2, 4096], P(None, None, 'mp'), may hold values from 0.1 to 1
- cotangent: bfloat16 [4, 64, 2, 4096], P(None, None, None, 'mp'), may hold values from -6 to 6
Outputs:
- outputs: bfloat16 [4, 64, 2, 4096], P(None, 'dp', 'section', 'mp')
- input_grad: bfloat16 [4, 64, 2, 13, 13, 384], P(None, 'dp', 'section', None, None, 'mp')
- conv_weight_grad: float32 [2, 3456, 256], P('section', 'dp', 'mp')
- conv_bias_grad: float32 [2, 256], P('section', 'mp')
- conv_stitch_grad: float32 [2, 2, 256], P('section', None, 'mp')
- fc_weight_grad: float32 [2, 9216, 4096], P('section', 'dp', 'mp')
- fc_bias_grad: float32 [2, 4096], P('section', 'mp')
- fc_stitch_grad: float32 [2, 2, 4096], P('section', None, 'mp')
Inputs may be any that keep to these rules, and one draw needn't show every extreme that they name: `group_ids`: exactly one micro-batch has group 1; the others have group 0.
All inputs are finite; a program needn't handle non-finite values.
Results may differ from a plain program's by a relative error of at most 0.012.
Values may be sent and summed in bfloat16 or wider, within the bound.
No kernel may reach another device: no remote copies, remote signals or barrier semaphores. Data moves between devices by JAX's collectives and lax.ppermute only.
A program may use at most 576 MiB of HBM per device.

v0:
```python
from functools import partial

import jax
import jax.numpy as jnp
from jax import lax
from jax.sharding import PartitionSpec as P

MAP_LOW = 11
POOL_LOW = 5


def from_behind(value, axis, steps):
    count = lax.axis_size(axis)
    pairs = [(source, (source + steps) % count) for source in range(count)]
    return lax.ppermute(value, axis, pairs)


def as_sent(value):
    return jax.tree.map(lambda a: a.astype(jnp.bfloat16) if a.dtype == jnp.float32 else a, value)


def valid_maps(group_ids, map_side, pooled_side):
    low_group = group_ids == 1
    extent = jnp.where(low_group, MAP_LOW, map_side)
    pooled_extent = jnp.where(low_group, POOL_LOW, pooled_side)
    valid_rows = (jnp.arange(map_side)[None, :] < extent[:, None]).astype(jnp.float32)
    pooled_rows = (jnp.arange(pooled_side)[None, :] < pooled_extent[:, None]).astype(jnp.float32)
    return (
        valid_rows[:, :, None] * valid_rows[:, None, :],
        pooled_rows[:, :, None] * pooled_rows[:, None, :],
    )


def pool_mean(source, pooled_side):
    running = None
    for tap_index in range(9):
        tap_row, tap_col = (tap_index // 3, tap_index % 3)
        window = source[
            :,
            :,
            tap_row : tap_row + 2 * pooled_side - 1 : 2,
            tap_col : tap_col + 2 * pooled_side - 1 : 2,
            :,
        ]
        running = window if running is None else running + window
    return running / 9.0


def pool_back(pool_grad, map_side):
    pooled_side = pool_grad.shape[2]
    spread = pool_grad / 9.0
    result = jnp.zeros(
        pool_grad.shape[:2] + (map_side, map_side) + pool_grad.shape[4:], jnp.float32
    )
    for tap_index in range(9):
        tap_row, tap_col = (tap_index // 3, tap_index % 3)
        result = result.at[
            :,
            :,
            tap_row : tap_row + 2 * pooled_side - 1 : 2,
            tap_col : tap_col + 2 * pooled_side - 1 : 2,
            :,
        ].add(spread)
    return result


def stitch_shape(weights, extra_dims):
    return weights.reshape((1,) + weights.shape[:2] + (1,) * extra_dims + weights.shape[2:])


def stitch_mix(weights, tower_maps):
    shaped = stitch_shape(weights, tower_maps.ndim - 3)
    return jnp.sum(shaped * tower_maps[:, None], axis=2)


def stitch_back(weights, tower_grads):
    shaped = stitch_shape(weights, tower_grads.ndim - 3)
    return jnp.sum(shaped * tower_grads[:, :, None], axis=1)


def stitch_weight_grad(tower_grads, tower_maps):
    extra_dims = tower_maps.ndim - 3
    summed_axes = (0,) + tuple(range(3, 3 + extra_dims))
    return jnp.sum(tower_grads[:, :, None] * tower_maps[:, None], axis=summed_axes)


def conv_taps(padded, tap_weights, map_side):
    running = None
    for tap_index in range(9):
        tap_row, tap_col = (tap_index // 3, tap_index % 3)
        window = padded[:, :, tap_row : tap_row + map_side, tap_col : tap_col + map_side, :]
        tap_term = jnp.einsum(
            "nthwc,tcd->nthwd",
            window,
            tap_weights[:, tap_index],
            preferred_element_type=jnp.float32,
        )
        running = tap_term if running is None else running + tap_term
    return running


def conv_weight_grad(padded, conv_grad, map_side):
    pieces = []
    for tap_index in range(9):
        tap_row, tap_col = (tap_index // 3, tap_index % 3)
        window = padded[:, :, tap_row : tap_row + map_side, tap_col : tap_col + map_side, :]
        pieces.append(
            jnp.einsum("nthwc,nthwd->tcd", window, conv_grad, preferred_element_type=jnp.float32)
        )
    stacked = jnp.stack(pieces, axis=1)
    return stacked.reshape(stacked.shape[0], 9 * stacked.shape[2], stacked.shape[3])


def conv_input_grad(conv_grad, tap_weights, map_side):
    channels = tap_weights.shape[2]
    result = jnp.zeros(conv_grad.shape[:2] + (map_side + 2, map_side + 2, channels), jnp.float32)
    for tap_index in range(9):
        tap_row, tap_col = (tap_index // 3, tap_index % 3)
        tap_term = jnp.einsum(
            "nthwd,tcd->nthwc",
            conv_grad,
            tap_weights[:, tap_index],
            preferred_element_type=jnp.float32,
        )
        result = result.at[:, :, tap_row : tap_row + map_side, tap_col : tap_col + map_side, :].add(
            tap_term
        )
    return result[:, :, 1 : map_side + 1, 1 : map_side + 1, :]


def on_device(
    conv_input,
    group_ids,
    conv_weight,
    conv_bias,
    conv_stitch,
    fc_weight,
    fc_bias,
    fc_stitch,
    cotangent,
):
    micro_count = conv_input.shape[0]
    images = conv_input.shape[1]
    map_side = conv_input.shape[3]
    pooled_side = (map_side - 3) // 2 + 1
    in_local = conv_input.shape[5]
    mp_count = lax.axis_size("mp")
    in_full = in_local * mp_count
    out_local = conv_weight.shape[2]
    out_full = out_local * mp_count
    hid_local = fc_weight.shape[2]
    dp_count = lax.axis_size("dp")
    dp_index = lax.axis_index("dp")
    conv_section = lax.axis_index("section") == 0
    feats = fc_weight.shape[1] * dp_count
    kernel_rows = conv_weight.shape[1] * dp_count
    conv_masks, pool_masks = valid_maps(group_ids, map_side, pooled_side)
    kernel = lax.all_gather(conv_weight, "dp", axis=1, tiled=True)
    bias_used, stitch_used = (conv_bias, conv_stitch)
    tap_weights = kernel.reshape(2, 9, in_full, out_local)
    matrix = lax.all_gather(fc_weight, "dp", axis=1, tiled=True)
    message_shape = (images, 2, pooled_side, pooled_side, out_local)

    def conv_forward(batch_index, full_maps):
        padded = jnp.pad(full_maps, ((0, 0), (0, 0), (1, 1), (1, 1), (0, 0)))
        conv_out = conv_taps(padded, tap_weights, map_side) + bias_used[None, :, None, None, :]
        pooled = (
            pool_mean(jax.nn.gelu(conv_out), pooled_side)
            * pool_masks[batch_index][None, None, :, :, None]
        )
        return (padded, conv_out, pooled, stitch_mix(stitch_used, pooled).astype(jnp.bfloat16))

    def conv_backward(batch_index, padded, conv_out, pooled, incoming):
        shared_grad = incoming.astype(jnp.float32)
        pooled_grad = (
            stitch_back(stitch_used, shared_grad) * pool_masks[batch_index][None, None, :, :, None]
        )
        stitch_grad = stitch_weight_grad(shared_grad, pooled)
        act_grad = pool_back(pooled_grad, map_side)
        conv_grad = jax.vjp(jax.nn.gelu, conv_out)[1](act_grad)[0].astype(jnp.bfloat16)
        bias_grad = jnp.sum(conv_grad.astype(jnp.float32), axis=(0, 2, 3))
        kernel_grad = conv_weight_grad(padded, conv_grad, map_side)
        partial_in = conv_input_grad(conv_grad, tap_weights, map_side)
        return (kernel_grad, bias_grad, stitch_grad, partial_in)

    def back_zeros():
        return jnp.zeros((images, 2, map_side, map_side, in_full), jnp.float32)

    def conv_tick(step_index, operands):
        carried, incoming, full_maps = operands
        carried = dict(carried)
        back_out = None
        message = None
        if step_index >= 2:
            finished = step_index - 2
            slot_index = finished % 2
            kernel_grad, bias_grad, stitch_grad, back_out = conv_backward(
                finished,
                carried["kept_padded"][slot_index],
                carried["kept_conv"][slot_index],
                carried["kept_pooled"][slot_index],
                incoming,
            )
            carried["conv_grad"] = carried["conv_grad"] + kernel_grad
            carried["conv_bias"] = carried["conv_bias"] + bias_grad
            carried["conv_stitch"] = carried["conv_stitch"] + stitch_grad
        if step_index < micro_count:
            slot_index = step_index % 2
            padded, conv_out, pooled, message = conv_forward(step_index, full_maps)
            carried["kept_padded"] = carried["kept_padded"].at[slot_index].set(padded)
            carried["kept_conv"] = carried["kept_conv"].at[slot_index].set(conv_out)
            carried["kept_pooled"] = carried["kept_pooled"].at[slot_index].set(pooled)
        return (carried, back_out, message)

    def spare_tick(step_index, operands):
        back_out = back_zeros() if step_index >= 2 else None
        message = jnp.zeros(message_shape, jnp.bfloat16) if step_index < micro_count else None
        return (operands[0], back_out, message)

    carried = {
        "kept_padded": jnp.zeros((2, images, 2, map_side + 2, map_side + 2, in_full), jnp.bfloat16),
        "kept_conv": jnp.zeros((2, images, 2, map_side, map_side, out_local), jnp.float32),
        "kept_pooled": jnp.zeros((2, images, 2, pooled_side, pooled_side, out_local), jnp.float32),
        "conv_grad": jnp.zeros((2, kernel_rows, out_local), jnp.float32),
        "conv_bias": jnp.zeros((2, out_local), jnp.float32),
        "conv_stitch": jnp.zeros((2, 2, out_local), jnp.float32),
    }
    input_grads = jnp.zeros((2, micro_count, images, map_side, map_side, in_local), jnp.bfloat16)
    fc_grad = jnp.zeros(matrix.shape, jnp.float32)
    fc_bias_part = jnp.zeros((2, hid_local), jnp.float32)
    fc_stitch_part = jnp.zeros((2, 2, hid_local), jnp.float32)
    all_outputs = jnp.zeros((2, micro_count, images, hid_local), jnp.bfloat16)
    incoming = jnp.zeros(message_shape, jnp.bfloat16)
    for step_index in range(micro_count + 2):
        full_maps = None
        if step_index < micro_count:
            mask_map = conv_masks[step_index][None, None, :, :, None]
            local_maps = conv_input[step_index] * mask_map.astype(jnp.bfloat16)
            full_maps = lax.all_gather(local_maps, "mp", axis=4, tiled=True)
        carried, back_out, conv_message = lax.cond(
            conv_section,
            partial(conv_tick, step_index),
            partial(spare_tick, step_index),
            (carried, incoming, full_maps),
        )
        if step_index >= 2:
            finished = step_index - 2
            summed_in = lax.psum_scatter(back_out, "mp", scatter_dimension=4, tiled=True)
            grad_in = (summed_in * conv_masks[finished][None, None, :, :, None]).astype(
                jnp.bfloat16
            )
            input_grads = input_grads.at[:, finished].set(jnp.moveaxis(grad_in, 1, 0))
        fc_message = None
        if 1 <= step_index <= micro_count:
            finished = step_index - 1
            fc_full_maps = lax.all_gather(incoming, "mp", axis=4, tiled=True)
            flat_rows = fc_full_maps.reshape(images, 2, feats)
            pre_act = (
                jnp.einsum("ntf,tfk->ntk", flat_rows, matrix, preferred_element_type=jnp.float32)
                + fc_bias[None]
            )
            cot_rows = lax.dynamic_slice_in_dim(
                cotangent[finished], dp_index * images, images, 0
            ).astype(jnp.float32)
            activated, pull_back = jax.vjp(jax.nn.gelu, pre_act)
            own_out = stitch_mix(fc_stitch, activated)
            pre_grad = pull_back(stitch_back(fc_stitch, cot_rows))[0].astype(jnp.bfloat16)
            matrix_grad = jnp.einsum(
                "ntf,ntk->tfk", flat_rows, pre_grad, preferred_element_type=jnp.float32
            )
            row_grads = jnp.einsum(
                "ntk,tfk->ntf", pre_grad, matrix, preferred_element_type=jnp.float32
            )
            fc_bias_grad = jnp.sum(pre_grad.astype(jnp.float32), axis=0)
            fc_stitch_grad = stitch_weight_grad(cot_rows, activated)
            shaped_grads = row_grads.reshape(images, 2, pooled_side, pooled_side, out_full)
            summed = lax.psum_scatter(shaped_grads, "mp", scatter_dimension=4, tiled=True)
            matrix_grad, bias_grad, stitch_grad, own_out, fc_message = (
                matrix_grad,
                fc_bias_grad,
                fc_stitch_grad,
                own_out,
                summed.astype(jnp.bfloat16),
            )
            fc_grad = fc_grad + matrix_grad
            fc_bias_part = fc_bias_part + bias_grad
            fc_stitch_part = fc_stitch_part + stitch_grad
            all_outputs = all_outputs.at[:, finished].set(
                jnp.moveaxis(own_out, 1, 0).astype(jnp.bfloat16)
            )
        if step_index <= micro_count:
            if conv_message is None:
                message = fc_message
            elif fc_message is None:
                message = conv_message
            else:
                message = jnp.where(conv_section, conv_message, fc_message)
            incoming = from_behind(message, "section", 1)
    kernel_part, conv_bias_part, conv_stitch_part = (
        carried["conv_grad"],
        carried["conv_bias"],
        carried["conv_stitch"],
    )
    conv_grad_rows = jax.tree.map(
        lambda part: part.astype(jnp.float32),
        lax.psum_scatter(as_sent(kernel_part), "dp", scatter_dimension=1, tiled=True),
    )
    fc_grad_rows = lax.psum_scatter(
        fc_grad.astype(jnp.bfloat16), "dp", scatter_dimension=1, tiled=True
    ).astype(jnp.float32)
    fc_share = jnp.float32(1.0)
    conv_bias_sum, conv_stitch_sum, fc_bias_sum, fc_stitch_sum = lax.psum(
        (conv_bias_part, conv_stitch_part, fc_bias_part * fc_share, fc_stitch_part * fc_share), "dp"
    )
    arrived = (
        lax.all_to_all(input_grads, "section", split_axis=0, concat_axis=0, tiled=True),
        lax.all_to_all(
            as_sent(conv_grad_rows), "section", split_axis=0, concat_axis=0, tiled=True
        ).astype(conv_grad_rows.dtype),
        lax.all_to_all(
            conv_bias_sum.astype(jnp.bfloat16), "section", split_axis=0, concat_axis=0, tiled=True
        ).astype(conv_bias_sum.dtype),
        lax.all_to_all(
            conv_stitch_sum.astype(jnp.bfloat16), "section", split_axis=0, concat_axis=0, tiled=True
        ).astype(conv_stitch_sum.dtype),
        lax.all_to_all(all_outputs, "section", split_axis=0, concat_axis=0, tiled=True),
        lax.all_to_all(
            fc_grad_rows.astype(jnp.bfloat16), "section", split_axis=0, concat_axis=0, tiled=True
        ).astype(fc_grad_rows.dtype),
        lax.all_to_all(
            fc_bias_sum.astype(jnp.bfloat16), "section", split_axis=0, concat_axis=0, tiled=True
        ).astype(fc_bias_sum.dtype),
        lax.all_to_all(
            fc_stitch_sum.astype(jnp.bfloat16), "section", split_axis=0, concat_axis=0, tiled=True
        ).astype(fc_stitch_sum.dtype),
    )
    input_grad = arrived[0][0][:, :, None]
    outputs = arrived[4][1][:, :, None]
    return (
        outputs,
        input_grad,
        arrived[1][0:1],
        arrived[2][0:1],
        arrived[3][0:1],
        arrived[5][1:2],
        arrived[6][1:2],
        arrived[7][1:2],
    )


def solution(mesh):
    placed = (
        P(None, "dp", None, None, None, "mp"),
        P(),
        P(None, "dp", "mp"),
        P(None, "mp"),
        P(None, None, "mp"),
        P(None, "dp", "mp"),
        P(None, "mp"),
        P(None, None, "mp"),
        P(None, None, None, "mp"),
    )
    return jax.shard_map(
        on_device,
        mesh=mesh,
        in_specs=placed,
        out_specs=(
            P(None, "dp", "section", "mp"),
            P(None, "dp", "section", None, None, "mp"),
            P("section", "dp", "mp"),
            P("section", "mp"),
            P("section", None, "mp"),
            P("section", "dp", "mp"),
            P("section", "mp"),
            P("section", None, "mp"),
        ),
        check_vma=False,
    )
```

profile of v0, /device:TPU:8, one launch (start us, length us, event | category | flops | bytes accessed | tf_op | source)
XLA Modules:
  0.0 3691.5 jit_solution(17078878517419549728)
XLA Ops:
  13.9 16.1 copy.727
  31.4 11.9 bitcast_multiply_fusion.7
  44.1 16.8 copy.728
  60.9 12.0 bitcast_multiply_fusion.6
  74.6 33.5 all_gather.31
  112.9 131.4 %all-gather.6.cloned.1.call-done = bf16[16,2,13,13,384]{0,1,3,2,4:T(2,128)(2,1)} async-done(((bf16[16,2,13,13,96]{0,1,3,2,4:T(2,128)(2,1)}), bf16[16,2,13,13,384]{0,1,3,2,4:T(2,128)(2,1)}) %all-gather.6.cloned.1.call-update) | async-done | bytes 4153360 | tf_op jit(solution)/shard_map/all_gather | solution.py:239
  244.3 120.8 %conditional.6 = (f32[2,16,2,13,13,64]{5,1,4,3,2,0:T(8,128)}, bf16[2,16,2,15,15,384]{5,1,4,3,2,0:T(8,128)(2,1)}, f32[2,16,2,6,6,64]{5,1,4,3,2,0:T(8,128)S(1)}, bf16[16,2,6,6,64]{4,0,3,2,1:T(8,128)(2,1)}) conditional(s32[]{:T(128)} %convert_element_type.257, () %tuple.280, (bf16[16,2,13,13,384]{0,1,3,2,4:T(2,128)(2,1)}, ...), branch_computations={%region_0.1_spmd, %region_1.3_spmd} | conditional | flops 2160683008 | bytes 137218720 | solution.py:240
  244.4 72.2 %copy.568 = bf16[16,2,13,13,384]{4,0,3,2,1:T(8,128)(2,1)} copy(bf16[16,2,13,13,384]{0,1,3,2,4:T(2,128)(2,1)} %get-tuple-element.1294) | data formatting | bytes 8306688 | tf_op jit(solution)/shard_map
  378.3 38.3 %all_gather.32 = bf16[16,2,6,6,256]{0,1,3,2,4:T(2,128)(2,1)} all-gather(bf16[16,2,6,6,64]{0,1,3,2,4:T(2,128)(2,1)} %copy.570), channel_id=1, replica_groups=mesh['section'=2,'dp'=4,'mp'=4] {'mp'}, dimensions={4}, use_global_device_ids=true | all-gather | bytes 737280 | tf_op jit(solution)/shard_map/all_gather | solution.py:256
  428.1 447.4 %all-gather.8.cloned.1.call-done = bf16[2,9216,1024]{2,1,0:T(8,128)(2,1)} async-done(((bf16[2,2304,1024]{2,1,0:T(8,128)(2,1)}), bf16[2,9216,1024]{2,1,0:T(8,128)(2,1)}) %all-gather.8.cloned.1.call-update) | async-done | bytes 37748752 | tf_op jit(solution)/shard_map/all_gather | solution.py:161
  875.4 17.0 multiply_multiply_fusion.27
  894.5 21.4 convolution_bitcast_fusion.7
  917.6 26.8 copy.703
  944.4 20.7 reshape.3079
  965.2 16.1 copy.729
  981.3 11.9 bitcast_multiply_fusion.5
  993.2 84.6 %all-gather.10.cloned.1.call-done = bf16[16,2,13,13,384]{0,1,3,2,4:T(2,128)(2,1)} async-done(((bf16[16,2,13,13,96]{0,1,3,2,4:T(2,128)(2,1)}), bf16[16,2,13,13,384]{0,1,3,2,4:T(2,128)(2,1)}) %all-gather.10.cloned.1.call-update) | async-done | bytes 4153360 | tf_op jit(solution)/shard_map/all_gather | solution.py:239
  1077.9 110.7 %conditional.7 = (f32[2,16,2,13,13,64]{5,1,4,3,2,0:T(8,128)}, bf16[2,16,2,15,15,384]{5,1,4,3,2,0:T(8,128)(2,1)}, f32[2,16,2,6,6,64]{5,1,4,3,2,0:T(8,128)}, bf16[16,2,6,6,64]{4,3,2,0,1:T(8,128)(2,1)S(1)}) conditional(s32[]{:T(128)} %convert_element_type.257, (f32[2,16,2,13,13,64]{5,1,4,3,2,0:T(8,128)}, bf16[2,16,2,15,15,384]{5,1,4,3,2,0:T(8,128)(2,1)}, ...), branch_computations={%region_4.5_spmd, %region_5.0_spmd} | conditional | flops 2160019456 | bytes 119065072 | solution.py:240
  1077.9 72.6 %copy.573 = bf16[16,2,13,13,384]{4,0,3,2,1:T(8,128)(2,1)} copy(bf16[16,2,13,13,384]{0,1,3,2,4:T(2,128)(2,1)} %get-tuple-element.1299) | data formatting | bytes 8306688 | tf_op jit(solution)/shard_map
  1212.3 55.9 %all_gather.35 = bf16[16,2,6,6,256]{0,1,3,2,4:T(2,128)(2,1)} all-gather(bf16[16,2,6,6,64]{0,1,3,2,4:T(2,128)(2,1)S(1)} %copy.577), channel_id=1, replica_groups=mesh['section'=2,'dp'=4,'mp'=4] {'mp'}, dimensions={4}, use_global_device_ids=true | all-gather | bytes 737280 | tf_op jit(solution)/shard_map/all_gather | solution.py:256
  1277.8 14.9 multiply_multiply_fusion.26
  1294.7 15.9 convolution_bitcast_fusion.6
  1312.4 26.8 copy.705
  1339.2 20.7 reshape.3081
  1360.2 16.7 copy.730
  1376.9 11.9 bitcast_multiply_fusion.4
  1390.1 238.5 %conditional.8 = (f32[2,64]{1,0:T(2,128)S(1)}, f32[2,3456,64]{1,2,0:T(8,128)}, f32[2,2,64]{2,1,0:T(2,128)S(1)}, f32[2,16,2,13,13,64]{5,1,4,3,2,0:T(8,128)}, bf16...) conditional(s32[]{:T(128)} %convert_element_type.257, ...), branch_computations={%region_10.11_spmd, %region_11.26_spmd} | conditional | flops 6972377600 | bytes 440872224 | solution.py:240
  1390.3 72.4 %copy.502 = bf16[16,2,13,13,384]{4,0,3,2,1:T(8,128)(2,1)} copy(bf16[16,2,13,13,384]{0,1,3,2,4:T(2,128)(2,1)} %get-tuple-element.1316) | data formatting | bytes 8306688 | tf_op jit(solution)/shard_map
  1653.7 30.0 all_gather.37
  1693.2 14.5 multiply_multiply_fusion.25
  1709.9 15.9 convolution_bitcast_fusion.5
  1727.6 26.8 copy.707
  1754.4 20.6 reshape.3083
  1775.1 227.5 %conditional.9 = (f32[2,64]{1,0:T(2,128)S(1)}, f32[2,3456,64]{1,2,0:T(8,128)}, f32[2,2,64]{2,1,0:T(2,128)S(1)}, f32[2,16,2,13,13,64]{5,1,4,3,2,0:T(8,128)}, bf16...) conditional(s32[]{:T(128)} %convert_element_type.257, ...), branch_computations={%region_29.30_spmd, %region_30.45_spmd} | conditional | flops 6972820480 | bytes 424066848 | solution.py:240
  1775.5 71.1 %copy.524 = bf16[16,2,13,13,384]{4,0,3,2,1:T(8,128)(2,1)} copy(bf16[16,2,13,13,384]{0,1,3,2,4:T(2,128)(2,1)} %get-tuple-element.1328) | data formatting | bytes 8306688 | tf_op jit(solution)/shard_map
  2027.6 30.0 all_gather.39
  2067.2 14.5 multiply_multiply_fusion.24
  2083.8 15.9 convolution_bitcast_fusion.4
  2101.5 26.8 copy.715
  2128.3 20.6 reshape.3091
  2149.1 25.1 reduce-scatter.43.cloned.1.call-done
  2187.7 117.7 %conditional.10 = (f32[2,64]{1,0:T(2,128)S(1)}, f32[2,3456,64]{1,2,0:T(8,128)}, f32[2,2,64]{2,1,0:T(2,128)S(1)}, f32[16,2,13,13,384]{4,0,3,2,1:T(8,128)}) conditional(s32[]{:T(128)} %convert_element_type.257, (f32[2,64]{1,0:T(2,128)S(1)}, f32[2,3456,64]{1,2,0:T(8,128)}, f32[2,2,64]{2,1,0:T(2,128)S(1)}) %tuple.288, (f32[2,2,64]{2,1,0:T(2,128)S(1)}, ...), branch_computations={%region_50.51_spmd, %region_51.65_spmd} | conditional | flops 4812801024 | bytes 279742784 | solution.py:240
  2305.4 118.1 %conditional.11 = (f32[2,64]{1,0:T(2,128)S(1)}, f32[2,3456,64]{1,2,0:T(8,128)}, f32[2,2,64]{2,1,0:T(2,128)S(1)}, f32[16,2,13,13,384]{4,0,3,2,1:T(8,128)}) conditional(s32[]{:T(128)} %convert_element_type.257, (f32[2,64]{1,0:T(2,128)S(1)}, f32[2,3456,64]{1,2,0:T(8,128)}, f32[2,2,64]{2,1,0:T(2,128)S(1)}) %tuple.290, (f32[2,2,64]{2,1,0:T(2,128)S(1)}, ...), branch_computations={%region_68.69_spmd, %region_69.83_spmd} | conditional | flops 4812801024 | bytes 279742784 | solution.py:240
  2429.2 43.0 %copy.709 = f32[16,2,13,13,384]{0,3,2,1,4:T(8,128)} copy(f32[16,2,13,13,384]{4,0,3,2,1:T(8,128)} %get-tuple-element.944) | data formatting | bytes 16613376
  2472.2 42.3 %reshape.3085 = f32[384,5408]{1,0:T(8,128)} reshape(f32[384,2,13,13,16]{4,3,2,1,0:T(8,128)} %bitcast.517) | data formatting | bytes 16613376
  2514.6 44.1 %copy.711 = f32[16,2,13,13,384]{0,3,2,1,4:T(8,128)} copy(f32[16,2,13,13,384]{4,0,3,2,1:T(8,128)} %get-tuple-element.945) | data formatting | bytes 16613376
  2558.7 42.6 %reshape.3087 = f32[384,5408]{1,0:T(8,128)} reshape(f32[384,2,13,13,16]{4,3,2,1,0:T(8,128)} %bitcast.520) | data formatting | bytes 16613376
  2601.4 44.0 %copy.713 = f32[16,2,13,13,384]{0,3,2,1,4:T(8,128)} copy(f32[16,2,13,13,384]{4,0,3,2,1:T(8,128)} %get-tuple-element.952) | data formatting | bytes 16613376
  2645.4 42.6 %reshape.3089 = f32[384,5408]{1,0:T(8,128)} reshape(f32[384,2,13,13,16]{4,3,2,1,0:T(8,128)} %bitcast.523) | data formatting | bytes 16613376
  2689.0 31.6 fusion.553
  2720.6 43.1 %copy.717 = f32[16,2,13,13,384]{0,3,2,1,4:T(8,128)} copy(f32[16,2,13,13,384]{4,0,3,2,1:T(8,128)} %get-tuple-element.956) | data formatting | bytes 16613376
  2763.7 42.3 %reshape.3093 = f32[384,5408]{1,0:T(8,128)} reshape(f32[384,2,13,13,16]{4,3,2,1,0:T(8,128)} %bitcast.529) | data formatting | bytes 16613376
  2807.1 32.8 fusion.554
  2839.9 27.9 fusion.555
  2867.9 81.0 %add_convert_fusion = bf16[2,9216,1024]{2,1,0:T(8,128)(2,1)} fusion(f32[2,9216,1024]{2,1,0:T(8,128)} %fusion.555, f32[2,9216,1024]{2,1,0:T(8,128)} %fusion.553, f32[2,9216,1024]{2,1,0:T(8,128)} %fusion.554, bf16[16,2,9216]{2,0,1:T(8,128)(2,1)S(1)} %copy-done.14, bf16[16,2,1024]{2,0,1:T(8,128)(2,1)S(1)} %copy-done.42), kind=kOutput, calls=%fused_computation.634 | convolution fusion | flops 679477248 | bytes 264896512 | tf_op jit(solution)/shard_map/ntf,ntk->tfk/dot_general | solution.py:268
  2954.2 21.5 all-reduce.13
  2980.5 11.6 reshape.3086
  2992.1 13.0 copy.710
  3031.7 13.2 copy.712
  3061.4 13.0 copy.714
  3090.7 13.2 copy.718
  3114.7 69.8 %all_to_all.48 = bf16[2,4,16,13,13,96]{5,2,4,3,1,0:T(8,128)(2,1)} all-to-all(bf16[2,4,16,13,13,96]{5,2,4,3,1,0:T(8,128)(2,1)} %copy.603), channel_id=1, replica_groups=mesh['section'=2,'dp'=4,'mp'=4] {'section'}, dimensions={0} | all-to-all | bytes 8306688 | tf_op jit(solution)/shard_map/all_to_all | solution.py:316
  3184.5 381.7 %reduce-scatter.29.cloned.1.call-done = bf16[2,2304,1024]{2,1,0:T(8,128)(2,1)} async-done(((bf16[2,9216,1024]{2,1,0:T(8,128)(2,1)}), bf16[2,2304,1024]{2,1,0:T(8,128)(2,1)}) %reduce-scatter.29.cloned.1.call-update) | async-done | bytes 9437200 | tf_op jit(solution)/shard_map/reduce_scatter | solution.py:308
  3580.9 96.5 %all-to-all-done.5 = bf16[2,2304,1024]{2,1,0:T(8,128)(2,1)} async-done(((bf16[2,2304,1024]{2,1,0:T(8,128)(2,1)}), bf16[2,2304,1024]{2,1,0:T(8,128)(2,1)}, u32[]{:S(2)}, u32[]{:S(2)}) %all-to-all-start.5) | async-done | bytes 9437216 | tf_op jit(solution)/shard_map/all_to_all | solution.py:327
  (631 shorter events, 923.2 us)
Async XLA Ops:
  7.2 237.1 %all-gather.6.cloned.1.call-start = ((), (), s32[]{:S(2)}) async-start(), calls=%async_computation.18 | async-start | bytes 41533440 | tf_op jit(solution)/shard_map/all_gather | solution.py:239
  13.9 16.1 copy-start.87
  43.3 832.1 %all-gather.8.cloned.1.call-start = ((), (), s32[]{:S(2)}) async-start(), calls=%async_computation.19 | async-start | bytes 47185920 | tf_op jit(solution)/shard_map/all_gather | solution.py:161
  44.0 1033.8 %all-gather.10.cloned.1.call-start = ((), (), s32[]{:S(2)}) async-start(), calls=%async_computation.20 | async-start | bytes 41533440 | tf_op jit(solution)/shard_map/all_gather | solution.py:239
  72.9 1115.7 %reduce-scatter.31.cloned.1.call-start = ((), (), s32[]{:S(2)}) async-start(), calls=%async_computation.24 | async-start | bytes 1474560
  74.6 169.7 %copy-start.63 = (f32[2,2,64]{2,1,0:T(2,128)S(1)}, f32[2,2,64]{2,1,0:T(2,128)}, u32[]{:S(2)}) copy-start(f32[2,2,64]{2,1,0:T(2,128)} %param.137) | copy-start | bytes 3076
  74.6 169.7 %copy-start.66 = (f32[2,64]{1,0:T(2,128)S(1)}, f32[2,64]{1,0:T(2,128)}, u32[]{:S(2)}) copy-start(f32[2,64]{1,0:T(2,128)} %param.136) | copy-start | bytes 1540
  112.9 131.4 %copy-start.61 = (f32[4,6,6]{2,1,0:T(8,128)}, f32[4,6,6]{2,1,0:T(8,128)S(1)}, u32[]{:S(2)}) copy-start(f32[4,6,6]{2,1,0:T(8,128)S(1)} %broadcast_multiply_fusion.1) | copy-start | bytes 1732
  365.1 51.5 %copy-start.17 = (f32[2,16,2,6,6,64]{5,1,4,3,2,0:T(8,128)}, f32[2,16,2,6,6,64]{5,1,4,3,2,0:T(8,128)S(1)}, u32[]{:S(2)}) copy-start(f32[2,16,2,6,6,64]{5,1,4,3,2,0:T(8,128)S(1)} %get-tuple-element.931) | copy-start | bytes 1769476
  365.1 9.6 collective-permute-start
  416.6 458.9 %copy-start.45 = (f32[2,1024]{1,0:T(2,128)S(1)}, f32[2,1024]{1,0:T(2,128)}, u32[]{:S(2)}) copy-start(f32[2,1024]{1,0:T(2,128)} %param.139) | copy-start | bytes 24580
  428.0 464.4 %copy-start.7 = (bf16[16,2,9216]{2,0,1:T(8,128)(2,1)}, bf16[16,2,9216]{2,0,1:T(8,128)(2,1)S(1)}, u32[]{:S(2)}) copy-start(bf16[16,2,9216]{2,0,1:T(8,128)(2,1)S(1)} %reshape.2751) | copy-start | bytes 1769476
  428.1 464.4 %copy-start.51 = (f32[2,2,1024]{2,1,0:T(2,128)S(1)}, f32[2,2,1024]{2,1,0:T(2,128)}, u32[]{:S(2)}) copy-start(f32[2,2,1024]{2,1,0:T(2,128)} %param.140) | copy-start | bytes 49156
  944.4 20.8 copy-start.28
  965.1 423.8 %all-gather.12.cloned.1.call-start = ((), (), s32[]{:S(2)}) async-start(), calls=%async_computation.21 | async-start | bytes 41533440 | tf_op jit(solution)/shard_map/all_gather | solution.py:239
  965.2 16.1 copy-start.80
  993.2 84.7 %copy-start.64 = (f32[2,2,64]{2,1,0:T(2,128)S(1)}, f32[2,2,64]{2,1,0:T(2,128)}, u32[]{:S(2)}) copy-start(f32[2,2,64]{2,1,0:T(2,128)} %param.137) | copy-start | bytes 3076
  993.2 84.7 %copy-start.67 = (f32[2,64]{1,0:T(2,128)S(1)}, f32[2,64]{1,0:T(2,128)}, u32[]{:S(2)}) copy-start(f32[2,64]{1,0:T(2,128)} %param.136) | copy-start | bytes 1540
  993.2 635.5 %reduce-scatter.33.cloned.1.call-start = ((), (), s32[]{:S(2)}) async-start(), calls=%async_computation.25 | async-start | bytes 1474560
  1200.0 11.2 collective-permute-start.1
  1211.2 57.1 %copy-start.29 = (bf16[16,2,6,6,64]{4,3,2,0,1:T(8,128)(2,1)}, bf16[16,2,6,6,64]{4,3,2,0,1:T(8,128)(2,1)S(1)}, u32[]{:S(2)}) copy-start(bf16[16,2,6,6,64]{4,3,2,0,1:T(8,128)(2,1)S(1)} %collective-permute-done.1) | copy-start | bytes 442372
  1277.7 14.9 copy-start.9
  1277.7 14.9 copy-start.52
  1339.2 20.9 copy-start.27
  1359.9 415.2 %all-gather.14.cloned.1.call-start = ((), (), s32[]{:S(2)}) async-start(), calls=%async_computation.22 | async-start | bytes 41533440 | tf_op jit(solution)/shard_map/all_gather | solution.py:239
  1360.2 16.7 copy-start.79
  1388.9 613.8 %reduce-scatter.35.cloned.1.call-start = ((), (), s32[]{:S(2)}) async-start(), calls=%async_computation.26 | async-start | bytes 1474560
  1462.9 22.9 copy-start.25
  1562.4 10.8 copy-start.3
  1628.6 11.2 copy-start.19
  1640.9 11.6 collective-permute-start.2
  1652.5 31.1 copy-start.31
  1683.7 9.5 copy-start.46
  1693.2 14.6 copy-start.11
  1693.2 14.6 copy-start.53
  1754.4 20.7 copy-start.20
  1775.0 399.3 %reduce-scatter.43.cloned.1.call-start = ((), (), s32[]{:S(2)}) async-start(), calls=%async_computation.30 | async-start | bytes 1474560
  1846.9 22.9 copy-start.23
  2002.6 11.4 copy-start.21
  2015.0 11.4 collective-permute-start.3
  2026.4 31.2 copy-start.33
  2057.6 9.5 copy-start.47
  2067.1 14.6 copy-start.13
  2067.1 14.6 copy-start.54
  2148.8 829.2 %reduce-scatter.47.cloned.1.call-start = ((), (), s32[]{:S(2)}) async-start(), calls=%async_computation.32 | async-start | bytes 1105920
  2180.0 7.7 copy-start.22
  2180.0 7.7 copy-start.34
  2186.2 119.2 %collective-permute-start.4 = (bf16[16,2,6,6,64]{4,3,2,0,1:T(8,128)(2,1)}, bf16[16,2,6,6,64]{4,3,2,0,1:T(8,128)(2,1)}, u32[]{:S(2)}, u32[]{:S(2)}) collective-permute-start(bf16[16,2,6,6,64]{4,3,2,0,1:T(8,128)(2,1)} %copy.716), channel_id=1, source_target_pairs={{0,16},{16,0},{1,17},{17,1},{2,18},{18,2},{3,19},{19,3},{4,20},{20... | collective-permute-start | bytes 442376 | tf_op jit(solution)/shard_map/ppermute | solution.py:15
  2429.1 551.3 %reduce-scatter.37.cloned.1.call-start = ((), (), s32[]{:S(2)}) async-start(), calls=%async_computation.27 | async-start | bytes 10567680
  2514.5 505.6 %reduce-scatter.39.cloned.1.call-start = ((), (), s32[]{:S(2)}) async-start(), calls=%async_computation.28 | async-start | bytes 10567680
  2601.3 448.4 %reduce-scatter.41.cloned.1.call-start = ((), (), s32[]{:S(2)}) async-start(), calls=%async_computation.29 | async-start | bytes 10567680
  2688.0 391.1 %reduce-scatter.45.cloned.1.call-start = ((), (), s32[]{:S(2)}) async-start(), calls=%async_computation.31 | async-start | bytes 10567680
  2806.0 33.9 copy-start.12
  2806.1 33.9 copy-start.40
  2806.1 760.1 %reduce-scatter.29.cloned.1.call-start = ((), (), s32[]{:S(2)}) async-start(), calls=%async_computation.23 | async-start | bytes 47185920 | tf_op jit(solution)/shard_map/reduce_scatter | solution.py:308
  2839.9 27.9 copy-start.14
  2839.9 27.9 copy-start.42
  2950.6 54.6 %all-to-all-start = ((bf16[2,4,16,1024]{3,2,1,0:T(8,128)(2,1)}), bf16[2,4,16,1024]{3,2,1,0:T(8,128)(2,1)S(1)}, u32[]{:S(2)}, u32[]{:S(2)}) async-start(bf16[2,4,16,1024]{3,2,1,0:T(8,128)(2,1)} %copy.597), calls=%async_computation | async-start | bytes 524288 | tf_op jit(solution)/shard_map/all_to_all | solution.py:326
  3005.2 6.9 all-to-all-start.3
  3012.0 32.9 all-to-all-start.4
  3044.9 29.5 all-to-all-start.6
  3074.4 29.5 all-to-all-start.7
  3103.9 10.7 all-to-all-start.2
  3566.2 111.3 %all-to-all-start.5 = ((bf16[2,2304,1024]{2,1,0:T(8,128)(2,1)}), bf16[2,2304,1024]{2,1,0:T(8,128)(2,1)}, u32[]{:S(2)}, u32[]{:S(2)}) async-start(bf16[2,2304,1024]{2,1,0:T(8,128)(2,1)} %reduce-scatter.29.cloned.1.call-done), calls=%async_computation.6 | async-start | bytes 18874368 | tf_op jit(solution)/shard_map/all_to_all | solution.py:327
  (51 other events, 151.3 us)
Sparse Core Ops, SparseCore 0:
  43.4 200.8 all-gather.5
  245.9 629.5 all-gather.7
  877.0 200.8 all-gather.9
  1080.3 25.7 reduce-scatter.30
  1108.1 224.9 all-gather.11
  1360.0 25.0 reduce-scatter.32
  1389.0 199.0 all-gather.13
  1775.1 25.2 reduce-scatter.34
  2149.0 25.2 reduce-scatter.42
  2429.3 21.6 reduce-scatter.46
  2514.7 71.2 reduce-scatter.36
  2601.4 71.1 reduce-scatter.38
  2688.1 71.0 reduce-scatter.40
  2806.2 72.2 reduce-scatter.44
  2949.2 616.9 reduce-scatter.28
where the time goes:
time: 3730 us; the launch traced here: 3690 us
  local copies, waits for them, and re-layouts  1240 us (33%)
  waiting for transfers between devices  1210 us (32%)
  matrix products  557 us (15%)
  other arithmetic  358 us (10%)
  blocking collectives  279 us (7%)
    unnamed x179, local copies, waits for them, and re-layouts  764 us
    all_gather x1, waiting for transfers between devices, on_device(): matrix = lax.all_gather(fc_weight, 'dp', axis=1, tiled=True)  447 us
    reduce_scatter x1, waiting for transfers between devices, on_device(): lax.psum_scatter(fc_grad.astype(jnp.bfloat16), 'dp', scatter_dimension=1,...  382 us
    another operation x28, local copies, waits for them, and re-layouts  315 us
    scatter-add x36, other arithmetic, pool_back(): result = result.at[:, :, tap_row:tap_row + 2 * pooled_side - 1:2, tap_col...  242 us
    all_gather x4, waiting for transfers between devices, on_device(): full_maps = lax.all_gather(local_maps, 'mp', axis=4, tiled=True)  216 us
    dot_general x4, matrix products, on_device(): jnp.einsum('ntf,ntk->tfk', flat_rows, pre_grad, preferred_element_type=jn...  173 us
    all_gather x4, blocking collectives, on_device(): fc_full_maps = lax.all_gather(incoming, 'mp', axis=4, tiled=True)  154 us
  transfers between devices with their start and end apart: 27, of which 11 were waited for; matrix products, arithmetic and copies ran while one was open for 50% of the time, Pallas kernels for 0%

commit v1 on v0

v1 whole, which is shorter than its diff:
```python
from functools import partial

import jax
import jax.numpy as jnp
from jax import lax
from jax.experimental import pallas as pl
from jax.experimental.pallas import tpu as pltpu
from jax.sharding import PartitionSpec as P


MAP_LOW = 11
POOL_LOW = 5
SIDE = 13
POOLED = 6
CELLS = SIDE * SIDE
PLACES = POOLED * POOLED
IMG = 16
BLK = 96
GROUP = 43
WIRE = (GROUP * IMG, 4 * BLK)
BIG = 32 << 20
MID = 20 << 20
SMALL = 8 << 20
F32 = jnp.float32
BF16 = jnp.bfloat16


def swap(value, axis, bit):
    count = lax.axis_size(axis)
    return lax.ppermute(value, axis, [(i, i ^ bit) for i in range(count)])


def sum_over(value, axis):
    bit = 1
    while bit < lax.axis_size(axis):
        value = value + swap(value, axis, bit)
        bit *= 2
    return value


def relative(value, index, axis=0):
    return jnp.concatenate(
        [lax.dynamic_slice_in_dim(value, index ^ k, 1, axis) for k in range(4)], axis
    )


def lane_index(rows=IMG):
    return lax.broadcasted_iota(jnp.int32, (rows, 128), 1)


def join4(parts, lane):
    last = parts[3]
    return [jnp.where(lane < BLK, parts[j], pltpu.roll(last, 96 - 32 * j, 1)) for j in range(3)]


def last_part(tiles, lane):
    a, b, c = [pltpu.roll(tiles[j], 32 + 32 * j, 1) for j in range(3)]
    return jnp.where(lane < 32, a, jnp.where(lane < 64, b, c))


def tiles_of(row):
    return [row[:, 0:128], row[:, 128:256], row[:, 256:384]]


def exchange(rows, lane):
    rows = [tiles_of(row) for row in rows]
    out = []
    for k in range(3):
        last = rows[3][k]
        out.append(
            [
                jnp.where(lane < BLK, rows[j][k], pltpu.roll(last, 96 - 32 * j, 1))
                for j in range(3)
            ]
        )
    thirds = [last_part(rows[q], lane) for q in range(3)]
    out.append([jnp.where(lane < BLK, thirds[j], rows[3][j]) for j in range(3)])
    return [jnp.concatenate(tiles, 1) for tiles in out]


def cell_keep(cell, extent):
    row = lax.div(cell, SIDE)
    col = cell - row * SIDE
    return jnp.logical_and(row < extent, col < extent).astype(F32).astype(BF16)


def at(cell):
    return pl.ds(pl.multiple_of(cell * IMG, IMG), IMG)


def pack_kernel(sel, maps, first, second, rows):
    tower = sel[0]

    def widen(step, _):
        rows[pl.ds(step * 208, 208), :BLK] = maps[0, pl.ds(step * 208, 208), :].astype(F32)
        return 0

    lax.fori_loop(0, 26, widen, 0, unroll=2)
    lane = lane_index()

    def cell(index):
        start = 2 * index + tower
        return jnp.concatenate(
            [
                rows[pl.ds(start, 8, stride=2 * CELLS), :],
                rows[pl.ds(start + 16 * CELLS, 8, stride=2 * CELLS), :],
            ],
            0,
        ).astype(BF16)

    def fill(wire):
        def one(step, _):
            parts = [cell(jnp.minimum(step + GROUP * q, CELLS - 1)) for q in range(4)]
            wire[at(step), :] = jnp.concatenate(join4(parts, lane), 1)
            return 0

        lax.fori_loop(0, GROUP, one, 0, unroll=4)

    pl.when(pl.program_id(0) == 0)(partial(fill, first))
    pl.when(pl.program_id(0) == 1)(partial(fill, second))


def pack_maps(maps, tower, batches):
    return pl.pallas_call(
        pack_kernel,
        grid_spec=pltpu.PrefetchScalarGridSpec(
            num_scalar_prefetch=1,
            grid=(2,),
            in_specs=[pl.BlockSpec((1, IMG * CELLS * 2, BLK), lambda i, sel: (sel[1 + i], 0, 0))],
            out_specs=[pl.BlockSpec(WIRE, lambda i, sel: (0, 0))] * 2,
            scratch_shapes=[pltpu.VMEM((IMG * CELLS * 2, 128), F32)],
        ),
        out_shape=[jax.ShapeDtypeStruct(WIRE, BF16)] * 2,
        compiler_params=pltpu.CompilerParams(vmem_limit_bytes=MID),
        name="pack_maps",
    )(jnp.stack([tower, *batches]).astype(jnp.int32), maps)


def unpack_kernel(sel, w0, w1, w2, w3, maps):
    lane = lane_index()
    extent = sel[0]

    def one(step, _):
        rows = exchange([w[at(step), :] for w in (w0, w1, w2, w3)], lane)
        for q in range(4):
            cell = step + GROUP * q
            row = rows[q] * cell_keep(cell, extent)

            def store():
                maps[at(cell), :] = row

            if q < 3:
                store()
            else:
                pl.when(cell < CELLS)(store)
        return 0

    lax.fori_loop(0, GROUP, one, 0, unroll=4)


def unpack_maps(wires, extent):
    return pl.pallas_call(
        unpack_kernel,
        in_specs=[pl.BlockSpec(memory_space=pltpu.SMEM)]
        + [pl.BlockSpec(memory_space=pltpu.VMEM)] * 4,
        out_specs=pl.BlockSpec(memory_space=pltpu.VMEM),
        out_shape=jax.ShapeDtypeStruct((CELLS * IMG, 4 * BLK), BF16),
        compiler_params=pltpu.CompilerParams(vmem_limit_bytes=MID),
        name="unpack_maps",
    )(extent.reshape(1), *wires)


def pack_grad_kernel(sel, grad, *wires):
    lane = lane_index()
    extent = sel[0]

    def one(step, _):
        rows = []
        for q in range(4):
            cell = jnp.minimum(step + GROUP * q, CELLS - 1)
            rows.append(grad[at(cell), :] * cell_keep(cell, extent))
        for wire, row in zip(wires, exchange(rows, lane)):
            wire[at(step), :] = row
        return 0

    lax.fori_loop(0, GROUP, one, 0, unroll=4)


def pack_grad(grad, extent):
    return pl.pallas_call(
        pack_grad_kernel,
        in_specs=[
            pl.BlockSpec(memory_space=pltpu.SMEM),
            pl.BlockSpec(memory_space=pltpu.VMEM),
        ],
        out_specs=[pl.BlockSpec(memory_space=pltpu.VMEM)] * 4,
        out_shape=[jax.ShapeDtypeStruct(WIRE, BF16)] * 4,
        compiler_params=pltpu.CompilerParams(vmem_limit_bytes=MID),
        name="pack_grad",
    )(extent.reshape(1), grad)


def place_grad_kernel(sel, wire, *refs):
    out = refs[-1]
    lane = lane_index()

    def one(step, _):
        tiles = tiles_of(wire[at(step), :])
        for q in range(3):
            out[0, at(step + GROUP * q), :] = tiles[q][:, :BLK]
        part = last_part(tiles, lane)[:, :BLK]
        cell = step + GROUP * 3

        @pl.when(cell < CELLS)
        def _():
            out[0, at(cell), :] = part

        return 0

    lax.fori_loop(0, GROUP, one, 0, unroll=4)


def place_grad(wire, batch, total):
    args = [batch.reshape(1).astype(jnp.int32), wire]
    in_specs = [pl.BlockSpec(WIRE, lambda i, sel: (0, 0))]
    alias = {}
    if total is not None:
        args.append(total)
        in_specs.append(pl.BlockSpec(memory_space=pl.ANY))
        alias = {2: 0}
    return pl.pallas_call(
        place_grad_kernel,
        grid_spec=pltpu.PrefetchScalarGridSpec(
            num_scalar_prefetch=1,
            grid=(1,),
            in_specs=in_specs,
            out_specs=pl.BlockSpec((1, CELLS * IMG, BLK), lambda i, sel: (sel[0], 0, 0)),
        ),
        out_shape=jax.ShapeDtypeStruct((4, CELLS * IMG, BLK), BF16),
        input_output_aliases=alias,
        compiler_params=pltpu.CompilerParams(vmem_limit_bytes=SMALL),
        name="place_grad",
    )(*args)


def kernels_kernel(sel, *refs):
    blocks, (rows_out, extra_out) = refs[:8], refs[8:]
    d, m = sel[0], sel[1]
    odd = lax.rem(m, 2) == 1
    for k in range(4):
        for x in range(2):
            own = blocks[k][x].astype(F32)
            other = blocks[4 + k][x].astype(F32)
            even_rows = jnp.where(odd, other, own)
            odd_rows = jnp.where(odd, own, other)
            turned = jnp.concatenate([even_rows, odd_rows], 0).T.astype(BF16)
            tile = pl.multiple_of((lax.div(m, 2) ^ x) * 128, 128)
            for part in range(9):
                index = 9 * (d ^ k) + part
                first = lax.div(index, 4) * (4 * BLK)
                block = lax.rem(index, 4) ^ m
                for piece in range(3):
                    place = first + jnp.where(
                        block == 3, 128 * piece + BLK, 128 * block + 32 * piece
                    )
                    start = part * BLK + 32 * piece
                    rows_out[pl.ds(pl.multiple_of(place, 32), 32), pl.ds(tile, 128)] = turned[
                        start : start + 32
                    ]
            if k == 0:
                extra_out[:, pl.ds(tile, 128)] = turned[9 * BLK : 9 * BLK + 32]


def gather_kernels(conv_weight, extras, s, d, m):
    own = lax.dynamic_index_in_dim(conv_weight.transpose(0, 2, 1), s, 0, keepdims=False)
    rows = own.shape[1]
    count = lax.axis_size("dp")
    if count == 4:
        own = jnp.concatenate([own, extras, jnp.zeros((64, 32 - extras.shape[1]), BF16)], 1)
        near = jnp.stack([own, swap(own, "mp", 2)])
        column = [near] + [swap(near, "dp", k) for k in (1, 2, 3)]
        across = [swap(part, "mp", 1) for part in column]
        kernel, extra = pl.pallas_call(
            kernels_kernel,
            in_specs=[pl.BlockSpec(memory_space=pltpu.SMEM)]
            + [pl.BlockSpec(memory_space=pltpu.VMEM)] * 8,
            out_specs=[pl.BlockSpec(memory_space=pltpu.VMEM)] * 2,
            out_shape=[
                jax.ShapeDtypeStruct((4 * rows, 256), BF16),
                jax.ShapeDtypeStruct((32, 256), BF16),
            ],
            compiler_params=pltpu.CompilerParams(vmem_limit_bytes=BIG),
            name="kernels",
        )(jnp.stack([d, m]).astype(jnp.int32), *column, *across)
        return kernel, extra[: extras.shape[1]]
    own = jnp.concatenate([own.T, extras.T], 0)
    full = lax.all_gather(lax.all_gather(own, "dp", axis=0), "mp", axis=2, tiled=True)
    kernel = relative(full[:, :rows].reshape(9, 4, BLK, 256), m, 1)
    last = kernel[:, 3].reshape(9, 3, 32, 256)
    kernel = jnp.concatenate([kernel[:, :3], last], 2)
    return kernel.reshape(36 * BLK, 256), full[0, rows:]


def split_kernel(sel, grad, keep, send):
    d, m = sel[0], sel[1]
    odd = lax.rem(m, 2) == 1
    lane = lane_index(32)

    def one(tap, _):
        for block in range(4):
            index = tap * 4 + (block ^ m)
            part = lax.div(index, 9)
            place = ((part ^ d) * 9 + index - part * 9) * BLK
            for piece in range(3):
                start = tap * 4 * BLK + (128 * piece + BLK if block == 3 else 128 * block + 32 * piece)
                rows = grad[pl.ds(pl.multiple_of(start, 32), 32), :]
                t0, t1 = rows[:, 0:128], rows[:, 128:256]
                low = jnp.where(lane < 64, t0, pltpu.roll(t1, 64, 1)).astype(BF16)
                high = jnp.where(lane < 64, pltpu.roll(t0, 64, 1), t1).astype(BF16)
                here = pl.ds(pl.multiple_of(place + 32 * piece, 32), 32)
                keep[here, :] = jnp.where(odd, high, low)
                send[here, :] = jnp.where(odd, low, high)
        return 0

    lax.fori_loop(0, 9, one, 0)


def scatter_kernels(grad, d, m):
    count = lax.axis_size("dp")
    if count == 4:
        keep, send = pl.pallas_call(
            split_kernel,
            in_specs=[
                pl.BlockSpec(memory_space=pltpu.SMEM),
                pl.BlockSpec(memory_space=pltpu.VMEM),
            ],
            out_specs=[pl.BlockSpec(memory_space=pltpu.VMEM)] * 2,
            out_shape=[jax.ShapeDtypeStruct((36 * BLK, 128), BF16)] * 2,
            compiler_params=pltpu.CompilerParams(vmem_limit_bytes=MID),
            name="split_kernels",
        )(jnp.stack([d, m]).astype(jnp.int32), grad)
        pair = keep.astype(F32) + swap(send, "mp", 1).astype(F32)
        pair = pair.reshape(4, 9 * BLK, 128)
        total = pair[0]
        for k in (1, 2, 3):
            total = total + swap(pair[k].astype(BF16), "dp", k).astype(F32)
        turned = total.T.reshape(2, 64, 9 * BLK)
        x = lax.div(m, 2)
        mine = lax.dynamic_index_in_dim(turned, x, 0, keepdims=False)
        other = lax.dynamic_index_in_dim(turned, 1 - x, 0, keepdims=False)
        mine = mine + swap(other.astype(BF16), "mp", 2).astype(F32)
        return mine.T
    grad = grad.reshape(9, 3, 128, 256)
    last = grad[:, :, BLK:].reshape(9, 1, BLK, 256)
    grad = jnp.concatenate([grad[:, :, :BLK], last], 1)
    grad = relative(grad, m, 1).reshape(36 * BLK, 256).astype(BF16)
    grad = lax.psum_scatter(grad, "mp", scatter_dimension=1, tiled=True)
    return lax.psum_scatter(grad, "dp", scatter_dimension=0, tiled=True).astype(F32)


def all_acts(acts, place):
    return jnp.concatenate([a[:, place].reshape(4 * IMG, 256) for a in acts], 0)


def all_grads(grads):
    return jnp.concatenate([g[r] for r in range(4) for g in grads], 0)


def fc_forward_kernel(a0, a1, a2, a3, weight, own, send):
    rows = jnp.concatenate([all_acts((a0, a1, a2, a3), p) for p in range(9)], 1)
    for n in range(weight.shape[1] // 256):
        here = slice(n * 256, (n + 1) * 256)
        term = jnp.dot(rows, weight[:, here], preferred_element_type=F32)
        for r in range(4):
            for k in range(4):
                part = term[(4 * r + k) * IMG : (4 * r + k + 1) * IMG]
                if k == 0:
                    own[r, :, here] = part
                else:
                    send[k - 1, r, :, here] = part.astype(BF16)


def fc_forward(acts, weight):
    hid = weight.shape[1]
    return pl.pallas_call(
        fc_forward_kernel,
        in_specs=[pl.BlockSpec(memory_space=pltpu.VMEM)] * 5,
        out_specs=[pl.BlockSpec(memory_space=pltpu.VMEM)] * 2,
        out_shape=[
            jax.ShapeDtypeStruct((4, IMG, hid), F32),
            jax.ShapeDtypeStruct((3, 4, IMG, hid), BF16),
        ],
        compiler_params=pltpu.CompilerParams(vmem_limit_bytes=MID),
        name="fc_forward",
    )(*acts, weight)


def fc_rows_kernel(g0, g1, g2, g3, weight, keep, send):
    rows = all_grads((g0, g1, g2, g3))
    for p in range(9):
        term = lax.dot_general(
            rows,
            weight[p * 256 : (p + 1) * 256, :],
            (((1,), (1,)), ((), ())),
            preferred_element_type=F32,
        )
        term = term.reshape(4, 4, IMG, 256)
        for r in range(4):
            if r % 2 == 0:
                keep[r // 2, :, p] = term[r]
            else:
                send[r // 2, :, p] = term[r].astype(BF16)


def fc_rows(grads, weight):
    hid = weight.shape[1]
    return pl.pallas_call(
        fc_rows_kernel,
        in_specs=[pl.BlockSpec(memory_space=pltpu.VMEM)] * 5,
        out_specs=[pl.BlockSpec(memory_space=pltpu.VMEM)] * 2,
        out_shape=[
            jax.ShapeDtypeStruct((2, 4, 9, IMG, 256), F32),
            jax.ShapeDtypeStruct((2, 4, 9, IMG, 256), BF16),
        ],
        compiler_params=pltpu.CompilerParams(vmem_limit_bytes=MID),
        name="fc_rows",
    )(*grads, weight)


def fc_matrix_kernel(a0, a1, a2, a3, g0, g1, g2, g3, out, part, sent):
    grads = all_grads((g0, g1, g2, g3))

    def copy(p):
        return pltpu.make_async_copy(
            part.at[p % 3], out.at[pl.ds(p * 256, 256)], sent.at[p % 3]
        )

    for p in range(9):
        rows = all_acts((a0, a1, a2, a3), p).T
        if p >= 3:
            copy(p - 3).wait()
        part[p % 3] = jnp.dot(rows, grads, preferred_element_type=F32)
        copy(p).start()
    for p in range(6, 9):
        copy(p).wait()


def fc_matrix(acts, grads):
    hid = grads[0].shape[2]
    return pl.pallas_call(
        fc_matrix_kernel,
        in_specs=[pl.BlockSpec(memory_space=pltpu.VMEM)] * 8,
        out_specs=pl.BlockSpec(memory_space=pl.ANY),
        out_shape=jax.ShapeDtypeStruct((9 * 256, hid), F32),
        scratch_shapes=[pltpu.VMEM((3, 256, hid), F32), pltpu.SemaphoreType.DMA((3,))],
        compiler_params=pltpu.CompilerParams(vmem_limit_bytes=MID),
        name="fc_matrix",
    )(*acts, *grads)


def fc_section(shared, weight, bias, stitch, cotangent, s, d, m):
    count = lax.axis_size("dp")
    hid = weight.shape[2]
    cot = lax.dynamic_slice_in_dim(cotangent, d * IMG, IMG, 1).transpose(2, 0, 1, 3)
    cot = relative(cot, m, 1).astype(F32)
    bias_own = lax.dynamic_index_in_dim(bias, s, 0, keepdims=False)
    own_weight = lax.dynamic_index_in_dim(weight, s, 0, keepdims=False)
    if count == 4:
        parts = shared.reshape(4, 9, IMG, 256)
        chunk = [lax.dynamic_index_in_dim(parts, d ^ k, 0, keepdims=False) for k in range(4)]
        near = jnp.stack([chunk[0]] + [swap(chunk[k], "dp", k) for k in (1, 2, 3)])
        far = swap(near, "mp", 2)
        acts = [near, swap(near, "mp", 1), far, swap(far, "mp", 1)]
        pre, send = fc_forward(acts, own_weight)
        for k in (1, 2, 3):
            pre = pre + swap(send[k - 1], "dp", k).astype(F32)
    else:
        flat = shared.transpose(1, 0, 2).reshape(IMG, count, -1).transpose(1, 0, 2)
        flat = lax.all_to_all(flat, "dp", 0, 0, tiled=True)
        flat = lax.all_gather(flat, "mp", axis=0)
        flat = relative(flat, m)
        pre = jnp.einsum("rdnf,fk->drnk", flat, own_weight, preferred_element_type=F32)
        pre = lax.psum_scatter(pre.astype(BF16), "dp", scatter_dimension=0, tiled=True)
        pre = pre.reshape(4, IMG, hid).astype(F32)
    pre = pre + bias_own
    active, pull = jax.vjp(jax.nn.gelu, pre)
    to_own = lax.dynamic_index_in_dim(stitch, s, 1, keepdims=False)
    mixed = to_own[0] * cot[0] + to_own[1] * cot[1]
    pre_grad = pull(mixed)[0].astype(BF16)
    sent = active.astype(BF16)
    other = swap(sent, "section", 1).astype(F32)
    row = lax.dynamic_index_in_dim(stitch, s, 0, keepdims=False)
    by_own = lax.dynamic_index_in_dim(row, s, 0, keepdims=False)
    by_other = lax.dynamic_index_in_dim(row, 1 - s, 0, keepdims=False)
    outputs = relative((by_own * active + by_other * other).astype(BF16), m)
    cot_own = lax.dynamic_index_in_dim(cot, s, 0, keepdims=False)
    own_sum = jnp.sum(cot_own * active, (0, 1))
    other_sum = jnp.sum(cot_own * other, (0, 1))
    first = jnp.where(s == 0, own_sum, other_sum)
    second = jnp.where(s == 0, other_sum, own_sum)
    bias_sum = jnp.sum(pre_grad.astype(F32), (0, 1))
    small = sum_over(jnp.stack([first, second, bias_sum]), "dp")
    if count == 4:
        grads = [pre_grad] + [swap(pre_grad, "dp", k) for k in (1, 2, 3)]
        rows, send = fc_rows(grads, own_weight)
        rows = rows + swap(send, "mp", 1).astype(F32)
        rows = rows[0] + swap(rows[1].astype(BF16), "mp", 2).astype(F32)
        rows = rows.astype(BF16)
        back = jnp.stack([rows[0]] + [swap(rows[k], "dp", k) for k in (1, 2, 3)])
        shared_grad = relative(back, d).reshape(PLACES, IMG, 256)
        matrix = fc_matrix(acts, grads)
    else:
        grads = lax.all_gather(pre_grad, "dp", axis=0)
        rows = jnp.einsum("drnk,fk->rdnf", grads, own_weight, preferred_element_type=F32)
        rows = relative(rows, m).astype(BF16)
        rows = lax.psum_scatter(rows, "mp", scatter_dimension=0, tiled=True)[0]
        rows = lax.all_to_all(rows, "dp", 0, 0, tiled=True)
        shared_grad = rows.transpose(1, 0, 2).reshape(IMG, PLACES, 256).transpose(1, 0, 2)
        matrix = jnp.einsum("rdnf,drnk->fk", flat, grads, preferred_element_type=F32)
    return shared_grad, outputs, matrix, small


def pool_mean(cells):
    total = None
    for a in range(3):
        for b in range(3):
            part = cells[a : a + 11 : 2, b : b + 11 : 2]
            total = part if total is None else total + part
    return total / 9.0


def conv_grad_kernel(sel, own, other, slope, pooled, pooled_other, columns, out, sums):
    extent = sel[0]
    by_own, by_other = columns[0:1, :], columns[1:2, :]
    spread = []
    own_sum = other_sum = None
    for p in range(POOLED):
        line = []
        for q in range(POOLED):
            place = POOLED * p + q
            mine = own[place].astype(F32)
            crossed = other[place].astype(F32)
            keep = jnp.logical_and(p < extent, q < extent).astype(F32) / 9.0
            line.append((by_own * mine + by_other * crossed) * keep)
            first = mine * pooled[place]
            second = mine * pooled_other[place].astype(F32)
            own_sum = first if own_sum is None else own_sum + first
            other_sum = second if other_sum is None else other_sum + second
        spread.append(line)
    bias_sum = jnp.zeros((IMG, 256), F32)

    def over(values, index):
        near, far = index // 2, index // 2 - 1
        if index % 2 == 1:
            return values[near]
        if index == 0:
            return values[0]
        if near >= POOLED:
            return values[far]
        return values[near] + values[far]

    for i in range(SIDE):
        line = [over([spread[p][q] for p in range(POOLED)], i) for q in range(POOLED)]
        for j in range(SIDE):
            cell = SIDE * i + j
            value = (slope[cell] * over(line, j)).astype(BF16)
            out[cell] = value
            bias_sum = bias_sum + value.astype(F32)
    for row, total in enumerate((own_sum, other_sum, bias_sum)):
        sums[row : row + 1, :] = jnp.sum(total, 0, keepdims=True)


def conv_gradient(own, other, slope, pooled, pooled_other, columns, extent):
    return pl.pallas_call(
        conv_grad_kernel,
        in_specs=[pl.BlockSpec(memory_space=pltpu.SMEM)]
        + [pl.BlockSpec(memory_space=pltpu.VMEM)] * 6,
        out_specs=[pl.BlockSpec(memory_space=pltpu.VMEM)] * 2,
        out_shape=[
            jax.ShapeDtypeStruct((CELLS, IMG, 256), BF16),
            jax.ShapeDtypeStruct((3, 256), F32),
        ],
        compiler_params=pltpu.CompilerParams(vmem_limit_bytes=MID),
        name="conv_gradient",
    )(extent.reshape(1), own, other, slope, pooled, pooled_other, columns)


def on_device(
    conv_input,
    group_ids,
    conv_weight,
    conv_bias,
    conv_stitch,
    fc_weight,
    fc_bias,
    fc_stitch,
    cotangent,
):
    s = lax.axis_index("section")
    d = lax.axis_index("dp")
    m = lax.axis_index("mp")
    assert conv_input.shape == (4, IMG, 2, SIDE, SIDE, BLK) and lax.axis_size("mp") == 4
    low_group = lax.dynamic_index_in_dim(group_ids, m, 0, keepdims=False) == 1
    extent = jnp.where(low_group, MAP_LOW, SIDE)
    pooled_extent = jnp.where(low_group, POOL_LOW, POOLED)
    inside = jnp.arange(POOLED) < pooled_extent
    pool_map = (inside[:, None] & inside[None, :]).astype(F32)[:, :, None, None]

    by_row = conv_input.transpose(0, 1, 3, 4, 2, 5).reshape(4, IMG * CELLS * 2, BLK)
    wires = [None] * 4
    wires[3], wires[2] = pack_maps(by_row, s, (m ^ 3, m ^ 2))
    wires[1], wires[0] = pack_maps(by_row, s, (m ^ 1, m))
    arrived = [wires[0]] + [swap(wires[k], "mp", k) for k in (1, 2, 3)]

    small_params = jnp.concatenate([conv_bias, conv_stitch.reshape(4, 64)], 0)
    thirds = []
    rest = small_params
    for _ in range(3):
        piece = lax.reduce_precision(rest, 8, 7)
        thirds.append(piece.astype(BF16))
        rest = rest - piece
    extras = jnp.stack(thirds, 1).reshape(18, 64).T
    kernel, extra = gather_kernels(conv_weight, extras, s, d, m)
    params = jnp.sum(extra.astype(F32).reshape(6, 3, 256), 1)
    bias_own = lax.dynamic_index_in_dim(params, s, 0, keepdims=False)
    stitch = params[2:].reshape(2, 2, 256)

    maps = unpack_maps(arrived, extent).reshape(SIDE, SIDE, IMG, 4 * BLK)
    taps = kernel.reshape(3, 3, 4 * BLK, 256)
    conv_out = lax.conv_general_dilated(
        maps,
        taps,
        (1, 1),
        ((1, 1), (1, 1)),
        dimension_numbers=("HWNC", "HWIO", "HWNC"),
        preferred_element_type=F32,
    )
    conv_out = conv_out + bias_own
    active, pull = jax.vjp(jax.nn.gelu, conv_out)
    slope = pull(jnp.ones_like(conv_out))[0]
    pooled = pool_mean(active) * pool_map
    other = swap(pooled.astype(BF16), "section", 1)
    stitch_row = lax.dynamic_index_in_dim(stitch, s, 0, keepdims=False)
    by_own = lax.dynamic_index_in_dim(stitch_row, s, 0, keepdims=False)
    by_other = lax.dynamic_index_in_dim(stitch_row, 1 - s, 0, keepdims=False)
    shared = (by_own * pooled + by_other * other.astype(F32)).astype(BF16).reshape(PLACES, IMG, 256)

    shared_grad, outputs, matrix, fc_small = fc_section(
        shared, fc_weight, fc_bias, fc_stitch, cotangent, s, d, m
    )
    other_grad = swap(shared_grad, "section", 1)
    stitch_col = lax.dynamic_index_in_dim(stitch, s, 1, keepdims=False)
    own_col = lax.dynamic_index_in_dim(stitch_col, s, 0, keepdims=False)
    other_col = lax.dynamic_index_in_dim(stitch_col, 1 - s, 0, keepdims=False)
    conv_grad, sums = conv_gradient(
        shared_grad,
        other_grad,
        slope.reshape(CELLS, IMG, 256),
        pooled.reshape(PLACES, IMG, 256),
        other.reshape(PLACES, IMG, 256),
        jnp.stack([own_col, other_col]),
        pooled_extent,
    )
    conv_grad = conv_grad.reshape(SIDE, SIDE, IMG, 256)
    own_sum, other_sum, bias_sum = sums
    first = jnp.where(s == 0, own_sum, other_sum)
    second = jnp.where(s == 0, other_sum, own_sum)
    conv_small = sum_over(sum_over(jnp.stack([first, second, bias_sum]), "dp"), "mp")
    conv_small = lax.dynamic_slice_in_dim(conv_small, m * 64, 64, 1)

    input_part = lax.conv_general_dilated(
        conv_grad,
        taps[::-1, ::-1],
        (1, 1),
        ((1, 1), (1, 1)),
        dimension_numbers=("HWNC", "HWOI", "HWNC"),
        preferred_element_type=F32,
    )
    grad_wires = pack_grad(input_part.astype(BF16).reshape(CELLS * IMG, 4 * BLK), extent)
    returned = [grad_wires[0]] + [swap(grad_wires[k], "mp", k) for k in (1, 2, 3)]
    input_grad = None
    for k in range(4):
        input_grad = place_grad(returned[k], m ^ k, input_grad)
    input_grad = input_grad.reshape(4, 1, SIDE, SIDE, IMG, BLK).transpose(0, 4, 1, 2, 3, 5)

    kernel_grad = lax.conv_general_dilated(
        maps,
        conv_grad,
        (1, 1),
        ((1, 1), (1, 1)),
        dimension_numbers=("HWCN", "HWIO", "HWNC"),
        preferred_element_type=F32,
    )
    kernel_rows = scatter_kernels(kernel_grad.reshape(36 * BLK, 256), d, m)
    return (
        outputs[:, :, None],
        input_grad,
        kernel_rows[None],
        conv_small[2][None],
        conv_small[:2][None],
        matrix[None],
        fc_small[2][None],
        fc_small[:2][None],
    )


def solution(mesh):
    placed = (
        P(None, "dp", None, None, None, "mp"),
        P(),
        P(None, "dp", "mp"),
        P(None, "mp"),
        P(None, None, "mp"),
        P(None, "dp", "mp"),
        P(None, "mp"),
        P(None, None, "mp"),
        P(None, None, None, "mp"),
    )
    return jax.shard_map(
        on_device,
        mesh=mesh,
        in_specs=placed,
        out_specs=(
            P(None, "dp", "section", "mp"),
            P(None, "dp", "section", None, None, "mp"),
            P("section", "dp", "mp"),
            P("section", "mp"),
            P("section", None, "mp"),
            P("section", "dp", "mp"),
            P("section", "mp"),
            P("section", None, "mp"),
        ),
        check_vma=False,
    )
```

time: 3730 us -> 235 us (0.06)
  local copies, waits for them, and re-layouts: 1240 us -> 22.7 us
  waiting for transfers between devices: 1210 us -> 85.4 us
  matrix products: 557 us -> 21.8 us
  other arithmetic: 358 us -> 10.9 us
  blocking collectives: 279 us -> 0 us
  Pallas kernels: 0 us -> 44.8 us
    unnamed x179 -> x66, local copies, waits for them, and re-layouts: 764 us -> 12.3 us
    all_gather x5 -> x0, waiting for transfers between devices: 663 us -> none  [the longest x1 447 us: on_device(): matrix = lax.all_gather(fc_weight, 'dp', axis=1, tiled=True)]
    dot_general x120 -> x0, matrix products: 557 us -> none  [the longest x4 173 us: on_device(): jnp.einsum('ntf,ntk->tfk', flat_rows, pre_grad, preferred_element_type=jn...]
    reduce_scatter x1 -> x0, waiting for transfers between devices: 382 us -> none  [on_device(): lax.psum_scatter(fc_grad.astype(jnp.bfloat16), 'dp', scatter_dimension=1,...]
    another operation x29 -> x1, local copies, waits for them, and re-layouts: 315 us -> 1.12 us
    scatter-add x36 -> x0, other arithmetic: 242 us -> none  [pool_back(): result = result.at[:, :, tap_row:tap_row + 2 * pooled_side - 1:2, tap_col...]
    all_gather x5 -> x0, blocking collectives: 188 us -> none  [the longest x4 154 us: on_device(): fc_full_maps = lax.all_gather(incoming, 'mp', axis=4, tiled=True)]
    all_to_all x7 -> x0, waiting for transfers between devices: 98.8 us -> none  [the longest x1 96.5 us: on_device(): lax.all_to_all(fc_grad_rows.astype(jnp.bfloat16), 'section', split_axis=0...]
  transfers between devices with their start and end apart: 27 -> 45, of which waited for: 11 -> 18; matrix products, arithmetic and copies ran while one was open for 50% -> 11% of each run, Pallas kernels for 0% -> 17%
where the time goes in v1:
time: 235 us; the launch traced here: 231 us
  waiting for transfers between devices  85.4 us (36%)
  Pallas kernels  44.8 us (19%)
  starting transfers between devices  43.6 us (19%)
  local copies, waits for them, and re-layouts  22.7 us (10%)
  matrix products  21.8 us (9%)
  other arithmetic  10.9 us (5%)
    ppermute x45, waiting for transfers between devices, swap(): return lax.ppermute(value, axis, [(i, i ^ bit) for i in range(count)])  85.4 us
    ppermute x45, starting transfers between devices, swap(): return lax.ppermute(value, axis, [(i, i ^ bit) for i in range(count)])  43.6 us
    pallas_call x4, Pallas kernels, place_grad(): pl.pallas_call(place_grad_kernel, grid_spec=pltpu.PrefetchScalarGridSpec(...  16.2 us
    unnamed x66, local copies, waits for them, and re-layouts  12.3 us
    conv_general_dilated x1, matrix products, on_device(): lax.conv_general_dilated(maps, taps, (1, 1), ((1, 1), (1, 1)), dimension_...  9.34 us
    pallas_call x2, Pallas kernels, pack_maps(): pl.pallas_call(pack_kernel, grid_spec=pltpu.PrefetchScalarGridSpec(num_sc...  7.16 us
    conv_general_dilated x1, matrix products, on_device(): lax.conv_general_dilated(conv_grad, taps[::-1, ::-1], (1, 1), ((1, 1), (1...  6.82 us
    conv_general_dilated x1, matrix products, on_device(): lax.conv_general_dilated(maps, conv_grad, (1, 1), ((1, 1), (1, 1)), dimen...  5.64 us
  transfers between devices with their start and end apart: 45, of which 18 were waited for; matrix products, arithmetic and copies ran while one was open for 11% of the time, Pallas kernels for 17%

profile of v1, /device:TPU:8, one launch (start us, length us, event | category | flops | bytes accessed | tf_op | source)
XLA Modules:
  0.0 231.2 jit_solution(8287473291119721462)
XLA Ops:
  1.8 1.5 collective-permute-start
  3.4 2.6 %copy-done.4 = bf16[4,16,2,13,13,96]{5,2,4,3,1,0:T(2,128)(2,1)S(1)} copy-done((bf16[4,16,2,13,13,96]{5,2,4,3,1,0:T(2,128)(2,1)S(1)}, bf16[4,16,2,13,13,96]{5,2,4,3,1,0:T(2,128)(2,1)}, u32[]{:S(2)}) %copy-start.4) | copy-done | bytes 4153368
  6.0 3.2 %pack_maps.2 = (bf16[688,384]{1,0:T(8,128)(2,1)S(1)}, bf16[688,384]{1,0:T(8,128)(2,1)S(1)}) custom-call(s32[3]{0:T(128)S(1)} %get-tuple-element.116.sel, bf16[4,5408,96]{2,1,0:T(8,128)(2,1)S(1)} %bitcast.146), custom_call_target="tpu_custom_call" | custom-call | tf_op jit(solution)/shard_map/pack_maps/pallas_call | solution.py:124
  9.2 4.0 %pack_maps.3 = (bf16[688,384]{1,0:T(8,128)(2,1)S(1)}, bf16[688,384]{1,0:T(8,128)(2,1)}) custom-call(s32[3]{0:T(128)S(1)} %get-tuple-element.117.sel, bf16[4,5408,96]{2,1,0:T(8,128)(2,1)S(1)} %bitcast.147), custom_call_target="tpu_custom_call" | custom-call | tf_op jit(solution)/shard_map/pack_maps/pallas_call | solution.py:124
  14.5 3.0 %collective-permute-start.2 = (bf16[2,64,896]{2,1,0:T(8,128)(2,1)}, bf16[2,64,896]{2,1,0:T(8,128)(2,1)}, u32[]{:S(2)}, u32[]{:S(2)}) collective-permute-start(bf16[2,64,896]{2,1,0:T(8,128)(2,1)} %pad_maximum_fusion.3.refs_0_), channel_id=1, source_target_pairs={{0,8},{4,12},{8,0},{12,4},{1,9},{5,13},{9,1},{13,5},{2,10},{6,14},... | collective-permute-start | bytes 688136 | tf_op jit(solution)/shard_map/ppermute | solution.py:30
  18.0 6.7 %collective-permute-done.1.refs_1_ = bf16[2,64,896]{2,1,0:T(8,128)(2,1)} collective-permute-done((bf16[2,64,896]{2,1,0:T(8,128)(2,1)}, bf16[2,64,896]{2,1,0:T(8,128)(2,1)}, u32[]{:S(2)}, u32[]{:S(2)}) %collective-permute-start.1) | collective-permute-done | bytes 229408 | tf_op jit(solution)/shard_map/ppermute | solution.py:30
  26.5 7.3 %collective-permute-done.2.refs_2_ = bf16[2,64,896]{2,1,0:T(8,128)(2,1)} collective-permute-done((bf16[2,64,896]{2,1,0:T(8,128)(2,1)}, bf16[2,64,896]{2,1,0:T(8,128)(2,1)}, u32[]{:S(2)}, u32[]{:S(2)}) %collective-permute-start.2) | collective-permute-done | bytes 229408 | tf_op jit(solution)/shard_map/ppermute | solution.py:30
  33.7 4.8 %collective-permute-done.3.refs_3_ = bf16[2,64,896]{2,1,0:T(8,128)(2,1)} collective-permute-done((bf16[2,64,896]{2,1,0:T(8,128)(2,1)}, bf16[2,64,896]{2,1,0:T(8,128)(2,1)}, u32[]{:S(2)}, u32[]{:S(2)}) %collective-permute-start.3) | collective-permute-done | bytes 229408 | tf_op jit(solution)/shard_map/ppermute | solution.py:30
  40.8 1.0 copy-done.18
  41.9 1.0 copy-done.20
  42.9 3.9 %unpack_maps.1 = bf16[2704,384]{1,0:T(8,128)(2,1)S(1)} custom-call(s32[1]{0:T(128)S(6)} %select_n.153.sel, bf16[688,384]{1,0:T(8,128)(2,1)S(1)} %get-tuple-element.27.w0, bf16[688,384]{1,0:T(8,128)(2,1)S(1)} %collective-permute-done.8.w1, bf16[688,384]{1,0:T(8,128)(2,1)S(1)} %copy-done.18, bf16[688,384]{1,0:T(8,128)(2,1)S(1)} %copy-done.20), custom_call_target="tpu_custom_call" | custom-call | tf_op jit(solution)/shard_map/unpack_maps/pallas_call | solution.py:162
  46.8 1.3 copy-done.8
  48.1 2.4 %kernels.1 = (bf16[3456,256]{1,0:T(8,128)(2,1)S(1)}, bf16[32,256]{1,0:T(8,128)(2,1)S(1)}) custom-call(s32[2]{0:T(128)S(1)} %pad_add_fusion.sel, bf16[2,64,896]{2,1,0:T(8,128)(2,1)} %pad_maximum_fusion.3.refs_0_, bf16[2,64,896]{2,1,0:T(8,128)(2,1)} %collective-permute-done.1.refs_1_, bf16[2,64,896]{2,1,0:T(8,128)(2,1)} %collective-permute-done.2.refs_2_, ...), custom_call_target="tpu_custom_call" | custom-call | tf_op jit(solution)/shard_map/kernels/pallas_call | solution.py:283
  50.5 1.2 copy-done.27
  51.8 9.3 %fusion.5 = (f32[13,13,16,256]{3,2,1,0:T(8,128)S(1)}, f32[13,13,16,256]{3,2,1,0:T(8,128)S(1)}) fusion(f32[256]{0:T(256)S(1)} %bitcast.190, bf16[13,13,16,384]{3,2,1,0:T(8,128)(2,1)} %bitcast.151, bf16[3,3,384,256]{3,2,1,0:T(8,128)(2,1)} %bitcast.156), kind=kOutput, calls=%fused_computation.8 | convolution fusion | flops 4319653888 | bytes 9384960 | tf_op jit(solution)/shard_map/conv_general_dilated | solution.py:630
  62.1 1.5 collective-permute-start.11
  63.6 8.2 %collective-permute-done.11 = bf16[6,6,16,256]{3,2,1,0:T(8,128)(2,1)} collective-permute-done((bf16[6,6,16,256]{3,2,1,0:T(8,128)(2,1)}, bf16[6,6,16,256]{3,2,1,0:T(8,128)(2,1)}, u32[]{:S(2)}, u32[]{:S(2)}) %collective-permute-start.11) | collective-permute-done | bytes 294944 | tf_op jit(solution)/shard_map/ppermute | solution.py:30
  71.8 1.1 add_convert_fusion
  73.6 1.6 collective-permute-start.14
  75.1 1.8 collective-permute-start.13
  77.7 5.0 %dynamic-slice_bitcast_fusion.weight = bf16[2304,1024]{1,0:T(8,128)(2,1)} fusion(bf16[2,2304,1024]{2,1,0:T(8,128)(2,1)} %param.14, s32[]{:T(128)S(6)} %select_n.150), kind=kLoop, calls=%fused_computation | loop fusion | bytes 9437188 | tf_op jit(solution)/shard_map/jit(dynamic_index_in_dim)/squeeze | solution.py:467
  84.7 1.1 constant_dynamic-slice_fusion.11
  85.9 5.6 %collective-permute-done.16.a2 = bf16[4,9,16,256]{3,2,1,0:T(8,128)(2,1)S(1)} collective-permute-done((bf16[4,9,16,256]{3,2,1,0:T(8,128)(2,1)S(1)}, bf16[4,9,16,256]{3,2,1,0:T(8,128)(2,1)S(1)}, u32[]{:S(2)}, u32[]{:S(2)}) %collective-permute-start.16) | collective-permute-done | bytes 294944 | tf_op jit(solution)/shard_map/ppermute | solution.py:30
  91.6 1.5 collective-permute-done.17.a3
  93.1 2.3 %copy-done.2 = bf16[2304,1024]{1,0:T(8,128)(2,1)S(1)} copy-done((bf16[2304,1024]{1,0:T(8,128)(2,1)S(1)}, bf16[2304,1024]{1,0:T(8,128)(2,1)}, u32[]{:S(2)}) %copy-start.2) | copy-done | bytes 4718616
  95.4 1.4 fc_forward.1
  96.9 1.5 collective-permute-start.20
  98.4 3.4 %collective-permute-start.19 = (bf16[4,16,1024]{2,1,0:T(8,128)(2,1)S(1)}, bf16[4,16,1024]{2,1,0:T(8,128)(2,1)S(1)}, u32[]{:S(2)}, u32[]{:S(2)}) collective-permute-start(bf16[4,16,1024]{2,1,0:T(8,128)(2,1)S(1)} %get-tuple-element.84), channel_id=1, source_target_pairs={{0,8},{4,12},{8,0},{12,4},{1,9},{5,13},{9,1},{13,5},{2,10},{6,14},... | collective-permute-start | bytes 393224 | tf_op jit(solution)/shard_map/ppermute | solution.py:30
  101.9 4.8 %collective-permute-done.20 = bf16[4,16,1024]{2,1,0:T(8,128)(2,1)S(1)} collective-permute-done((bf16[4,16,1024]{2,1,0:T(8,128)(2,1)S(1)}, bf16[4,16,1024]{2,1,0:T(8,128)(2,1)S(1)}, u32[]{:S(2)}, u32[]{:S(2)}) %collective-permute-start.20) | collective-permute-done | bytes 131104 | tf_op jit(solution)/shard_map/ppermute | solution.py:30
  106.8 3.1 %collective-permute-done.19 = bf16[4,16,1024]{2,1,0:T(8,128)(2,1)S(1)} collective-permute-done((bf16[4,16,1024]{2,1,0:T(8,128)(2,1)S(1)}, bf16[4,16,1024]{2,1,0:T(8,128)(2,1)S(1)}, u32[]{:S(2)}, u32[]{:S(2)}) %collective-permute-start.19) | collective-permute-done | bytes 131104 | tf_op jit(solution)/shard_map/ppermute | solution.py:30
  111.6 1.9 collective-permute-start.22
  115.0 3.4 %collective-permute-done.22.g1 = bf16[4,16,1024]{2,1,0:T(8,128)(2,1)S(1)} collective-permute-done((bf16[4,16,1024]{2,1,0:T(8,128)(2,1)S(1)}, bf16[4,16,1024]{2,1,0:T(8,128)(2,1)S(1)}, u32[]{:S(2)}, u32[]{:S(2)}) %collective-permute-start.22) | collective-permute-done | bytes 131104 | tf_op jit(solution)/shard_map/ppermute | solution.py:30
  118.5 5.3 %collective-permute-done.23.g2 = bf16[4,16,1024]{2,1,0:T(8,128)(2,1)S(1)} collective-permute-done((bf16[4,16,1024]{2,1,0:T(8,128)(2,1)S(1)}, bf16[4,16,1024]{2,1,0:T(8,128)(2,1)S(1)}, u32[]{:S(2)}, u32[]{:S(2)}) %collective-permute-start.23) | collective-permute-done | bytes 131104 | tf_op jit(solution)/shard_map/ppermute | solution.py:30
  123.8 3.0 %collective-permute-done.24.g3 = bf16[4,16,1024]{2,1,0:T(8,128)(2,1)S(1)} collective-permute-done((bf16[4,16,1024]{2,1,0:T(8,128)(2,1)S(1)}, bf16[4,16,1024]{2,1,0:T(8,128)(2,1)S(1)}, u32[]{:S(2)}, u32[]{:S(2)}) %collective-permute-start.24) | collective-permute-done | bytes 131104 | tf_op jit(solution)/shard_map/ppermute | solution.py:30
  126.8 2.4 %fc_rows.1 = (f32[2,4,9,16,256]{4,3,2,1,0:T(8,128)S(1)}, bf16[2,4,9,16,256]{4,3,2,1,0:T(8,128)(2,1)}) custom-call(bf16[4,16,1024]{2,1,0:T(8,128)(2,1)S(1)} %get-tuple-element.63.g0, bf16[4,16,1024]{2,1,0:T(8,128)(2,1)S(1)} %collective-permute-done.22.g1, bf16[4,16,1024]{2,1,0:T(8,128)(2,1)S(1)} %collective-permute-done.23.g2, ...), custom_call_target="tpu_custom_call" | custom-call | tf_op jit(solution)/shard_map/fc_rows/pallas_call | solution.py:417
  130.3 1.6 collective-permute-start.21
  131.9 4.6 %collective-permute-done.21 = bf16[4,16,1024]{2,1,0:T(8,128)(2,1)} collective-permute-done((bf16[4,16,1024]{2,1,0:T(8,128)(2,1)}, bf16[4,16,1024]{2,1,0:T(8,128)(2,1)}, u32[]{:S(2)}, u32[]{:S(2)}) %collective-permute-start.21) | collective-permute-done | bytes 131104 | tf_op jit(solution)/shard_map/ppermute | solution.py:30
  136.5 1.2 fusion.25
  137.7 1.6 convert_add_fusion.1
  139.5 1.2 collective-permute-start.26
  140.9 7.2 %collective-permute-done.26 = bf16[4,9,16,256]{3,2,1,0:T(8,128)(2,1)S(1)} collective-permute-done((bf16[4,9,16,256]{3,2,1,0:T(8,128)(2,1)S(1)}, bf16[4,9,16,256]{3,2,1,0:T(8,128)(2,1)S(1)}, u32[]{:S(2)}, u32[]{:S(2)}) %collective-permute-start.26) | collective-permute-done | bytes 294944 | tf_op jit(solution)/shard_map/ppermute | solution.py:30
  148.2 1.4 collective-permute-start.29
  149.6 1.0 collective-permute-start.28
  150.6 1.1 collective-permute-start.27
  151.8 3.4 %collective-permute-done.29 = bf16[9,16,256]{2,1,0:T(8,128)(2,1)S(1)} collective-permute-done((bf16[9,16,256]{2,1,0:T(8,128)(2,1)S(1)}, bf16[9,16,256]{2,1,0:T(8,128)(2,1)S(1)}, u32[]{:S(2)}, u32[]{:S(2)}) %collective-permute-start.29) | collective-permute-done | bytes 73760 | tf_op jit(solution)/shard_map/ppermute | solution.py:30
  155.3 1.6 collective-permute-start.30
  157.6 4.5 %fc_matrix.1 = f32[2304,1024]{1,0:T(8,128)} custom-call(bf16[4,9,16,256]{3,2,1,0:T(8,128)(2,1)S(1)} %copy-done.7, bf16[4,9,16,256]{3,2,1,0:T(8,128)(2,1)S(1)} %copy-done.13, bf16[4,9,16,256]{3,2,1,0:T(8,128)(2,1)S(1)} %copy-done.11, bf16[4,9,16,256]{3,2,1,0:T(8,128)(2,1)S(1)} %copy-done.15, bf16[4,16,1024]{2,1,0:T(8,128)(2,1)S(1)} %get-tuple-element.63.g0, ...), custom_call_target="tpu_custom_call" | custom-call | tf_op jit(solution)/shard_map/fc_matrix/pallas_call | solution.py:450
  162.2 3.2 %collective-permute-start.44 = (f32[3,1024]{1,0:T(4,128)S(1)}, f32[3,1024]{1,0:T(4,128)S(1)}, u32[]{:S(2)}, u32[]{:S(2)}) collective-permute-start(f32[3,1024]{1,0:T(4,128)S(1)} %fusion.33), channel_id=1, source_target_pairs={{0,8},{4,12},{8,0},{12,4},{1,9},{5,13},{9,1},{13,5},{2,10},{6,14},... | collective-permute-start | bytes 36872 | tf_op jit(solution)/shard_map/ppermute | solution.py:30
  165.4 1.6 conv_gradient.1
  167.1 5.6 %fusion.40 = f32[3,3,384,256]{3,2,1,0:T(8,128)S(1)} fusion(bf16[13,13,16,384]{3,2,1,0:T(8,128)(2,1)S(1)} %bitcast.152, bf16[13,13,16,256]{3,2,1,0:T(8,128)(2,1)S(1)} %bitcast.158), kind=kOutput, calls=%fused_computation.129 | convolution fusion | flops 4306501632 | bytes 7000064 | tf_op jit(solution)/shard_map/conv_general_dilated | solution.py:686
  172.8 1.7 split_kernels.1
  174.6 2.1 collective-permute-start.40
  176.7 2.5 %collective-permute-done.40 = f32[3,256]{1,0:T(4,128)S(1)} collective-permute-done((f32[3,256]{1,0:T(4,128)S(1)}, f32[3,256]{1,0:T(4,128)S(1)}, u32[]{:S(2)}, u32[]{:S(2)}) %collective-permute-start.40) | collective-permute-done | bytes 3104 | tf_op jit(solution)/shard_map/ppermute | solution.py:30
  180.4 1.2 collective-permute-start.42
  181.9 1.9 collective-permute-start.37
  183.8 2.5 %collective-permute-start.36 = (bf16[864,128]{1,0:T(8,128)(2,1)S(1)}, bf16[864,128]{1,0:T(8,128)(2,1)S(1)}, u32[]{:S(2)}, u32[]{:S(2)}) collective-permute-start(bf16[864,128]{1,0:T(8,128)(2,1)S(1)} %get-tuple-element.78), channel_id=1, source_target_pairs={{0,8},{4,12},{8,0},{12,4},{1,9},{5,13},{9,1},{13,5},{2,10},{6,14},... | collective-permute-start | bytes 663560 | tf_op jit(solution)/shard_map/ppermute | solution.py:30
  186.3 6.8 %convolution_convert_fusion = bf16[13,13,16,384]{3,2,1,0:T(8,128)(2,1)S(1)} fusion(bf16[13,13,16,256]{3,2,1,0:T(8,128)(2,1)S(1)} %bitcast.159, bf16[3,3,384,256]{3,2,1,0:T(8,128)(2,1)S(1)} %bitcast.157), kind=kOutput, calls=%fused_computation.10 | convolution fusion | flops 4307539968 | bytes 5230592 | tf_op jit(solution)/shard_map/conv_general_dilated | solution.py:671
  193.2 3.7 %pack_grad.1 = (bf16[688,384]{1,0:T(8,128)(2,1)S(1)}, bf16[688,384]{1,0:T(8,128)(2,1)}, bf16[688,384]{1,0:T(8,128)(2,1)}, bf16[688,384]{1,0:T(8,128)(2,1)}) custom-call(s32[1]{0:T(128)S(6)} %select_n.153.sel, bf16[2704,384]{1,0:T(8,128)(2,1)S(1)} %bitcast.153), custom_call_target="tpu_custom_call" | custom-call | tf_op jit(solution)/shard_map/pack_grad/pallas_call | solution.py:190
  197.0 4.0 %place_grad.4.refs_0_ = bf16[4,2704,96]{2,1,0:T(8,128)(2,1)} custom-call(s32[1]{0:T(128)} %bitcast.2.sel, bf16[688,384]{1,0:T(8,128)(2,1)S(1)} %get-tuple-element.40.wire), custom_call_target="tpu_custom_call" | custom-call | tf_op jit(solution)/shard_map/place_grad/pallas_call | solution.py:231
  201.0 1.2 collective-permute-start.32
  205.4 4.0 %place_grad.5.refs_0_ = bf16[4,2704,96]{2,1,0:T(8,128)(2,1)} custom-call(s32[1]{0:T(128)} %bitcast.14.sel, bf16[688,384]{1,0:T(8,128)(2,1)S(1)} %collective-permute-done.33.wire, bf16[4,2704,96]{2,1,0:T(8,128)(2,1)} %place_grad.4.refs_0_), custom_call_target="tpu_custom_call", output_to_operand_aliasing={{}: (2, {})} | custom-call | tf_op jit(solution)/shard_map/place_grad/pallas_call | solution.py:231
  209.4 13.0 %collective-permute-done.32.wire = bf16[688,384]{1,0:T(8,128)(2,1)S(1)} collective-permute-done((bf16[688,384]{1,0:T(8,128)(2,1)}, bf16[688,384]{1,0:T(8,128)(2,1)S(1)}, u32[]{:S(2)}, u32[]{:S(2)}) %collective-permute-start.32) | collective-permute-done | bytes 528416 | tf_op jit(solution)/shard_map/ppermute | solution.py:30
  222.4 4.0 %place_grad.6.refs_0_ = bf16[4,2704,96]{2,1,0:T(8,128)(2,1)} custom-call(s32[1]{0:T(128)} %bitcast.18.sel, bf16[688,384]{1,0:T(8,128)(2,1)S(1)} %collective-permute-done.32.wire, bf16[4,2704,96]{2,1,0:T(8,128)(2,1)} %place_grad.5.refs_0_), custom_call_target="tpu_custom_call", output_to_operand_aliasing={{}: (2, {})} | custom-call | tf_op jit(solution)/shard_map/place_grad/pallas_call | solution.py:231
  226.4 4.0 %place_grad.7 = bf16[4,2704,96]{2,1,0:T(8,128)(2,1)} custom-call(s32[1]{0:T(128)} %bitcast.17.sel, bf16[688,384]{1,0:T(8,128)(2,1)S(1)} %collective-permute-done.31.wire, bf16[4,2704,96]{2,1,0:T(8,128)(2,1)} %place_grad.6.refs_0_), custom_call_target="tpu_custom_call", output_to_operand_aliasing={{}: (2, {})} | custom-call | tf_op jit(solution)/shard_map/place_grad/pallas_call | solution.py:231
  (175 shorter events, 22.3 us)
Async XLA Ops:
  1.8 12.0 %collective-permute-start = (bf16[64,896]{1,0:T(8,128)(2,1)S(1)}, bf16[64,896]{1,0:T(8,128)(2,1)S(1)}, u32[]{:S(2)}, u32[]{:S(2)}) collective-permute-start(bf16[64,896]{1,0:T(8,128)(2,1)S(1)} %maximum_maximum_fusion), channel_id=1, source_target_pairs={{0,2},{1,3},{2,0},{3,1},{4,6},{5,7},{6,4},{7,5},{8,10},{9,11},{10,... | collective-permute-start | bytes 344072 | tf_op jit(solution)/shard_map/ppermute | solution.py:30
  9.1 29.4 %collective-permute-start.8 = (bf16[688,384]{1,0:T(8,128)(2,1)S(1)}, bf16[688,384]{1,0:T(8,128)(2,1)S(1)}, u32[]{:S(2)}, u32[]{:S(2)}) collective-permute-start(bf16[688,384]{1,0:T(8,128)(2,1)S(1)} %get-tuple-element.28), channel_id=1, source_target_pairs={{0,1},{1,0},{2,3},{3,2},{4,5},{5,4},{6,7},{7,6},{8,9},{9,8},{10,11... | collective-permute-start | bytes 1585160 | tf_op jit(solution)/shard_map/ppermute | solution.py:30
  9.2 16.0 %copy-start.32 = (s32[4]{0:T(128)S(1)}, s32[4]{0:T(128)}, u32[]{:S(2)}) copy-start(s32[4]{0:T(128)} %param.10) | copy-start | bytes 52
  13.2 25.9 %collective-permute-start.9 = (bf16[688,384]{1,0:T(8,128)(2,1)}, bf16[688,384]{1,0:T(8,128)(2,1)S(1)}, u32[]{:S(2)}, u32[]{:S(2)}) collective-permute-start(bf16[688,384]{1,0:T(8,128)(2,1)} %get-tuple-element.29), channel_id=1, source_target_pairs={{0,2},{1,3},{2,0},{3,1},{4,6},{5,7},{6,4},{7,5},{8,10},{9,11},{10,... | collective-permute-start | bytes 1585160 | tf_op jit(solution)/shard_map/ppermute | solution.py:30
  14.5 10.2 %collective-permute-start.1 = (bf16[2,64,896]{2,1,0:T(8,128)(2,1)}, bf16[2,64,896]{2,1,0:T(8,128)(2,1)}, u32[]{:S(2)}, u32[]{:S(2)}) collective-permute-start(bf16[2,64,896]{2,1,0:T(8,128)(2,1)} %pad_maximum_fusion.3.refs_0_), channel_id=1, source_target_pairs={{0,4},{4,0},{8,12},{12,8},{1,5},{5,1},{9,13},{13,9},{2,6},{6,2},{1... | collective-permute-start | bytes 688136 | tf_op jit(solution)/shard_map/ppermute | solution.py:30
  14.5 19.2 %collective-permute-start.2 = (bf16[2,64,896]{2,1,0:T(8,128)(2,1)}, bf16[2,64,896]{2,1,0:T(8,128)(2,1)}, u32[]{:S(2)}, u32[]{:S(2)}) collective-permute-start(bf16[2,64,896]{2,1,0:T(8,128)(2,1)} %pad_maximum_fusion.3.refs_0_), channel_id=1, source_target_pairs={{0,8},{4,12},{8,0},{12,4},{1,9},{5,13},{9,1},{13,5},{2,10},{6,14},... | collective-permute-start | bytes 688136 | tf_op jit(solution)/shard_map/ppermute | solution.py:30
  17.6 21.0 %collective-permute-start.3 = (bf16[2,64,896]{2,1,0:T(8,128)(2,1)}, bf16[2,64,896]{2,1,0:T(8,128)(2,1)}, u32[]{:S(2)}, u32[]{:S(2)}) collective-permute-start(bf16[2,64,896]{2,1,0:T(8,128)(2,1)} %pad_maximum_fusion.3.refs_0_), channel_id=1, source_target_pairs={{0,12},{4,8},{8,4},{12,0},{1,13},{5,9},{9,5},{13,1},{2,14},{6,10},... | collective-permute-start | bytes 688136 | tf_op jit(solution)/shard_map/ppermute | solution.py:30
  24.7 15.3 %collective-permute-start.10 = (bf16[688,384]{1,0:T(8,128)(2,1)S(1)}, bf16[688,384]{1,0:T(8,128)(2,1)S(1)}, u32[]{:S(2)}, u32[]{:S(2)}) collective-permute-start(bf16[688,384]{1,0:T(8,128)(2,1)S(1)} %get-tuple-element.30), channel_id=1, source_target_pairs={{0,3},{1,2},{2,1},{3,0},{4,7},{5,6},{6,5},{7,4},{8,11},{9,10},{10,... | collective-permute-start | bytes 1585160 | tf_op jit(solution)/shard_map/ppermute | solution.py:30
  33.7 14.4 %collective-permute-start.4 = (bf16[2,64,896]{2,1,0:T(8,128)(2,1)}, bf16[2,64,896]{2,1,0:T(8,128)(2,1)}, u32[]{:S(2)}, u32[]{:S(2)}) collective-permute-start(bf16[2,64,896]{2,1,0:T(8,128)(2,1)} %pad_maximum_fusion.3.refs_0_), channel_id=1, source_target_pairs={{0,1},{1,0},{2,3},{3,2},{4,5},{5,4},{6,7},{7,6},{8,9},{9,8},{10,11... | collective-permute-start | bytes 688136 | tf_op jit(solution)/shard_map/ppermute | solution.py:30
  38.5 9.6 %collective-permute-start.5 = (bf16[2,64,896]{2,1,0:T(8,128)(2,1)}, bf16[2,64,896]{2,1,0:T(8,128)(2,1)}, u32[]{:S(2)}, u32[]{:S(2)}) collective-permute-start(bf16[2,64,896]{2,1,0:T(8,128)(2,1)} %collective-permute-done.1.refs_1_), channel_id=1, source_target_pairs={{0,1},{1,0},{2,3},{3,2},{4,5},{5,4},{6,7},{7,6},{8,9},{9,8},{10,11... | collective-permute-start | bytes 688136 | tf_op jit(solution)/shard_map/ppermute | solution.py:30
  38.5 9.6 %collective-permute-start.6 = (bf16[2,64,896]{2,1,0:T(8,128)(2,1)}, bf16[2,64,896]{2,1,0:T(8,128)(2,1)}, u32[]{:S(2)}, u32[]{:S(2)}) collective-permute-start(bf16[2,64,896]{2,1,0:T(8,128)(2,1)} %collective-permute-done.2.refs_2_), channel_id=1, source_target_pairs={{0,1},{1,0},{2,3},{3,2},{4,5},{5,4},{6,7},{7,6},{8,9},{9,8},{10,11... | collective-permute-start | bytes 688136 | tf_op jit(solution)/shard_map/ppermute | solution.py:30
  39.9 8.2 %collective-permute-start.7 = (bf16[2,64,896]{2,1,0:T(8,128)(2,1)}, bf16[2,64,896]{2,1,0:T(8,128)(2,1)}, u32[]{:S(2)}, u32[]{:S(2)}) collective-permute-start(bf16[2,64,896]{2,1,0:T(8,128)(2,1)} %collective-permute-done.3.refs_3_), channel_id=1, source_target_pairs={{0,1},{1,0},{2,3},{3,2},{4,5},{5,4},{6,7},{7,6},{8,9},{9,8},{10,11... | collective-permute-start | bytes 688136 | tf_op jit(solution)/shard_map/ppermute | solution.py:30
  62.1 9.7 %collective-permute-start.11 = (bf16[6,6,16,256]{3,2,1,0:T(8,128)(2,1)}, bf16[6,6,16,256]{3,2,1,0:T(8,128)(2,1)}, u32[]{:S(2)}, u32[]{:S(2)}) collective-permute-start(bf16[6,6,16,256]{3,2,1,0:T(8,128)(2,1)} %get-tuple-element.66), channel_id=1, source_target_pairs={{0,16},{16,0},{1,17},{17,1},{2,18},{18,2},{3,19},{19,3},{4,20},{20... | collective-permute-start | bytes 884744 | tf_op jit(solution)/shard_map/ppermute | solution.py:30
  73.6 9.2 %collective-permute-start.14 = (bf16[9,16,256]{2,1,0:T(8,128)(2,1)}, bf16[9,16,256]{2,1,0:T(8,128)(2,1)}, u32[]{:S(2)}, u32[]{:S(2)}) collective-permute-start(bf16[9,16,256]{2,1,0:T(8,128)(2,1)} %get-tuple-element.94), channel_id=1, source_target_pairs={{0,12},{4,8},{8,4},{12,0},{1,13},{5,9},{9,5},{13,1},{2,14},{6,10},... | collective-permute-start | bytes 221192 | tf_op jit(solution)/shard_map/ppermute | solution.py:30
  75.1 7.6 %collective-permute-start.13 = (bf16[9,16,256]{2,1,0:T(8,128)(2,1)}, bf16[9,16,256]{2,1,0:T(8,128)(2,1)}, u32[]{:S(2)}, u32[]{:S(2)}) collective-permute-start(bf16[9,16,256]{2,1,0:T(8,128)(2,1)} %get-tuple-element.95), channel_id=1, source_target_pairs={{0,8},{4,12},{8,0},{12,4},{1,9},{5,13},{9,1},{13,5},{2,10},{6,14},... | collective-permute-start | bytes 221192 | tf_op jit(solution)/shard_map/ppermute | solution.py:30
  76.9 14.5 %copy-start.30 = (f32[2,2,1024]{2,1,0:T(2,128)S(1)}, f32[2,2,1024]{2,1,0:T(2,128)}, u32[]{:S(2)}) copy-start(f32[2,2,1024]{2,1,0:T(2,128)} %param.16) | copy-start | bytes 49156
  76.9 5.8 %collective-permute-start.12 = (bf16[9,16,256]{2,1,0:T(8,128)(2,1)S(1)}, bf16[9,16,256]{2,1,0:T(8,128)(2,1)}, u32[]{:S(2)}, u32[]{:S(2)}) collective-permute-start(bf16[9,16,256]{2,1,0:T(8,128)(2,1)S(1)} %get-tuple-element.96), channel_id=1, source_target_pairs={{0,4},{4,0},{8,12},{12,8},{1,5},{5,1},{9,13},{13,9},{2,6},{6,2},{1... | collective-permute-start | bytes 221192 | tf_op jit(solution)/shard_map/ppermute | solution.py:30
  83.8 13.0 %copy-start.6 = (bf16[4,9,16,256]{3,2,1,0:T(8,128)(2,1)}, bf16[4,9,16,256]{3,2,1,0:T(8,128)(2,1)S(1)}, u32[]{:S(2)}) copy-start(bf16[4,9,16,256]{3,2,1,0:T(8,128)(2,1)S(1)} %pad_maximum_fusion.a0) | copy-start | bytes 884740
  83.8 7.7 %collective-permute-start.16 = (bf16[4,9,16,256]{3,2,1,0:T(8,128)(2,1)S(1)}, bf16[4,9,16,256]{3,2,1,0:T(8,128)(2,1)S(1)}, u32[]{:S(2)}, u32[]{:S(2)}) collective-permute-start(bf16[4,9,16,256]{3,2,1,0:T(8,128)(2,1)S(1)} %pad_maximum_fusion.a0), channel_id=1, source_target_pairs={{0,2},{1,3},{2,0},{3,1},{4,6},{5,7},{6,4},{7,5},{8,10},{9,11},{10,... | collective-permute-start | bytes 884744 | tf_op jit(solution)/shard_map/ppermute | solution.py:30
  85.8 5.7 %collective-permute-start.15 = (bf16[4,9,16,256]{3,2,1,0:T(8,128)(2,1)S(1)}, bf16[4,9,16,256]{3,2,1,0:T(8,128)(2,1)S(1)}, u32[]{:S(2)}, u32[]{:S(2)}) collective-permute-start(bf16[4,9,16,256]{3,2,1,0:T(8,128)(2,1)S(1)} %pad_maximum_fusion.a0), channel_id=1, source_target_pairs={{0,1},{1,0},{2,3},{3,2},{4,5},{5,4},{6,7},{7,6},{8,9},{9,8},{10,11... | collective-permute-start | bytes 884744 | tf_op jit(solution)/shard_map/ppermute | solution.py:30
  91.5 5.3 %copy-start.10 = (bf16[4,9,16,256]{3,2,1,0:T(8,128)(2,1)}, bf16[4,9,16,256]{3,2,1,0:T(8,128)(2,1)S(1)}, u32[]{:S(2)}) copy-start(bf16[4,9,16,256]{3,2,1,0:T(8,128)(2,1)S(1)} %collective-permute-done.16.a2) | copy-start | bytes 884740
  91.5 1.6 collective-permute-start.17
  91.5 10.3 %copy-start.31 = (f32[2,1024]{1,0:T(2,128)S(1)}, f32[2,1024]{1,0:T(2,128)}, u32[]{:S(2)}) copy-start(f32[2,1024]{1,0:T(2,128)} %param.15) | copy-start | bytes 24580
  91.6 5.2 %copy-start.12 = (bf16[4,9,16,256]{3,2,1,0:T(8,128)(2,1)}, bf16[4,9,16,256]{3,2,1,0:T(8,128)(2,1)S(1)}, u32[]{:S(2)}) copy-start(bf16[4,9,16,256]{3,2,1,0:T(8,128)(2,1)S(1)} %collective-permute-done.15.a1) | copy-start | bytes 884740
  95.4 31.4 %copy-start.3 = (bf16[2304,1024]{1,0:T(8,128)(2,1)S(1)}, bf16[2304,1024]{1,0:T(8,128)(2,1)}, u32[]{:S(2)}) copy-start(bf16[2304,1024]{1,0:T(8,128)(2,1)} %dynamic-slice_bitcast_fusion.weight) | copy-start | bytes 14155780
  96.9 9.9 %collective-permute-start.20 = (bf16[4,16,1024]{2,1,0:T(8,128)(2,1)S(1)}, bf16[4,16,1024]{2,1,0:T(8,128)(2,1)S(1)}, u32[]{:S(2)}, u32[]{:S(2)}) collective-permute-start(bf16[4,16,1024]{2,1,0:T(8,128)(2,1)S(1)} %get-tuple-element.83), channel_id=1, source_target_pairs={{0,12},{4,8},{8,4},{12,0},{1,13},{5,9},{9,5},{13,1},{2,14},{6,10},... | collective-permute-start | bytes 393224 | tf_op jit(solution)/shard_map/ppermute | solution.py:30
  98.4 11.5 %collective-permute-start.19 = (bf16[4,16,1024]{2,1,0:T(8,128)(2,1)S(1)}, bf16[4,16,1024]{2,1,0:T(8,128)(2,1)S(1)}, u32[]{:S(2)}, u32[]{:S(2)}) collective-permute-start(bf16[4,16,1024]{2,1,0:T(8,128)(2,1)S(1)} %get-tuple-element.84), channel_id=1, source_target_pairs={{0,8},{4,12},{8,0},{12,4},{1,9},{5,13},{9,1},{13,5},{2,10},{6,14},... | collective-permute-start | bytes 393224 | tf_op jit(solution)/shard_map/ppermute | solution.py:30
  101.8 8.7 %collective-permute-start.18 = (bf16[4,16,1024]{2,1,0:T(8,128)(2,1)S(1)}, bf16[4,16,1024]{2,1,0:T(8,128)(2,1)S(1)}, u32[]{:S(2)}, u32[]{:S(2)}) collective-permute-start(bf16[4,16,1024]{2,1,0:T(8,128)(2,1)S(1)} %get-tuple-element.82), channel_id=1, source_target_pairs={{0,4},{4,0},{8,12},{12,8},{1,5},{5,1},{9,13},{13,9},{2,6},{6,2},{1... | collective-permute-start | bytes 393224 | tf_op jit(solution)/shard_map/ppermute | solution.py:30
  101.9 21.9 %copy-start.29 = (f32[2,4,16,1024]{3,2,1,0:T(8,128)}, f32[2,4,16,1024]{3,2,1,0:T(8,128)S(1)}, u32[]{:S(2)}) copy-start(f32[2,4,16,1024]{3,2,1,0:T(8,128)S(1)} %maximum_convert_fusion) | copy-start | bytes 1572868
  111.6 6.9 %collective-permute-start.22 = (bf16[4,16,1024]{2,1,0:T(8,128)(2,1)S(1)}, bf16[4,16,1024]{2,1,0:T(8,128)(2,1)S(1)}, u32[]{:S(2)}, u32[]{:S(2)}) collective-permute-start(bf16[4,16,1024]{2,1,0:T(8,128)(2,1)S(1)} %get-tuple-element.63.g0), channel_id=1, source_target_pairs={{0,4},{4,0},{8,12},{12,8},{1,5},{5,1},{9,13},{13,9},{2,6},{6,2},{1... | collective-permute-start | bytes 393224 | tf_op jit(solution)/shard_map/ppermute | solution.py:30
  113.5 10.3 %collective-permute-start.23 = (bf16[4,16,1024]{2,1,0:T(8,128)(2,1)S(1)}, bf16[4,16,1024]{2,1,0:T(8,128)(2,1)S(1)}, u32[]{:S(2)}, u32[]{:S(2)}) collective-permute-start(bf16[4,16,1024]{2,1,0:T(8,128)(2,1)S(1)} %get-tuple-element.63.g0), channel_id=1, source_target_pairs={{0,8},{4,12},{8,0},{12,4},{1,9},{5,13},{9,1},{13,5},{2,10},{6,14},... | collective-permute-start | bytes 393224 | tf_op jit(solution)/shard_map/ppermute | solution.py:30
  114.3 12.5 %collective-permute-start.24 = (bf16[4,16,1024]{2,1,0:T(8,128)(2,1)S(1)}, bf16[4,16,1024]{2,1,0:T(8,128)(2,1)S(1)}, u32[]{:S(2)}, u32[]{:S(2)}) collective-permute-start(bf16[4,16,1024]{2,1,0:T(8,128)(2,1)S(1)} %get-tuple-element.63.g0), channel_id=1, source_target_pairs={{0,12},{4,8},{8,4},{12,0},{1,13},{5,9},{9,5},{13,1},{2,14},{6,10},... | collective-permute-start | bytes 393224 | tf_op jit(solution)/shard_map/ppermute | solution.py:30
  118.5 10.8 %copy-start.21 = (bf16[4,16,1024]{2,1,0:T(8,128)(2,1)}, bf16[4,16,1024]{2,1,0:T(8,128)(2,1)S(1)}, u32[]{:S(2)}) copy-start(bf16[4,16,1024]{2,1,0:T(8,128)(2,1)S(1)} %collective-permute-done.22.g1) | copy-start | bytes 393220
  123.8 6.5 %copy-start.23 = (bf16[4,16,1024]{2,1,0:T(8,128)(2,1)}, bf16[4,16,1024]{2,1,0:T(8,128)(2,1)S(1)}, u32[]{:S(2)}) copy-start(bf16[4,16,1024]{2,1,0:T(8,128)(2,1)S(1)} %collective-permute-done.23.g2) | copy-start | bytes 393220
  130.3 7.4 %collective-permute-start.25 = (bf16[2,4,9,16,256]{4,3,2,1,0:T(8,128)(2,1)}, bf16[2,4,9,16,256]{4,3,2,1,0:T(8,128)(2,1)}, u32[]{:S(2)}, u32[]{:S(2)}) collective-permute-start(bf16[2,4,9,16,256]{4,3,2,1,0:T(8,128)(2,1)} %get-tuple-element.35), channel_id=1, source_target_pairs={{0,1},{1,0},{2,3},{3,2},{4,5},{5,4},{6,7},{7,6},{8,9},{9,8},{10,11... | collective-permute-start | bytes 1769480 | tf_op jit(solution)/shard_map/ppermute | solution.py:30
  130.3 6.2 %collective-permute-start.21 = (bf16[4,16,1024]{2,1,0:T(8,128)(2,1)}, bf16[4,16,1024]{2,1,0:T(8,128)(2,1)}, u32[]{:S(2)}, u32[]{:S(2)}) collective-permute-start(bf16[4,16,1024]{2,1,0:T(8,128)(2,1)} %get-tuple-element.79), channel_id=1, source_target_pairs={{0,16},{16,0},{1,17},{17,1},{2,18},{18,2},{3,19},{19,3},{4,20},{20... | collective-permute-start | bytes 393224 | tf_op jit(solution)/shard_map/ppermute | solution.py:30
  139.3 18.2 %copy-start.7 = (bf16[4,9,16,256]{3,2,1,0:T(8,128)(2,1)S(1)}, bf16[4,9,16,256]{3,2,1,0:T(8,128)(2,1)}, u32[]{:S(2)}) copy-start(bf16[4,9,16,256]{3,2,1,0:T(8,128)(2,1)} %copy-done.6) | copy-start | bytes 884740
  139.4 18.2 %copy-start.11 = (bf16[4,9,16,256]{3,2,1,0:T(8,128)(2,1)S(1)}, bf16[4,9,16,256]{3,2,1,0:T(8,128)(2,1)}, u32[]{:S(2)}) copy-start(bf16[4,9,16,256]{3,2,1,0:T(8,128)(2,1)} %copy-done.10) | copy-start | bytes 884740
  139.4 18.2 %copy-start.13 = (bf16[4,9,16,256]{3,2,1,0:T(8,128)(2,1)S(1)}, bf16[4,9,16,256]{3,2,1,0:T(8,128)(2,1)}, u32[]{:S(2)}) copy-start(bf16[4,9,16,256]{3,2,1,0:T(8,128)(2,1)} %copy-done.12) | copy-start | bytes 884740
  139.4 18.2 %copy-start.15 = (bf16[4,9,16,256]{3,2,1,0:T(8,128)(2,1)S(1)}, bf16[4,9,16,256]{3,2,1,0:T(8,128)(2,1)}, u32[]{:S(2)}) copy-start(bf16[4,9,16,256]{3,2,1,0:T(8,128)(2,1)} %copy-done.14) | copy-start | bytes 884740
  139.4 18.2 %copy-start.22 = (bf16[4,16,1024]{2,1,0:T(8,128)(2,1)S(1)}, bf16[4,16,1024]{2,1,0:T(8,128)(2,1)}, u32[]{:S(2)}) copy-start(bf16[4,16,1024]{2,1,0:T(8,128)(2,1)} %copy-done.21) | copy-start | bytes 393220
  139.4 18.2 %copy-start.24 = (bf16[4,16,1024]{2,1,0:T(8,128)(2,1)S(1)}, bf16[4,16,1024]{2,1,0:T(8,128)(2,1)}, u32[]{:S(2)}) copy-start(bf16[4,16,1024]{2,1,0:T(8,128)(2,1)} %copy-done.23) | copy-start | bytes 393220
  139.4 18.2 %copy-start.26 = (bf16[4,16,1024]{2,1,0:T(8,128)(2,1)S(1)}, bf16[4,16,1024]{2,1,0:T(8,128)(2,1)}, u32[]{:S(2)}) copy-start(bf16[4,16,1024]{2,1,0:T(8,128)(2,1)} %copy-done.25) | copy-start | bytes 393220
  139.5 8.6 %collective-permute-start.26 = (bf16[4,9,16,256]{3,2,1,0:T(8,128)(2,1)S(1)}, bf16[4,9,16,256]{3,2,1,0:T(8,128)(2,1)S(1)}, u32[]{:S(2)}, u32[]{:S(2)}) collective-permute-start(bf16[4,9,16,256]{3,2,1,0:T(8,128)(2,1)S(1)} %fusion.11), channel_id=1, source_target_pairs={{0,2},{1,3},{2,0},{3,1},{4,6},{5,7},{6,4},{7,5},{8,10},{9,11},{10,... | collective-permute-start | bytes 884744 | tf_op jit(solution)/shard_map/ppermute | solution.py:30
  140.7 21.5 %collective-permute-start.43 = (f32[3,1024]{1,0:T(4,128)S(1)}, f32[3,1024]{1,0:T(4,128)S(1)}, u32[]{:S(2)}, u32[]{:S(2)}) collective-permute-start(f32[3,1024]{1,0:T(4,128)S(1)} %pad_maximum_fusion.4), channel_id=1, source_target_pairs={{0,4},{4,0},{8,12},{12,8},{1,5},{5,1},{9,13},{13,9},{2,6},{6,2},{1... | collective-permute-start | bytes 36872 | tf_op jit(solution)/shard_map/ppermute | solution.py:30
  148.2 6.9 %collective-permute-start.29 = (bf16[9,16,256]{2,1,0:T(8,128)(2,1)S(1)}, bf16[9,16,256]{2,1,0:T(8,128)(2,1)S(1)}, u32[]{:S(2)}, u32[]{:S(2)}) collective-permute-start(bf16[9,16,256]{2,1,0:T(8,128)(2,1)S(1)} %get-tuple-element.90), channel_id=1, source_target_pairs={{0,12},{4,8},{8,4},{12,0},{1,13},{5,9},{9,5},{13,1},{2,14},{6,10},... | collective-permute-start | bytes 221192 | tf_op jit(solution)/shard_map/ppermute | solution.py:30
  149.6 5.6 %collective-permute-start.28 = (bf16[9,16,256]{2,1,0:T(8,128)(2,1)S(1)}, bf16[9,16,256]{2,1,0:T(8,128)(2,1)S(1)}, u32[]{:S(2)}, u32[]{:S(2)}) collective-permute-start(bf16[9,16,256]{2,1,0:T(8,128)(2,1)S(1)} %get-tuple-element.91), channel_id=1, source_target_pairs={{0,8},{4,12},{8,0},{12,4},{1,9},{5,13},{9,1},{13,5},{2,10},{6,14},... | collective-permute-start | bytes 221192 | tf_op jit(solution)/shard_map/ppermute | solution.py:30
  150.6 4.5 %collective-permute-start.27 = (bf16[9,16,256]{2,1,0:T(8,128)(2,1)S(1)}, bf16[9,16,256]{2,1,0:T(8,128)(2,1)S(1)}, u32[]{:S(2)}, u32[]{:S(2)}) collective-permute-start(bf16[9,16,256]{2,1,0:T(8,128)(2,1)S(1)} %get-tuple-element.92), channel_id=1, source_target_pairs={{0,4},{4,0},{8,12},{12,8},{1,5},{5,1},{9,13},{13,9},{2,6},{6,2},{1... | collective-permute-start | bytes 221192 | tf_op jit(solution)/shard_map/ppermute | solution.py:30
  155.3 10.1 %collective-permute-start.30 = (bf16[36,16,256]{2,1,0:T(8,128)(2,1)S(1)}, bf16[36,16,256]{2,1,0:T(8,128)(2,1)S(1)}, u32[]{:S(2)}, u32[]{:S(2)}) collective-permute-start(bf16[36,16,256]{2,1,0:T(8,128)(2,1)S(1)} %bitcast.154), channel_id=1, source_target_pairs={{0,16},{16,0},{1,17},{17,1},{2,18},{18,2},{3,19},{19,3},{4,20},{20... | collective-permute-start | bytes 884744 | tf_op jit(solution)/shard_map/ppermute | solution.py:30
  162.2 5.0 %copy-start.9 = (bf16[2704,384]{1,0:T(8,128)(2,1)S(1)}, bf16[2704,384]{1,0:T(8,128)(2,1)}, u32[]{:S(2)}) copy-start(bf16[2704,384]{1,0:T(8,128)(2,1)} %copy-done.8) | copy-start | bytes 6230020
  162.2 14.4 %collective-permute-start.44 = (f32[3,1024]{1,0:T(4,128)S(1)}, f32[3,1024]{1,0:T(4,128)S(1)}, u32[]{:S(2)}, u32[]{:S(2)}) collective-permute-start(f32[3,1024]{1,0:T(4,128)S(1)} %fusion.33), channel_id=1, source_target_pairs={{0,8},{4,12},{8,0},{12,4},{1,9},{5,13},{9,1},{13,5},{2,10},{6,14},... | collective-permute-start | bytes 36872 | tf_op jit(solution)/shard_map/ppermute | solution.py:30
  167.0 7.5 %collective-permute-start.39 = (f32[3,256]{1,0:T(4,128)S(1)}, f32[3,256]{1,0:T(4,128)S(1)}, u32[]{:S(2)}, u32[]{:S(2)}) collective-permute-start(f32[3,256]{1,0:T(4,128)S(1)} %pad_maximum_fusion.6), channel_id=1, source_target_pairs={{0,4},{4,0},{8,12},{12,8},{1,5},{5,1},{9,13},{13,9},{2,6},{6,2},{1... | collective-permute-start | bytes 9224 | tf_op jit(solution)/shard_map/ppermute | solution.py:30
  174.5 7.2 %collective-permute-start.34 = (bf16[3456,128]{1,0:T(8,128)(2,1)S(1)}, bf16[3456,128]{1,0:T(8,128)(2,1)S(1)}, u32[]{:S(2)}, u32[]{:S(2)}) collective-permute-start(bf16[3456,128]{1,0:T(8,128)(2,1)S(1)} %get-tuple-element.42), channel_id=1, source_target_pairs={{0,1},{1,0},{2,3},{3,2},{4,5},{5,4},{6,7},{7,6},{8,9},{9,8},{10,11... | collective-permute-start | bytes 2654216 | tf_op jit(solution)/shard_map/ppermute | solution.py:30
  174.6 4.6 %collective-permute-start.40 = (f32[3,256]{1,0:T(4,128)S(1)}, f32[3,256]{1,0:T(4,128)S(1)}, u32[]{:S(2)}, u32[]{:S(2)}) collective-permute-start(f32[3,256]{1,0:T(4,128)S(1)} %fusion.32), channel_id=1, source_target_pairs={{0,8},{4,12},{8,0},{12,4},{1,9},{5,13},{9,1},{13,5},{2,10},{6,14},... | collective-permute-start | bytes 9224 | tf_op jit(solution)/shard_map/ppermute | solution.py:30
  179.1 1.3 collective-permute-start.41
  180.4 20.6 %collective-permute-start.42 = (f32[3,256]{1,0:T(4,128)S(1)}, f32[3,256]{1,0:T(4,128)S(1)}, u32[]{:S(2)}, u32[]{:S(2)}) collective-permute-start(f32[3,256]{1,0:T(4,128)S(1)} %add.277), channel_id=1, source_target_pairs={{0,2},{1,3},{2,0},{3,1},{4,6},{5,7},{6,4},{7,5},{8,10},{9,11},{10,... | collective-permute-start | bytes 9224 | tf_op jit(solution)/shard_map/ppermute | solution.py:30
  181.9 20.4 %collective-permute-start.37 = (bf16[864,128]{1,0:T(8,128)(2,1)S(1)}, bf16[864,128]{1,0:T(8,128)(2,1)S(1)}, u32[]{:S(2)}, u32[]{:S(2)}) collective-permute-start(bf16[864,128]{1,0:T(8,128)(2,1)S(1)} %get-tuple-element.77), channel_id=1, source_target_pairs={{0,12},{4,8},{8,4},{12,0},{1,13},{5,9},{9,5},{13,1},{2,14},{6,10},... | collective-permute-start | bytes 663560 | tf_op jit(solution)/shard_map/ppermute | solution.py:30
  183.8 19.3 %collective-permute-start.36 = (bf16[864,128]{1,0:T(8,128)(2,1)S(1)}, bf16[864,128]{1,0:T(8,128)(2,1)S(1)}, u32[]{:S(2)}, u32[]{:S(2)}) collective-permute-start(bf16[864,128]{1,0:T(8,128)(2,1)S(1)} %get-tuple-element.78), channel_id=1, source_target_pairs={{0,8},{4,12},{8,0},{12,4},{1,9},{5,13},{9,1},{13,5},{2,10},{6,14},... | collective-permute-start | bytes 663560 | tf_op jit(solution)/shard_map/ppermute | solution.py:30
  186.3 16.8 %collective-permute-start.35 = (bf16[864,128]{1,0:T(8,128)(2,1)S(1)}, bf16[864,128]{1,0:T(8,128)(2,1)S(1)}, u32[]{:S(2)}, u32[]{:S(2)}) collective-permute-start(bf16[864,128]{1,0:T(8,128)(2,1)S(1)} %get-tuple-element.76), channel_id=1, source_target_pairs={{0,4},{4,0},{8,12},{12,8},{1,5},{5,1},{9,13},{13,9},{2,6},{6,2},{1... | collective-permute-start | bytes 663560 | tf_op jit(solution)/shard_map/ppermute | solution.py:30
  196.8 29.6 %collective-permute-start.31 = (bf16[688,384]{1,0:T(8,128)(2,1)}, bf16[688,384]{1,0:T(8,128)(2,1)S(1)}, u32[]{:S(2)}, u32[]{:S(2)}) collective-permute-start(bf16[688,384]{1,0:T(8,128)(2,1)} %get-tuple-element.37), channel_id=1, source_target_pairs={{0,3},{1,2},{2,1},{3,0},{4,7},{5,6},{6,5},{7,4},{8,11},{9,10},{10,... | collective-permute-start | bytes 1585160 | tf_op jit(solution)/shard_map/ppermute | solution.py:30
  201.0 21.4 %collective-permute-start.32 = (bf16[688,384]{1,0:T(8,128)(2,1)}, bf16[688,384]{1,0:T(8,128)(2,1)S(1)}, u32[]{:S(2)}, u32[]{:S(2)}) collective-permute-start(bf16[688,384]{1,0:T(8,128)(2,1)} %get-tuple-element.38), channel_id=1, source_target_pairs={{0,2},{1,3},{2,0},{3,1},{4,6},{5,7},{6,4},{7,5},{8,10},{9,11},{10,... | collective-permute-start | bytes 1585160 | tf_op jit(solution)/shard_map/ppermute | solution.py:30
  202.3 3.1 %collective-permute-start.33 = (bf16[688,384]{1,0:T(8,128)(2,1)}, bf16[688,384]{1,0:T(8,128)(2,1)S(1)}, u32[]{:S(2)}, u32[]{:S(2)}) collective-permute-start(bf16[688,384]{1,0:T(8,128)(2,1)} %get-tuple-element.39), channel_id=1, source_target_pairs={{0,1},{1,0},{2,3},{3,2},{4,5},{5,4},{6,7},{7,6},{8,9},{9,8},{10,11... | collective-permute-start | bytes 1585160 | tf_op jit(solution)/shard_map/ppermute | solution.py:30
  203.5 27.0 %collective-permute-start.38 = (bf16[64,864]{1,0:T(8,128)(2,1)S(1)}, bf16[64,864]{1,0:T(8,128)(2,1)S(1)}, u32[]{:S(2)}, u32[]{:S(2)}) collective-permute-start(bf16[64,864]{1,0:T(8,128)(2,1)S(1)} %fusion.27), channel_id=1, source_target_pairs={{0,2},{1,3},{2,0},{3,1},{4,6},{5,7},{6,4},{7,5},{8,10},{9,11},{10,... | collective-permute-start | bytes 331784 | tf_op jit(solution)/shard_map/ppermute | solution.py:30
  222.4 8.8 %copy-start.1 = (bf16[2,864,64]{1,2,0:T(8,128)(2,1)S(1)}, bf16[2,864,64]{1,2,0:T(8,128)(2,1)}, u32[]{:S(2)}) copy-start(bf16[2,864,64]{1,2,0:T(8,128)(2,1)} %param.11) | copy-start | bytes 663556
  (14 other events, 25.9 us)

commit v2 on v0

v2 whole, which is shorter than its diff:
```python
from functools import partial

import jax
import jax.numpy as jnp
from jax import lax
from jax.experimental import pallas as pl
from jax.experimental.pallas import tpu as pltpu
from jax.sharding import PartitionSpec as P


MAP_LOW = 11
POOL_LOW = 5
SIDE = 13
POOLED = 6
CELLS = SIDE * SIDE
PLACES = POOLED * POOLED
IMG = 16
BLK = 96
OUT = 256
ROWS = 9 * BLK
WHOLE = (0, 13)
HALVES = ((0, 7), (7, 13))
SCOPE = 4 << 20
F32 = jnp.float32
BF16 = jnp.bfloat16
VMEM = pl.BlockSpec(memory_space=pltpu.VMEM)
SMEM = pl.BlockSpec(memory_space=pltpu.SMEM)
ANY = pl.BlockSpec(memory_space=pl.ANY)
HBM = pl.BlockSpec(memory_space=pltpu.HBM)


def swap(value, axis, bit):
    count = lax.axis_size(axis)
    return lax.ppermute(value, axis, [(i, i ^ bit) for i in range(count)])


def sum_over(value, axis):
    bit = 1
    while bit < lax.axis_size(axis):
        value = value + swap(value, axis, bit)
        bit *= 2
    return value


def relative(value, index, axis=0):
    return jnp.concatenate(
        [lax.dynamic_slice_in_dim(value, index ^ k, 1, axis) for k in range(4)], axis
    )


def scalars(*values):
    return jnp.stack(values).astype(jnp.int32)


S, D, M, GROUPS = range(4)
COST = pl.CostEstimate(flops=1, bytes_accessed=1, transcendentals=0)


def is_low(sel):
    return sel[GROUPS + sel[M]] == 1


def struct(shape, dtype):
    return jax.ShapeDtypeStruct(shape, dtype)


def call(body, name, inputs, outs, after=(), scratch=(), limit=SCOPE, specs=None, out_specs=None):
    if specs is None:
        specs = [SMEM if v.dtype == jnp.int32 else VMEM for v in inputs]
    count = len(inputs)

    def kernel(*refs):
        body(*refs[:count], *refs[count + len(after) :])

    single = not isinstance(outs, (list, tuple))
    if out_specs is None:
        out_specs = VMEM if single else [VMEM] * len(outs)
    return pl.pallas_call(
        kernel,
        in_specs=specs + [VMEM] * len(after),
        out_specs=out_specs,
        out_shape=outs if single else list(outs),
        scratch_shapes=list(scratch),
        compiler_params=pltpu.CompilerParams(vmem_limit_bytes=limit),
        cost_estimate=COST,
        name=name,
    )(*inputs, *after)


def lane_index(rows=IMG):
    return lax.broadcasted_iota(jnp.int32, (rows, 128), 1)


def join4(parts, lane):
    last = parts[3]
    return [jnp.where(lane < BLK, parts[j], pltpu.roll(last, 96 - 32 * j, 1)) for j in range(3)]


def last_part(tiles, lane):
    a, b, c = [pltpu.roll(tiles[j], 32 + 32 * j, 1) for j in range(3)]
    return jnp.where(lane < 32, a, jnp.where(lane < 64, b, c))


def tiles_of(row):
    return [row[:, 0:128], row[:, 128:256], row[:, 256:384]]


def exchange(rows, lane):
    rows = [tiles_of(row) for row in rows]
    out = []
    for k in range(3):
        last = rows[3][k]
        out.append(
            [
                jnp.where(lane < BLK, rows[j][k], pltpu.roll(last, 96 - 32 * j, 1))
                for j in range(3)
            ]
        )
    thirds = [last_part(rows[q], lane) for q in range(3)]
    out.append([jnp.where(lane < BLK, thirds[j], rows[3][j]) for j in range(3)])
    return [jnp.concatenate(tiles, 1) for tiles in out]


def chunk_cells(chunk):
    return SIDE * chunk[0], SIDE * (chunk[1] - chunk[0])


def chunk_group(chunk):
    return -(-chunk_cells(chunk)[1] // 4)


def wire_shape(chunk):
    return (chunk_group(chunk) * IMG, 4 * BLK)


def masked(row, cell, whole):
    if cell // SIDE >= MAP_LOW or cell % SIDE >= MAP_LOW:
        return row * whole
    return row


def whole_map(sel):
    return jnp.where(is_low(sel), 0.0, 1.0).astype(BF16)


def at(cell):
    return pl.ds(cell * IMG, IMG)


def pack_kernel(count, sel, maps, *refs):
    wires, token, rows = refs[count:-2], refs[-2], refs[-1]
    token[...] = jnp.zeros(token.shape, F32)
    tower = sel[S]

    def widen(step, _):
        rows[pl.ds(step * 208, 208), :BLK] = maps[0, pl.ds(step * 208, 208), :].astype(F32)
        return 0

    lax.fori_loop(0, 26, widen, 0, unroll=2)
    lane = lane_index()

    def cell(index):
        start = 2 * index + tower
        return jnp.concatenate(
            [
                rows[pl.ds(start, 8, stride=2 * CELLS), :],
                rows[pl.ds(start + 16 * CELLS, 8, stride=2 * CELLS), :],
            ],
            0,
        ).astype(BF16)

    def fill(wire):
        group = chunk_group(WHOLE)
        for step in range(group):
            parts = [cell(min(step + group * q, CELLS - 1)) for q in range(4)]
            wire[at(step), :] = jnp.concatenate(join4(parts, lane), 1)

    pl.when(pl.program_id(0) == 0)(partial(fill, wires[0]))
    pl.when(pl.program_id(0) == 1)(partial(fill, wires[1]))


def pack_maps(maps, sel, first, after=()):
    shape = wire_shape(WHOLE)
    return pl.pallas_call(
        partial(pack_kernel, len(after)),
        grid_spec=pltpu.PrefetchScalarGridSpec(
            num_scalar_prefetch=1,
            grid=(2,),
            in_specs=[pl.BlockSpec((1, IMG * CELLS * 2, BLK), lambda i, sel: (sel[M] ^ (first - i), 0, 0))]
            + [VMEM] * len(after),
            out_specs=[pl.BlockSpec(shape, lambda i, sel: (0, 0))] * 2
            + [pl.BlockSpec((8, 128), lambda i, sel: (0, 0))],
            scratch_shapes=[pltpu.VMEM((IMG * CELLS * 2, 128), F32)],
        ),
        out_shape=[struct(shape, BF16)] * 2 + [struct((8, 128), F32)],
        compiler_params=pltpu.CompilerParams(vmem_limit_bytes=12 << 20),
        cost_estimate=COST,
        name="pack_maps",
    )(sel, maps, *after)


def unpack_kernel(sel, w0, w1, w2, w3, maps):
    lane = lane_index()
    whole = whole_map(sel)
    group = chunk_group(WHOLE)
    for step in range(group):
        rows = exchange([w[at(step), :] for w in (w0, w1, w2, w3)], lane)
        for q in range(4):
            cell = step + group * q
            if cell < CELLS:
                maps[at(cell), :] = masked(rows[q], cell, whole)


def pack_grad_kernel(chunk, sel, grad, *wires):
    lane = lane_index()
    whole = whole_map(sel)
    first, cells = chunk_cells(chunk)
    group = chunk_group(chunk)
    for step in range(group):
        rows = []
        for q in range(4):
            cell = min(step + group * q, cells - 1)
            rows.append(masked(grad[at(cell), :], first + cell, whole))
        for wire, row in zip(wires, exchange(rows, lane)):
            wire[at(step), :] = row


def pack_grad(grad, sel, chunk, after=()):
    shape = struct(wire_shape(chunk), BF16)
    return call(partial(pack_grad_kernel, chunk), "pack_grad", [sel, grad], [shape] * 4, after)


def place_grad_kernel(chunk, ks, sel, *refs):
    wires = refs[: len(ks)]
    out, parts, sent = refs[-3:]
    lane = lane_index()
    first, cells = chunk_cells(chunk)
    group = chunk_group(chunk)
    copies = []
    for index, (k, wire) in enumerate(zip(ks, wires)):
        for step in range(group):
            tiles = tiles_of(wire[at(step), :])
            tiles.append(last_part(tiles, lane))
            for q in range(4):
                if step + group * q < cells:
                    parts[index, at(step + group * q), :] = tiles[q][:, :BLK]
        place = out.at[sel[M] ^ k, pl.ds(first * IMG, cells * IMG)]
        copies.append(pltpu.make_async_copy(parts.at[index], place, sent.at[index]))
        copies[-1].start()
    for copy in copies:
        copy.wait()


def place_grad(wires, sel, chunk, ks, total):
    args = [sel, *wires]
    in_specs = [SMEM] + [VMEM] * len(wires)
    alias = {}
    if total is not None:
        alias = {len(args): 0}
        args.append(total)
        in_specs.append(ANY)
    cells = chunk_cells(chunk)[1]
    return pl.pallas_call(
        partial(place_grad_kernel, chunk, ks),
        in_specs=in_specs,
        out_specs=ANY,
        out_shape=struct((4, CELLS * IMG, BLK), BF16),
        scratch_shapes=[
            pltpu.VMEM((len(ks), cells * IMG, BLK), BF16),
            pltpu.SemaphoreType.DMA((len(ks),)),
        ],
        input_output_aliases=alias,
        compiler_params=pltpu.CompilerParams(vmem_limit_bytes=8 << 20),
        cost_estimate=COST,
        name="place_grad",
    )(*args)


def join_kernel(*refs):
    for k, part in enumerate(refs[:-1]):
        refs[-1][k] = part[...]


def own_kernel(sel, weight_in, bias_in, stitch_in, out, weight, bias, stitch, done):
    copies = [
        pltpu.make_async_copy(weight_in.at[sel[S]], weight, done.at[0]),
        pltpu.make_async_copy(bias_in, bias, done.at[1]),
        pltpu.make_async_copy(stitch_in, stitch, done.at[2]),
    ]
    for copy in copies:
        copy.start()
    for copy in copies:
        copy.wait()
    out[:, :ROWS] = weight[...]
    values = jnp.concatenate([bias[...], stitch[0], stitch[1], jnp.zeros((2, 64), F32)], 0)
    pieces = []
    for _ in range(3):
        pieces.append(values.astype(BF16).astype(F32))
        values = values - pieces[-1]
    zeros = jnp.zeros((BLK, 64), F32)
    rows = jnp.concatenate([zeros, *pieces, jnp.zeros((8, 64), F32)], 0)
    last = slice(ROWS - BLK, ROWS + 32)
    tile = jnp.where(lane_index(64) < BLK, out[:, last].astype(F32), rows.T)
    out[:, last] = tile.astype(BF16)


def kernels_kernel(sel, *refs):
    rows_out, params = refs[6:]
    blocks = []
    for first, second, third in (refs[:3], refs[3:6]):
        blocks += [first.at[0], first.at[1], second, third]
    d, m = sel[D], sel[M]
    odd = lax.rem(m, 2) == 1
    for k in range(4):
        for x in range(2):
            own = blocks[k][x].astype(F32)
            other = blocks[4 + k][x].astype(F32)
            even_rows = jnp.where(odd, other, own)
            odd_rows = jnp.where(odd, own, other)
            turned = jnp.concatenate([even_rows, odd_rows], 0).T
            tile = pl.multiple_of((lax.div(m, 2) ^ x) * 128, 128)
            if k == 0:
                values = turned[ROWS : ROWS + 8] + turned[ROWS + 8 : ROWS + 16]
                params[:, pl.ds(tile, 128)] = values + turned[ROWS + 16 : ROWS + 24]
            turned = turned.astype(BF16)
            for part in range(9):
                index = 9 * (d ^ k) + part
                first = lax.div(index, 4) * (4 * BLK)
                block = lax.rem(index, 4) ^ m
                for piece in range(3):
                    place = first + jnp.where(
                        block == 3, 128 * piece + BLK, 128 * block + 32 * piece
                    )
                    start = part * BLK + 32 * piece
                    rows_out[pl.ds(pl.multiple_of(place, 32), 32), pl.ds(tile, 128)] = turned[
                        start : start + 32
                    ]


def gather_kernels(conv_weight, conv_bias, conv_stitch, sel, s, m, token):
    turned = conv_weight.transpose(0, 2, 1)
    rows = turned.shape[2]
    if lax.axis_size("dp") == 4:
        shape = struct((64, rows + 32), BF16)
        inputs = [turned, conv_bias, conv_stitch]
        own = call(
            own_kernel,
            "own_kernels",
            [sel] + [pltpu.with_memory_space_constraint(v, pltpu.HBM) for v in inputs],
            shape,
            scratch=[pltpu.VMEM((64, rows), BF16)]
            + [pltpu.VMEM(v.shape, F32) for v in inputs[1:]]
            + [pltpu.SemaphoreType.DMA((3,))],
            specs=[SMEM] + [HBM] * 3,
        )
        near = call(
            join_kernel,
            "join_kernels",
            [own, swap(own, "mp", 2)],
            struct((2, *own.shape), BF16),
            (token,),
        )
        column = [swap(near, "dp", k) for k in (1, 2, 3)]
        first = call(
            join_kernel, "join_columns", [near, column[0]], struct((2, *near.shape), BF16)
        )
        column = [first, *column[1:]]
        across = [swap(part, "mp", 1) for part in column]
        kernel, params = call(
            kernels_kernel,
            "kernels",
            [sel, *column, *across],
            [struct((4 * rows, OUT), BF16), struct((8, OUT), F32)],
        )
        return kernel, params, near
    own = lax.dynamic_index_in_dim(conv_weight, s, 0, keepdims=False)
    full = lax.all_gather(lax.all_gather(own, "dp", axis=0), "mp", axis=2, tiled=True)
    kernel = relative(full.reshape(9, 4, BLK, OUT), m, 1)
    last = kernel[:, 3].reshape(9, 3, 32, OUT)
    kernel = jnp.concatenate([kernel[:, :3], last], 2).reshape(36 * BLK, OUT)
    params = jnp.concatenate([conv_bias, conv_stitch.reshape(4, 64), jnp.zeros((2, 64), F32)], 0)
    params = lax.all_gather(params, "mp", axis=1, tiled=True)
    return kernel, params, jnp.zeros((8, 128), F32)


def split_kernel(sel, grad, small, keep, send):
    d, m = sel[D], sel[M]
    odd = lax.rem(m, 2) == 1
    lane = lane_index(32)

    def write(rows, place):
        count = rows.shape[0]
        t0, t1 = rows[:, 0:128], rows[:, 128:256]
        low = jnp.where(lane[:count] < 64, t0, pltpu.roll(t1, 64, 1)).astype(BF16)
        high = jnp.where(lane[:count] < 64, pltpu.roll(t0, 64, 1), t1).astype(BF16)
        here = pl.ds(pl.multiple_of(place, 16), count)
        keep[here, :] = jnp.where(odd, high, low)
        send[here, :] = jnp.where(odd, low, high)

    for tap in range(9):
        for block in range(4):
            index = tap * 4 + (block ^ m)
            part = lax.div(index, 9)
            place = (part ^ d) * (ROWS + 16) + (index - part * 9) * BLK
            for piece in range(3):
                start = tap * 4 * BLK + (128 * piece + BLK if block == 3 else 128 * block + 32 * piece)
                write(grad[start : start + 32, :], place + 32 * piece)
    sums = jnp.concatenate([small[...], jnp.zeros((16 - small.shape[0], OUT), F32)], 0)
    for part in range(4):
        write(sums, part * (ROWS + 16) + ROWS)


def pair_kernel(keep, arrived, own, *sends):
    size = ROWS + 16
    for k in range(4):
        here = slice(k * size, (k + 1) * size)
        total = keep[here, :].astype(F32) + arrived[here, :].astype(F32)
        if k == 0:
            own[...] = total
        else:
            sends[k - 1][...] = total.astype(BF16)


def turn_kernel(sel, own, a, b, c, mine, send):
    total = own[...] + a[...].astype(F32) + b[...].astype(F32) + c[...].astype(F32)
    total = jnp.concatenate([total, jnp.zeros((16, 128), F32)], 0).T
    low = sel[M] < 2
    mine[...] = jnp.where(low, total[:64], total[64:])
    send[...] = jnp.where(low, total[64:], total[:64]).astype(BF16)


def finish_kernel(sel, mine, arrived, rows, bias, stitch):
    rows[...] = mine[:, :ROWS] + arrived[:, :ROWS].astype(F32)
    last = slice(ROWS - BLK, ROWS + 32)
    small = (mine[:, last] + arrived[:, last].astype(F32)).T
    stitch[pl.ds(sel[S], 1), :] = small[BLK : BLK + 1]
    stitch[pl.ds(1 - sel[S], 1), :] = small[BLK + 1 : BLK + 2]
    bias[...] = small[BLK + 2 : BLK + 3]


def scatter_kernels(grad, small, sel, s, m, meanwhile):
    rows = grad.shape[0] // lax.axis_size("dp")
    small_shapes = [struct((1, 64), F32), struct((2, 64), F32)]
    if lax.axis_size("dp") == 4:
        size = ROWS + 16
        keep, send = call(
            split_kernel, "split_kernels", [sel, grad, small], [struct((4 * size, 128), BF16)] * 2
        )
        own, *sends = call(
            pair_kernel,
            "pair_kernels",
            [keep, swap(send, "mp", 1)],
            [struct((size, 128), F32)] + [struct((size, 128), BF16)] * 3,
            meanwhile(keep),
        )
        arrived = [swap(part, "dp", k) for k, part in zip((1, 2, 3), sends)]
        mine, other = call(
            turn_kernel,
            "turn_kernels",
            [sel, own, *arrived],
            [struct((64, ROWS + 32), F32), struct((64, ROWS + 32), BF16)],
        )
        result, bias, stitch = call(
            finish_kernel,
            "finish_kernels",
            [sel, mine, swap(other, "mp", 2)],
            [struct((64, ROWS), F32), *small_shapes],
        )
        return result.T, bias, stitch
    grad = grad.reshape(9, 3, 128, OUT)
    last = grad[:, :, BLK:].reshape(9, 1, BLK, OUT)
    grad = jnp.concatenate([grad[:, :, :BLK], last], 1)
    grad = relative(grad, m, 1).reshape(36 * BLK, OUT).astype(BF16)
    grad = lax.psum_scatter(grad, "mp", scatter_dimension=1, tiled=True)
    grad = lax.psum_scatter(grad, "dp", scatter_dimension=0, tiled=True).astype(F32)
    small = sum_over(sum_over(small, "dp"), "mp")
    small = lax.dynamic_slice_in_dim(small, m * 64, 64, 1)
    stitch = jnp.stack([jnp.where(s == 0, small[0], small[1]), jnp.where(s == 0, small[1], small[0])])
    meanwhile(small)
    return grad, small[2:3], stitch


def gelu_parts(value):
    scale = 0.7978845608028654
    square = value * value
    curve = jnp.tanh(scale * value * (1.0 + 0.044715 * square))
    return curve, square, scale


def gelu(value):
    curve, _, _ = gelu_parts(value)
    return 0.5 * value * (1.0 + curve)


def gelu_slope(value):
    curve, square, scale = gelu_parts(value)
    bend = (0.5 * scale) * value * (1.0 - curve * curve) * (1.0 + 0.134145 * square)
    return 0.5 * (1.0 + curve) + bend


def place_of(sel, k, p):
    return 9 * (lax.rem(sel[D], 4) ^ k) + p


def half_kernel(first, sel, pooled, out):
    for k in range(2):
        for p in range(9):
            out[k, p] = pooled[place_of(sel, first + k, p)].astype(BF16)


def pool_kernel(sel, conv_out, params, pooled, far):
    extent = jnp.where(is_low(sel), POOL_LOW, POOLED)
    shift = params[pl.ds(sel[S], 1), :]
    lines = []
    for i in range(SIDE):
        cells = [gelu(conv_out[i, j] + shift) for j in range(SIDE)]
        lines.append([cells[2 * q] + cells[2 * q + 1] + cells[2 * q + 2] for q in range(POOLED)])
        if i >= 2 and i % 2 == 0:
            p = i // 2 - 1
            for q in range(POOLED):
                total = lines[i - 2][q] + lines[i - 1][q] + lines[i][q]
                keep = jnp.logical_and(p < extent, q < extent).astype(F32) / 9.0
                total = total * keep
                pooled[POOLED * p + q] = total
    half_kernel(2, sel, pooled, far)


def slope_kernel(sel, conv_out, params, slope, token):
    token[...] = jnp.zeros(token.shape, F32)
    shift = params[pl.ds(sel[S], 1), :]
    for i in range(SIDE):
        for j in range(SIDE):
            slope[SIDE * i + j] = gelu_slope(conv_out[i, j] + shift)


def entry(params, t, u):
    return params[pl.ds(2 + 2 * t + u, 1), :]


def stitch_kernel(first, sel, pooled, other, params, *chunks):
    s = sel[S]
    by_own, by_other = entry(params, s, s), entry(params, s, 1 - s)
    for k, chunk in enumerate(chunks):
        for p in range(9):
            mixed = by_own * pooled[place_of(sel, first + k, p)] + by_other * other[k, p].astype(F32)
            chunk[p] = mixed.astype(BF16)


def conv_grad_kernel(
    sel, near, far, near_other, far_other, slope, pooled, near_pooled, far_pooled, params, out, sums, mixed
):
    extent, s = jnp.where(is_low(sel), POOL_LOW, POOLED), sel[S]
    by_own, by_other = entry(params, s, s), entry(params, 1 - s, s)
    own_sum = other_sum = jnp.zeros((IMG, OUT), F32)
    for k in range(4):
        grad = (near, far)[k // 2]
        grad_other = (near_other, far_other)[k // 2]
        pooled_other = (near_pooled, far_pooled)[k // 2]
        for p in range(9):
            place = place_of(sel, k, p)
            mine = grad[k % 2, p].astype(F32)
            mixed[place] = by_own * mine + by_other * grad_other[k % 2, p].astype(F32)
            own_sum = own_sum + mine * pooled[place]
            other_sum = other_sum + mine * pooled_other[k % 2, p].astype(F32)
    spread = []
    for p in range(POOLED):
        line = []
        for q in range(POOLED):
            keep = jnp.logical_and(p < extent, q < extent).astype(F32) / 9.0
            line.append(mixed[POOLED * p + q] * keep)
        spread.append(line)
    bias_sum = jnp.zeros((IMG, OUT), F32)

    def over(values, index):
        near, far = index // 2, index // 2 - 1
        if index % 2 == 1 or index == 0:
            return values[near]
        if near >= POOLED:
            return values[far]
        return values[near] + values[far]

    for i in range(SIDE):
        line = [over([spread[p][q] for p in range(POOLED)], i) for q in range(POOLED)]
        for j in range(SIDE):
            cell = SIDE * i + j
            value = (slope[cell] * over(line, j)).astype(BF16)
            out[cell] = value
            bias_sum = bias_sum + value.astype(F32)
    for row, total in enumerate((own_sum, other_sum, bias_sum)):
        sums[row : row + 1, :] = jnp.sum(total, 0, keepdims=True)


def all_acts(acts, place):
    return jnp.concatenate([a[:, place].reshape(4 * IMG, OUT) for a in acts], 0)


def all_grads(grads):
    return jnp.concatenate([g[r] for r in range(4) for g in grads], 0)


def load_kernel(sel, weight, out, token, done):
    token[...] = jnp.zeros(token.shape, F32)
    count = done.shape[0]
    size = weight.shape[1] // count
    copies = []
    for part in range(count):
        here = pl.ds(part * size, size)
        copies.append(pltpu.make_async_copy(weight.at[sel[S], here], out.at[here], done.at[part]))
        copies[-1].start()
    for copy in copies:
        copy.wait()


def load_matrix(weight, sel, s, after):
    if lax.axis_size("dp") != 4:
        return lax.dynamic_index_in_dim(weight, s, 0, keepdims=False), ()
    matrix, token = call(
        load_kernel,
        "load_matrix",
        [sel, pltpu.with_memory_space_constraint(weight, pltpu.HBM)],
        [struct(weight.shape[1:], BF16), struct((8, 128), F32)],
        after,
        scratch=[pltpu.SemaphoreType.DMA((9,))],
        specs=[SMEM, HBM],
    )
    return matrix, (token,)


def fc_forward_kernel(a0, a1, a2, a3, weight, own, *sends):
    rows = jnp.concatenate([all_acts((a0, a1, a2, a3), p) for p in range(9)], 1)
    for n in range(weight.shape[1] // 256):
        here = slice(n * 256, (n + 1) * 256)
        term = jnp.dot(rows, weight[:, here], preferred_element_type=F32)
        for r in range(4):
            for k in range(4):
                part = term[(4 * r + k) * IMG : (4 * r + k + 1) * IMG]
                if k == 0:
                    own[r, :, here] = part
                else:
                    sends[k - 1][r, :, here] = part.astype(BF16)


def fc_active_kernel(sel, own, a, b, c, bias, stitch, cot, grad, active, sent, sums):
    s, m = sel[S], sel[M]
    for n in range(own.shape[2] // 256):
        here = slice(n * 256, (n + 1) * 256)
        shift = bias[pl.ds(s, 1), here]
        w0, w1 = stitch[0, pl.ds(s, 1), here], stitch[1, pl.ds(s, 1), here]
        sum0 = sum1 = jnp.zeros((IMG, 256), F32)
        for r in range(4):
            value = own[r, :, here] + a[r, :, here].astype(F32)
            value = value + (b[r, :, here].astype(F32) + c[r, :, here].astype(F32)) + shift
            curve, square, scale = gelu_parts(value)
            half = 0.5 * (1.0 + curve)
            bend = (0.5 * scale) * value * (1.0 - curve * curve) * (1.0 + 0.134145 * square)
            result = value * half
            c0, c1 = cot[0, m ^ r, :, here].astype(F32), cot[1, m ^ r, :, here].astype(F32)
            grad[r, :, here] = ((half + bend) * (w0 * c0 + w1 * c1)).astype(BF16)
            active[r, :, here] = result
            sent[r, :, here] = result.astype(BF16)
            sum0 = sum0 + c0 * result
            sum1 = sum1 + c1 * result
        for t, total in enumerate((sum0, sum1)):
            sums[4 * t + n : 4 * t + n + 1, :] = jnp.sum(total, 0, keepdims=True)


def fc_rows_kernel(g0, g1, weight, keep, send):
    rows = all_grads((g0, g1))
    for p in range(9):
        term = lax.dot_general(
            rows,
            weight[p * 256 : (p + 1) * 256, :],
            (((1,), (1,)), ((), ())),
            preferred_element_type=F32,
        )
        term = term.reshape(4, 2, IMG, 256)
        for r in range(4):
            if r % 2 == 0:
                keep[r // 2, :, p] = term[r]
            else:
                send[r // 2, :, p] = term[r].astype(BF16)


def cross_kernel(keep, arrived, out):
    out[...] = (keep[1] + arrived[1].astype(F32)).astype(BF16)


def home_kernel(keep, arrived, crossed, sums, *chunks):
    high = sums[...].astype(BF16).astype(F32)
    small = jnp.concatenate([high, sums[...] - high], 0).astype(BF16)
    for k in range(2):
        total = keep[0, k] + arrived[0, k].astype(F32) + crossed[k].astype(F32)
        chunks[k][0:9] = total.astype(BF16)
        chunks[k][9] = small


def fc_matrix_kernel(a0, a1, a2, a3, g0, g1, g2, g3, out, bias, token, part, sent):
    token[...] = jnp.zeros(token.shape, F32)
    grads = all_grads((g0, g1, g2, g3))

    def copy(p):
        return pltpu.make_async_copy(part.at[p % 3], out.at[pl.ds(p * 256, 256)], sent.at[p % 3])

    for p in range(9):
        rows = all_acts((a0, a1, a2, a3), p).T
        if p >= 3:
            copy(p - 3).wait()
        part[p % 3] = jnp.dot(rows, grads, preferred_element_type=F32)
        copy(p).start()
    bias[...] = jnp.sum(grads.astype(F32), 0, keepdims=True)
    for p in range(6, 9):
        copy(p).wait()


def outputs_kernel(sel, active, arrived, stitch, out, token):
    token[...] = jnp.zeros(token.shape, F32)
    s, m = sel[S], sel[M]
    for n in range(active.shape[2] // 256):
        here = slice(n * 256, (n + 1) * 256)
        by_own = jnp.where(s == 0, stitch[0, 0:1, here], stitch[1, 1:2, here])
        by_other = jnp.where(s == 0, stitch[0, 1:2, here], stitch[1, 0:1, here])
        for r in range(4):
            mixed = by_own * active[r, :, here] + by_other * arrived[r, :, here].astype(F32)
            out[m ^ r, :, here] = mixed.astype(BF16)


def plane_sum(near, far):
    total = jnp.zeros((8, OUT), F32)
    for half in (near, far):
        for k in range(2):
            plane = half[k, 9].astype(F32)
            total = total + (plane[0:8] + plane[8:16])
    return total


def stitch_sums_kernel(sel, near, far, near_other, far_other, out, own, other):
    s = sel[S]
    own[...] = plane_sum(near, far)
    other[...] = plane_sum(near_other, far_other)
    for n in range(4):
        here = slice(n * OUT, (n + 1) * OUT)
        out[pl.ds(s, 1), here] = own[pl.ds(4 * s + n, 1), :]
        out[pl.ds(1 - s, 1), here] = other[pl.ds(4 * s + n, 1), :]


def fc_section(pooled, near, far, params, own_weight, bias, stitch, cotangent, sel, s, d, m, slope_of):
    count = lax.axis_size("dp")
    hid = own_weight.shape[1]
    cot = lax.dynamic_slice_in_dim(cotangent, d * IMG, IMG, 1).transpose(2, 0, 1, 3)
    plane = struct((9, IMG, OUT), BF16)
    block = struct((4, IMG, hid), BF16)
    token = struct((8, 128), F32)
    chunks = [None] * 4
    chunks[2:] = call(
        partial(stitch_kernel, 2), "stitch_far", [sel, pooled, far, params], [plane] * 2
    )
    chunks[:2] = call(
        partial(stitch_kernel, 0), "stitch_near", [sel, pooled, near, params], [plane] * 2, chunks[2:3]
    )
    slope, after = slope_of((chunks[0],))
    if count == 4:
        moved = [chunks[0]] + [swap(chunks[k], "dp", k) for k in (1, 2, 3)]
        own_acts = call(join_kernel, "join_acts", moved, struct((4, 9, IMG, OUT), BF16), (after,))
        far_acts = swap(own_acts, "mp", 2)
        acts = [own_acts, swap(own_acts, "mp", 1), far_acts, swap(far_acts, "mp", 1)]
        pre, *sends = call(
            fc_forward_kernel,
            "fc_forward",
            [*acts, own_weight],
            [struct((4, IMG, hid), F32)] + [block] * 3,
        )
        arrived = [swap(part, "dp", k) for k, part in zip((1, 2, 3), sends)]
    else:
        shared = by_position(chunks, d)
        flat = shared.transpose(1, 0, 2).reshape(IMG, count, -1).transpose(1, 0, 2)
        flat = lax.all_to_all(flat, "dp", 0, 0, tiled=True)
        flat = lax.all_gather(flat, "mp", axis=0)
        flat = relative(flat, m)
        pre = jnp.einsum("rdnf,fk->drnk", flat, own_weight, preferred_element_type=F32)
        pre = lax.psum_scatter(pre.astype(BF16), "dp", scatter_dimension=0, tiled=True)
        pre = pre.reshape(4, IMG, hid).astype(F32)
        arrived = [jnp.zeros(block.shape, BF16)] * 3
    pre_grad, active, sent, sums = call(
        fc_active_kernel,
        "fc_active",
        [sel, pre, *arrived, bias, stitch, cot],
        [block, struct(block.shape, F32), block, struct((8, OUT), F32)],
    )
    outputs, output_token = call(
        outputs_kernel, "outputs", [sel, active, swap(sent, "section", 1), stitch], [block, token]
    )
    half = struct((2, 10, IMG, OUT), BF16)
    if count == 4:
        grads = [pre_grad] + [swap(pre_grad, "dp", k) for k in (1, 2, 3)]
        pair = struct((2, 2, 9, IMG, OUT), F32)
        ten = struct(half.shape[1:], BF16)

        def home(ks, name, after=()):
            keep, send = call(
                fc_rows_kernel,
                "fc_rows_" + name,
                [*[grads[k] for k in ks], own_weight],
                [pair, struct(pair.shape, BF16)],
                after,
            )
            arrived = swap(send, "mp", 1)
            crossing = call(
                cross_kernel, "cross_" + name, [keep, arrived], struct(pair.shape[1:], BF16)
            )
            crossed = swap(crossing, "mp", 2)
            return call(home_kernel, "home_" + name, [keep, arrived, crossed, sums], [ten] * 2)

        first, second = home((0, 1), "near")
        near_grad = call(join_kernel, "join_near", [first, swap(second, "dp", 1)], half)
        near_back = (near_grad, swap(near_grad, "section", 1))
        first, second = home((2, 3), "far", (first, output_token))
        matrix_grad, bias_sum, after = call(
            fc_matrix_kernel,
            "fc_matrix",
            [*acts, *grads],
            [struct(own_weight.shape, F32), struct((1, hid), F32), token],
            (first,),
            scratch=[pltpu.VMEM((3, 256, hid), F32), pltpu.SemaphoreType.DMA((3,))],
            limit=10 << 20,
            out_specs=[HBM, VMEM, VMEM],
        )
        moved = [swap(first, "dp", 2), swap(second, "dp", 3)]
        far_grad = call(join_kernel, "join_far", moved, half, (after,))
        far_back = (far_grad, swap(far_grad, "section", 1))
    else:
        grads = lax.all_gather(pre_grad, "dp", axis=0)
        rows = jnp.einsum("drnk,fk->rdnf", grads, own_weight, preferred_element_type=F32)
        rows = relative(rows, m).astype(BF16)
        rows = lax.psum_scatter(rows, "mp", scatter_dimension=0, tiled=True)[0]
        rows = lax.all_to_all(rows, "dp", 0, 0, tiled=True)
        back = rows.transpose(1, 0, 2).reshape(IMG, 4, 9, OUT).transpose(1, 2, 0, 3)
        matrix_grad = jnp.einsum("rdnf,drnk->fk", flat, grads, preferred_element_type=F32)
        bias_sum = jnp.sum(grads.astype(F32), (0, 1, 2))[None]
        total = sum_over(sums, "dp")
        high = lax.reduce_precision(total, 8, 7)
        small = jnp.concatenate([high, total - high], 0).astype(BF16)
        small = jnp.stack([small] + [jnp.zeros_like(small)] * 3)
        back = jnp.concatenate([relative(back, lax.rem(d, 4)), small[:, None]], 1)
        near_back, far_back = [(part, swap(part, "section", 1)) for part in (back[:2], back[2:])]
    stitch_sum = call(
        stitch_sums_kernel,
        "stitch_sums",
        [sel, near_back[0], far_back[0], near_back[1], far_back[1]],
        struct((2, hid), F32),
        scratch=[pltpu.VMEM((8, OUT), F32)] * 2,
    )
    grads = [near_back[0], far_back[0], near_back[1], far_back[1]]
    return grads, slope, outputs, matrix_grad, bias_sum, stitch_sum


def by_position(chunks, d):
    return relative(jnp.stack(chunks), lax.rem(d, 4)).reshape(PLACES, IMG, OUT)


def conv(maps, taps, rows, form, kind=F32):
    return lax.conv_general_dilated(
        maps,
        taps,
        (1, 1),
        (rows, (1, 1)),
        dimension_numbers=form,
        preferred_element_type=F32,
    ).astype(kind)


def on_device(
    conv_input,
    group_ids,
    conv_weight,
    conv_bias,
    conv_stitch,
    fc_weight,
    fc_bias,
    fc_stitch,
    cotangent,
):
    s = lax.axis_index("section")
    d = lax.axis_index("dp")
    m = lax.axis_index("mp")
    assert conv_input.shape == (4, IMG, 2, SIDE, SIDE, BLK) and lax.axis_size("mp") == 4
    sel = jnp.concatenate([scalars(s, d, m), group_ids])

    by_row = conv_input.transpose(0, 1, 3, 4, 2, 5).reshape(4, IMG * CELLS * 2, BLK)
    by_row = pltpu.with_memory_space_constraint(by_row, pltpu.HBM)
    far3, far2, token = pack_maps(by_row, sel, 3)
    kernel, params, early = gather_kernels(conv_weight, conv_bias, conv_stitch, sel, s, m, token)
    near1, near0, token = pack_maps(by_row, sel, 1, (token, early))
    wires = [near0, swap(near1, "mp", 1), swap(far2, "mp", 2), swap(far3, "mp", 3)]

    taps = kernel.reshape(3, 3, 4 * BLK, OUT)
    maps = call(
        unpack_kernel, "unpack_maps", [sel, *wires], struct((CELLS * IMG, 4 * BLK), BF16)
    )
    maps = maps.reshape(SIDE, SIDE, IMG, 4 * BLK)
    conv_out = conv(maps, taps, (1, 1), ("HWNC", "HWIO", "HWNC"))
    half = struct((2, 9, IMG, OUT), BF16)
    pooled, far = call(
        pool_kernel, "pool", [sel, conv_out, params], [struct((PLACES, IMG, OUT), F32), half]
    )
    matrix, after = load_matrix(fc_weight, sel, s, (pooled,))
    near = call(partial(half_kernel, 0), "pool_near", [sel, pooled], half, after)
    far = swap(far, "section", 1)
    near = swap(near, "section", 1)

    def slope_of(after):
        return call(
            slope_kernel,
            "slope",
            [sel, conv_out, params],
            [struct((CELLS, IMG, OUT), F32), struct((8, 128), F32)],
            after,
        )

    back, slope, outputs, matrix_grad, fc_bias_sum, fc_stitch_sum = fc_section(
        pooled, near, far, params, matrix, fc_bias, fc_stitch, cotangent, sel, s, d, m, slope_of
    )
    conv_grad, sums = call(
        conv_grad_kernel,
        "conv_gradient",
        [sel, *back, slope, pooled, near, far, params],
        [struct((CELLS, IMG, OUT), BF16), struct((3, OUT), F32)],
        scratch=[pltpu.VMEM((PLACES, IMG, OUT), F32)],
    )
    conv_grad = conv_grad.reshape(SIDE, SIDE, IMG, OUT)

    kernel_grad = conv(maps, conv_grad, (1, 1), ("HWCN", "HWIO", "HWNC"))
    back_taps = taps[::-1, ::-1]
    wires = []

    def send_input_grad(after):
        chunk = HALVES[len(wires)]
        padding = ((1, -5), (-6, 1))[len(wires)]
        part = conv(conv_grad, back_taps, padding, ("HWNC", "HWOI", "HWNC"), BF16)
        sends = pack_grad(part.reshape(-1, 4 * BLK), sel, chunk, after)
        wires.append([sends[0]] + [swap(sends[k], "mp", k) for k in (1, 2, 3)])
        return (sends[0],)

    kernel_rows, conv_bias_sum, conv_stitch_sum = scatter_kernels(
        kernel_grad.reshape(36 * BLK, OUT), sums, sel, s, m, lambda mark: send_input_grad((mark,))
    )
    send_input_grad(())
    input_grad = place_grad(wires[0], sel, HALVES[0], (0, 1, 2, 3), None)
    input_grad = place_grad(wires[1][:2], sel, HALVES[1], (0, 1), input_grad)
    input_grad = place_grad(wires[1][2:], sel, HALVES[1], (2, 3), input_grad)
    input_grad = input_grad.reshape(4, 1, SIDE, SIDE, IMG, BLK).transpose(0, 4, 1, 2, 3, 5)
    return (
        outputs[:, :, None],
        input_grad,
        kernel_rows[None],
        conv_bias_sum,
        conv_stitch_sum[None],
        matrix_grad[None],
        fc_bias_sum,
        fc_stitch_sum[None],
    )


def solution(mesh):
    placed = (
        P(None, "dp", None, None, None, "mp"),
        P(),
        P(None, "dp", "mp"),
        P(None, "mp"),
        P(None, None, "mp"),
        P(None, "dp", "mp"),
        P(None, "mp"),
        P(None, None, "mp"),
        P(None, None, None, "mp"),
    )
    return jax.shard_map(
        on_device,
        mesh=mesh,
        in_specs=placed,
        out_specs=(
            P(None, "dp", "section", "mp"),
            P(None, "dp", "section", None, None, "mp"),
            P("section", "dp", "mp"),
            P("section", "mp"),
            P("section", None, "mp"),
            P("section", "dp", "mp"),
            P("section", "mp"),
            P("section", None, "mp"),
        ),
        check_vma=False,
    )
```

time: 3730 us -> 192 us (0.05)
  local copies, waits for them, and re-layouts: 1240 us -> 4.8 us
  waiting for transfers between devices: 1210 us -> 80.4 us
  matrix products: 557 us -> 18.6 us
  other arithmetic: 358 us -> 0.82 us
  blocking collectives: 279 us -> 0 us
  Pallas kernels: 0 us -> 45 us
    unnamed x179 -> x27, local copies, waits for them, and re-layouts: 764 us -> 4.62 us
    all_gather x5 -> x0, waiting for transfers between devices: 663 us -> none  [the longest x1 447 us: on_device(): matrix = lax.all_gather(fc_weight, 'dp', axis=1, tiled=True)]
    dot_general x120 -> x0, matrix products: 557 us -> none  [the longest x4 173 us: on_device(): jnp.einsum('ntf,ntk->tfk', flat_rows, pre_grad, preferred_element_type=jn...]
    reduce_scatter x1 -> x0, waiting for transfers between devices: 382 us -> none  [on_device(): lax.psum_scatter(fc_grad.astype(jnp.bfloat16), 'dp', scatter_dimension=1,...]
    another operation x29 -> x0, local copies, waits for them, and re-layouts: 315 us -> none
    scatter-add x36 -> x0, other arithmetic: 242 us -> none  [pool_back(): result = result.at[:, :, tap_row:tap_row + 2 * pooled_side - 1:2, tap_col...]
    all_gather x5 -> x0, blocking collectives: 188 us -> none  [the longest x4 154 us: on_device(): fc_full_maps = lax.all_gather(incoming, 'mp', axis=4, tiled=True)]
    all_to_all x7 -> x0, waiting for transfers between devices: 98.8 us -> none  [the longest x1 96.5 us: on_device(): lax.all_to_all(fc_grad_rows.astype(jnp.bfloat16), 'section', split_axis=0...]
  transfers between devices with their start and end apart: 27 -> 45, of which waited for: 11 -> 25; matrix products, arithmetic and copies ran while one was open for 50% -> 4% of each run, Pallas kernels for 0% -> 16%
where the time goes in v2:
time: 192 us; the launch traced here: 190 us
  waiting for transfers between devices  80.4 us (42%)
  Pallas kernels  45 us (23%)
  starting transfers between devices  39.2 us (20%)
  matrix products  18.6 us (10%)
  local copies, waits for them, and re-layouts  4.8 us (2%)
    ppermute x45, waiting for transfers between devices, swap(): return lax.ppermute(value, axis, [(i, i ^ bit) for i in range(count)])  80.4 us
    ppermute x45, starting transfers between devices, swap(): return lax.ppermute(value, axis, [(i, i ^ bit) for i in range(count)])  39.2 us
    pallas_call x32, Pallas kernels, call(): pl.pallas_call(kernel, in_specs=specs + [VMEM] * len(after), out_specs=ou...  33.9 us
    conv_general_dilated x4, matrix products, conv(): lax.conv_general_dilated(maps, taps, (1, 1), (rows, (1, 1)), dimension_nu...  18.6 us
    pallas_call x2, Pallas kernels, pack_maps(): pl.pallas_call(partial(pack_kernel, len(after)), grid_spec=pltpu.Prefetch...  6.21 us
    pallas_call x3, Pallas kernels, place_grad(): pl.pallas_call(partial(place_grad_kernel, chunk, ks), in_specs=in_specs,...  4.89 us
    unnamed x27, local copies, waits for them, and re-layouts  4.62 us
  transfers between devices with their start and end apart: 45, of which 25 were waited for; matrix products, arithmetic and copies ran while one was open for 4% of the time, Pallas kernels for 16%

profile of v2, /device:TPU:8, one launch (start us, length us, event | category | flops | bytes accessed | tf_op | source)
XLA Modules:
  0.0 189.9 jit_solution(4977404828503477704)
XLA Ops:
  1.5 1.6 own_kernels.1.refs_0_
  3.0 1.6 collective-permute-start
  4.6 2.8 %pack_maps.2 = (bf16[688,384]{1,0:T(8,128)(2,1)S(1)}, bf16[688,384]{1,0:T(8,128)(2,1)S(1)}, f32[8,128]{1,0:T(8,128)S(1)}) custom-call(s32[7]{0:T(128)S(1)} %pad_add_fusion.sel.refs_0_, bf16[4,5408,96]{2,1,0:T(8,128)(2,1)} %bitcast.51), custom_call_target="tpu_custom_call" | custom-call | flops 1 | bytes 1 | tf_op jit(solution)/shard_map/pack_maps/pallas_call | solution.py:184
  8.3 2.9 %collective-permute-start.5 = (bf16[2,64,896]{2,1,0:T(8,128)(2,1)S(1)}, bf16[2,64,896]{2,1,0:T(8,128)(2,1)S(1)}, u32[]{:S(2)}, u32[]{:S(2)}) collective-permute-start(bf16[2,64,896]{2,1,0:T(8,128)(2,1)S(1)} %join_kernels.1.refs_1_.refs_0_), channel_id=1, source_target_pairs={{0,8},{4,12},{8,0},{12,4},{1,9},{5,13},{9,1},{13,5},{2,10},{6,14},... | collective-permute-start | bytes 688136 | tf_op jit(solution)/shard_map/ppermute | solution.py:34
  11.2 3.4 %pack_maps.3 = (bf16[688,384]{1,0:T(8,128)(2,1)S(1)}, bf16[688,384]{1,0:T(8,128)(2,1)S(1)}, f32[8,128]{1,0:T(8,128)}) custom-call(s32[7]{0:T(128)S(1)} %pad_add_fusion.sel.refs_0_, bf16[4,5408,96]{2,1,0:T(8,128)(2,1)} %bitcast.52, f32[8,128]{1,0:T(8,128)S(1)} %get-tuple-element.67.refs_2_.refs_0_, bf16[2,64,896]{2,1,0:T(8,128)(2,1)S(1)} %join_kernels.1.refs_1_.refs_0_), custom_call_target="tpu_custom_call" | custom-call | flops 1 | bytes 1 | tf_op jit(solution)/shard_map/pack_maps/pallas_call | solution.py:184
  14.6 1.6 collective-permute-start.1
  16.2 1.3 collective-permute-done.4.refs_1_
  17.5 1.7 collective-permute-start.6
  19.3 2.0 %collective-permute-done.5.refs_2_ = bf16[2,64,896]{2,1,0:T(8,128)(2,1)S(1)} collective-permute-done((bf16[2,64,896]{2,1,0:T(8,128)(2,1)S(1)}, bf16[2,64,896]{2,1,0:T(8,128)(2,1)S(1)}, u32[]{:S(2)}, u32[]{:S(2)}) %collective-permute-start.5) | collective-permute-done | bytes 229408 | tf_op jit(solution)/shard_map/ppermute | solution.py:34
  21.3 9.6 %collective-permute-done.6.refs_3_ = bf16[2,64,896]{2,1,0:T(8,128)(2,1)S(1)} collective-permute-done((bf16[2,64,896]{2,1,0:T(8,128)(2,1)S(1)}, bf16[2,64,896]{2,1,0:T(8,128)(2,1)S(1)}, u32[]{:S(2)}, u32[]{:S(2)}) %collective-permute-start.6) | collective-permute-done | bytes 229408 | tf_op jit(solution)/shard_map/ppermute | solution.py:34
  31.4 1.4 unpack_maps.1
  32.9 1.4 kernels.1
  34.2 5.6 %fusion.refs_1_ = f32[13,13,16,256]{3,2,1,0:T(8,128)S(1)} fusion(bf16[13,13,16,384]{3,2,1,0:T(8,128)(2,1)S(1)} %bitcast.39, bf16[3,3,384,256]{3,2,1,0:T(8,128)(2,1)S(1)} %bitcast.44), kind=kOutput, calls=%fused_computation.5 | convolution fusion | flops 4306501632 | bytes 6615040 | tf_op jit(solution)/shard_map/conv_general_dilated | solution.py:861
  39.9 1.6 pool.1
  41.5 1.6 collective-permute-start.11
  43.1 2.9 %load_matrix.1 = (bf16[2304,1024]{1,0:T(8,128)(2,1)S(1)}, f32[8,128]{1,0:T(8,128)S(1)}) custom-call(s32[7]{0:T(128)S(1)} %pad_add_fusion.sel.refs_0_, bf16[2,2304,1024]{2,1,0:T(8,128)(2,1)} %refs_1_.1, f32[36,16,256]{2,1,0:T(8,128)S(1)} %get-tuple-element.74.refs_2_.refs_1_.refs_6_), custom_call_target="tpu_custom_call" | custom-call | flops 1 | bytes 1 | tf_op jit(solution)/shard_map/load_matrix/pallas_call | solution.py:78
  48.6 2.0 %collective-permute-start.13 = (bf16[9,16,256]{2,1,0:T(8,128)(2,1)S(1)}, bf16[9,16,256]{2,1,0:T(8,128)(2,1)S(1)}, u32[]{:S(2)}, u32[]{:S(2)}) collective-permute-start(bf16[9,16,256]{2,1,0:T(8,128)(2,1)S(1)} %get-tuple-element.77.refs_4_), channel_id=1, source_target_pairs={{0,8},{4,12},{8,0},{12,4},{1,9},{5,13},{9,1},{13,5},{2,10},{6,14},... | collective-permute-start | bytes 221192 | tf_op jit(solution)/shard_map/ppermute | solution.py:34
  50.6 2.2 %collective-permute-done.10.refs_2_.refs_7_ = bf16[2,9,16,256]{3,2,1,0:T(8,128)(2,1)S(1)} collective-permute-done((bf16[2,9,16,256]{3,2,1,0:T(8,128)(2,1)S(1)}, bf16[2,9,16,256]{3,2,1,0:T(8,128)(2,1)S(1)}, u32[]{:S(2)}, u32[]{:S(2)}) %collective-permute-start.10) | collective-permute-done | bytes 147488 | tf_op jit(solution)/shard_map/ppermute | solution.py:34
  53.9 2.7 %collective-permute-start.14 = (bf16[9,16,256]{2,1,0:T(8,128)(2,1)S(1)}, bf16[9,16,256]{2,1,0:T(8,128)(2,1)S(1)}, u32[]{:S(2)}, u32[]{:S(2)}) collective-permute-start(bf16[9,16,256]{2,1,0:T(8,128)(2,1)S(1)} %get-tuple-element.80), channel_id=1, source_target_pairs={{0,12},{4,8},{8,4},{12,0},{1,13},{5,9},{9,5},{13,1},{2,14},{6,10},... | collective-permute-start | bytes 221192 | tf_op jit(solution)/shard_map/ppermute | solution.py:34
  56.6 2.1 %slope.1 = (f32[169,16,256]{2,1,0:T(8,128)S(1)}, f32[8,128]{1,0:T(8,128)S(1)}) custom-call(s32[7]{0:T(128)S(1)} %pad_add_fusion.sel.refs_0_, f32[13,13,16,256]{3,2,1,0:T(8,128)S(1)} %fusion.refs_1_, f32[8,256]{1,0:T(8,128)S(1)} %get-tuple-element.73.refs_2_.refs_3_.refs_9_, bf16[9,16,256]{2,1,0:T(8,128)(2,1)S(1)} %get-tuple-element.78.refs_3_.refs_0_), custom_call_target="tpu_custom_call" | custom-call | flops 1 | bytes 1 | tf_op jit(solution)/shard_map/slope/pallas_call | solution.py:78
  58.7 1.5 copy-done.5
  60.9 7.8 %collective-permute-done.16.refs_2_ = bf16[4,9,16,256]{3,2,1,0:T(8,128)(2,1)S(1)} collective-permute-done((bf16[4,9,16,256]{3,2,1,0:T(8,128)(2,1)S(1)}, bf16[4,9,16,256]{3,2,1,0:T(8,128)(2,1)S(1)}, u32[]{:S(2)}, u32[]{:S(2)}) %collective-permute-start.16) | collective-permute-done | bytes 294944 | tf_op jit(solution)/shard_map/ppermute | solution.py:34
  68.8 1.6 collective-permute-done.17.refs_3_
  70.4 2.1 %fc_forward.1 = (f32[4,16,1024]{2,1,0:T(8,128)S(1)}, bf16[4,16,1024]{2,1,0:T(8,128)(2,1)}, bf16[4,16,1024]{2,1,0:T(8,128)(2,1)}, bf16[4,16,1024]{2,1,0:T(8,128)(2,1)}) custom-call(bf16[4,9,16,256]{3,2,1,0:T(8,128)(2,1)S(1)} %join_acts.1.refs_0_, bf16[4,9,16,256]{3,2,1,0:T(8,128)(2,1)S(1)} %collective-permute-done.15.refs_1_, ...), custom_call_target="tpu_custom_call" | custom-call | flops 1 | bytes 1 | tf_op jit(solution)/shard_map/fc_forward/pallas_call | solution.py:78
  72.5 1.3 collective-permute-start.18
  74.2 1.7 collective-permute-start.20
  76.2 2.8 %collective-permute-done.18.refs_2_ = bf16[4,16,1024]{2,1,0:T(8,128)(2,1)S(1)} collective-permute-done((bf16[4,16,1024]{2,1,0:T(8,128)(2,1)}, bf16[4,16,1024]{2,1,0:T(8,128)(2,1)S(1)}, u32[]{:S(2)}, u32[]{:S(2)}) %collective-permute-start.18) | collective-permute-done | bytes 131104 | tf_op jit(solution)/shard_map/ppermute | solution.py:34
  79.0 5.0 %collective-permute-done.19.refs_3_ = bf16[4,16,1024]{2,1,0:T(8,128)(2,1)} collective-permute-done((bf16[4,16,1024]{2,1,0:T(8,128)(2,1)}, bf16[4,16,1024]{2,1,0:T(8,128)(2,1)}, u32[]{:S(2)}, u32[]{:S(2)}) %collective-permute-start.19) | collective-permute-done | bytes 131104 | tf_op jit(solution)/shard_map/ppermute | solution.py:34
  84.1 3.9 %collective-permute-done.20.refs_4_ = bf16[4,16,1024]{2,1,0:T(8,128)(2,1)} collective-permute-done((bf16[4,16,1024]{2,1,0:T(8,128)(2,1)}, bf16[4,16,1024]{2,1,0:T(8,128)(2,1)}, u32[]{:S(2)}, u32[]{:S(2)}) %collective-permute-start.20) | collective-permute-done | bytes 131104 | tf_op jit(solution)/shard_map/ppermute | solution.py:34
  88.0 1.3 fc_active.1
  89.4 5.0 %collective-permute-done.22.refs_1_.refs_5_ = bf16[4,16,1024]{2,1,0:T(8,128)(2,1)S(1)} collective-permute-done((bf16[4,16,1024]{2,1,0:T(8,128)(2,1)S(1)}, bf16[4,16,1024]{2,1,0:T(8,128)(2,1)S(1)}, u32[]{:S(2)}, u32[]{:S(2)}) %collective-permute-start.22) | collective-permute-done | bytes 131104 | tf_op jit(solution)/shard_map/ppermute | solution.py:34
  94.3 2.3 %copy-done.3 = bf16[2304,1024]{1,0:T(8,128)(2,1)S(1)} copy-done((bf16[2304,1024]{1,0:T(8,128)(2,1)S(1)}, bf16[2304,1024]{1,0:T(8,128)(2,1)}, u32[]{:S(2)}) %copy-start.3) | copy-done | bytes 4718616
  96.7 1.6 fc_rows_near.1
  98.4 1.6 collective-permute-done.23.refs_1_
  100.8 1.5 collective-permute-start.27
  102.3 3.3 %collective-permute-done.21.refs_2_ = bf16[4,16,1024]{2,1,0:T(8,128)(2,1)S(1)} collective-permute-done((bf16[4,16,1024]{2,1,0:T(8,128)(2,1)S(1)}, bf16[4,16,1024]{2,1,0:T(8,128)(2,1)S(1)}, u32[]{:S(2)}, u32[]{:S(2)}) %collective-permute-start.21) | collective-permute-done | bytes 131104 | tf_op jit(solution)/shard_map/ppermute | solution.py:34
  105.7 1.2 outputs.1
  107.0 3.4 %collective-permute-done.26.refs_0_.refs_6_ = bf16[4,16,1024]{2,1,0:T(8,128)(2,1)S(1)} collective-permute-done((bf16[4,16,1024]{2,1,0:T(8,128)(2,1)S(1)}, bf16[4,16,1024]{2,1,0:T(8,128)(2,1)S(1)}, u32[]{:S(2)}, u32[]{:S(2)}) %collective-permute-start.26) | collective-permute-done | bytes 131104 | tf_op jit(solution)/shard_map/ppermute | solution.py:34
  110.3 3.4 %collective-permute-done.27.refs_1_.refs_7_ = bf16[4,16,1024]{2,1,0:T(8,128)(2,1)S(1)} collective-permute-done((bf16[4,16,1024]{2,1,0:T(8,128)(2,1)S(1)}, bf16[4,16,1024]{2,1,0:T(8,128)(2,1)S(1)}, u32[]{:S(2)}, u32[]{:S(2)}) %collective-permute-start.27) | collective-permute-done | bytes 131104 | tf_op jit(solution)/shard_map/ppermute | solution.py:34
  113.8 1.6 fc_rows_far.1
  115.5 1.6 collective-permute-done.28.refs_1_
  117.1 1.7 collective-permute-start.29
  118.9 4.2 %collective-permute-done.29.refs_2_ = bf16[2,9,16,256]{3,2,1,0:T(8,128)(2,1)S(1)} collective-permute-done((bf16[2,9,16,256]{3,2,1,0:T(8,128)(2,1)S(1)}, bf16[2,9,16,256]{3,2,1,0:T(8,128)(2,1)S(1)}, u32[]{:S(2)}, u32[]{:S(2)}) %collective-permute-start.29) | collective-permute-done | bytes 147488 | tf_op jit(solution)/shard_map/ppermute | solution.py:34
  123.2 1.5 collective-permute-start.31
  124.7 1.6 collective-permute-start.32
  126.2 5.2 %fc_matrix.1 = (f32[2304,1024]{1,0:T(8,128)}, f32[1,1024]{1,0:T(1,128)}, f32[8,128]{1,0:T(8,128)S(1)}) custom-call(bf16[4,9,16,256]{3,2,1,0:T(8,128)(2,1)S(1)} %join_acts.1.refs_0_, bf16[4,9,16,256]{3,2,1,0:T(8,128)(2,1)S(1)} %collective-permute-done.15.refs_1_, bf16[4,9,16,256]{3,2,1,0:T(8,128)(2,1)S(1)} %collective-permute-done.16.refs_2_, ...), custom_call_target="tpu_custom_call" | custom-call | flops 1 | bytes 1 | tf_op jit(solution)/shard_map/fc_matrix/pallas_call | solution.py:78
  131.6 1.6 collective-permute-start.33
  133.1 3.8 %collective-permute-done.33.refs_4_ = bf16[2,10,16,256]{3,2,1,0:T(8,128)(2,1)S(1)} collective-permute-done((bf16[2,10,16,256]{3,2,1,0:T(8,128)(2,1)S(1)}, bf16[2,10,16,256]{3,2,1,0:T(8,128)(2,1)S(1)}, u32[]{:S(2)}, u32[]{:S(2)}) %collective-permute-start.33) | collective-permute-done | bytes 163872 | tf_op jit(solution)/shard_map/ppermute | solution.py:34
  136.9 1.2 conv_gradient.1
  138.5 5.8 %fusion.1 = f32[3,3,384,256]{3,2,1,0:T(8,128)S(1)} fusion(bf16[13,13,16,384]{3,2,1,0:T(8,128)(2,1)S(1)} %bitcast.40, bf16[13,13,16,256]{3,2,1,0:T(8,128)(2,1)S(1)} %bitcast.47), kind=kOutput, calls=%fused_computation.6 | convolution fusion | flops 4306501632 | bytes 7000064 | tf_op jit(solution)/shard_map/conv_general_dilated | solution.py:861
  145.8 4.0 %convolution_convert_fusion = bf16[7,13,16,384]{3,2,1,0:T(8,128)(2,1)S(1)} fusion(bf16[13,13,16,256]{3,2,1,0:T(8,128)(2,1)S(1)} %bitcast.48, bf16[3,3,384,256]{3,2,1,0:T(8,128)(2,1)S(1)} %bitcast.45), kind=kOutput, calls=%fused_computation | convolution fusion | flops 2328397824 | bytes 4272128 | tf_op jit(solution)/shard_map/conv_general_dilated | solution.py:861
  151.2 1.7 collective-permute-start.38
  153.1 2.8 %collective-permute-start.41 = (bf16[880,128]{1,0:T(8,128)(2,1)S(1)}, bf16[880,128]{1,0:T(8,128)(2,1)S(1)}, u32[]{:S(2)}, u32[]{:S(2)}) collective-permute-start(bf16[880,128]{1,0:T(8,128)(2,1)S(1)} %get-tuple-element.116), channel_id=1, source_target_pairs={{0,4},{4,0},{8,12},{12,8},{1,5},{5,1},{9,13},{13,9},{2,6},{6,2},{1... | collective-permute-start | bytes 675848 | tf_op jit(solution)/shard_map/ppermute | solution.py:34
  156.3 1.2 collective-permute-start.43
  157.5 3.2 %convolution_convert_fusion.1 = bf16[6,13,16,384]{3,2,1,0:T(8,128)(2,1)S(1)} fusion(bf16[13,13,16,256]{3,2,1,0:T(8,128)(2,1)S(1)} %bitcast.49, bf16[3,3,384,256]{3,2,1,0:T(8,128)(2,1)S(1)} %bitcast.46), kind=kOutput, calls=%fused_computation.1 | convolution fusion | flops 1979142144 | bytes 4112384 | tf_op jit(solution)/shard_map/conv_general_dilated | solution.py:861
  161.7 3.6 %collective-permute-done.41.refs_2_ = bf16[880,128]{1,0:T(8,128)(2,1)S(1)} collective-permute-done((bf16[880,128]{1,0:T(8,128)(2,1)S(1)}, bf16[880,128]{1,0:T(8,128)(2,1)S(1)}, u32[]{:S(2)}, u32[]{:S(2)}) %collective-permute-start.41) | collective-permute-done | bytes 225312 | tf_op jit(solution)/shard_map/ppermute | solution.py:34
  165.3 6.6 %collective-permute-done.42.refs_3_ = bf16[880,128]{1,0:T(8,128)(2,1)S(1)} collective-permute-done((bf16[880,128]{1,0:T(8,128)(2,1)S(1)}, bf16[880,128]{1,0:T(8,128)(2,1)S(1)}, u32[]{:S(2)}, u32[]{:S(2)}) %collective-permute-start.42) | collective-permute-done | bytes 225312 | tf_op jit(solution)/shard_map/ppermute | solution.py:34
  171.9 1.6 collective-permute-start.34
  173.5 4.5 %collective-permute-done.43.refs_4_ = bf16[880,128]{1,0:T(8,128)(2,1)S(1)} collective-permute-done((bf16[880,128]{1,0:T(8,128)(2,1)S(1)}, bf16[880,128]{1,0:T(8,128)(2,1)S(1)}, u32[]{:S(2)}, u32[]{:S(2)}) %collective-permute-start.43) | collective-permute-done | bytes 225312 | tf_op jit(solution)/shard_map/ppermute | solution.py:34
  180.4 1.2 stitch_sums.1
  181.6 1.8 place_grad.3.refs_2_
  183.5 1.5 place_grad.4.refs_2_
  186.0 1.5 place_grad.5
  188.6 1.3 finish_kernels.1
  (96 shorter events, 18.3 us)
Async XLA Ops:
  0.6 75.3 %copy-start = (bf16[4,64,2,1024]{3,2,1,0:T(2,128)(2,1)S(1)}, bf16[4,64,2,1024]{3,2,1,0:T(2,128)(2,1)}, u32[]{:S(2)}) copy-start(bf16[4,64,2,1024]{3,2,1,0:T(2,128)(2,1)} %param.17) | copy-start | bytes 3145732
  3.0 5.0 %collective-permute-start = (bf16[64,896]{1,0:T(8,128)(2,1)S(1)}, bf16[64,896]{1,0:T(8,128)(2,1)S(1)}, u32[]{:S(2)}, u32[]{:S(2)}) collective-permute-start(bf16[64,896]{1,0:T(8,128)(2,1)S(1)} %own_kernels.1.refs_0_), channel_id=1, source_target_pairs={{0,2},{1,3},{2,0},{3,1},{4,6},{5,7},{6,4},{7,5},{8,10},{9,11},{10,... | collective-permute-start | bytes 344072 | tf_op jit(solution)/shard_map/ppermute | solution.py:34
  7.4 23.5 %collective-permute-start.2 = (bf16[688,384]{1,0:T(8,128)(2,1)S(1)}, bf16[688,384]{1,0:T(8,128)(2,1)S(1)}, u32[]{:S(2)}, u32[]{:S(2)}) collective-permute-start(bf16[688,384]{1,0:T(8,128)(2,1)S(1)} %get-tuple-element.70), channel_id=1, source_target_pairs={{0,2},{1,3},{2,0},{3,1},{4,6},{5,7},{6,4},{7,5},{8,10},{9,11},{10,... | collective-permute-start | bytes 1585160 | tf_op jit(solution)/shard_map/ppermute | solution.py:34
  8.0 9.5 %collective-permute-start.4 = (bf16[2,64,896]{2,1,0:T(8,128)(2,1)S(1)}, bf16[2,64,896]{2,1,0:T(8,128)(2,1)S(1)}, u32[]{:S(2)}, u32[]{:S(2)}) collective-permute-start(bf16[2,64,896]{2,1,0:T(8,128)(2,1)S(1)} %join_kernels.1.refs_1_.refs_0_), channel_id=1, source_target_pairs={{0,4},{4,0},{8,12},{12,8},{1,5},{5,1},{9,13},{13,9},{2,6},{6,2},{1... | collective-permute-start | bytes 688136 | tf_op jit(solution)/shard_map/ppermute | solution.py:34
  8.3 13.0 %collective-permute-start.5 = (bf16[2,64,896]{2,1,0:T(8,128)(2,1)S(1)}, bf16[2,64,896]{2,1,0:T(8,128)(2,1)S(1)}, u32[]{:S(2)}, u32[]{:S(2)}) collective-permute-start(bf16[2,64,896]{2,1,0:T(8,128)(2,1)S(1)} %join_kernels.1.refs_1_.refs_0_), channel_id=1, source_target_pairs={{0,8},{4,12},{8,0},{12,4},{1,9},{5,13},{9,1},{13,5},{2,10},{6,14},... | collective-permute-start | bytes 688136 | tf_op jit(solution)/shard_map/ppermute | solution.py:34
  11.2 20.2 %collective-permute-start.3 = (bf16[688,384]{1,0:T(8,128)(2,1)S(1)}, bf16[688,384]{1,0:T(8,128)(2,1)S(1)}, u32[]{:S(2)}, u32[]{:S(2)}) collective-permute-start(bf16[688,384]{1,0:T(8,128)(2,1)S(1)} %get-tuple-element.71), channel_id=1, source_target_pairs={{0,3},{1,2},{2,1},{3,0},{4,7},{5,6},{6,5},{7,4},{8,11},{9,10},{10,... | collective-permute-start | bytes 1585160 | tf_op jit(solution)/shard_map/ppermute | solution.py:34
  14.6 16.8 %collective-permute-start.1 = (bf16[688,384]{1,0:T(8,128)(2,1)S(1)}, bf16[688,384]{1,0:T(8,128)(2,1)S(1)}, u32[]{:S(2)}, u32[]{:S(2)}) collective-permute-start(bf16[688,384]{1,0:T(8,128)(2,1)S(1)} %get-tuple-element.69), channel_id=1, source_target_pairs={{0,1},{1,0},{2,3},{3,2},{4,5},{5,4},{6,7},{7,6},{8,9},{9,8},{10,11... | collective-permute-start | bytes 1585160 | tf_op jit(solution)/shard_map/ppermute | solution.py:34
  17.5 13.4 %collective-permute-start.6 = (bf16[2,64,896]{2,1,0:T(8,128)(2,1)S(1)}, bf16[2,64,896]{2,1,0:T(8,128)(2,1)S(1)}, u32[]{:S(2)}, u32[]{:S(2)}) collective-permute-start(bf16[2,64,896]{2,1,0:T(8,128)(2,1)S(1)} %join_kernels.1.refs_1_.refs_0_), channel_id=1, source_target_pairs={{0,12},{4,8},{8,4},{12,0},{1,13},{5,9},{9,5},{13,1},{2,14},{6,10},... | collective-permute-start | bytes 688136 | tf_op jit(solution)/shard_map/ppermute | solution.py:34
  21.3 11.6 %collective-permute-start.7 = (bf16[2,2,64,896]{3,2,1,0:T(8,128)(2,1)S(1)}, bf16[2,2,64,896]{3,2,1,0:T(8,128)(2,1)S(1)}, u32[]{:S(2)}, u32[]{:S(2)}) collective-permute-start(bf16[2,2,64,896]{3,2,1,0:T(8,128)(2,1)S(1)} %join_columns.1.refs_1_), channel_id=1, source_target_pairs={{0,1},{1,0},{2,3},{3,2},{4,5},{5,4},{6,7},{7,6},{8,9},{9,8},{10,11... | collective-permute-start | bytes 1376264 | tf_op jit(solution)/shard_map/ppermute | solution.py:34
  30.9 2.0 %collective-permute-start.8 = (bf16[2,64,896]{2,1,0:T(8,128)(2,1)S(1)}, bf16[2,64,896]{2,1,0:T(8,128)(2,1)S(1)}, u32[]{:S(2)}, u32[]{:S(2)}) collective-permute-start(bf16[2,64,896]{2,1,0:T(8,128)(2,1)S(1)} %collective-permute-done.5.refs_2_), channel_id=1, source_target_pairs={{0,1},{1,0},{2,3},{3,2},{4,5},{5,4},{6,7},{7,6},{8,9},{9,8},{10,11... | collective-permute-start | bytes 688136 | tf_op jit(solution)/shard_map/ppermute | solution.py:34
  30.9 1.9 %collective-permute-start.9 = (bf16[2,64,896]{2,1,0:T(8,128)(2,1)S(1)}, bf16[2,64,896]{2,1,0:T(8,128)(2,1)S(1)}, u32[]{:S(2)}, u32[]{:S(2)}) collective-permute-start(bf16[2,64,896]{2,1,0:T(8,128)(2,1)S(1)} %collective-permute-done.6.refs_3_), channel_id=1, source_target_pairs={{0,1},{1,0},{2,3},{3,2},{4,5},{5,4},{6,7},{7,6},{8,9},{9,8},{10,11... | collective-permute-start | bytes 688136 | tf_op jit(solution)/shard_map/ppermute | solution.py:34
  32.8 7.0 %copy-start.7 = (bf16[2704,384]{1,0:T(8,128)(2,1)}, bf16[2704,384]{1,0:T(8,128)(2,1)S(1)}, u32[]{:S(2)}) copy-start(bf16[2704,384]{1,0:T(8,128)(2,1)S(1)} %unpack_maps.1) | copy-start | bytes 6230020
  34.2 5.6 %copy-start.11 = (bf16[3456,256]{1,0:T(8,128)(2,1)}, bf16[3456,256]{1,0:T(8,128)(2,1)S(1)}, u32[]{:S(2)}) copy-start(bf16[3456,256]{1,0:T(8,128)(2,1)S(1)} %get-tuple-element.72) | copy-start | bytes 5308420
  41.5 6.5 %collective-permute-start.11 = (bf16[2,9,16,256]{3,2,1,0:T(8,128)(2,1)S(1)}, bf16[2,9,16,256]{3,2,1,0:T(8,128)(2,1)S(1)}, u32[]{:S(2)}, u32[]{:S(2)}) collective-permute-start(bf16[2,9,16,256]{3,2,1,0:T(8,128)(2,1)S(1)} %get-tuple-element.76), channel_id=1, source_target_pairs={{0,16},{16,0},{1,17},{17,1},{2,18},{18,2},{3,19},{19,3},{4,20},{20... | collective-permute-start | bytes 442376 | tf_op jit(solution)/shard_map/ppermute | solution.py:34
  46.0 24.3 %copy-start.2 = (bf16[2304,1024]{1,0:T(8,128)(2,1)}, bf16[2304,1024]{1,0:T(8,128)(2,1)S(1)}, u32[]{:S(2)}) copy-start(bf16[2304,1024]{1,0:T(8,128)(2,1)S(1)} %get-tuple-element.82.refs_4_.refs_2_) | copy-start | bytes 14155780
  46.6 6.3 %collective-permute-start.10 = (bf16[2,9,16,256]{3,2,1,0:T(8,128)(2,1)S(1)}, bf16[2,9,16,256]{3,2,1,0:T(8,128)(2,1)S(1)}, u32[]{:S(2)}, u32[]{:S(2)}) collective-permute-start(bf16[2,9,16,256]{3,2,1,0:T(8,128)(2,1)S(1)} %pool_near.1), channel_id=1, source_target_pairs={{0,16},{16,0},{1,17},{17,1},{2,18},{18,2},{3,19},{19,3},{4,20},{20... | collective-permute-start | bytes 442376 | tf_op jit(solution)/shard_map/ppermute | solution.py:34
  48.6 11.6 %collective-permute-start.13 = (bf16[9,16,256]{2,1,0:T(8,128)(2,1)S(1)}, bf16[9,16,256]{2,1,0:T(8,128)(2,1)S(1)}, u32[]{:S(2)}, u32[]{:S(2)}) collective-permute-start(bf16[9,16,256]{2,1,0:T(8,128)(2,1)S(1)} %get-tuple-element.77.refs_4_), channel_id=1, source_target_pairs={{0,8},{4,12},{8,0},{12,4},{1,9},{5,13},{9,1},{13,5},{2,10},{6,14},... | collective-permute-start | bytes 221192 | tf_op jit(solution)/shard_map/ppermute | solution.py:34
  53.5 6.7 %collective-permute-start.12 = (bf16[9,16,256]{2,1,0:T(8,128)(2,1)S(1)}, bf16[9,16,256]{2,1,0:T(8,128)(2,1)S(1)}, u32[]{:S(2)}, u32[]{:S(2)}) collective-permute-start(bf16[9,16,256]{2,1,0:T(8,128)(2,1)S(1)} %get-tuple-element.79), channel_id=1, source_target_pairs={{0,4},{4,0},{8,12},{12,8},{1,5},{5,1},{9,13},{13,9},{2,6},{6,2},{1... | collective-permute-start | bytes 221192 | tf_op jit(solution)/shard_map/ppermute | solution.py:34
  53.9 6.5 %collective-permute-start.14 = (bf16[9,16,256]{2,1,0:T(8,128)(2,1)S(1)}, bf16[9,16,256]{2,1,0:T(8,128)(2,1)S(1)}, u32[]{:S(2)}, u32[]{:S(2)}) collective-permute-start(bf16[9,16,256]{2,1,0:T(8,128)(2,1)S(1)} %get-tuple-element.80), channel_id=1, source_target_pairs={{0,12},{4,8},{8,4},{12,0},{1,13},{5,9},{9,5},{13,1},{2,14},{6,10},... | collective-permute-start | bytes 221192 | tf_op jit(solution)/shard_map/ppermute | solution.py:34
  58.6 1.5 copy-start.5
  60.4 8.3 %collective-permute-start.16 = (bf16[4,9,16,256]{3,2,1,0:T(8,128)(2,1)S(1)}, bf16[4,9,16,256]{3,2,1,0:T(8,128)(2,1)S(1)}, u32[]{:S(2)}, u32[]{:S(2)}) collective-permute-start(bf16[4,9,16,256]{3,2,1,0:T(8,128)(2,1)S(1)} %join_acts.1.refs_0_), channel_id=1, source_target_pairs={{0,2},{1,3},{2,0},{3,1},{4,6},{5,7},{6,4},{7,5},{8,10},{9,11},{10,... | collective-permute-start | bytes 884744 | tf_op jit(solution)/shard_map/ppermute | solution.py:34
  60.9 7.8 %collective-permute-start.15 = (bf16[4,9,16,256]{3,2,1,0:T(8,128)(2,1)S(1)}, bf16[4,9,16,256]{3,2,1,0:T(8,128)(2,1)S(1)}, u32[]{:S(2)}, u32[]{:S(2)}) collective-permute-start(bf16[4,9,16,256]{3,2,1,0:T(8,128)(2,1)S(1)} %join_acts.1.refs_0_), channel_id=1, source_target_pairs={{0,1},{1,0},{2,3},{3,2},{4,5},{5,4},{6,7},{7,6},{8,9},{9,8},{10,11... | collective-permute-start | bytes 884744 | tf_op jit(solution)/shard_map/ppermute | solution.py:34
  68.8 1.6 collective-permute-start.17
  70.3 17.6 %copy-start.9 = (f32[2,2,1024]{2,1,0:T(2,128)S(1)}, f32[2,2,1024]{2,1,0:T(2,128)}, u32[]{:S(2)}) copy-start(f32[2,2,1024]{2,1,0:T(2,128)} %refs_3_.3) | copy-start | bytes 49156
  70.3 17.6 %copy-start.10 = (f32[2,1024]{1,0:T(2,128)S(1)}, f32[2,1024]{1,0:T(2,128)}, u32[]{:S(2)}) copy-start(f32[2,1024]{1,0:T(2,128)} %refs_5_.1) | copy-start | bytes 24580
  72.5 6.6 %collective-permute-start.18 = (bf16[4,16,1024]{2,1,0:T(8,128)(2,1)}, bf16[4,16,1024]{2,1,0:T(8,128)(2,1)S(1)}, u32[]{:S(2)}, u32[]{:S(2)}) collective-permute-start(bf16[4,16,1024]{2,1,0:T(8,128)(2,1)} %get-tuple-element.84), channel_id=1, source_target_pairs={{0,4},{4,0},{8,12},{12,8},{1,5},{5,1},{9,13},{13,9},{2,6},{6,2},{1... | collective-permute-start | bytes 393224 | tf_op jit(solution)/shard_map/ppermute | solution.py:34
  73.7 10.3 %collective-permute-start.19 = (bf16[4,16,1024]{2,1,0:T(8,128)(2,1)}, bf16[4,16,1024]{2,1,0:T(8,128)(2,1)}, u32[]{:S(2)}, u32[]{:S(2)}) collective-permute-start(bf16[4,16,1024]{2,1,0:T(8,128)(2,1)} %get-tuple-element.85), channel_id=1, source_target_pairs={{0,8},{4,12},{8,0},{12,4},{1,9},{5,13},{9,1},{13,5},{2,10},{6,14},... | collective-permute-start | bytes 393224 | tf_op jit(solution)/shard_map/ppermute | solution.py:34
  74.2 13.7 %collective-permute-start.20 = (bf16[4,16,1024]{2,1,0:T(8,128)(2,1)}, bf16[4,16,1024]{2,1,0:T(8,128)(2,1)}, u32[]{:S(2)}, u32[]{:S(2)}) collective-permute-start(bf16[4,16,1024]{2,1,0:T(8,128)(2,1)} %get-tuple-element.86), channel_id=1, source_target_pairs={{0,12},{4,8},{8,4},{12,0},{1,13},{5,9},{9,5},{13,1},{2,14},{6,10},... | collective-permute-start | bytes 393224 | tf_op jit(solution)/shard_map/ppermute | solution.py:34
  89.3 5.0 %collective-permute-start.22 = (bf16[4,16,1024]{2,1,0:T(8,128)(2,1)S(1)}, bf16[4,16,1024]{2,1,0:T(8,128)(2,1)S(1)}, u32[]{:S(2)}, u32[]{:S(2)}) collective-permute-start(bf16[4,16,1024]{2,1,0:T(8,128)(2,1)S(1)} %get-tuple-element.90.refs_0_.refs_4_), channel_id=1, source_target_pairs={{0,4},{4,0},{8,12},{12,8},{1,5},{5,1},{9,13},{13,9},{2,6},{6,2},{1... | collective-permute-start | bytes 393224 | tf_op jit(solution)/shard_map/ppermute | solution.py:34
  94.3 2.3 %copy-start.3 = (bf16[2304,1024]{1,0:T(8,128)(2,1)S(1)}, bf16[2304,1024]{1,0:T(8,128)(2,1)}, u32[]{:S(2)}) copy-start(bf16[2304,1024]{1,0:T(8,128)(2,1)} %copy-done.2) | copy-start | bytes 14155780
  96.7 17.1 %copy-start.4 = (bf16[2304,1024]{1,0:T(8,128)(2,1)S(1)}, bf16[2304,1024]{1,0:T(8,128)(2,1)}, u32[]{:S(2)}) copy-start(bf16[2304,1024]{1,0:T(8,128)(2,1)} %copy-done.2) | copy-start | bytes 14155780
  98.3 1.6 collective-permute-start.23
  100.0 6.9 %collective-permute-start.24 = (bf16[2,9,16,256]{3,2,1,0:T(8,128)(2,1)S(1)}, bf16[2,9,16,256]{3,2,1,0:T(8,128)(2,1)S(1)}, u32[]{:S(2)}, u32[]{:S(2)}) collective-permute-start(bf16[2,9,16,256]{3,2,1,0:T(8,128)(2,1)S(1)} %cross_near.1), channel_id=1, source_target_pairs={{0,2},{1,3},{2,0},{3,1},{4,6},{5,7},{6,4},{7,5},{8,10},{9,11},{10,... | collective-permute-start | bytes 442376 | tf_op jit(solution)/shard_map/ppermute | solution.py:34
  100.3 5.3 %collective-permute-start.21 = (bf16[4,16,1024]{2,1,0:T(8,128)(2,1)S(1)}, bf16[4,16,1024]{2,1,0:T(8,128)(2,1)S(1)}, u32[]{:S(2)}, u32[]{:S(2)}) collective-permute-start(bf16[4,16,1024]{2,1,0:T(8,128)(2,1)S(1)} %get-tuple-element.88), channel_id=1, source_target_pairs={{0,16},{16,0},{1,17},{17,1},{2,18},{18,2},{3,19},{19,3},{4,20},{20... | collective-permute-start | bytes 393224 | tf_op jit(solution)/shard_map/ppermute | solution.py:34
  100.8 9.5 %collective-permute-start.26 = (bf16[4,16,1024]{2,1,0:T(8,128)(2,1)S(1)}, bf16[4,16,1024]{2,1,0:T(8,128)(2,1)S(1)}, u32[]{:S(2)}, u32[]{:S(2)}) collective-permute-start(bf16[4,16,1024]{2,1,0:T(8,128)(2,1)S(1)} %get-tuple-element.90.refs_0_.refs_4_), channel_id=1, source_target_pairs={{0,8},{4,12},{8,0},{12,4},{1,9},{5,13},{9,1},{13,5},{2,10},{6,14},... | collective-permute-start | bytes 393224 | tf_op jit(solution)/shard_map/ppermute | solution.py:34
  100.8 12.9 %collective-permute-start.27 = (bf16[4,16,1024]{2,1,0:T(8,128)(2,1)S(1)}, bf16[4,16,1024]{2,1,0:T(8,128)(2,1)S(1)}, u32[]{:S(2)}, u32[]{:S(2)}) collective-permute-start(bf16[4,16,1024]{2,1,0:T(8,128)(2,1)S(1)} %get-tuple-element.90.refs_0_.refs_4_), channel_id=1, source_target_pairs={{0,12},{4,8},{8,4},{12,0},{1,13},{5,9},{9,5},{13,1},{2,14},{6,10},... | collective-permute-start | bytes 393224 | tf_op jit(solution)/shard_map/ppermute | solution.py:34
  115.4 1.6 collective-permute-start.28
  117.1 19.9 %copy-start.6 = (f32[169,16,256]{2,1,0:T(8,128)S(1)}, f32[169,16,256]{2,1,0:T(8,128)}, u32[]{:S(2)}) copy-start(f32[169,16,256]{2,1,0:T(8,128)} %copy-done.5) | copy-start | bytes 8306692
  117.1 6.0 %collective-permute-start.29 = (bf16[2,9,16,256]{3,2,1,0:T(8,128)(2,1)S(1)}, bf16[2,9,16,256]{3,2,1,0:T(8,128)(2,1)S(1)}, u32[]{:S(2)}, u32[]{:S(2)}) collective-permute-start(bf16[2,9,16,256]{3,2,1,0:T(8,128)(2,1)S(1)} %cross_far.1), channel_id=1, source_target_pairs={{0,2},{1,3},{2,0},{3,1},{4,6},{5,7},{6,4},{7,5},{8,10},{9,11},{10,... | collective-permute-start | bytes 442376 | tf_op jit(solution)/shard_map/ppermute | solution.py:34
  118.8 5.8 %collective-permute-start.25 = (bf16[10,16,256]{2,1,0:T(8,128)(2,1)S(1)}, bf16[10,16,256]{2,1,0:T(8,128)(2,1)S(1)}, u32[]{:S(2)}, u32[]{:S(2)}) collective-permute-start(bf16[10,16,256]{2,1,0:T(8,128)(2,1)S(1)} %get-tuple-element.95), channel_id=1, source_target_pairs={{0,4},{4,0},{8,12},{12,8},{1,5},{5,1},{9,13},{13,9},{2,6},{6,2},{1... | collective-permute-start | bytes 245768 | tf_op jit(solution)/shard_map/ppermute | solution.py:34
  123.1 8.3 %collective-permute-start.30 = (bf16[10,16,256]{2,1,0:T(8,128)(2,1)S(1)}, bf16[10,16,256]{2,1,0:T(8,128)(2,1)S(1)}, u32[]{:S(2)}, u32[]{:S(2)}) collective-permute-start(bf16[10,16,256]{2,1,0:T(8,128)(2,1)S(1)} %get-tuple-element.99.refs_8_), channel_id=1, source_target_pairs={{0,8},{4,12},{8,0},{12,4},{1,9},{5,13},{9,1},{13,5},{2,10},{6,14},... | collective-permute-start | bytes 245768 | tf_op jit(solution)/shard_map/ppermute | solution.py:34
  123.2 8.4 %collective-permute-start.31 = (bf16[10,16,256]{2,1,0:T(8,128)(2,1)S(1)}, bf16[10,16,256]{2,1,0:T(8,128)(2,1)S(1)}, u32[]{:S(2)}, u32[]{:S(2)}) collective-permute-start(bf16[10,16,256]{2,1,0:T(8,128)(2,1)S(1)} %get-tuple-element.100), channel_id=1, source_target_pairs={{0,12},{4,8},{8,4},{12,0},{1,13},{5,9},{9,5},{13,1},{2,14},{6,10},... | collective-permute-start | bytes 245768 | tf_op jit(solution)/shard_map/ppermute | solution.py:34
  124.7 8.5 %collective-permute-start.32 = (bf16[2,10,16,256]{3,2,1,0:T(8,128)(2,1)S(1)}, bf16[2,10,16,256]{3,2,1,0:T(8,128)(2,1)S(1)}, u32[]{:S(2)}, u32[]{:S(2)}) collective-permute-start(bf16[2,10,16,256]{3,2,1,0:T(8,128)(2,1)S(1)} %join_near.1.refs_1_), channel_id=1, source_target_pairs={{0,16},{16,0},{1,17},{17,1},{2,18},{18,2},{3,19},{19,3},{4,20},{20... | collective-permute-start | bytes 491528 | tf_op jit(solution)/shard_map/ppermute | solution.py:34
  131.6 5.4 %collective-permute-start.33 = (bf16[2,10,16,256]{3,2,1,0:T(8,128)(2,1)S(1)}, bf16[2,10,16,256]{3,2,1,0:T(8,128)(2,1)S(1)}, u32[]{:S(2)}, u32[]{:S(2)}) collective-permute-start(bf16[2,10,16,256]{3,2,1,0:T(8,128)(2,1)S(1)} %join_far.1.refs_2_), channel_id=1, source_target_pairs={{0,16},{16,0},{1,17},{17,1},{2,18},{18,2},{3,19},{19,3},{4,20},{20... | collective-permute-start | bytes 491528 | tf_op jit(solution)/shard_map/ppermute | solution.py:34
  136.9 1.6 copy-start.8
  144.4 1.5 copy-start.12
  145.5 7.4 %collective-permute-start.40 = (bf16[3520,128]{1,0:T(8,128)(2,1)S(1)}, bf16[3520,128]{1,0:T(8,128)(2,1)S(1)}, u32[]{:S(2)}, u32[]{:S(2)}) collective-permute-start(bf16[3520,128]{1,0:T(8,128)(2,1)S(1)} %get-tuple-element.114), channel_id=1, source_target_pairs={{0,1},{1,0},{2,3},{3,2},{4,5},{5,4},{6,7},{7,6},{8,9},{9,8},{10,11... | collective-permute-start | bytes 2703368 | tf_op jit(solution)/shard_map/ppermute | solution.py:34
  150.9 5.5 %collective-permute-start.37 = (bf16[368,384]{1,0:T(8,128)(2,1)S(1)}, bf16[368,384]{1,0:T(8,128)(2,1)S(1)}, u32[]{:S(2)}, u32[]{:S(2)}) collective-permute-start(bf16[368,384]{1,0:T(8,128)(2,1)S(1)} %get-tuple-element.111), channel_id=1, source_target_pairs={{0,1},{1,0},{2,3},{3,2},{4,5},{5,4},{6,7},{7,6},{8,9},{9,8},{10,11... | collective-permute-start | bytes 847880 | tf_op jit(solution)/shard_map/ppermute | solution.py:34
  151.2 28.5 %collective-permute-start.38 = (bf16[368,384]{1,0:T(8,128)(2,1)S(1)}, bf16[368,384]{1,0:T(8,128)(2,1)S(1)}, u32[]{:S(2)}, u32[]{:S(2)}) collective-permute-start(bf16[368,384]{1,0:T(8,128)(2,1)S(1)} %get-tuple-element.112), channel_id=1, source_target_pairs={{0,2},{1,3},{2,0},{3,1},{4,6},{5,7},{6,4},{7,5},{8,10},{9,11},{10,... | collective-permute-start | bytes 847880 | tf_op jit(solution)/shard_map/ppermute | solution.py:34
  152.9 28.7 %collective-permute-start.39 = (bf16[368,384]{1,0:T(8,128)(2,1)S(1)}, bf16[368,384]{1,0:T(8,128)(2,1)S(1)}, u32[]{:S(2)}, u32[]{:S(2)}) collective-permute-start(bf16[368,384]{1,0:T(8,128)(2,1)S(1)} %get-tuple-element.113), channel_id=1, source_target_pairs={{0,3},{1,2},{2,1},{3,0},{4,7},{5,6},{6,5},{7,4},{8,11},{9,10},{10,... | collective-permute-start | bytes 847880 | tf_op jit(solution)/shard_map/ppermute | solution.py:34
  153.1 12.2 %collective-permute-start.41 = (bf16[880,128]{1,0:T(8,128)(2,1)S(1)}, bf16[880,128]{1,0:T(8,128)(2,1)S(1)}, u32[]{:S(2)}, u32[]{:S(2)}) collective-permute-start(bf16[880,128]{1,0:T(8,128)(2,1)S(1)} %get-tuple-element.116), channel_id=1, source_target_pairs={{0,4},{4,0},{8,12},{12,8},{1,5},{5,1},{9,13},{13,9},{2,6},{6,2},{1... | collective-permute-start | bytes 675848 | tf_op jit(solution)/shard_map/ppermute | solution.py:34
  156.0 15.9 %collective-permute-start.42 = (bf16[880,128]{1,0:T(8,128)(2,1)S(1)}, bf16[880,128]{1,0:T(8,128)(2,1)S(1)}, u32[]{:S(2)}, u32[]{:S(2)}) collective-permute-start(bf16[880,128]{1,0:T(8,128)(2,1)S(1)} %get-tuple-element.117), channel_id=1, source_target_pairs={{0,8},{4,12},{8,0},{12,4},{1,9},{5,13},{9,1},{13,5},{2,10},{6,14},... | collective-permute-start | bytes 675848 | tf_op jit(solution)/shard_map/ppermute | solution.py:34
  156.3 21.6 %collective-permute-start.43 = (bf16[880,128]{1,0:T(8,128)(2,1)S(1)}, bf16[880,128]{1,0:T(8,128)(2,1)S(1)}, u32[]{:S(2)}, u32[]{:S(2)}) collective-permute-start(bf16[880,128]{1,0:T(8,128)(2,1)S(1)} %get-tuple-element.118), channel_id=1, source_target_pairs={{0,12},{4,8},{8,4},{12,0},{1,13},{5,9},{9,5},{13,1},{2,14},{6,10},... | collective-permute-start | bytes 675848 | tf_op jit(solution)/shard_map/ppermute | solution.py:34
  165.3 18.1 %collective-permute-start.36 = (bf16[320,384]{1,0:T(8,128)(2,1)S(1)}, bf16[320,384]{1,0:T(8,128)(2,1)S(1)}, u32[]{:S(2)}, u32[]{:S(2)}) collective-permute-start(bf16[320,384]{1,0:T(8,128)(2,1)S(1)} %get-tuple-element.107), channel_id=1, source_target_pairs={{0,1},{1,0},{2,3},{3,2},{4,5},{5,4},{6,7},{7,6},{8,9},{9,8},{10,11... | collective-permute-start | bytes 737288 | tf_op jit(solution)/shard_map/ppermute | solution.py:34
  171.9 13.1 %collective-permute-start.34 = (bf16[320,384]{1,0:T(8,128)(2,1)S(1)}, bf16[320,384]{1,0:T(8,128)(2,1)S(1)}, u32[]{:S(2)}, u32[]{:S(2)}) collective-permute-start(bf16[320,384]{1,0:T(8,128)(2,1)S(1)} %get-tuple-element.104), channel_id=1, source_target_pairs={{0,2},{1,3},{2,0},{3,1},{4,6},{5,7},{6,4},{7,5},{8,10},{9,11},{10,... | collective-permute-start | bytes 737288 | tf_op jit(solution)/shard_map/ppermute | solution.py:34
  177.9 8.0 %collective-permute-start.35 = (bf16[320,384]{1,0:T(8,128)(2,1)S(1)}, bf16[320,384]{1,0:T(8,128)(2,1)S(1)}, u32[]{:S(2)}, u32[]{:S(2)}) collective-permute-start(bf16[320,384]{1,0:T(8,128)(2,1)S(1)} %get-tuple-element.105), channel_id=1, source_target_pairs={{0,3},{1,2},{2,1},{3,0},{4,7},{5,6},{6,5},{7,4},{8,11},{9,10},{10,... | collective-permute-start | bytes 737288 | tf_op jit(solution)/shard_map/ppermute | solution.py:34
  179.7 8.9 %collective-permute-start.44 = (bf16[64,896]{1,0:T(8,128)(2,1)S(1)}, bf16[64,896]{1,0:T(8,128)(2,1)S(1)}, u32[]{:S(2)}, u32[]{:S(2)}) collective-permute-start(bf16[64,896]{1,0:T(8,128)(2,1)S(1)} %get-tuple-element.120), channel_id=1, source_target_pairs={{0,2},{1,3},{2,0},{3,1},{4,6},{5,7},{6,4},{7,5},{8,10},{9,11},{10,... | collective-permute-start | bytes 344072 | tf_op jit(solution)/shard_map/ppermute | solution.py:34
  183.4 6.5 %copy-start.1 = (bf16[4,64,2,1024]{3,2,1,0:T(2,128)(2,1)S(1)}, bf16[4,64,2,1024]{3,2,1,0:T(2,128)(2,1)}, u32[]{:S(2)}) copy-start(bf16[4,64,2,1024]{3,2,1,0:T(2,128)(2,1)} %param.17) | copy-start | bytes 3145732

commit v3 on v2

--- a/solution.py
+++ b/solution.py
@@ -32,6 +32,12 @@
 def swap(value, axis, bit):
     count = lax.axis_size(axis)
     return lax.ppermute(value, axis, [(i, i ^ bit) for i in range(count)])
+
+
+def gather4(value):
+    near = swap(value, "dp", 1)
+    far = swap(value, "dp", 2)
+    return [value, near, far, swap(far, "dp", 1)]
 
 
 def sum_over(value, axis):
@@ -360,11 +366,9 @@
             struct((2, *own.shape), BF16),
             (token,),
         )
-        column = [swap(near, "dp", k) for k in (1, 2, 3)]
-        first = call(
-            join_kernel, "join_columns", [near, column[0]], struct((2, *near.shape), BF16)
-        )
-        column = [first, *column[1:]]
+        column = [near] + [swap(near, "dp", k) for k in (1, 2, 3)]
+        first = call(join_kernel, "join_columns", column[:2], struct((2, *near.shape), BF16))
+        column = [first, *column[2:]]
         across = [swap(part, "mp", 1) for part in column]
         kernel, params = call(
             kernels_kernel,
@@ -451,7 +455,7 @@
             "pair_kernels",
             [keep, swap(send, "mp", 1)],
             [struct((size, 128), F32)] + [struct((size, 128), BF16)] * 3,
-            meanwhile(keep),
+            meanwhile(),
         )
         arrived = [swap(part, "dp", k) for k, part in zip((1, 2, 3), sends)]
         mine, other = call(
@@ -476,7 +480,7 @@
     small = sum_over(sum_over(small, "dp"), "mp")
     small = lax.dynamic_slice_in_dim(small, m * 64, 64, 1)
     stitch = jnp.stack([jnp.where(s == 0, small[0], small[1]), jnp.where(s == 0, small[1], small[0])])
-    meanwhile(small)
+    meanwhile()
     return grad, small[2:3], stitch
 
 
@@ -525,8 +529,7 @@
     half_kernel(2, sel, pooled, far)
 
 
-def slope_kernel(sel, conv_out, params, slope, token):
-    token[...] = jnp.zeros(token.shape, F32)
+def slope_kernel(sel, conv_out, params, slope):
     shift = params[pl.ds(sel[S], 1), :]
     for i in range(SIDE):
         for j in range(SIDE):
@@ -553,13 +556,13 @@
     by_own, by_other = entry(params, s, s), entry(params, 1 - s, s)
     own_sum = other_sum = jnp.zeros((IMG, OUT), F32)
     for k in range(4):
-        grad = (near, far)[k // 2]
-        grad_other = (near_other, far_other)[k // 2]
+        grad = near.at[k] if k < 3 else far
+        grad_other = near_other.at[k] if k < 3 else far_other
         pooled_other = (near_pooled, far_pooled)[k // 2]
         for p in range(9):
             place = place_of(sel, k, p)
-            mine = grad[k % 2, p].astype(F32)
-            mixed[place] = by_own * mine + by_other * grad_other[k % 2, p].astype(F32)
+            mine = grad[p].astype(F32)
+            mixed[place] = by_own * mine + by_other * grad_other[p].astype(F32)
             own_sum = own_sum + mine * pooled[place]
             other_sum = other_sum + mine * pooled_other[k % 2, p].astype(F32)
     spread = []
@@ -664,8 +667,9 @@
             sums[4 * t + n : 4 * t + n + 1, :] = jnp.sum(total, 0, keepdims=True)
 
 
-def fc_rows_kernel(g0, g1, weight, keep, send):
-    rows = all_grads((g0, g1))
+def fc_rows_kernel(*refs):
+    grads, (weight, keep, send) = refs[:-3], refs[-3:]
+    rows = all_grads(grads)
     for p in range(9):
         term = lax.dot_general(
             rows,
@@ -673,7 +677,7 @@
             (((1,), (1,)), ((), ())),
             preferred_element_type=F32,
         )
-        term = term.reshape(4, 2, IMG, 256)
+        term = term.reshape(4, len(grads), IMG, 256)
         for r in range(4):
             if r % 2 == 0:
                 keep[r // 2, :, p] = term[r]
@@ -688,7 +692,7 @@
 def home_kernel(keep, arrived, crossed, sums, *chunks):
     high = sums[...].astype(BF16).astype(F32)
     small = jnp.concatenate([high, sums[...] - high], 0).astype(BF16)
-    for k in range(2):
+    for k in range(len(chunks)):
         total = keep[0, k] + arrived[0, k].astype(F32) + crossed[k].astype(F32)
         chunks[k][0:9] = total.astype(BF16)
         chunks[k][9] = small
@@ -712,8 +716,11 @@
         copy(p).wait()
 
 
-def outputs_kernel(sel, active, arrived, stitch, out, token):
-    token[...] = jnp.zeros(token.shape, F32)
+def copy_kernel(value, out):
+    out[...] = value[...]
+
+
+def outputs_kernel(sel, active, arrived, stitch, out):
     s, m = sel[S], sel[M]
     for n in range(active.shape[2] // 256):
         here = slice(n * 256, (n + 1) * 256)
@@ -726,10 +733,9 @@
 
 def plane_sum(near, far):
     total = jnp.zeros((8, OUT), F32)
-    for half in (near, far):
-        for k in range(2):
-            plane = half[k, 9].astype(F32)
-            total = total + (plane[0:8] + plane[8:16])
+    for plane in (near[0, 9], near[1, 9], near[2, 9], far[9]):
+        plane = plane.astype(F32)
+        total = total + (plane[0:8] + plane[8:16])
     return total
 
 
@@ -743,10 +749,9 @@
         out[pl.ds(1 - s, 1), here] = other[pl.ds(4 * s + n, 1), :]
 
 
-def fc_section(pooled, near, far, params, own_weight, bias, stitch, cotangent, sel, s, d, m, slope_of):
+def fc_section(pooled, near, far, params, own_weight, bias, stitch, cot, sel, s, d, m):
     count = lax.axis_size("dp")
     hid = own_weight.shape[1]
-    cot = lax.dynamic_slice_in_dim(cotangent, d * IMG, IMG, 1).transpose(2, 0, 1, 3)
     plane = struct((9, IMG, OUT), BF16)
     block = struct((4, IMG, hid), BF16)
     token = struct((8, 128), F32)
@@ -757,10 +762,9 @@
     chunks[:2] = call(
         partial(stitch_kernel, 0), "stitch_near", [sel, pooled, near, params], [plane] * 2, chunks[2:3]
     )
-    slope, after = slope_of((chunks[0],))
     if count == 4:
         moved = [chunks[0]] + [swap(chunks[k], "dp", k) for k in (1, 2, 3)]
-        own_acts = call(join_kernel, "join_acts", moved, struct((4, 9, IMG, OUT), BF16), (after,))
+        own_acts = call(join_kernel, "join_acts", moved, struct((4, 9, IMG, OUT), BF16))
         far_acts = swap(own_acts, "mp", 2)
         acts = [own_acts, swap(own_acts, "mp", 1), far_acts, swap(far_acts, "mp", 1)]
         pre, *sends = call(
@@ -786,46 +790,41 @@
         [sel, pre, *arrived, bias, stitch, cot],
         [block, struct(block.shape, F32), block, struct((8, OUT), F32)],
     )
-    outputs, output_token = call(
-        outputs_kernel, "outputs", [sel, active, swap(sent, "section", 1), stitch], [block, token]
-    )
-    half = struct((2, 10, IMG, OUT), BF16)
     if count == 4:
-        grads = [pre_grad] + [swap(pre_grad, "dp", k) for k in (1, 2, 3)]
-        pair = struct((2, 2, 9, IMG, OUT), F32)
-        ten = struct(half.shape[1:], BF16)
+        grads = gather4(pre_grad)
+        ten = struct((10, IMG, OUT), BF16)
 
         def home(ks, name, after=()):
+            shape = (2, len(ks), 9, IMG, OUT)
             keep, send = call(
                 fc_rows_kernel,
                 "fc_rows_" + name,
                 [*[grads[k] for k in ks], own_weight],
-                [pair, struct(pair.shape, BF16)],
+                [struct(shape, F32), struct(shape, BF16)],
                 after,
             )
             arrived = swap(send, "mp", 1)
-            crossing = call(
-                cross_kernel, "cross_" + name, [keep, arrived], struct(pair.shape[1:], BF16)
-            )
+            crossing = call(cross_kernel, "cross_" + name, [keep, arrived], struct(shape[1:], BF16))
             crossed = swap(crossing, "mp", 2)
-            return call(home_kernel, "home_" + name, [keep, arrived, crossed, sums], [ten] * 2)
-
-        first, second = home((0, 1), "near")
-        near_grad = call(join_kernel, "join_near", [first, swap(second, "dp", 1)], half)
-        near_back = (near_grad, swap(near_grad, "section", 1))
-        first, second = home((2, 3), "far", (first, output_token))
+            inputs = [keep, arrived, crossed, sums]
+            return call(home_kernel, "home_" + name, inputs, [ten] * len(ks))
+
+        chunks = home((0, 1, 2), "near")
+        moved = [chunks[0], swap(chunks[1], "dp", 1), swap(chunks[2], "dp", 2)]
+        (chunk,) = home((3,), "far", chunks[:1])
         matrix_grad, bias_sum, after = call(
             fc_matrix_kernel,
             "fc_matrix",
             [*acts, *grads],
             [struct(own_weight.shape, F32), struct((1, hid), F32), token],
-            (first,),
+            (chunk,),
             scratch=[pltpu.VMEM((3, 256, hid), F32), pltpu.SemaphoreType.DMA((3,))],
             limit=10 << 20,
             out_specs=[HBM, VMEM, VMEM],
         )
-        moved = [swap(first, "dp", 2), swap(second, "dp", 3)]
-        far_grad = call(join_kernel, "join_far", moved, half, (after,))
+        near_grad = call(join_kernel, "join_near", moved, struct((3, *ten.shape), BF16), (after,))
+        near_back = (near_grad, swap(near_grad, "section", 1))
+        far_grad = swap(chunk, "dp", 3)
         far_back = (far_grad, swap(far_grad, "section", 1))
     else:
         grads = lax.all_gather(pre_grad, "dp", axis=0)
@@ -841,7 +840,8 @@
         small = jnp.concatenate([high, total - high], 0).astype(BF16)
         small = jnp.stack([small] + [jnp.zeros_like(small)] * 3)
         back = jnp.concatenate([relative(back, lax.rem(d, 4)), small[:, None]], 1)
-        near_back, far_back = [(part, swap(part, "section", 1)) for part in (back[:2], back[2:])]
+        near_back, far_back = [(part, swap(part, "section", 1)) for part in (back[:3], back[3])]
+        after = sums
     stitch_sum = call(
         stitch_sums_kernel,
         "stitch_sums",
@@ -850,7 +850,7 @@
         scratch=[pltpu.VMEM((8, OUT), F32)] * 2,
     )
     grads = [near_back[0], far_back[0], near_back[1], far_back[1]]
-    return grads, slope, outputs, matrix_grad, bias_sum, stitch_sum
+    return grads, after, (active, sent), matrix_grad, bias_sum, stitch_sum
 
 
 def by_position(chunks, d):
@@ -889,12 +889,16 @@
     by_row = pltpu.with_memory_space_constraint(by_row, pltpu.HBM)
     far3, far2, token = pack_maps(by_row, sel, 3)
     kernel, params, early = gather_kernels(conv_weight, conv_bias, conv_stitch, sel, s, m, token)
-    near1, near0, token = pack_maps(by_row, sel, 1, (token, early))
+    cot = lax.dynamic_slice_in_dim(cotangent, d * IMG, IMG, 1).transpose(2, 0, 1, 3)
+    near1, near0, token = pack_maps(by_row, sel, 1, (token, early, cot))
     wires = [near0, swap(near1, "mp", 1), swap(far2, "mp", 2), swap(far3, "mp", 3)]
 
     taps = kernel.reshape(3, 3, 4 * BLK, OUT)
     maps = call(
-        unpack_kernel, "unpack_maps", [sel, *wires], struct((CELLS * IMG, 4 * BLK), BF16)
+        unpack_kernel,
+        "unpack_maps",
+        [sel, *wires],
+        struct((CELLS * IMG, 4 * BLK), BF16),
     )
     maps = maps.reshape(SIDE, SIDE, IMG, 4 * BLK)
     conv_out = conv(maps, taps, (1, 1), ("HWNC", "HWIO", "HWNC"))
@@ -907,23 +911,22 @@
     far = swap(far, "section", 1)
     near = swap(near, "section", 1)
 
-    def slope_of(after):
-        return call(
-            slope_kernel,
-            "slope",
-            [sel, conv_out, params],
-            [struct((CELLS, IMG, OUT), F32), struct((8, 128), F32)],
-            after,
-        )
-
-    back, slope, outputs, matrix_grad, fc_bias_sum, fc_stitch_sum = fc_section(
-        pooled, near, far, params, matrix, fc_bias, fc_stitch, cotangent, sel, s, d, m, slope_of
+    back, after, outputs, matrix_grad, fc_bias_sum, fc_stitch_sum = fc_section(
+        pooled, near, far, params, matrix, fc_bias, fc_stitch, cot, sel, s, d, m
+    )
+    slope = call(
+        slope_kernel,
+        "slope",
+        [sel, conv_out, params],
+        struct((CELLS, IMG, OUT), F32),
+        (back[0],),
     )
     conv_grad, sums = call(
         conv_grad_kernel,
         "conv_gradient",
         [sel, *back, slope, pooled, near, far, params],
         [struct((CELLS, IMG, OUT), BF16), struct((3, OUT), F32)],
+        (after,),
         scratch=[pltpu.VMEM((PLACES, IMG, OUT), F32)],
     )
     conv_grad = conv_grad.reshape(SIDE, SIDE, IMG, OUT)
@@ -932,18 +935,26 @@
     back_taps = taps[::-1, ::-1]
     wires = []
 
-    def send_input_grad(after):
-        chunk = HALVES[len(wires)]
-        padding = ((1, -5), (-6, 1))[len(wires)]
+    def send_input_grad(after=()):
+        chunk = len(wires)
+        padding = ((1, -5), (-6, 1))[chunk]
         part = conv(conv_grad, back_taps, padding, ("HWNC", "HWOI", "HWNC"), BF16)
-        sends = pack_grad(part.reshape(-1, 4 * BLK), sel, chunk, after)
+        sends = pack_grad(part.reshape(-1, 4 * BLK), sel, HALVES[chunk], after)
         wires.append([sends[0]] + [swap(sends[k], "mp", k) for k in (1, 2, 3)])
         return (sends[0],)
 
     kernel_rows, conv_bias_sum, conv_stitch_sum = scatter_kernels(
-        kernel_grad.reshape(36 * BLK, OUT), sums, sel, s, m, lambda mark: send_input_grad((mark,))
-    )
-    send_input_grad(())
+        kernel_grad.reshape(36 * BLK, OUT), sums, sel, s, m, send_input_grad
+    )
+    mark = send_input_grad(tuple(wires[0][2:]))
+    active, sent = outputs
+    sent = call(copy_kernel, "outputs_send", [sent], struct(sent.shape, BF16), mark)
+    outputs = call(
+        outputs_kernel,
+        "outputs",
+        [sel, active, swap(sent, "section", 1), fc_stitch],
+        struct(sent.shape, BF16),
+    )
     input_grad = place_grad(wires[0], sel, HALVES[0], (0, 1, 2, 3), None)
     input_grad = place_grad(wires[1][:2], sel, HALVES[1], (0, 1), input_grad)
     input_grad = place_grad(wires[1][2:], sel, HALVES[1], (2, 3), input_grad)

time: 192 us -> 181 us (0.943)
  waiting for transfers between devices: 80.4 us -> 72 us
  local copies, waits for them, and re-layouts: 4.8 us -> 0.25 us
  starting transfers between devices: 39.2 us -> 43.3 us
    ppermute x45, waiting for transfers between devices: 80.4 us -> 72 us  [swap(): return lax.ppermute(value, axis, [(i, i ^ bit) for i in range(count)])]
    unnamed x27 -> x9, local copies, waits for them, and re-layouts: 4.62 us -> 0.07 us
    ppermute x45, starting transfers between devices: 39.2 us -> 43.3 us  [swap(): return lax.ppermute(value, axis, [(i, i ^ bit) for i in range(count)])]
  transfers between devices with their start and end apart: 45 -> 45, of which waited for: 25 -> 25; matrix products, arithmetic and copies ran while one was open for 4% -> 4% of each run, Pallas kernels for 16% -> 17%
where the time goes in v3:
time: 181 us
  waiting for transfers between devices  72 us (40%)
  Pallas kernels  44.6 us (25%)
  starting transfers between devices  43.3 us (24%)
  matrix products  18.6 us (10%)
    ppermute x45, waiting for transfers between devices, swap(): return lax.ppermute(value, axis, [(i, i ^ bit) for i in range(count)])  72 us
    ppermute x45, starting transfers between devices, swap(): return lax.ppermute(value, axis, [(i, i ^ bit) for i in range(count)])  43.3 us
    pallas_call x32, Pallas kernels, call(): pl.pallas_call(kernel, in_specs=specs + [VMEM] * len(after), out_specs=ou...  32.7 us
    conv_general_dilated x4, matrix products, conv(): lax.conv_general_dilated(maps, taps, (1, 1), (rows, (1, 1)), dimension_nu...  18.6 us
    pallas_call x2, Pallas kernels, pack_maps(): pl.pallas_call(partial(pack_kernel, len(after)), grid_spec=pltpu.Prefetch...  6.99 us
    pallas_call x3, Pallas kernels, place_grad(): pl.pallas_call(partial(place_grad_kernel, chunk, ks), in_specs=in_specs,...  4.89 us
  transfers between devices with their start and end apart: 45, of which 25 were waited for; matrix products, arithmetic and copies ran while one was open for 4% of the time, Pallas kernels for 17%

profile of v3, /device:TPU:8, one launch (start us, length us, event | category | flops | bytes accessed | tf_op | source)
XLA Modules:
  0.0 180.6 jit_solution(1050008262184802883)
XLA Ops:
  1.5 1.6 own_kernels.1.refs_0_
  3.0 1.6 collective-permute-start
  4.6 3.6 %pack_maps.2 = (bf16[688,384]{1,0:T(8,128)(2,1)S(1)}, bf16[688,384]{1,0:T(8,128)(2,1)}, f32[8,128]{1,0:T(8,128)S(1)}) custom-call(s32[7]{0:T(128)S(1)} %pad_add_fusion.sel.refs_0_, bf16[4,5408,96]{2,1,0:T(8,128)(2,1)} %bitcast.52), custom_call_target="tpu_custom_call" | custom-call | flops 1 | bytes 1 | tf_op jit(solution)/shard_map/pack_maps/pallas_call | solution.py:190
  8.8 3.1 %collective-permute-start.6 = (bf16[2,64,896]{2,1,0:T(8,128)(2,1)S(1)}, bf16[2,64,896]{2,1,0:T(8,128)(2,1)S(1)}, u32[]{:S(2)}, u32[]{:S(2)}) collective-permute-start(bf16[2,64,896]{2,1,0:T(8,128)(2,1)S(1)} %join_kernels.1.refs_1_.refs_0_), channel_id=1, source_target_pairs={{0,12},{4,8},{8,4},{12,0},{1,13},{5,9},{9,5},{13,1},{2,14},{6,10},... | collective-permute-start | bytes 688136 | tf_op jit(solution)/shard_map/ppermute | solution.py:34
  12.2 3.4 %pack_maps.3 = (bf16[688,384]{1,0:T(8,128)(2,1)S(1)}, bf16[688,384]{1,0:T(8,128)(2,1)S(1)}, f32[8,128]{1,0:T(8,128)}) custom-call(s32[7]{0:T(128)S(1)} %pad_add_fusion.sel.refs_0_, bf16[4,5408,96]{2,1,0:T(8,128)(2,1)} %bitcast.53, f32[8,128]{1,0:T(8,128)S(1)} %get-tuple-element.62.refs_2_.refs_0_, bf16[2,64,896]{2,1,0:T(8,128)(2,1)S(1)} %join_kernels.1.refs_1_.refs_0_, ...), custom_call_target="tpu_custom_call" | custom-call | flops 1 | bytes 1 | tf_op jit(solution)/shard_map/pack_maps/pallas_call | solution.py:190
  15.6 1.6 collective-permute-start.1
  17.4 4.8 %collective-permute-start.5 = (bf16[2,64,896]{2,1,0:T(8,128)(2,1)S(1)}, bf16[2,64,896]{2,1,0:T(8,128)(2,1)S(1)}, u32[]{:S(2)}, u32[]{:S(2)}) collective-permute-start(bf16[2,64,896]{2,1,0:T(8,128)(2,1)S(1)} %join_kernels.1.refs_1_.refs_0_), channel_id=1, source_target_pairs={{0,8},{4,12},{8,0},{12,4},{1,9},{5,13},{9,1},{13,5},{2,10},{6,14},... | collective-permute-start | bytes 688136 | tf_op jit(solution)/shard_map/ppermute | solution.py:34
  22.2 4.9 %collective-permute-done.6.refs_3_ = bf16[2,64,896]{2,1,0:T(8,128)(2,1)S(1)} collective-permute-done((bf16[2,64,896]{2,1,0:T(8,128)(2,1)S(1)}, bf16[2,64,896]{2,1,0:T(8,128)(2,1)S(1)}, u32[]{:S(2)}, u32[]{:S(2)}) %collective-permute-start.6) | collective-permute-done | bytes 229408 | tf_op jit(solution)/shard_map/ppermute | solution.py:34
  27.1 3.7 %collective-permute-done.5.refs_2_ = bf16[2,64,896]{2,1,0:T(8,128)(2,1)S(1)} collective-permute-done((bf16[2,64,896]{2,1,0:T(8,128)(2,1)S(1)}, bf16[2,64,896]{2,1,0:T(8,128)(2,1)S(1)}, u32[]{:S(2)}, u32[]{:S(2)}) %collective-permute-start.5) | collective-permute-done | bytes 229408 | tf_op jit(solution)/shard_map/ppermute | solution.py:34
  31.7 1.4 unpack_maps.1
  33.2 1.4 kernels.1
  34.5 5.6 %fusion.refs_1_ = f32[13,13,16,256]{3,2,1,0:T(8,128)S(1)} fusion(bf16[13,13,16,384]{3,2,1,0:T(8,128)(2,1)S(1)} %bitcast.41, bf16[3,3,384,256]{3,2,1,0:T(8,128)(2,1)S(1)} %bitcast.45), kind=kOutput, calls=%fused_computation.5 | convolution fusion | flops 4306501632 | bytes 6615040 | tf_op jit(solution)/shard_map/conv_general_dilated | solution.py:861
  40.2 1.6 pool.1
  41.8 1.6 collective-permute-start.11
  43.4 2.9 %load_matrix.1 = (bf16[2304,1024]{1,0:T(8,128)(2,1)S(1)}, f32[8,128]{1,0:T(8,128)S(1)}) custom-call(s32[7]{0:T(128)S(1)} %pad_add_fusion.sel.refs_0_, bf16[2,2304,1024]{2,1,0:T(8,128)(2,1)} %refs_1_.1, f32[36,16,256]{2,1,0:T(8,128)S(1)} %get-tuple-element.69.refs_2_.refs_1_.refs_6_), custom_call_target="tpu_custom_call" | custom-call | flops 1 | bytes 1 | tf_op jit(solution)/shard_map/load_matrix/pallas_call | solution.py:84
  48.9 1.6 collective-permute-start.14
  50.5 1.9 %collective-permute-start.13 = (bf16[9,16,256]{2,1,0:T(8,128)(2,1)S(1)}, bf16[9,16,256]{2,1,0:T(8,128)(2,1)S(1)}, u32[]{:S(2)}, u32[]{:S(2)}) collective-permute-start(bf16[9,16,256]{2,1,0:T(8,128)(2,1)S(1)} %get-tuple-element.72.refs_4_), channel_id=1, source_target_pairs={{0,8},{4,12},{8,0},{12,4},{1,9},{5,13},{9,1},{13,5},{2,10},{6,14},... | collective-permute-start | bytes 221192 | tf_op jit(solution)/shard_map/ppermute | solution.py:34
  52.4 1.2 collective-permute-done.10.refs_2_.refs_7_
  54.9 1.5 collective-permute-done.14.refs_3_
  57.2 1.8 %collective-permute-done.12.refs_1_ = bf16[9,16,256]{2,1,0:T(8,128)(2,1)S(1)} collective-permute-done((bf16[9,16,256]{2,1,0:T(8,128)(2,1)S(1)}, bf16[9,16,256]{2,1,0:T(8,128)(2,1)S(1)}, u32[]{:S(2)}, u32[]{:S(2)}) %collective-permute-start.12) | collective-permute-done | bytes 73760 | tf_op jit(solution)/shard_map/ppermute | solution.py:34
  59.4 8.5 %collective-permute-done.16.refs_2_ = bf16[4,9,16,256]{3,2,1,0:T(8,128)(2,1)S(1)} collective-permute-done((bf16[4,9,16,256]{3,2,1,0:T(8,128)(2,1)S(1)}, bf16[4,9,16,256]{3,2,1,0:T(8,128)(2,1)S(1)}, u32[]{:S(2)}, u32[]{:S(2)}) %collective-permute-start.16) | collective-permute-done | bytes 294944 | tf_op jit(solution)/shard_map/ppermute | solution.py:34
  67.8 1.6 collective-permute-done.17.refs_3_
  69.4 1.4 fc_forward.1
  70.8 1.2 collective-permute-start.18
  72.0 1.3 collective-permute-start.19
  73.3 1.1 collective-permute-start.20
  74.3 2.8 %collective-permute-done.18.refs_2_ = bf16[4,16,1024]{2,1,0:T(8,128)(2,1)S(1)} collective-permute-done((bf16[4,16,1024]{2,1,0:T(8,128)(2,1)S(1)}, bf16[4,16,1024]{2,1,0:T(8,128)(2,1)S(1)}, u32[]{:S(2)}, u32[]{:S(2)}) %collective-permute-start.18) | collective-permute-done | bytes 131104 | tf_op jit(solution)/shard_map/ppermute | solution.py:34
  77.1 5.7 %collective-permute-done.19.refs_3_ = bf16[4,16,1024]{2,1,0:T(8,128)(2,1)S(1)} collective-permute-done((bf16[4,16,1024]{2,1,0:T(8,128)(2,1)S(1)}, bf16[4,16,1024]{2,1,0:T(8,128)(2,1)S(1)}, u32[]{:S(2)}, u32[]{:S(2)}) %collective-permute-start.19) | collective-permute-done | bytes 131104 | tf_op jit(solution)/shard_map/ppermute | solution.py:34
  82.8 3.3 %collective-permute-done.20.refs_4_ = bf16[4,16,1024]{2,1,0:T(8,128)(2,1)S(1)} collective-permute-done((bf16[4,16,1024]{2,1,0:T(8,128)(2,1)S(1)}, bf16[4,16,1024]{2,1,0:T(8,128)(2,1)S(1)}, u32[]{:S(2)}, u32[]{:S(2)}) %collective-permute-start.20) | collective-permute-done | bytes 131104 | tf_op jit(solution)/shard_map/ppermute | solution.py:34
  87.1 2.6 %collective-permute-start.21 = (bf16[4,16,1024]{2,1,0:T(8,128)(2,1)S(1)}, bf16[4,16,1024]{2,1,0:T(8,128)(2,1)S(1)}, u32[]{:S(2)}, u32[]{:S(2)}) collective-permute-start(bf16[4,16,1024]{2,1,0:T(8,128)(2,1)S(1)} %get-tuple-element.83.refs_0_.refs_4_), channel_id=1, source_target_pairs={{0,4},{4,0},{8,12},{12,8},{1,5},{5,1},{9,13},{13,9},{2,6},{6,2},{1... | collective-permute-start | bytes 393224 | tf_op jit(solution)/shard_map/ppermute | solution.py:34
  89.7 4.2 %collective-permute-done.22.refs_2_.refs_6_ = bf16[4,16,1024]{2,1,0:T(8,128)(2,1)S(1)} collective-permute-done((bf16[4,16,1024]{2,1,0:T(8,128)(2,1)S(1)}, bf16[4,16,1024]{2,1,0:T(8,128)(2,1)S(1)}, u32[]{:S(2)}, u32[]{:S(2)}) %collective-permute-start.22) | collective-permute-done | bytes 131104 | tf_op jit(solution)/shard_map/ppermute | solution.py:34
  93.9 1.4 collective-permute-done.21.refs_1_.refs_5_
  95.2 1.7 fc_rows_near.1
  97.0 1.8 collective-permute-done.23.refs_1_
  99.6 6.7 %collective-permute-done.24.refs_2_ = bf16[3,9,16,256]{3,2,1,0:T(8,128)(2,1)S(1)} collective-permute-done((bf16[3,9,16,256]{3,2,1,0:T(8,128)(2,1)S(1)}, bf16[3,9,16,256]{3,2,1,0:T(8,128)(2,1)S(1)}, u32[]{:S(2)}, u32[]{:S(2)}) %collective-permute-start.24) | collective-permute-done | bytes 221216 | tf_op jit(solution)/shard_map/ppermute | solution.py:34
  106.4 1.7 fc_rows_far.1
  108.7 1.5 collective-permute-start.26
  110.6 4.1 %collective-permute-done.29.refs_2_ = bf16[1,9,16,256]{3,2,1,0:T(8,128)(2,1)S(1)} collective-permute-done((bf16[1,9,16,256]{3,2,1,0:T(8,128)(2,1)S(1)}, bf16[1,9,16,256]{3,2,1,0:T(8,128)(2,1)S(1)}, u32[]{:S(2)}, u32[]{:S(2)}) %collective-permute-start.29) | collective-permute-done | bytes 73760 | tf_op jit(solution)/shard_map/ppermute | solution.py:34
  114.7 5.2 %fc_matrix.1 = (f32[2304,1024]{1,0:T(8,128)}, f32[1,1024]{1,0:T(1,128)}, f32[8,128]{1,0:T(8,128)S(1)}) custom-call(bf16[4,9,16,256]{3,2,1,0:T(8,128)(2,1)S(1)} %join_acts.1.refs_0_, bf16[4,9,16,256]{3,2,1,0:T(8,128)(2,1)S(1)} %collective-permute-done.15.refs_1_, bf16[4,9,16,256]{3,2,1,0:T(8,128)(2,1)S(1)} %collective-permute-done.16.refs_2_, ...), custom_call_target="tpu_custom_call" | custom-call | flops 1 | bytes 1 | tf_op jit(solution)/shard_map/fc_matrix/pallas_call | solution.py:84
  120.8 1.7 collective-permute-start.30
  122.5 2.8 %collective-permute-done.30.refs_2_ = bf16[10,16,256]{2,1,0:T(8,128)(2,1)S(1)} collective-permute-done((bf16[10,16,256]{2,1,0:T(8,128)(2,1)S(1)}, bf16[10,16,256]{2,1,0:T(8,128)(2,1)S(1)}, u32[]{:S(2)}, u32[]{:S(2)}) %collective-permute-start.30) | collective-permute-done | bytes 81952 | tf_op jit(solution)/shard_map/ppermute | solution.py:34
  125.2 1.2 collective-permute-start.32
  126.5 2.1 %slope.1.refs_5_ = f32[169,16,256]{2,1,0:T(8,128)S(1)} custom-call(s32[7]{0:T(128)S(1)} %pad_add_fusion.sel.refs_0_, f32[13,13,16,256]{3,2,1,0:T(8,128)S(1)} %fusion.refs_1_, f32[8,256]{1,0:T(8,128)S(1)} %get-tuple-element.68.refs_2_.refs_3_.refs_9_, bf16[3,10,16,256]{3,2,1,0:T(8,128)(2,1)S(1)} %join_near.1.refs_3_.refs_1_), custom_call_target="tpu_custom_call" | custom-call | flops 1 | bytes 1 | tf_op jit(solution)/shard_map/slope/pallas_call | solution.py:84
  128.6 1.1 collective-permute-done.32.refs_4_
  129.7 1.2 conv_gradient.1
  130.9 5.7 %fusion.1 = f32[3,3,384,256]{3,2,1,0:T(8,128)S(1)} fusion(bf16[13,13,16,384]{3,2,1,0:T(8,128)(2,1)S(1)} %bitcast.42, bf16[13,13,16,256]{3,2,1,0:T(8,128)(2,1)S(1)} %bitcast.48), kind=kOutput, calls=%fused_computation.6 | convolution fusion | flops 4306501632 | bytes 7000064 | tf_op jit(solution)/shard_map/conv_general_dilated | solution.py:861
  136.6 1.1 split_kernels.1
  137.8 4.0 %convolution_convert_fusion = bf16[7,13,16,384]{3,2,1,0:T(8,128)(2,1)S(1)} fusion(bf16[13,13,16,256]{3,2,1,0:T(8,128)(2,1)S(1)} %bitcast.49, bf16[3,3,384,256]{3,2,1,0:T(8,128)(2,1)S(1)} %bitcast.46), kind=kOutput, calls=%fused_computation | convolution fusion | flops 2328397824 | bytes 4272128 | tf_op jit(solution)/shard_map/conv_general_dilated | solution.py:861
  142.9 2.0 %collective-permute-start.33 = (bf16[368,384]{1,0:T(8,128)(2,1)S(1)}, bf16[368,384]{1,0:T(8,128)(2,1)S(1)}, u32[]{:S(2)}, u32[]{:S(2)}) collective-permute-start(bf16[368,384]{1,0:T(8,128)(2,1)S(1)} %get-tuple-element.94), channel_id=1, source_target_pairs={{0,2},{1,3},{2,0},{3,1},{4,6},{5,7},{6,4},{7,5},{8,10},{9,11},{10,... | collective-permute-start | bytes 847880 | tf_op jit(solution)/shard_map/ppermute | solution.py:34
  145.3 2.5 %collective-permute-start.41 = (bf16[880,128]{1,0:T(8,128)(2,1)S(1)}, bf16[880,128]{1,0:T(8,128)(2,1)S(1)}, u32[]{:S(2)}, u32[]{:S(2)}) collective-permute-start(bf16[880,128]{1,0:T(8,128)(2,1)S(1)} %get-tuple-element.106), channel_id=1, source_target_pairs={{0,4},{4,0},{8,12},{12,8},{1,5},{5,1},{9,13},{13,9},{2,6},{6,2},{1... | collective-permute-start | bytes 675848 | tf_op jit(solution)/shard_map/ppermute | solution.py:34
  147.8 1.1 collective-permute-start.42
  148.9 3.6 %collective-permute-done.33.refs_2_ = bf16[368,384]{1,0:T(8,128)(2,1)S(1)} collective-permute-done((bf16[368,384]{1,0:T(8,128)(2,1)S(1)}, bf16[368,384]{1,0:T(8,128)(2,1)S(1)}, u32[]{:S(2)}, u32[]{:S(2)}) %collective-permute-start.33) | collective-permute-done | bytes 282656 | tf_op jit(solution)/shard_map/ppermute | solution.py:34
  152.6 1.6 collective-permute-start.43
  154.2 3.2 %convolution_convert_fusion.1 = bf16[6,13,16,384]{3,2,1,0:T(8,128)(2,1)S(1)} fusion(bf16[13,13,16,256]{3,2,1,0:T(8,128)(2,1)S(1)} %bitcast.50, bf16[3,3,384,256]{3,2,1,0:T(8,128)(2,1)S(1)} %bitcast.47), kind=kOutput, calls=%fused_computation.1 | convolution fusion | flops 1979142144 | bytes 4112384 | tf_op jit(solution)/shard_map/conv_general_dilated | solution.py:861
  159.1 1.8 collective-permute-start.36
  161.0 3.5 %collective-permute-done.42.refs_3_ = bf16[880,128]{1,0:T(8,128)(2,1)S(1)} collective-permute-done((bf16[880,128]{1,0:T(8,128)(2,1)S(1)}, bf16[880,128]{1,0:T(8,128)(2,1)S(1)}, u32[]{:S(2)}, u32[]{:S(2)}) %collective-permute-start.42) | collective-permute-done | bytes 225312 | tf_op jit(solution)/shard_map/ppermute | solution.py:34
  164.5 5.0 %collective-permute-done.43.refs_4_ = bf16[880,128]{1,0:T(8,128)(2,1)S(1)} collective-permute-done((bf16[880,128]{1,0:T(8,128)(2,1)S(1)}, bf16[880,128]{1,0:T(8,128)(2,1)S(1)}, u32[]{:S(2)}, u32[]{:S(2)}) %collective-permute-start.43) | collective-permute-done | bytes 225312 | tf_op jit(solution)/shard_map/ppermute | solution.py:34
  169.6 1.2 collective-permute-start.35
  171.9 1.2 stitch_sums.1
  173.1 1.8 %place_grad.3.refs_2_ = bf16[4,2704,96]{2,1,0:T(8,128)(2,1)} custom-call(s32[7]{0:T(128)S(1)} %pad_add_fusion.sel.refs_0_, bf16[368,384]{1,0:T(8,128)(2,1)S(1)} %get-tuple-element.100.refs_0_.refs_2_, bf16[368,384]{1,0:T(8,128)(2,1)S(1)} %collective-permute-done.39.refs_1_, bf16[368,384]{1,0:T(8,128)(2,1)S(1)} %collective-permute-done.33.refs_2_, ...), custom_call_target="tpu_custom_call" | custom-call | flops 1 | bytes 1 | tf_op jit(solution)/shard_map/place_grad/pallas_call | solution.py:269
  174.9 1.3 outputs.1
  176.2 1.5 place_grad.4.refs_2_
  177.8 1.5 place_grad.5
  179.3 1.3 finish_kernels.1
  (78 shorter events, 16.4 us)
Async XLA Ops:
  0.6 11.3 %copy-start = (bf16[4,64,2,1024]{3,2,1,0:T(2,128)(2,1)S(1)}, bf16[4,64,2,1024]{3,2,1,0:T(2,128)(2,1)}, u32[]{:S(2)}) copy-start(bf16[4,64,2,1024]{3,2,1,0:T(2,128)(2,1)} %param.17) | copy-start | bytes 3145732
  3.0 5.7 %collective-permute-start = (bf16[64,896]{1,0:T(8,128)(2,1)S(1)}, bf16[64,896]{1,0:T(8,128)(2,1)S(1)}, u32[]{:S(2)}, u32[]{:S(2)}) collective-permute-start(bf16[64,896]{1,0:T(8,128)(2,1)S(1)} %own_kernels.1.refs_0_), channel_id=1, source_target_pairs={{0,2},{1,3},{2,0},{3,1},{4,6},{5,7},{6,4},{7,5},{8,10},{9,11},{10,... | collective-permute-start | bytes 344072 | tf_op jit(solution)/shard_map/ppermute | solution.py:34
  8.2 22.6 %collective-permute-start.2 = (bf16[688,384]{1,0:T(8,128)(2,1)}, bf16[688,384]{1,0:T(8,128)(2,1)S(1)}, u32[]{:S(2)}, u32[]{:S(2)}) collective-permute-start(bf16[688,384]{1,0:T(8,128)(2,1)} %get-tuple-element.65), channel_id=1, source_target_pairs={{0,2},{1,3},{2,0},{3,1},{4,6},{5,7},{6,4},{7,5},{8,10},{9,11},{10,... | collective-permute-start | bytes 1585160 | tf_op jit(solution)/shard_map/ppermute | solution.py:34
  8.8 8.6 %collective-permute-start.4 = (bf16[2,64,896]{2,1,0:T(8,128)(2,1)S(1)}, bf16[2,64,896]{2,1,0:T(8,128)(2,1)S(1)}, u32[]{:S(2)}, u32[]{:S(2)}) collective-permute-start(bf16[2,64,896]{2,1,0:T(8,128)(2,1)S(1)} %join_kernels.1.refs_1_.refs_0_), channel_id=1, source_target_pairs={{0,4},{4,0},{8,12},{12,8},{1,5},{5,1},{9,13},{13,9},{2,6},{6,2},{1... | collective-permute-start | bytes 688136 | tf_op jit(solution)/shard_map/ppermute | solution.py:34
  8.8 18.2 %collective-permute-start.6 = (bf16[2,64,896]{2,1,0:T(8,128)(2,1)S(1)}, bf16[2,64,896]{2,1,0:T(8,128)(2,1)S(1)}, u32[]{:S(2)}, u32[]{:S(2)}) collective-permute-start(bf16[2,64,896]{2,1,0:T(8,128)(2,1)S(1)} %join_kernels.1.refs_1_.refs_0_), channel_id=1, source_target_pairs={{0,12},{4,8},{8,4},{12,0},{1,13},{5,9},{9,5},{13,1},{2,14},{6,10},... | collective-permute-start | bytes 688136 | tf_op jit(solution)/shard_map/ppermute | solution.py:34
  12.0 19.8 %collective-permute-start.3 = (bf16[688,384]{1,0:T(8,128)(2,1)S(1)}, bf16[688,384]{1,0:T(8,128)(2,1)S(1)}, u32[]{:S(2)}, u32[]{:S(2)}) collective-permute-start(bf16[688,384]{1,0:T(8,128)(2,1)S(1)} %get-tuple-element.66), channel_id=1, source_target_pairs={{0,3},{1,2},{2,1},{3,0},{4,7},{5,6},{6,5},{7,4},{8,11},{9,10},{10,... | collective-permute-start | bytes 1585160 | tf_op jit(solution)/shard_map/ppermute | solution.py:34
  15.6 16.1 %collective-permute-start.1 = (bf16[688,384]{1,0:T(8,128)(2,1)S(1)}, bf16[688,384]{1,0:T(8,128)(2,1)S(1)}, u32[]{:S(2)}, u32[]{:S(2)}) collective-permute-start(bf16[688,384]{1,0:T(8,128)(2,1)S(1)} %get-tuple-element.64), channel_id=1, source_target_pairs={{0,1},{1,0},{2,3},{3,2},{4,5},{5,4},{6,7},{7,6},{8,9},{9,8},{10,11... | collective-permute-start | bytes 1585160 | tf_op jit(solution)/shard_map/ppermute | solution.py:34
  17.4 13.4 %collective-permute-start.5 = (bf16[2,64,896]{2,1,0:T(8,128)(2,1)S(1)}, bf16[2,64,896]{2,1,0:T(8,128)(2,1)S(1)}, u32[]{:S(2)}, u32[]{:S(2)}) collective-permute-start(bf16[2,64,896]{2,1,0:T(8,128)(2,1)S(1)} %join_kernels.1.refs_1_.refs_0_), channel_id=1, source_target_pairs={{0,8},{4,12},{8,0},{12,4},{1,9},{5,13},{9,1},{13,5},{2,10},{6,14},... | collective-permute-start | bytes 688136 | tf_op jit(solution)/shard_map/ppermute | solution.py:34
  27.1 6.1 %collective-permute-start.7 = (bf16[2,2,64,896]{3,2,1,0:T(8,128)(2,1)S(1)}, bf16[2,2,64,896]{3,2,1,0:T(8,128)(2,1)S(1)}, u32[]{:S(2)}, u32[]{:S(2)}) collective-permute-start(bf16[2,2,64,896]{3,2,1,0:T(8,128)(2,1)S(1)} %join_columns.1.refs_1_), channel_id=1, source_target_pairs={{0,1},{1,0},{2,3},{3,2},{4,5},{5,4},{6,7},{7,6},{8,9},{9,8},{10,11... | collective-permute-start | bytes 1376264 | tf_op jit(solution)/shard_map/ppermute | solution.py:34
  30.7 2.4 %collective-permute-start.9 = (bf16[2,64,896]{2,1,0:T(8,128)(2,1)S(1)}, bf16[2,64,896]{2,1,0:T(8,128)(2,1)S(1)}, u32[]{:S(2)}, u32[]{:S(2)}) collective-permute-start(bf16[2,64,896]{2,1,0:T(8,128)(2,1)S(1)} %collective-permute-done.6.refs_3_), channel_id=1, source_target_pairs={{0,1},{1,0},{2,3},{3,2},{4,5},{5,4},{6,7},{7,6},{8,9},{9,8},{10,11... | collective-permute-start | bytes 688136 | tf_op jit(solution)/shard_map/ppermute | solution.py:34
  30.8 2.4 %collective-permute-start.8 = (bf16[2,64,896]{2,1,0:T(8,128)(2,1)S(1)}, bf16[2,64,896]{2,1,0:T(8,128)(2,1)S(1)}, u32[]{:S(2)}, u32[]{:S(2)}) collective-permute-start(bf16[2,64,896]{2,1,0:T(8,128)(2,1)S(1)} %collective-permute-done.5.refs_2_), channel_id=1, source_target_pairs={{0,1},{1,0},{2,3},{3,2},{4,5},{5,4},{6,7},{7,6},{8,9},{9,8},{10,11... | collective-permute-start | bytes 688136 | tf_op jit(solution)/shard_map/ppermute | solution.py:34
  41.8 6.5 %collective-permute-start.11 = (bf16[2,9,16,256]{3,2,1,0:T(8,128)(2,1)S(1)}, bf16[2,9,16,256]{3,2,1,0:T(8,128)(2,1)S(1)}, u32[]{:S(2)}, u32[]{:S(2)}) collective-permute-start(bf16[2,9,16,256]{3,2,1,0:T(8,128)(2,1)S(1)} %get-tuple-element.71), channel_id=1, source_target_pairs={{0,16},{16,0},{1,17},{17,1},{2,18},{18,2},{3,19},{19,3},{4,20},{20... | collective-permute-start | bytes 442376 | tf_op jit(solution)/shard_map/ppermute | solution.py:34
  46.9 6.7 %collective-permute-start.10 = (bf16[2,9,16,256]{3,2,1,0:T(8,128)(2,1)S(1)}, bf16[2,9,16,256]{3,2,1,0:T(8,128)(2,1)S(1)}, u32[]{:S(2)}, u32[]{:S(2)}) collective-permute-start(bf16[2,9,16,256]{3,2,1,0:T(8,128)(2,1)S(1)} %pool_near.1), channel_id=1, source_target_pairs={{0,16},{16,0},{1,17},{17,1},{2,18},{18,2},{3,19},{19,3},{4,20},{20... | collective-permute-start | bytes 442376 | tf_op jit(solution)/shard_map/ppermute | solution.py:34
  48.9 7.6 %collective-permute-start.14 = (bf16[9,16,256]{2,1,0:T(8,128)(2,1)S(1)}, bf16[9,16,256]{2,1,0:T(8,128)(2,1)S(1)}, u32[]{:S(2)}, u32[]{:S(2)}) collective-permute-start(bf16[9,16,256]{2,1,0:T(8,128)(2,1)S(1)} %get-tuple-element.75), channel_id=1, source_target_pairs={{0,12},{4,8},{8,4},{12,0},{1,13},{5,9},{9,5},{13,1},{2,14},{6,10},... | collective-permute-start | bytes 221192 | tf_op jit(solution)/shard_map/ppermute | solution.py:34
  50.5 6.7 %collective-permute-start.13 = (bf16[9,16,256]{2,1,0:T(8,128)(2,1)S(1)}, bf16[9,16,256]{2,1,0:T(8,128)(2,1)S(1)}, u32[]{:S(2)}, u32[]{:S(2)}) collective-permute-start(bf16[9,16,256]{2,1,0:T(8,128)(2,1)S(1)} %get-tuple-element.72.refs_4_), channel_id=1, source_target_pairs={{0,8},{4,12},{8,0},{12,4},{1,9},{5,13},{9,1},{13,5},{2,10},{6,14},... | collective-permute-start | bytes 221192 | tf_op jit(solution)/shard_map/ppermute | solution.py:34
  54.2 4.8 %collective-permute-start.12 = (bf16[9,16,256]{2,1,0:T(8,128)(2,1)S(1)}, bf16[9,16,256]{2,1,0:T(8,128)(2,1)S(1)}, u32[]{:S(2)}, u32[]{:S(2)}) collective-permute-start(bf16[9,16,256]{2,1,0:T(8,128)(2,1)S(1)} %get-tuple-element.74), channel_id=1, source_target_pairs={{0,4},{4,0},{8,12},{12,8},{1,5},{5,1},{9,13},{13,9},{2,6},{6,2},{1... | collective-permute-start | bytes 221192 | tf_op jit(solution)/shard_map/ppermute | solution.py:34
  59.1 8.7 %collective-permute-start.16 = (bf16[4,9,16,256]{3,2,1,0:T(8,128)(2,1)S(1)}, bf16[4,9,16,256]{3,2,1,0:T(8,128)(2,1)S(1)}, u32[]{:S(2)}, u32[]{:S(2)}) collective-permute-start(bf16[4,9,16,256]{3,2,1,0:T(8,128)(2,1)S(1)} %join_acts.1.refs_0_), channel_id=1, source_target_pairs={{0,2},{1,3},{2,0},{3,1},{4,6},{5,7},{6,4},{7,5},{8,10},{9,11},{10,... | collective-permute-start | bytes 884744 | tf_op jit(solution)/shard_map/ppermute | solution.py:34
  59.3 8.5 %collective-permute-start.15 = (bf16[4,9,16,256]{3,2,1,0:T(8,128)(2,1)S(1)}, bf16[4,9,16,256]{3,2,1,0:T(8,128)(2,1)S(1)}, u32[]{:S(2)}, u32[]{:S(2)}) collective-permute-start(bf16[4,9,16,256]{3,2,1,0:T(8,128)(2,1)S(1)} %join_acts.1.refs_0_), channel_id=1, source_target_pairs={{0,1},{1,0},{2,3},{3,2},{4,5},{5,4},{6,7},{7,6},{8,9},{9,8},{10,11... | collective-permute-start | bytes 884744 | tf_op jit(solution)/shard_map/ppermute | solution.py:34
  67.8 1.6 collective-permute-start.17
  69.4 16.6 %copy-start.2 = (f32[2,2,1024]{2,1,0:T(2,128)S(1)}, f32[2,2,1024]{2,1,0:T(2,128)}, u32[]{:S(2)}) copy-start(f32[2,2,1024]{2,1,0:T(2,128)} %refs_3_.3) | copy-start | bytes 49156
  69.4 16.6 %copy-start.3 = (f32[2,1024]{1,0:T(2,128)S(1)}, f32[2,1024]{1,0:T(2,128)}, u32[]{:S(2)}) copy-start(f32[2,1024]{1,0:T(2,128)} %refs_5_.1) | copy-start | bytes 24580
  70.8 6.3 %collective-permute-start.18 = (bf16[4,16,1024]{2,1,0:T(8,128)(2,1)S(1)}, bf16[4,16,1024]{2,1,0:T(8,128)(2,1)S(1)}, u32[]{:S(2)}, u32[]{:S(2)}) collective-permute-start(bf16[4,16,1024]{2,1,0:T(8,128)(2,1)S(1)} %get-tuple-element.78), channel_id=1, source_target_pairs={{0,4},{4,0},{8,12},{12,8},{1,5},{5,1},{9,13},{13,9},{2,6},{6,2},{1... | collective-permute-start | bytes 393224 | tf_op jit(solution)/shard_map/ppermute | solution.py:34
  72.0 10.8 %collective-permute-start.19 = (bf16[4,16,1024]{2,1,0:T(8,128)(2,1)S(1)}, bf16[4,16,1024]{2,1,0:T(8,128)(2,1)S(1)}, u32[]{:S(2)}, u32[]{:S(2)}) collective-permute-start(bf16[4,16,1024]{2,1,0:T(8,128)(2,1)S(1)} %get-tuple-element.79), channel_id=1, source_target_pairs={{0,8},{4,12},{8,0},{12,4},{1,9},{5,13},{9,1},{13,5},{2,10},{6,14},... | collective-permute-start | bytes 393224 | tf_op jit(solution)/shard_map/ppermute | solution.py:34
  73.3 12.8 %collective-permute-start.20 = (bf16[4,16,1024]{2,1,0:T(8,128)(2,1)S(1)}, bf16[4,16,1024]{2,1,0:T(8,128)(2,1)S(1)}, u32[]{:S(2)}, u32[]{:S(2)}) collective-permute-start(bf16[4,16,1024]{2,1,0:T(8,128)(2,1)S(1)} %get-tuple-element.80), channel_id=1, source_target_pairs={{0,12},{4,8},{8,4},{12,0},{1,13},{5,9},{9,5},{13,1},{2,14},{6,10},... | collective-permute-start | bytes 393224 | tf_op jit(solution)/shard_map/ppermute | solution.py:34
  86.9 6.9 %collective-permute-start.22 = (bf16[4,16,1024]{2,1,0:T(8,128)(2,1)S(1)}, bf16[4,16,1024]{2,1,0:T(8,128)(2,1)S(1)}, u32[]{:S(2)}, u32[]{:S(2)}) collective-permute-start(bf16[4,16,1024]{2,1,0:T(8,128)(2,1)S(1)} %get-tuple-element.83.refs_0_.refs_4_), channel_id=1, source_target_pairs={{0,8},{4,12},{8,0},{12,4},{1,9},{5,13},{9,1},{13,5},{2,10},{6,14},... | collective-permute-start | bytes 393224 | tf_op jit(solution)/shard_map/ppermute | solution.py:34
  87.1 8.1 %collective-permute-start.21 = (bf16[4,16,1024]{2,1,0:T(8,128)(2,1)S(1)}, bf16[4,16,1024]{2,1,0:T(8,128)(2,1)S(1)}, u32[]{:S(2)}, u32[]{:S(2)}) collective-permute-start(bf16[4,16,1024]{2,1,0:T(8,128)(2,1)S(1)} %get-tuple-element.83.refs_0_.refs_4_), channel_id=1, source_target_pairs={{0,4},{4,0},{8,12},{12,8},{1,5},{5,1},{9,13},{13,9},{2,6},{6,2},{1... | collective-permute-start | bytes 393224 | tf_op jit(solution)/shard_map/ppermute | solution.py:34
  96.9 1.9 %collective-permute-start.23 = (bf16[2,3,9,16,256]{4,3,2,1,0:T(8,128)(2,1)S(1)}, bf16[2,3,9,16,256]{4,3,2,1,0:T(8,128)(2,1)S(1)}, u32[]{:S(2)}, u32[]{:S(2)}) collective-permute-start(bf16[2,3,9,16,256]{4,3,2,1,0:T(8,128)(2,1)S(1)} %get-tuple-element.85), channel_id=1, source_target_pairs={{0,1},{1,0},{2,3},{3,2},{4,5},{5,4},{6,7},{7,6},{8,9},{9,8},{10,11... | collective-permute-start | bytes 1327112 | tf_op jit(solution)/shard_map/ppermute | solution.py:34
  98.8 7.5 %collective-permute-start.24 = (bf16[3,9,16,256]{3,2,1,0:T(8,128)(2,1)S(1)}, bf16[3,9,16,256]{3,2,1,0:T(8,128)(2,1)S(1)}, u32[]{:S(2)}, u32[]{:S(2)}) collective-permute-start(bf16[3,9,16,256]{3,2,1,0:T(8,128)(2,1)S(1)} %cross_near.1), channel_id=1, source_target_pairs={{0,2},{1,3},{2,0},{3,1},{4,6},{5,7},{6,4},{7,5},{8,10},{9,11},{10,... | collective-permute-start | bytes 663560 | tf_op jit(solution)/shard_map/ppermute | solution.py:34
  99.1 7.3 %collective-permute-start.27 = (bf16[4,16,1024]{2,1,0:T(8,128)(2,1)S(1)}, bf16[4,16,1024]{2,1,0:T(8,128)(2,1)S(1)}, u32[]{:S(2)}, u32[]{:S(2)}) collective-permute-start(bf16[4,16,1024]{2,1,0:T(8,128)(2,1)S(1)} %collective-permute-done.22.refs_2_.refs_6_), channel_id=1, source_target_pairs={{0,4},{4,0},{8,12},{12,8},{1,5},{5,1},{9,13},{13,9},{2,6},{6,2},{1... | collective-permute-start | bytes 393224 | tf_op jit(solution)/shard_map/ppermute | solution.py:34
  108.1 2.1 %collective-permute-start.28 = (bf16[2,1,9,16,256]{4,3,2,1,0:T(8,128)(2,1)S(1)}, bf16[2,1,9,16,256]{4,3,2,1,0:T(8,128)(2,1)S(1)}, u32[]{:S(2)}, u32[]{:S(2)}) collective-permute-start(bf16[2,1,9,16,256]{4,3,2,1,0:T(8,128)(2,1)S(1)} %get-tuple-element.91), channel_id=1, source_target_pairs={{0,1},{1,0},{2,3},{3,2},{4,5},{5,4},{6,7},{7,6},{8,9},{9,8},{10,11... | collective-permute-start | bytes 442376 | tf_op jit(solution)/shard_map/ppermute | solution.py:34
  108.2 11.7 %collective-permute-start.25 = (bf16[10,16,256]{2,1,0:T(8,128)(2,1)S(1)}, bf16[10,16,256]{2,1,0:T(8,128)(2,1)S(1)}, u32[]{:S(2)}, u32[]{:S(2)}) collective-permute-start(bf16[10,16,256]{2,1,0:T(8,128)(2,1)S(1)} %get-tuple-element.88), channel_id=1, source_target_pairs={{0,4},{4,0},{8,12},{12,8},{1,5},{5,1},{9,13},{13,9},{2,6},{6,2},{1... | collective-permute-start | bytes 245768 | tf_op jit(solution)/shard_map/ppermute | solution.py:34
  108.7 11.2 %collective-permute-start.26 = (bf16[10,16,256]{2,1,0:T(8,128)(2,1)S(1)}, bf16[10,16,256]{2,1,0:T(8,128)(2,1)S(1)}, u32[]{:S(2)}, u32[]{:S(2)}) collective-permute-start(bf16[10,16,256]{2,1,0:T(8,128)(2,1)S(1)} %get-tuple-element.89), channel_id=1, source_target_pairs={{0,8},{4,12},{8,0},{12,4},{1,9},{5,13},{9,1},{13,5},{2,10},{6,14},... | collective-permute-start | bytes 245768 | tf_op jit(solution)/shard_map/ppermute | solution.py:34
  110.3 4.4 %collective-permute-start.29 = (bf16[1,9,16,256]{3,2,1,0:T(8,128)(2,1)S(1)}, bf16[1,9,16,256]{3,2,1,0:T(8,128)(2,1)S(1)}, u32[]{:S(2)}, u32[]{:S(2)}) collective-permute-start(bf16[1,9,16,256]{3,2,1,0:T(8,128)(2,1)S(1)} %cross_far.1), channel_id=1, source_target_pairs={{0,2},{1,3},{2,0},{3,1},{4,6},{5,7},{6,4},{7,5},{8,10},{9,11},{10,... | collective-permute-start | bytes 221192 | tf_op jit(solution)/shard_map/ppermute | solution.py:34
  120.0 9.7 %collective-permute-start.31 = (bf16[3,10,16,256]{3,2,1,0:T(8,128)(2,1)S(1)}, bf16[3,10,16,256]{3,2,1,0:T(8,128)(2,1)S(1)}, u32[]{:S(2)}, u32[]{:S(2)}) collective-permute-start(bf16[3,10,16,256]{3,2,1,0:T(8,128)(2,1)S(1)} %join_near.1.refs_3_.refs_1_), channel_id=1, source_target_pairs={{0,16},{16,0},{1,17},{17,1},{2,18},{18,2},{3,19},{19,3},{4,20},{20... | collective-permute-start | bytes 737288 | tf_op jit(solution)/shard_map/ppermute | solution.py:34
  120.8 4.4 %collective-permute-start.30 = (bf16[10,16,256]{2,1,0:T(8,128)(2,1)S(1)}, bf16[10,16,256]{2,1,0:T(8,128)(2,1)S(1)}, u32[]{:S(2)}, u32[]{:S(2)}) collective-permute-start(bf16[10,16,256]{2,1,0:T(8,128)(2,1)S(1)} %home_far.1.refs_8_), channel_id=1, source_target_pairs={{0,12},{4,8},{8,4},{12,0},{1,13},{5,9},{9,5},{13,1},{2,14},{6,10},... | collective-permute-start | bytes 245768 | tf_op jit(solution)/shard_map/ppermute | solution.py:34
  125.2 4.4 %collective-permute-start.32 = (bf16[10,16,256]{2,1,0:T(8,128)(2,1)S(1)}, bf16[10,16,256]{2,1,0:T(8,128)(2,1)S(1)}, u32[]{:S(2)}, u32[]{:S(2)}) collective-permute-start(bf16[10,16,256]{2,1,0:T(8,128)(2,1)S(1)} %collective-permute-done.30.refs_2_), channel_id=1, source_target_pairs={{0,16},{16,0},{1,17},{17,1},{2,18},{18,2},{3,19},{19,3},{4,20},{20... | collective-permute-start | bytes 245768 | tf_op jit(solution)/shard_map/ppermute | solution.py:34
  137.8 7.4 %collective-permute-start.40 = (bf16[3520,128]{1,0:T(8,128)(2,1)S(1)}, bf16[3520,128]{1,0:T(8,128)(2,1)S(1)}, u32[]{:S(2)}, u32[]{:S(2)}) collective-permute-start(bf16[3520,128]{1,0:T(8,128)(2,1)S(1)} %get-tuple-element.104), channel_id=1, source_target_pairs={{0,1},{1,0},{2,3},{3,2},{4,5},{5,4},{6,7},{7,6},{8,9},{9,8},{10,11... | collective-permute-start | bytes 2703368 | tf_op jit(solution)/shard_map/ppermute | solution.py:34
  142.9 9.7 %collective-permute-start.33 = (bf16[368,384]{1,0:T(8,128)(2,1)S(1)}, bf16[368,384]{1,0:T(8,128)(2,1)S(1)}, u32[]{:S(2)}, u32[]{:S(2)}) collective-permute-start(bf16[368,384]{1,0:T(8,128)(2,1)S(1)} %get-tuple-element.94), channel_id=1, source_target_pairs={{0,2},{1,3},{2,0},{3,1},{4,6},{5,7},{6,4},{7,5},{8,10},{9,11},{10,... | collective-permute-start | bytes 847880 | tf_op jit(solution)/shard_map/ppermute | solution.py:34
  144.9 13.2 %collective-permute-start.34 = (bf16[368,384]{1,0:T(8,128)(2,1)S(1)}, bf16[368,384]{1,0:T(8,128)(2,1)S(1)}, u32[]{:S(2)}, u32[]{:S(2)}) collective-permute-start(bf16[368,384]{1,0:T(8,128)(2,1)S(1)} %get-tuple-element.95), channel_id=1, source_target_pairs={{0,3},{1,2},{2,1},{3,0},{4,7},{5,6},{6,5},{7,4},{8,11},{9,10},{10,... | collective-permute-start | bytes 847880 | tf_op jit(solution)/shard_map/ppermute | solution.py:34
  145.1 26.4 %collective-permute-start.39 = (bf16[368,384]{1,0:T(8,128)(2,1)S(1)}, bf16[368,384]{1,0:T(8,128)(2,1)S(1)}, u32[]{:S(2)}, u32[]{:S(2)}) collective-permute-start(bf16[368,384]{1,0:T(8,128)(2,1)S(1)} %get-tuple-element.101), channel_id=1, source_target_pairs={{0,1},{1,0},{2,3},{3,2},{4,5},{5,4},{6,7},{7,6},{8,9},{9,8},{10,11... | collective-permute-start | bytes 847880 | tf_op jit(solution)/shard_map/ppermute | solution.py:34
  145.3 15.5 %collective-permute-start.41 = (bf16[880,128]{1,0:T(8,128)(2,1)S(1)}, bf16[880,128]{1,0:T(8,128)(2,1)S(1)}, u32[]{:S(2)}, u32[]{:S(2)}) collective-permute-start(bf16[880,128]{1,0:T(8,128)(2,1)S(1)} %get-tuple-element.106), channel_id=1, source_target_pairs={{0,4},{4,0},{8,12},{12,8},{1,5},{5,1},{9,13},{13,9},{2,6},{6,2},{1... | collective-permute-start | bytes 675848 | tf_op jit(solution)/shard_map/ppermute | solution.py:34
  147.8 16.7 %collective-permute-start.42 = (bf16[880,128]{1,0:T(8,128)(2,1)S(1)}, bf16[880,128]{1,0:T(8,128)(2,1)S(1)}, u32[]{:S(2)}, u32[]{:S(2)}) collective-permute-start(bf16[880,128]{1,0:T(8,128)(2,1)S(1)} %get-tuple-element.107), channel_id=1, source_target_pairs={{0,8},{4,12},{8,0},{12,4},{1,9},{5,13},{9,1},{13,5},{2,10},{6,14},... | collective-permute-start | bytes 675848 | tf_op jit(solution)/shard_map/ppermute | solution.py:34
  152.6 17.0 %collective-permute-start.43 = (bf16[880,128]{1,0:T(8,128)(2,1)S(1)}, bf16[880,128]{1,0:T(8,128)(2,1)S(1)}, u32[]{:S(2)}, u32[]{:S(2)}) collective-permute-start(bf16[880,128]{1,0:T(8,128)(2,1)S(1)} %get-tuple-element.108), channel_id=1, source_target_pairs={{0,12},{4,8},{8,4},{12,0},{1,13},{5,9},{9,5},{13,1},{2,14},{6,10},... | collective-permute-start | bytes 675848 | tf_op jit(solution)/shard_map/ppermute | solution.py:34
  159.1 18.7 %collective-permute-start.36 = (bf16[320,384]{1,0:T(8,128)(2,1)S(1)}, bf16[320,384]{1,0:T(8,128)(2,1)S(1)}, u32[]{:S(2)}, u32[]{:S(2)}) collective-permute-start(bf16[320,384]{1,0:T(8,128)(2,1)S(1)} %get-tuple-element.97), channel_id=1, source_target_pairs={{0,2},{1,3},{2,0},{3,1},{4,6},{5,7},{6,4},{7,5},{8,10},{9,11},{10,... | collective-permute-start | bytes 737288 | tf_op jit(solution)/shard_map/ppermute | solution.py:34
  160.8 15.4 %collective-permute-start.38 = (bf16[320,384]{1,0:T(8,128)(2,1)S(1)}, bf16[320,384]{1,0:T(8,128)(2,1)S(1)}, u32[]{:S(2)}, u32[]{:S(2)}) collective-permute-start(bf16[320,384]{1,0:T(8,128)(2,1)S(1)} %get-tuple-element.99), channel_id=1, source_target_pairs={{0,1},{1,0},{2,3},{3,2},{4,5},{5,4},{6,7},{7,6},{8,9},{9,8},{10,11... | collective-permute-start | bytes 737288 | tf_op jit(solution)/shard_map/ppermute | solution.py:34
  164.5 13.2 %collective-permute-start.37 = (bf16[320,384]{1,0:T(8,128)(2,1)S(1)}, bf16[320,384]{1,0:T(8,128)(2,1)S(1)}, u32[]{:S(2)}, u32[]{:S(2)}) collective-permute-start(bf16[320,384]{1,0:T(8,128)(2,1)S(1)} %get-tuple-element.98), channel_id=1, source_target_pairs={{0,3},{1,2},{2,1},{3,0},{4,7},{5,6},{6,5},{7,4},{8,11},{9,10},{10,... | collective-permute-start | bytes 737288 | tf_op jit(solution)/shard_map/ppermute | solution.py:34
  169.6 5.4 %collective-permute-start.35 = (bf16[4,16,1024]{2,1,0:T(8,128)(2,1)S(1)}, bf16[4,16,1024]{2,1,0:T(8,128)(2,1)S(1)}, u32[]{:S(2)}, u32[]{:S(2)}) collective-permute-start(bf16[4,16,1024]{2,1,0:T(8,128)(2,1)S(1)} %outputs_send.1), channel_id=1, source_target_pairs={{0,16},{16,0},{1,17},{17,1},{2,18},{18,2},{3,19},{19,3},{4,20},{20... | collective-permute-start | bytes 393224 | tf_op jit(solution)/shard_map/ppermute | solution.py:34
  171.5 7.8 %collective-permute-start.44 = (bf16[64,896]{1,0:T(8,128)(2,1)S(1)}, bf16[64,896]{1,0:T(8,128)(2,1)S(1)}, u32[]{:S(2)}, u32[]{:S(2)}) collective-permute-start(bf16[64,896]{1,0:T(8,128)(2,1)S(1)} %get-tuple-element.110), channel_id=1, source_target_pairs={{0,2},{1,3},{2,0},{3,1},{4,6},{5,7},{6,4},{7,5},{8,10},{9,11},{10,... | collective-permute-start | bytes 344072 | tf_op jit(solution)/shard_map/ppermute | solution.py:34
  176.2 4.4 %copy-start.1 = (bf16[4,64,2,1024]{3,2,1,0:T(2,128)(2,1)S(1)}, bf16[4,64,2,1024]{3,2,1,0:T(2,128)(2,1)}, u32[]{:S(2)}) copy-start(bf16[4,64,2,1024]{3,2,1,0:T(2,128)(2,1)} %param.17) | copy-start | bytes 3145732

commit v4 on v3

--- a/solution.py
+++ b/solution.py
@@ -93,6 +93,22 @@
     )(*inputs, *after)
 
 
+def pass_on(value, after):
+    def kernel(*refs):
+        pass
+
+    return pl.pallas_call(
+        kernel,
+        in_specs=[ANY] + [VMEM] * len(after),
+        out_specs=ANY,
+        out_shape=struct(value.shape, value.dtype),
+        input_output_aliases={0: 0},
+        compiler_params=pltpu.CompilerParams(vmem_limit_bytes=SCOPE),
+        cost_estimate=COST,
+        name="pass_on",
+    )(value, *after)
+
+
 def lane_index(rows=IMG):
     return lax.broadcasted_iota(jnp.int32, (rows, 128), 1)
 
@@ -196,7 +212,7 @@
             + [VMEM] * len(after),
             out_specs=[pl.BlockSpec(shape, lambda i, sel: (0, 0))] * 2
             + [pl.BlockSpec((8, 128), lambda i, sel: (0, 0))],
-            scratch_shapes=[pltpu.VMEM((IMG * CELLS * 2, 128), F32)],
+            scratch_shapes=[pltpu.VMEM((IMG * CELLS * 2 + 2 * CELLS + 14, 128), F32)],
         ),
         out_shape=[struct(shape, BF16)] * 2 + [struct((8, 128), F32)],
         compiler_params=pltpu.CompilerParams(vmem_limit_bytes=12 << 20),
@@ -442,7 +458,7 @@
     bias[...] = small[BLK + 2 : BLK + 3]
 
 
-def scatter_kernels(grad, small, sel, s, m, meanwhile):
+def scatter_kernels(grad, small, sel, s, m, meanwhile, finish_fc):
     rows = grad.shape[0] // lax.axis_size("dp")
     small_shapes = [struct((1, 64), F32), struct((2, 64), F32)]
     if lax.axis_size("dp") == 4:
@@ -457,7 +473,10 @@
             [struct((size, 128), F32)] + [struct((size, 128), BF16)] * 3,
             meanwhile(),
         )
-        arrived = [swap(part, "dp", k) for k, part in zip((1, 2, 3), sends)]
+        last = call(
+            copy_kernel, "last_kernels", sends[2:], struct((size, 128), BF16), finish_fc(own)
+        )
+        arrived = [swap(part, "dp", k) for k, part in zip((1, 2, 3), (*sends[:2], last))]
         mine, other = call(
             turn_kernel,
             "turn_kernels",
@@ -470,7 +489,7 @@
             [sel, mine, swap(other, "mp", 2)],
             [struct((64, ROWS), F32), *small_shapes],
         )
-        return result.T, bias, stitch
+        return result.T, bias, stitch, own
     grad = grad.reshape(9, 3, 128, OUT)
     last = grad[:, :, BLK:].reshape(9, 1, BLK, OUT)
     grad = jnp.concatenate([grad[:, :, :BLK], last], 1)
@@ -481,7 +500,8 @@
     small = lax.dynamic_slice_in_dim(small, m * 64, 64, 1)
     stitch = jnp.stack([jnp.where(s == 0, small[0], small[1]), jnp.where(s == 0, small[1], small[0])])
     meanwhile()
-    return grad, small[2:3], stitch
+    finish_fc(small)
+    return grad, small[2:3], stitch, small
 
 
 def gelu_parts(value):
@@ -749,9 +769,9 @@
         out[pl.ds(1 - s, 1), here] = other[pl.ds(4 * s + n, 1), :]
 
 
-def fc_section(pooled, near, far, params, own_weight, bias, stitch, cot, sel, s, d, m):
+def fc_section(pooled, near, far, params, weight, bias, stitch, cot, sel, s, d, m):
     count = lax.axis_size("dp")
-    hid = own_weight.shape[1]
+    hid = weight.shape[2]
     plane = struct((9, IMG, OUT), BF16)
     block = struct((4, IMG, hid), BF16)
     token = struct((8, 128), F32)
@@ -762,9 +782,10 @@
     chunks[:2] = call(
         partial(stitch_kernel, 0), "stitch_near", [sel, pooled, near, params], [plane] * 2, chunks[2:3]
     )
+    own_weight, after = load_matrix(weight, sel, s, chunks[:1])
     if count == 4:
         moved = [chunks[0]] + [swap(chunks[k], "dp", k) for k in (1, 2, 3)]
-        own_acts = call(join_kernel, "join_acts", moved, struct((4, 9, IMG, OUT), BF16))
+        own_acts = call(join_kernel, "join_acts", moved, struct((4, 9, IMG, OUT), BF16), after)
         far_acts = swap(own_acts, "mp", 2)
         acts = [own_acts, swap(own_acts, "mp", 1), far_acts, swap(far_acts, "mp", 1)]
         pre, *sends = call(
@@ -794,6 +815,8 @@
         grads = gather4(pre_grad)
         ten = struct((10, IMG, OUT), BF16)
 
+        marks = []
+
         def home(ks, name, after=()):
             shape = (2, len(ks), 9, IMG, OUT)
             keep, send = call(
@@ -807,22 +830,25 @@
             crossing = call(cross_kernel, "cross_" + name, [keep, arrived], struct(shape[1:], BF16))
             crossed = swap(crossing, "mp", 2)
             inputs = [keep, arrived, crossed, sums]
+            marks.append(crossing)
             return call(home_kernel, "home_" + name, inputs, [ten] * len(ks))
 
         chunks = home((0, 1, 2), "near")
         moved = [chunks[0], swap(chunks[1], "dp", 1), swap(chunks[2], "dp", 2)]
-        (chunk,) = home((3,), "far", chunks[:1])
-        matrix_grad, bias_sum, after = call(
-            fc_matrix_kernel,
-            "fc_matrix",
-            [*acts, *grads],
-            [struct(own_weight.shape, F32), struct((1, hid), F32), token],
-            (chunk,),
-            scratch=[pltpu.VMEM((3, 256, hid), F32), pltpu.SemaphoreType.DMA((3,))],
-            limit=10 << 20,
-            out_specs=[HBM, VMEM, VMEM],
-        )
-        near_grad = call(join_kernel, "join_near", moved, struct((3, *ten.shape), BF16), (after,))
+        (chunk,) = home((3,), "far", marks[:1])
+        def matrix_gradient(after, grads=tuple(grads)):
+            return call(
+                fc_matrix_kernel,
+                "fc_matrix",
+                [*acts, *grads],
+                [struct(own_weight.shape, F32), struct((1, hid), F32), token],
+                after,
+                scratch=[pltpu.VMEM((3, 256, hid), F32), pltpu.SemaphoreType.DMA((3,))],
+                limit=10 << 20,
+                out_specs=[HBM, VMEM, VMEM],
+            )
+
+        near_grad = call(join_kernel, "join_near", moved, struct((3, *ten.shape), BF16), (chunk,))
         near_back = (near_grad, swap(near_grad, "section", 1))
         far_grad = swap(chunk, "dp", 3)
         far_back = (far_grad, swap(far_grad, "section", 1))
@@ -835,13 +861,16 @@
         back = rows.transpose(1, 0, 2).reshape(IMG, 4, 9, OUT).transpose(1, 2, 0, 3)
         matrix_grad = jnp.einsum("rdnf,drnk->fk", flat, grads, preferred_element_type=F32)
         bias_sum = jnp.sum(grads.astype(F32), (0, 1, 2))[None]
+
+        def matrix_gradient(after):
+            return matrix_grad, bias_sum, sums
+
         total = sum_over(sums, "dp")
         high = lax.reduce_precision(total, 8, 7)
         small = jnp.concatenate([high, total - high], 0).astype(BF16)
         small = jnp.stack([small] + [jnp.zeros_like(small)] * 3)
         back = jnp.concatenate([relative(back, lax.rem(d, 4)), small[:, None]], 1)
         near_back, far_back = [(part, swap(part, "section", 1)) for part in (back[:3], back[3])]
-        after = sums
     stitch_sum = call(
         stitch_sums_kernel,
         "stitch_sums",
@@ -850,7 +879,7 @@
         scratch=[pltpu.VMEM((8, OUT), F32)] * 2,
     )
     grads = [near_back[0], far_back[0], near_back[1], far_back[1]]
-    return grads, after, (active, sent), matrix_grad, bias_sum, stitch_sum
+    return grads, (active, sent), matrix_gradient, stitch_sum
 
 
 def by_position(chunks, d):
@@ -906,13 +935,12 @@
     pooled, far = call(
         pool_kernel, "pool", [sel, conv_out, params], [struct((PLACES, IMG, OUT), F32), half]
     )
-    matrix, after = load_matrix(fc_weight, sel, s, (pooled,))
-    near = call(partial(half_kernel, 0), "pool_near", [sel, pooled], half, after)
+    near = call(partial(half_kernel, 0), "pool_near", [sel, pooled], half)
     far = swap(far, "section", 1)
     near = swap(near, "section", 1)
 
-    back, after, outputs, matrix_grad, fc_bias_sum, fc_stitch_sum = fc_section(
-        pooled, near, far, params, matrix, fc_bias, fc_stitch, cot, sel, s, d, m
+    back, outputs, matrix_gradient, fc_stitch_sum = fc_section(
+        pooled, near, far, params, fc_weight, fc_bias, fc_stitch, cot, sel, s, d, m
     )
     slope = call(
         slope_kernel,
@@ -926,27 +954,35 @@
         "conv_gradient",
         [sel, *back, slope, pooled, near, far, params],
         [struct((CELLS, IMG, OUT), BF16), struct((3, OUT), F32)],
-        (after,),
         scratch=[pltpu.VMEM((PLACES, IMG, OUT), F32)],
     )
     conv_grad = conv_grad.reshape(SIDE, SIDE, IMG, OUT)
 
-    kernel_grad = conv(maps, conv_grad, (1, 1), ("HWCN", "HWIO", "HWNC"))
     back_taps = taps[::-1, ::-1]
     wires = []
 
     def send_input_grad(after=()):
         chunk = len(wires)
-        padding = ((1, -5), (-6, 1))[chunk]
+        low, high = HALVES[chunk]
+        padding = (1 - low, 1 - SIDE + high)
         part = conv(conv_grad, back_taps, padding, ("HWNC", "HWOI", "HWNC"), BF16)
         sends = pack_grad(part.reshape(-1, 4 * BLK), sel, HALVES[chunk], after)
         wires.append([sends[0]] + [swap(sends[k], "mp", k) for k in (1, 2, 3)])
         return (sends[0],)
 
-    kernel_rows, conv_bias_sum, conv_stitch_sum = scatter_kernels(
-        kernel_grad.reshape(36 * BLK, OUT), sums, sel, s, m, send_input_grad
-    )
-    mark = send_input_grad(tuple(wires[0][2:]))
+    maps = pass_on(maps, send_input_grad())
+    kernel_grad = conv(maps, conv_grad, (1, 1), ("HWCN", "HWIO", "HWNC"))
+    results = []
+
+    def finish_fc(begun):
+        results.extend(matrix_gradient((begun,)))
+        return results[-1:]
+
+    kernel_rows, conv_bias_sum, conv_stitch_sum, begun = scatter_kernels(
+        kernel_grad.reshape(36 * BLK, OUT), sums, sel, s, m, lambda: (), finish_fc
+    )
+    matrix_grad, fc_bias_sum, _ = results
+    mark = send_input_grad((*wires[0][2:], begun))
     active, sent = outputs
     sent = call(copy_kernel, "outputs_send", [sent], struct(sent.shape, BF16), mark)
     outputs = call(

time: 181 us -> 176 us (0.972)
  waiting for transfers between devices: 72 us -> 68.3 us
    ppermute x45, waiting for transfers between devices: 72 us -> 68.3 us  [swap(): return lax.ppermute(value, axis, [(i, i ^ bit) for i in range(count)])]
    pallas_call x32 -> x33, Pallas kernels: 32.7 us -> 32.9 us  [call(): pl.pallas_call(kernel, in_specs=specs + [VMEM] * len(after), out_specs=ou...]
  transfers between devices with their start and end apart: 45 -> 45, of which waited for: 25 -> 21; matrix products, arithmetic and copies ran while one was open for 4% -> 2% of each run, Pallas kernels for 17% -> 18%
where the time goes in v4:
time: 176 us
  waiting for transfers between devices  68.3 us (39%)
  Pallas kernels  44.8 us (25%)
  starting transfers between devices  42.4 us (24%)
  matrix products  18.6 us (11%)
    ppermute x45, waiting for transfers between devices, swap(): return lax.ppermute(value, axis, [(i, i ^ bit) for i in range(count)])  68.3 us
    ppermute x45, starting transfers between devices, swap(): return lax.ppermute(value, axis, [(i, i ^ bit) for i in range(count)])  42.4 us
    pallas_call x33, Pallas kernels, call(): pl.pallas_call(kernel, in_specs=specs + [VMEM] * len(after), out_specs=ou...  32.9 us
    conv_general_dilated x4, matrix products, conv(): lax.conv_general_dilated(maps, taps, (1, 1), (rows, (1, 1)), dimension_nu...  18.6 us
    pallas_call x2, Pallas kernels, pack_maps(): pl.pallas_call(partial(pack_kernel, len(after)), grid_spec=pltpu.Prefetch...  6.99 us
    pallas_call x3, Pallas kernels, place_grad(): pl.pallas_call(partial(place_grad_kernel, chunk, ks), in_specs=in_specs,...  4.89 us
  transfers between devices with their start and end apart: 45, of which 21 were waited for; matrix products, arithmetic and copies ran while one was open for 2% of the time, Pallas kernels for 18%

profile of v4, /device:TPU:8, one launch (start us, length us, event | category | flops | bytes accessed | tf_op | source)
XLA Modules:
  0.0 176.2 jit_solution(8015253256893338654)
XLA Ops:
  1.5 1.6 own_kernels.1.refs_0_
  3.0 1.6 collective-permute-start
  4.6 3.6 %pack_maps.2 = (bf16[688,384]{1,0:T(8,128)(2,1)S(1)}, bf16[688,384]{1,0:T(8,128)(2,1)}, f32[8,128]{1,0:T(8,128)S(1)}) custom-call(s32[7]{0:T(128)S(1)} %pad_add_fusion.sel.refs_0_, bf16[4,5408,96]{2,1,0:T(8,128)(2,1)} %bitcast.52), custom_call_target="tpu_custom_call" | custom-call | flops 1 | bytes 1 | tf_op jit(solution)/shard_map/pack_maps/pallas_call | solution.py:206
  8.8 3.0 %collective-permute-start.5 = (bf16[2,64,896]{2,1,0:T(8,128)(2,1)S(1)}, bf16[2,64,896]{2,1,0:T(8,128)(2,1)S(1)}, u32[]{:S(2)}, u32[]{:S(2)}) collective-permute-start(bf16[2,64,896]{2,1,0:T(8,128)(2,1)S(1)} %join_kernels.1.refs_1_.refs_0_), channel_id=1, source_target_pairs={{0,8},{4,12},{8,0},{12,4},{1,9},{5,13},{9,1},{13,5},{2,10},{6,14},... | collective-permute-start | bytes 688136 | tf_op jit(solution)/shard_map/ppermute | solution.py:34
  12.1 3.4 %pack_maps.3 = (bf16[688,384]{1,0:T(8,128)(2,1)S(1)}, bf16[688,384]{1,0:T(8,128)(2,1)S(1)}, f32[8,128]{1,0:T(8,128)}) custom-call(s32[7]{0:T(128)S(1)} %pad_add_fusion.sel.refs_0_, bf16[4,5408,96]{2,1,0:T(8,128)(2,1)} %bitcast.53, f32[8,128]{1,0:T(8,128)S(1)} %get-tuple-element.62.refs_2_.refs_0_, bf16[2,64,896]{2,1,0:T(8,128)(2,1)S(1)} %join_kernels.1.refs_1_.refs_0_, ...), custom_call_target="tpu_custom_call" | custom-call | flops 1 | bytes 1 | tf_op jit(solution)/shard_map/pack_maps/pallas_call | solution.py:206
  15.5 1.6 collective-permute-start.1
  17.1 1.1 collective-permute-done.4.refs_1_
  18.2 1.7 collective-permute-start.6
  20.0 2.0 %collective-permute-done.5.refs_2_ = bf16[2,64,896]{2,1,0:T(8,128)(2,1)S(1)} collective-permute-done((bf16[2,64,896]{2,1,0:T(8,128)(2,1)S(1)}, bf16[2,64,896]{2,1,0:T(8,128)(2,1)S(1)}, u32[]{:S(2)}, u32[]{:S(2)}) %collective-permute-start.5) | collective-permute-done | bytes 229408 | tf_op jit(solution)/shard_map/ppermute | solution.py:34
  22.0 9.6 %collective-permute-done.6.refs_3_ = bf16[2,64,896]{2,1,0:T(8,128)(2,1)S(1)} collective-permute-done((bf16[2,64,896]{2,1,0:T(8,128)(2,1)S(1)}, bf16[2,64,896]{2,1,0:T(8,128)(2,1)S(1)}, u32[]{:S(2)}, u32[]{:S(2)}) %collective-permute-start.6) | collective-permute-done | bytes 229408 | tf_op jit(solution)/shard_map/ppermute | solution.py:34
  32.1 1.4 unpack_maps.1
  33.6 1.4 kernels.1
  34.9 5.6 %fusion.refs_1_ = f32[13,13,16,256]{3,2,1,0:T(8,128)S(1)} fusion(bf16[13,13,16,384]{3,2,1,0:T(8,128)(2,1)S(1)} %bitcast.38, bf16[3,3,384,256]{3,2,1,0:T(8,128)(2,1)S(1)} %bitcast.45), kind=kOutput, calls=%fused_computation.5 | convolution fusion | flops 4306501632 | bytes 6615040 | tf_op jit(solution)/shard_map/conv_general_dilated | solution.py:890
  40.5 1.6 pool.1
  42.2 1.6 collective-permute-start.11
  44.9 4.1 %collective-permute-done.11.refs_2_.refs_8_ = bf16[2,9,16,256]{3,2,1,0:T(8,128)(2,1)S(1)} collective-permute-done((bf16[2,9,16,256]{3,2,1,0:T(8,128)(2,1)S(1)}, bf16[2,9,16,256]{3,2,1,0:T(8,128)(2,1)S(1)}, u32[]{:S(2)}, u32[]{:S(2)}) %collective-permute-start.11) | collective-permute-done | bytes 147488 | tf_op jit(solution)/shard_map/ppermute | solution.py:34
  49.5 2.0 %collective-permute-start.13 = (bf16[9,16,256]{2,1,0:T(8,128)(2,1)S(1)}, bf16[9,16,256]{2,1,0:T(8,128)(2,1)S(1)}, u32[]{:S(2)}, u32[]{:S(2)}) collective-permute-start(bf16[9,16,256]{2,1,0:T(8,128)(2,1)S(1)} %get-tuple-element.71.refs_4_), channel_id=1, source_target_pairs={{0,8},{4,12},{8,0},{12,4},{1,9},{5,13},{9,1},{13,5},{2,10},{6,14},... | collective-permute-start | bytes 221192 | tf_op jit(solution)/shard_map/ppermute | solution.py:34
  53.3 1.9 %collective-permute-start.14 = (bf16[9,16,256]{2,1,0:T(8,128)(2,1)S(1)}, bf16[9,16,256]{2,1,0:T(8,128)(2,1)S(1)}, u32[]{:S(2)}, u32[]{:S(2)}) collective-permute-start(bf16[9,16,256]{2,1,0:T(8,128)(2,1)S(1)} %get-tuple-element.74), channel_id=1, source_target_pairs={{0,12},{4,8},{8,4},{12,0},{1,13},{5,9},{9,5},{13,1},{2,14},{6,10},... | collective-permute-start | bytes 221192 | tf_op jit(solution)/shard_map/ppermute | solution.py:34
  55.2 2.9 %load_matrix.1 = (bf16[2304,1024]{1,0:T(8,128)(2,1)S(1)}, f32[8,128]{1,0:T(8,128)S(1)}) custom-call(s32[7]{0:T(128)S(1)} %pad_add_fusion.sel.refs_0_, bf16[2,2304,1024]{2,1,0:T(8,128)(2,1)} %refs_1_.1, bf16[9,16,256]{2,1,0:T(8,128)(2,1)S(1)} %get-tuple-element.72.refs_2_.refs_0_), custom_call_target="tpu_custom_call" | custom-call | flops 1 | bytes 1 | tf_op jit(solution)/shard_map/load_matrix/pallas_call | solution.py:84
  58.2 2.2 %collective-permute-start.16 = (bf16[4,9,16,256]{3,2,1,0:T(8,128)(2,1)S(1)}, bf16[4,9,16,256]{3,2,1,0:T(8,128)(2,1)S(1)}, u32[]{:S(2)}, u32[]{:S(2)}) collective-permute-start(bf16[4,9,16,256]{3,2,1,0:T(8,128)(2,1)S(1)} %join_acts.1.refs_0_), channel_id=1, source_target_pairs={{0,2},{1,3},{2,0},{3,1},{4,6},{5,7},{6,4},{7,5},{8,10},{9,11},{10,... | collective-permute-start | bytes 884744 | tf_op jit(solution)/shard_map/ppermute | solution.py:34
  60.4 6.4 %collective-permute-done.16.refs_2_ = bf16[4,9,16,256]{3,2,1,0:T(8,128)(2,1)S(1)} collective-permute-done((bf16[4,9,16,256]{3,2,1,0:T(8,128)(2,1)S(1)}, bf16[4,9,16,256]{3,2,1,0:T(8,128)(2,1)S(1)}, u32[]{:S(2)}, u32[]{:S(2)}) %collective-permute-start.16) | collective-permute-done | bytes 294944 | tf_op jit(solution)/shard_map/ppermute | solution.py:34
  66.8 1.6 collective-permute-done.17.refs_3_
  68.4 1.4 fc_forward.1
  69.8 2.9 %collective-permute-start.18 = (bf16[4,16,1024]{2,1,0:T(8,128)(2,1)S(1)}, bf16[4,16,1024]{2,1,0:T(8,128)(2,1)S(1)}, u32[]{:S(2)}, u32[]{:S(2)}) collective-permute-start(bf16[4,16,1024]{2,1,0:T(8,128)(2,1)S(1)} %get-tuple-element.78), channel_id=1, source_target_pairs={{0,4},{4,0},{8,12},{12,8},{1,5},{5,1},{9,13},{13,9},{2,6},{6,2},{1... | collective-permute-start | bytes 393224 | tf_op jit(solution)/shard_map/ppermute | solution.py:34
  73.4 0.9 collective-permute-start.20
  74.3 3.6 %collective-permute-done.18.refs_2_ = bf16[4,16,1024]{2,1,0:T(8,128)(2,1)S(1)} collective-permute-done((bf16[4,16,1024]{2,1,0:T(8,128)(2,1)S(1)}, bf16[4,16,1024]{2,1,0:T(8,128)(2,1)S(1)}, u32[]{:S(2)}, u32[]{:S(2)}) %collective-permute-start.18) | collective-permute-done | bytes 131104 | tf_op jit(solution)/shard_map/ppermute | solution.py:34
  77.8 5.0 %collective-permute-done.19.refs_3_ = bf16[4,16,1024]{2,1,0:T(8,128)(2,1)S(1)} collective-permute-done((bf16[4,16,1024]{2,1,0:T(8,128)(2,1)S(1)}, bf16[4,16,1024]{2,1,0:T(8,128)(2,1)S(1)}, u32[]{:S(2)}, u32[]{:S(2)}) %collective-permute-start.19) | collective-permute-done | bytes 131104 | tf_op jit(solution)/shard_map/ppermute | solution.py:34
  82.9 3.4 %collective-permute-done.20.refs_4_ = bf16[4,16,1024]{2,1,0:T(8,128)(2,1)S(1)} collective-permute-done((bf16[4,16,1024]{2,1,0:T(8,128)(2,1)S(1)}, bf16[4,16,1024]{2,1,0:T(8,128)(2,1)S(1)}, u32[]{:S(2)}, u32[]{:S(2)}) %collective-permute-start.20) | collective-permute-done | bytes 131104 | tf_op jit(solution)/shard_map/ppermute | solution.py:34
  86.3 0.9 fc_active.1
  87.2 2.6 %collective-permute-start.22 = (bf16[4,16,1024]{2,1,0:T(8,128)(2,1)S(1)}, bf16[4,16,1024]{2,1,0:T(8,128)(2,1)S(1)}, u32[]{:S(2)}, u32[]{:S(2)}) collective-permute-start(bf16[4,16,1024]{2,1,0:T(8,128)(2,1)S(1)} %get-tuple-element.83.refs_0_.refs_4_), channel_id=1, source_target_pairs={{0,8},{4,12},{8,0},{12,4},{1,9},{5,13},{9,1},{13,5},{2,10},{6,14},... | collective-permute-start | bytes 393224 | tf_op jit(solution)/shard_map/ppermute | solution.py:34
  89.8 3.5 %collective-permute-done.21.refs_1_.refs_5_ = bf16[4,16,1024]{2,1,0:T(8,128)(2,1)S(1)} collective-permute-done((bf16[4,16,1024]{2,1,0:T(8,128)(2,1)S(1)}, bf16[4,16,1024]{2,1,0:T(8,128)(2,1)S(1)}, u32[]{:S(2)}, u32[]{:S(2)}) %collective-permute-start.21) | collective-permute-done | bytes 131104 | tf_op jit(solution)/shard_map/ppermute | solution.py:34
  93.3 2.0 %collective-permute-done.22.refs_2_.refs_6_ = bf16[4,16,1024]{2,1,0:T(8,128)(2,1)S(1)} collective-permute-done((bf16[4,16,1024]{2,1,0:T(8,128)(2,1)S(1)}, bf16[4,16,1024]{2,1,0:T(8,128)(2,1)S(1)}, u32[]{:S(2)}, u32[]{:S(2)}) %collective-permute-start.22) | collective-permute-done | bytes 131104 | tf_op jit(solution)/shard_map/ppermute | solution.py:34
  95.3 1.7 fc_rows_near.1
  97.0 2.2 %collective-permute-start.27 = (bf16[4,16,1024]{2,1,0:T(8,128)(2,1)S(1)}, bf16[4,16,1024]{2,1,0:T(8,128)(2,1)S(1)}, u32[]{:S(2)}, u32[]{:S(2)}) collective-permute-start(bf16[4,16,1024]{2,1,0:T(8,128)(2,1)S(1)} %collective-permute-done.22.refs_2_.refs_6_), channel_id=1, source_target_pairs={{0,4},{4,0},{8,12},{12,8},{1,5},{5,1},{9,13},{13,9},{2,6},{6,2},{1... | collective-permute-start | bytes 393224 | tf_op jit(solution)/shard_map/ppermute | solution.py:34
  99.6 3.7 %collective-permute-done.27.refs_0_.refs_7_ = bf16[4,16,1024]{2,1,0:T(8,128)(2,1)S(1)} collective-permute-done((bf16[4,16,1024]{2,1,0:T(8,128)(2,1)S(1)}, bf16[4,16,1024]{2,1,0:T(8,128)(2,1)S(1)}, u32[]{:S(2)}, u32[]{:S(2)}) %collective-permute-start.27) | collective-permute-done | bytes 131104 | tf_op jit(solution)/shard_map/ppermute | solution.py:34
  103.3 1.7 fc_rows_far.1
  105.0 1.8 collective-permute-done.24.refs_2_
  106.9 1.7 collective-permute-start.25
  108.6 0.9 collective-permute-start.26
  109.9 4.1 %collective-permute-done.29.refs_2_ = bf16[1,9,16,256]{3,2,1,0:T(8,128)(2,1)S(1)} collective-permute-done((bf16[1,9,16,256]{3,2,1,0:T(8,128)(2,1)S(1)}, bf16[1,9,16,256]{3,2,1,0:T(8,128)(2,1)S(1)}, u32[]{:S(2)}, u32[]{:S(2)}) %collective-permute-start.29) | collective-permute-done | bytes 73760 | tf_op jit(solution)/shard_map/ppermute | solution.py:34
  114.1 1.6 collective-permute-start.31
  115.7 1.1 collective-permute-start.30
  116.7 3.4 %collective-permute-done.30.refs_2_ = bf16[10,16,256]{2,1,0:T(8,128)(2,1)S(1)} collective-permute-done((bf16[10,16,256]{2,1,0:T(8,128)(2,1)S(1)}, bf16[10,16,256]{2,1,0:T(8,128)(2,1)S(1)}, u32[]{:S(2)}, u32[]{:S(2)}) %collective-permute-start.30) | collective-permute-done | bytes 81952 | tf_op jit(solution)/shard_map/ppermute | solution.py:34
  120.6 2.1 %slope.1.refs_5_ = f32[169,16,256]{2,1,0:T(8,128)S(1)} custom-call(s32[7]{0:T(128)S(1)} %pad_add_fusion.sel.refs_0_, f32[13,13,16,256]{3,2,1,0:T(8,128)S(1)} %fusion.refs_1_, f32[8,256]{1,0:T(8,128)S(1)} %get-tuple-element.68.refs_2_.refs_3_.refs_9_, bf16[3,10,16,256]{3,2,1,0:T(8,128)(2,1)S(1)} %join_near.1.refs_3_.refs_1_), custom_call_target="tpu_custom_call" | custom-call | flops 1 | bytes 1 | tf_op jit(solution)/shard_map/slope/pallas_call | solution.py:84
  122.7 1.9 %collective-permute-done.32.refs_4_ = bf16[10,16,256]{2,1,0:T(8,128)(2,1)S(1)} collective-permute-done((bf16[10,16,256]{2,1,0:T(8,128)(2,1)S(1)}, bf16[10,16,256]{2,1,0:T(8,128)(2,1)S(1)}, u32[]{:S(2)}, u32[]{:S(2)}) %collective-permute-start.32) | collective-permute-done | bytes 81952 | tf_op jit(solution)/shard_map/ppermute | solution.py:34
  124.5 1.2 conv_gradient.1
  125.7 3.8 %convolution_convert_fusion = bf16[7,13,16,384]{3,2,1,0:T(8,128)(2,1)S(1)} fusion(bf16[13,13,16,256]{3,2,1,0:T(8,128)(2,1)S(1)} %bitcast.48, bf16[3,3,384,256]{3,2,1,0:T(8,128)(2,1)S(1)} %bitcast.46), kind=kOutput, calls=%fused_computation | convolution fusion | flops 2328397824 | bytes 4272128 | tf_op jit(solution)/shard_map/conv_general_dilated | solution.py:890
  129.5 1.0 pack_grad.2
  130.6 6.0 %fusion.1 = f32[3,3,384,256]{3,2,1,0:T(8,128)S(1)} fusion(bf16[13,13,16,384]{3,2,1,0:T(8,128)(2,1)S(1)} %pass_on.1, bf16[13,13,16,256]{3,2,1,0:T(8,128)(2,1)S(1)} %bitcast.49), kind=kOutput, calls=%fused_computation.6 | convolution fusion | flops 4306501632 | bytes 7000064 | tf_op jit(solution)/shard_map/conv_general_dilated | solution.py:890
  136.6 1.1 split_kernels.1
  138.2 1.5 collective-permute-start.34
  140.5 3.5 %collective-permute-start.41 = (bf16[880,128]{1,0:T(8,128)(2,1)S(1)}, bf16[880,128]{1,0:T(8,128)(2,1)S(1)}, u32[]{:S(2)}, u32[]{:S(2)}) collective-permute-start(bf16[880,128]{1,0:T(8,128)(2,1)S(1)} %get-tuple-element.105), channel_id=1, source_target_pairs={{0,4},{4,0},{8,12},{12,8},{1,5},{5,1},{9,13},{13,9},{2,6},{6,2},{1... | collective-permute-start | bytes 675848 | tf_op jit(solution)/shard_map/ppermute | solution.py:34
  144.6 5.2 %fc_matrix.1 = (f32[2304,1024]{1,0:T(8,128)}, f32[1,1024]{1,0:T(1,128)}, f32[8,128]{1,0:T(8,128)S(1)}) custom-call(bf16[4,9,16,256]{3,2,1,0:T(8,128)(2,1)S(1)} %join_acts.1.refs_0_, bf16[4,9,16,256]{3,2,1,0:T(8,128)(2,1)S(1)} %collective-permute-done.15.refs_1_, bf16[4,9,16,256]{3,2,1,0:T(8,128)(2,1)S(1)} %collective-permute-done.16.refs_2_, ...), custom_call_target="tpu_custom_call" | custom-call | flops 1 | bytes 1 | tf_op jit(solution)/shard_map/fc_matrix/pallas_call | solution.py:84
  149.9 1.0 collective-permute-start.43
  150.9 3.2 %convolution_convert_fusion.1 = bf16[6,13,16,384]{3,2,1,0:T(8,128)(2,1)S(1)} fusion(bf16[13,13,16,256]{3,2,1,0:T(8,128)(2,1)S(1)} %bitcast.50, bf16[3,3,384,256]{3,2,1,0:T(8,128)(2,1)S(1)} %bitcast.47), kind=kOutput, calls=%fused_computation.1 | convolution fusion | flops 1979142144 | bytes 4112384 | tf_op jit(solution)/shard_map/conv_general_dilated | solution.py:890
  154.1 1.0 pack_grad.3
  155.5 4.7 %collective-permute-done.42.refs_3_ = bf16[880,128]{1,0:T(8,128)(2,1)S(1)} collective-permute-done((bf16[880,128]{1,0:T(8,128)(2,1)S(1)}, bf16[880,128]{1,0:T(8,128)(2,1)S(1)}, u32[]{:S(2)}, u32[]{:S(2)}) %collective-permute-start.42) | collective-permute-done | bytes 225312 | tf_op jit(solution)/shard_map/ppermute | solution.py:34
  160.2 5.5 %collective-permute-done.43.refs_4_ = bf16[880,128]{1,0:T(8,128)(2,1)S(1)} collective-permute-done((bf16[880,128]{1,0:T(8,128)(2,1)S(1)}, bf16[880,128]{1,0:T(8,128)(2,1)S(1)}, u32[]{:S(2)}, u32[]{:S(2)}) %collective-permute-start.43) | collective-permute-done | bytes 225312 | tf_op jit(solution)/shard_map/ppermute | solution.py:34
  167.3 1.2 stitch_sums.1
  168.4 1.8 %place_grad.3.refs_2_ = bf16[4,2704,96]{2,1,0:T(8,128)(2,1)} custom-call(s32[7]{0:T(128)S(1)} %pad_add_fusion.sel.refs_0_, bf16[368,384]{1,0:T(8,128)(2,1)S(1)} %get-tuple-element.95.refs_1_.refs_0_, bf16[368,384]{1,0:T(8,128)(2,1)S(1)} %collective-permute-done.40.refs_1_, bf16[368,384]{1,0:T(8,128)(2,1)S(1)} %collective-permute-done.33.refs_2_, ...), custom_call_target="tpu_custom_call" | custom-call | flops 1 | bytes 1 | tf_op jit(solution)/shard_map/place_grad/pallas_call | solution.py:285
  170.6 1.2 outputs.1
  171.9 1.5 place_grad.4.refs_2_
  173.4 1.5 place_grad.5
  175.0 1.3 finish_kernels.1
  (80 shorter events, 12.2 us)
Async XLA Ops:
  0.6 11.2 %copy-start = (bf16[4,64,2,1024]{3,2,1,0:T(2,128)(2,1)S(1)}, bf16[4,64,2,1024]{3,2,1,0:T(2,128)(2,1)}, u32[]{:S(2)}) copy-start(bf16[4,64,2,1024]{3,2,1,0:T(2,128)(2,1)} %param.17) | copy-start | bytes 3145732
  3.0 5.7 %collective-permute-start = (bf16[64,896]{1,0:T(8,128)(2,1)S(1)}, bf16[64,896]{1,0:T(8,128)(2,1)S(1)}, u32[]{:S(2)}, u32[]{:S(2)}) collective-permute-start(bf16[64,896]{1,0:T(8,128)(2,1)S(1)} %own_kernels.1.refs_0_), channel_id=1, source_target_pairs={{0,2},{1,3},{2,0},{3,1},{4,6},{5,7},{6,4},{7,5},{8,10},{9,11},{10,... | collective-permute-start | bytes 344072 | tf_op jit(solution)/shard_map/ppermute | solution.py:34
  8.2 23.5 %collective-permute-start.2 = (bf16[688,384]{1,0:T(8,128)(2,1)}, bf16[688,384]{1,0:T(8,128)(2,1)S(1)}, u32[]{:S(2)}, u32[]{:S(2)}) collective-permute-start(bf16[688,384]{1,0:T(8,128)(2,1)} %get-tuple-element.65), channel_id=1, source_target_pairs={{0,2},{1,3},{2,0},{3,1},{4,6},{5,7},{6,4},{7,5},{8,10},{9,11},{10,... | collective-permute-start | bytes 1585160 | tf_op jit(solution)/shard_map/ppermute | solution.py:34
  8.8 9.5 %collective-permute-start.4 = (bf16[2,64,896]{2,1,0:T(8,128)(2,1)S(1)}, bf16[2,64,896]{2,1,0:T(8,128)(2,1)S(1)}, u32[]{:S(2)}, u32[]{:S(2)}) collective-permute-start(bf16[2,64,896]{2,1,0:T(8,128)(2,1)S(1)} %join_kernels.1.refs_1_.refs_0_), channel_id=1, source_target_pairs={{0,4},{4,0},{8,12},{12,8},{1,5},{5,1},{9,13},{13,9},{2,6},{6,2},{1... | collective-permute-start | bytes 688136 | tf_op jit(solution)/shard_map/ppermute | solution.py:34
  8.8 13.1 %collective-permute-start.5 = (bf16[2,64,896]{2,1,0:T(8,128)(2,1)S(1)}, bf16[2,64,896]{2,1,0:T(8,128)(2,1)S(1)}, u32[]{:S(2)}, u32[]{:S(2)}) collective-permute-start(bf16[2,64,896]{2,1,0:T(8,128)(2,1)S(1)} %join_kernels.1.refs_1_.refs_0_), channel_id=1, source_target_pairs={{0,8},{4,12},{8,0},{12,4},{1,9},{5,13},{9,1},{13,5},{2,10},{6,14},... | collective-permute-start | bytes 688136 | tf_op jit(solution)/shard_map/ppermute | solution.py:34
  11.9 20.2 %collective-permute-start.3 = (bf16[688,384]{1,0:T(8,128)(2,1)S(1)}, bf16[688,384]{1,0:T(8,128)(2,1)S(1)}, u32[]{:S(2)}, u32[]{:S(2)}) collective-permute-start(bf16[688,384]{1,0:T(8,128)(2,1)S(1)} %get-tuple-element.66), channel_id=1, source_target_pairs={{0,3},{1,2},{2,1},{3,0},{4,7},{5,6},{6,5},{7,4},{8,11},{9,10},{10,... | collective-permute-start | bytes 1585160 | tf_op jit(solution)/shard_map/ppermute | solution.py:34
  15.5 16.6 %collective-permute-start.1 = (bf16[688,384]{1,0:T(8,128)(2,1)S(1)}, bf16[688,384]{1,0:T(8,128)(2,1)S(1)}, u32[]{:S(2)}, u32[]{:S(2)}) collective-permute-start(bf16[688,384]{1,0:T(8,128)(2,1)S(1)} %get-tuple-element.64), channel_id=1, source_target_pairs={{0,1},{1,0},{2,3},{3,2},{4,5},{5,4},{6,7},{7,6},{8,9},{9,8},{10,11... | collective-permute-start | bytes 1585160 | tf_op jit(solution)/shard_map/ppermute | solution.py:34
  18.2 13.4 %collective-permute-start.6 = (bf16[2,64,896]{2,1,0:T(8,128)(2,1)S(1)}, bf16[2,64,896]{2,1,0:T(8,128)(2,1)S(1)}, u32[]{:S(2)}, u32[]{:S(2)}) collective-permute-start(bf16[2,64,896]{2,1,0:T(8,128)(2,1)S(1)} %join_kernels.1.refs_1_.refs_0_), channel_id=1, source_target_pairs={{0,12},{4,8},{8,4},{12,0},{1,13},{5,9},{9,5},{13,1},{2,14},{6,10},... | collective-permute-start | bytes 688136 | tf_op jit(solution)/shard_map/ppermute | solution.py:34
  22.0 11.6 %collective-permute-start.7 = (bf16[2,2,64,896]{3,2,1,0:T(8,128)(2,1)S(1)}, bf16[2,2,64,896]{3,2,1,0:T(8,128)(2,1)S(1)}, u32[]{:S(2)}, u32[]{:S(2)}) collective-permute-start(bf16[2,2,64,896]{3,2,1,0:T(8,128)(2,1)S(1)} %join_columns.1.refs_1_), channel_id=1, source_target_pairs={{0,1},{1,0},{2,3},{3,2},{4,5},{5,4},{6,7},{7,6},{8,9},{9,8},{10,11... | collective-permute-start | bytes 1376264 | tf_op jit(solution)/shard_map/ppermute | solution.py:34
  31.6 1.9 %collective-permute-start.8 = (bf16[2,64,896]{2,1,0:T(8,128)(2,1)S(1)}, bf16[2,64,896]{2,1,0:T(8,128)(2,1)S(1)}, u32[]{:S(2)}, u32[]{:S(2)}) collective-permute-start(bf16[2,64,896]{2,1,0:T(8,128)(2,1)S(1)} %collective-permute-done.5.refs_2_), channel_id=1, source_target_pairs={{0,1},{1,0},{2,3},{3,2},{4,5},{5,4},{6,7},{7,6},{8,9},{9,8},{10,11... | collective-permute-start | bytes 688136 | tf_op jit(solution)/shard_map/ppermute | solution.py:34
  31.6 1.9 %collective-permute-start.9 = (bf16[2,64,896]{2,1,0:T(8,128)(2,1)S(1)}, bf16[2,64,896]{2,1,0:T(8,128)(2,1)S(1)}, u32[]{:S(2)}, u32[]{:S(2)}) collective-permute-start(bf16[2,64,896]{2,1,0:T(8,128)(2,1)S(1)} %collective-permute-done.6.refs_3_), channel_id=1, source_target_pairs={{0,1},{1,0},{2,3},{3,2},{4,5},{5,4},{6,7},{7,6},{8,9},{9,8},{10,11... | collective-permute-start | bytes 688136 | tf_op jit(solution)/shard_map/ppermute | solution.py:34
  42.2 6.8 %collective-permute-start.11 = (bf16[2,9,16,256]{3,2,1,0:T(8,128)(2,1)S(1)}, bf16[2,9,16,256]{3,2,1,0:T(8,128)(2,1)S(1)}, u32[]{:S(2)}, u32[]{:S(2)}) collective-permute-start(bf16[2,9,16,256]{3,2,1,0:T(8,128)(2,1)S(1)} %get-tuple-element.70), channel_id=1, source_target_pairs={{0,16},{16,0},{1,17},{17,1},{2,18},{18,2},{3,19},{19,3},{4,20},{20... | collective-permute-start | bytes 442376 | tf_op jit(solution)/shard_map/ppermute | solution.py:34
  44.3 7.7 %collective-permute-start.10 = (bf16[2,9,16,256]{3,2,1,0:T(8,128)(2,1)S(1)}, bf16[2,9,16,256]{3,2,1,0:T(8,128)(2,1)S(1)}, u32[]{:S(2)}, u32[]{:S(2)}) collective-permute-start(bf16[2,9,16,256]{3,2,1,0:T(8,128)(2,1)S(1)} %pool_near.1), channel_id=1, source_target_pairs={{0,16},{16,0},{1,17},{17,1},{2,18},{18,2},{3,19},{19,3},{4,20},{20... | collective-permute-start | bytes 442376 | tf_op jit(solution)/shard_map/ppermute | solution.py:34
  49.5 8.6 %collective-permute-start.13 = (bf16[9,16,256]{2,1,0:T(8,128)(2,1)S(1)}, bf16[9,16,256]{2,1,0:T(8,128)(2,1)S(1)}, u32[]{:S(2)}, u32[]{:S(2)}) collective-permute-start(bf16[9,16,256]{2,1,0:T(8,128)(2,1)S(1)} %get-tuple-element.71.refs_4_), channel_id=1, source_target_pairs={{0,8},{4,12},{8,0},{12,4},{1,9},{5,13},{9,1},{13,5},{2,10},{6,14},... | collective-permute-start | bytes 221192 | tf_op jit(solution)/shard_map/ppermute | solution.py:34
  52.7 5.5 %collective-permute-start.12 = (bf16[9,16,256]{2,1,0:T(8,128)(2,1)S(1)}, bf16[9,16,256]{2,1,0:T(8,128)(2,1)S(1)}, u32[]{:S(2)}, u32[]{:S(2)}) collective-permute-start(bf16[9,16,256]{2,1,0:T(8,128)(2,1)S(1)} %get-tuple-element.73), channel_id=1, source_target_pairs={{0,4},{4,0},{8,12},{12,8},{1,5},{5,1},{9,13},{13,9},{2,6},{6,2},{1... | collective-permute-start | bytes 221192 | tf_op jit(solution)/shard_map/ppermute | solution.py:34
  53.3 4.9 %collective-permute-start.14 = (bf16[9,16,256]{2,1,0:T(8,128)(2,1)S(1)}, bf16[9,16,256]{2,1,0:T(8,128)(2,1)S(1)}, u32[]{:S(2)}, u32[]{:S(2)}) collective-permute-start(bf16[9,16,256]{2,1,0:T(8,128)(2,1)S(1)} %get-tuple-element.74), channel_id=1, source_target_pairs={{0,12},{4,8},{8,4},{12,0},{1,13},{5,9},{9,5},{13,1},{2,14},{6,10},... | collective-permute-start | bytes 221192 | tf_op jit(solution)/shard_map/ppermute | solution.py:34
  58.2 8.6 %collective-permute-start.16 = (bf16[4,9,16,256]{3,2,1,0:T(8,128)(2,1)S(1)}, bf16[4,9,16,256]{3,2,1,0:T(8,128)(2,1)S(1)}, u32[]{:S(2)}, u32[]{:S(2)}) collective-permute-start(bf16[4,9,16,256]{3,2,1,0:T(8,128)(2,1)S(1)} %join_acts.1.refs_0_), channel_id=1, source_target_pairs={{0,2},{1,3},{2,0},{3,1},{4,6},{5,7},{6,4},{7,5},{8,10},{9,11},{10,... | collective-permute-start | bytes 884744 | tf_op jit(solution)/shard_map/ppermute | solution.py:34
  60.4 6.4 %collective-permute-start.15 = (bf16[4,9,16,256]{3,2,1,0:T(8,128)(2,1)S(1)}, bf16[4,9,16,256]{3,2,1,0:T(8,128)(2,1)S(1)}, u32[]{:S(2)}, u32[]{:S(2)}) collective-permute-start(bf16[4,9,16,256]{3,2,1,0:T(8,128)(2,1)S(1)} %join_acts.1.refs_0_), channel_id=1, source_target_pairs={{0,1},{1,0},{2,3},{3,2},{4,5},{5,4},{6,7},{7,6},{8,9},{9,8},{10,11... | collective-permute-start | bytes 884744 | tf_op jit(solution)/shard_map/ppermute | solution.py:34
  66.8 1.6 collective-permute-start.17
  68.4 17.9 %copy-start.2 = (f32[2,2,1024]{2,1,0:T(2,128)S(1)}, f32[2,2,1024]{2,1,0:T(2,128)}, u32[]{:S(2)}) copy-start(f32[2,2,1024]{2,1,0:T(2,128)} %refs_3_.3) | copy-start | bytes 49156
  68.4 17.9 %copy-start.3 = (f32[2,1024]{1,0:T(2,128)S(1)}, f32[2,1024]{1,0:T(2,128)}, u32[]{:S(2)}) copy-start(f32[2,1024]{1,0:T(2,128)} %refs_5_.1) | copy-start | bytes 24580
  69.8 8.0 %collective-permute-start.18 = (bf16[4,16,1024]{2,1,0:T(8,128)(2,1)S(1)}, bf16[4,16,1024]{2,1,0:T(8,128)(2,1)S(1)}, u32[]{:S(2)}, u32[]{:S(2)}) collective-permute-start(bf16[4,16,1024]{2,1,0:T(8,128)(2,1)S(1)} %get-tuple-element.78), channel_id=1, source_target_pairs={{0,4},{4,0},{8,12},{12,8},{1,5},{5,1},{9,13},{13,9},{2,6},{6,2},{1... | collective-permute-start | bytes 393224 | tf_op jit(solution)/shard_map/ppermute | solution.py:34
  72.7 10.2 %collective-permute-start.19 = (bf16[4,16,1024]{2,1,0:T(8,128)(2,1)S(1)}, bf16[4,16,1024]{2,1,0:T(8,128)(2,1)S(1)}, u32[]{:S(2)}, u32[]{:S(2)}) collective-permute-start(bf16[4,16,1024]{2,1,0:T(8,128)(2,1)S(1)} %get-tuple-element.79), channel_id=1, source_target_pairs={{0,8},{4,12},{8,0},{12,4},{1,9},{5,13},{9,1},{13,5},{2,10},{6,14},... | collective-permute-start | bytes 393224 | tf_op jit(solution)/shard_map/ppermute | solution.py:34
  73.4 12.9 %collective-permute-start.20 = (bf16[4,16,1024]{2,1,0:T(8,128)(2,1)S(1)}, bf16[4,16,1024]{2,1,0:T(8,128)(2,1)S(1)}, u32[]{:S(2)}, u32[]{:S(2)}) collective-permute-start(bf16[4,16,1024]{2,1,0:T(8,128)(2,1)S(1)} %get-tuple-element.80), channel_id=1, source_target_pairs={{0,12},{4,8},{8,4},{12,0},{1,13},{5,9},{9,5},{13,1},{2,14},{6,10},... | collective-permute-start | bytes 393224 | tf_op jit(solution)/shard_map/ppermute | solution.py:34
  87.1 6.2 %collective-permute-start.21 = (bf16[4,16,1024]{2,1,0:T(8,128)(2,1)S(1)}, bf16[4,16,1024]{2,1,0:T(8,128)(2,1)S(1)}, u32[]{:S(2)}, u32[]{:S(2)}) collective-permute-start(bf16[4,16,1024]{2,1,0:T(8,128)(2,1)S(1)} %get-tuple-element.83.refs_0_.refs_4_), channel_id=1, source_target_pairs={{0,4},{4,0},{8,12},{12,8},{1,5},{5,1},{9,13},{13,9},{2,6},{6,2},{1... | collective-permute-start | bytes 393224 | tf_op jit(solution)/shard_map/ppermute | solution.py:34
  87.2 8.0 %collective-permute-start.22 = (bf16[4,16,1024]{2,1,0:T(8,128)(2,1)S(1)}, bf16[4,16,1024]{2,1,0:T(8,128)(2,1)S(1)}, u32[]{:S(2)}, u32[]{:S(2)}) collective-permute-start(bf16[4,16,1024]{2,1,0:T(8,128)(2,1)S(1)} %get-tuple-element.83.refs_0_.refs_4_), channel_id=1, source_target_pairs={{0,8},{4,12},{8,0},{12,4},{1,9},{5,13},{9,1},{13,5},{2,10},{6,14},... | collective-permute-start | bytes 393224 | tf_op jit(solution)/shard_map/ppermute | solution.py:34
  96.9 2.2 %collective-permute-start.23 = (bf16[2,3,9,16,256]{4,3,2,1,0:T(8,128)(2,1)S(1)}, bf16[2,3,9,16,256]{4,3,2,1,0:T(8,128)(2,1)S(1)}, u32[]{:S(2)}, u32[]{:S(2)}) collective-permute-start(bf16[2,3,9,16,256]{4,3,2,1,0:T(8,128)(2,1)S(1)} %get-tuple-element.85), channel_id=1, source_target_pairs={{0,1},{1,0},{2,3},{3,2},{4,5},{5,4},{6,7},{7,6},{8,9},{9,8},{10,11... | collective-permute-start | bytes 1327112 | tf_op jit(solution)/shard_map/ppermute | solution.py:34
  97.0 6.2 %collective-permute-start.27 = (bf16[4,16,1024]{2,1,0:T(8,128)(2,1)S(1)}, bf16[4,16,1024]{2,1,0:T(8,128)(2,1)S(1)}, u32[]{:S(2)}, u32[]{:S(2)}) collective-permute-start(bf16[4,16,1024]{2,1,0:T(8,128)(2,1)S(1)} %collective-permute-done.22.refs_2_.refs_6_), channel_id=1, source_target_pairs={{0,4},{4,0},{8,12},{12,8},{1,5},{5,1},{9,13},{13,9},{2,6},{6,2},{1... | collective-permute-start | bytes 393224 | tf_op jit(solution)/shard_map/ppermute | solution.py:34
  99.2 7.6 %collective-permute-start.24 = (bf16[3,9,16,256]{3,2,1,0:T(8,128)(2,1)S(1)}, bf16[3,9,16,256]{3,2,1,0:T(8,128)(2,1)S(1)}, u32[]{:S(2)}, u32[]{:S(2)}) collective-permute-start(bf16[3,9,16,256]{3,2,1,0:T(8,128)(2,1)S(1)} %cross_near.1.refs_2_), channel_id=1, source_target_pairs={{0,2},{1,3},{2,0},{3,1},{4,6},{5,7},{6,4},{7,5},{8,10},{9,11},{10,... | collective-permute-start | bytes 663560 | tf_op jit(solution)/shard_map/ppermute | solution.py:34
  105.0 4.6 %collective-permute-start.28 = (bf16[2,1,9,16,256]{4,3,2,1,0:T(8,128)(2,1)S(1)}, bf16[2,1,9,16,256]{4,3,2,1,0:T(8,128)(2,1)S(1)}, u32[]{:S(2)}, u32[]{:S(2)}) collective-permute-start(bf16[2,1,9,16,256]{4,3,2,1,0:T(8,128)(2,1)S(1)} %get-tuple-element.91), channel_id=1, source_target_pairs={{0,1},{1,0},{2,3},{3,2},{4,5},{5,4},{6,7},{7,6},{8,9},{9,8},{10,11... | collective-permute-start | bytes 442376 | tf_op jit(solution)/shard_map/ppermute | solution.py:34
  106.9 7.1 %collective-permute-start.25 = (bf16[10,16,256]{2,1,0:T(8,128)(2,1)S(1)}, bf16[10,16,256]{2,1,0:T(8,128)(2,1)S(1)}, u32[]{:S(2)}, u32[]{:S(2)}) collective-permute-start(bf16[10,16,256]{2,1,0:T(8,128)(2,1)S(1)} %get-tuple-element.88), channel_id=1, source_target_pairs={{0,4},{4,0},{8,12},{12,8},{1,5},{5,1},{9,13},{13,9},{2,6},{6,2},{1... | collective-permute-start | bytes 245768 | tf_op jit(solution)/shard_map/ppermute | solution.py:34
  108.6 5.4 %collective-permute-start.26 = (bf16[10,16,256]{2,1,0:T(8,128)(2,1)S(1)}, bf16[10,16,256]{2,1,0:T(8,128)(2,1)S(1)}, u32[]{:S(2)}, u32[]{:S(2)}) collective-permute-start(bf16[10,16,256]{2,1,0:T(8,128)(2,1)S(1)} %get-tuple-element.89), channel_id=1, source_target_pairs={{0,8},{4,12},{8,0},{12,4},{1,9},{5,13},{9,1},{13,5},{2,10},{6,14},... | collective-permute-start | bytes 245768 | tf_op jit(solution)/shard_map/ppermute | solution.py:34
  109.6 4.4 %collective-permute-start.29 = (bf16[1,9,16,256]{3,2,1,0:T(8,128)(2,1)S(1)}, bf16[1,9,16,256]{3,2,1,0:T(8,128)(2,1)S(1)}, u32[]{:S(2)}, u32[]{:S(2)}) collective-permute-start(bf16[1,9,16,256]{3,2,1,0:T(8,128)(2,1)S(1)} %cross_far.1), channel_id=1, source_target_pairs={{0,2},{1,3},{2,0},{3,1},{4,6},{5,7},{6,4},{7,5},{8,10},{9,11},{10,... | collective-permute-start | bytes 221192 | tf_op jit(solution)/shard_map/ppermute | solution.py:34
  114.1 10.5 %collective-permute-start.31 = (bf16[3,10,16,256]{3,2,1,0:T(8,128)(2,1)S(1)}, bf16[3,10,16,256]{3,2,1,0:T(8,128)(2,1)S(1)}, u32[]{:S(2)}, u32[]{:S(2)}) collective-permute-start(bf16[3,10,16,256]{3,2,1,0:T(8,128)(2,1)S(1)} %join_near.1.refs_3_.refs_1_), channel_id=1, source_target_pairs={{0,16},{16,0},{1,17},{17,1},{2,18},{18,2},{3,19},{19,3},{4,20},{20... | collective-permute-start | bytes 737288 | tf_op jit(solution)/shard_map/ppermute | solution.py:34
  115.7 4.4 %collective-permute-start.30 = (bf16[10,16,256]{2,1,0:T(8,128)(2,1)S(1)}, bf16[10,16,256]{2,1,0:T(8,128)(2,1)S(1)}, u32[]{:S(2)}, u32[]{:S(2)}) collective-permute-start(bf16[10,16,256]{2,1,0:T(8,128)(2,1)S(1)} %home_far.1.refs_3_), channel_id=1, source_target_pairs={{0,12},{4,8},{8,4},{12,0},{1,13},{5,9},{9,5},{13,1},{2,14},{6,10},... | collective-permute-start | bytes 245768 | tf_op jit(solution)/shard_map/ppermute | solution.py:34
  120.1 4.4 %collective-permute-start.32 = (bf16[10,16,256]{2,1,0:T(8,128)(2,1)S(1)}, bf16[10,16,256]{2,1,0:T(8,128)(2,1)S(1)}, u32[]{:S(2)}, u32[]{:S(2)}) collective-permute-start(bf16[10,16,256]{2,1,0:T(8,128)(2,1)S(1)} %collective-permute-done.30.refs_2_), channel_id=1, source_target_pairs={{0,16},{16,0},{1,17},{17,1},{2,18},{18,2},{3,19},{19,3},{4,20},{20... | collective-permute-start | bytes 245768 | tf_op jit(solution)/shard_map/ppermute | solution.py:34
  137.8 2.5 %collective-permute-start.35 = (bf16[3520,128]{1,0:T(8,128)(2,1)S(1)}, bf16[3520,128]{1,0:T(8,128)(2,1)S(1)}, u32[]{:S(2)}, u32[]{:S(2)}) collective-permute-start(bf16[3520,128]{1,0:T(8,128)(2,1)S(1)} %get-tuple-element.98), channel_id=1, source_target_pairs={{0,1},{1,0},{2,3},{3,2},{4,5},{5,4},{6,7},{7,6},{8,9},{9,8},{10,11... | collective-permute-start | bytes 2703368 | tf_op jit(solution)/shard_map/ppermute | solution.py:34
  137.8 12.0 %collective-permute-start.33 = (bf16[368,384]{1,0:T(8,128)(2,1)S(1)}, bf16[368,384]{1,0:T(8,128)(2,1)S(1)}, u32[]{:S(2)}, u32[]{:S(2)}) collective-permute-start(bf16[368,384]{1,0:T(8,128)(2,1)S(1)} %get-tuple-element.93), channel_id=1, source_target_pairs={{0,2},{1,3},{2,0},{3,1},{4,6},{5,7},{6,4},{7,5},{8,10},{9,11},{10,... | collective-permute-start | bytes 847880 | tf_op jit(solution)/shard_map/ppermute | solution.py:34
  138.2 15.9 %collective-permute-start.34 = (bf16[368,384]{1,0:T(8,128)(2,1)S(1)}, bf16[368,384]{1,0:T(8,128)(2,1)S(1)}, u32[]{:S(2)}, u32[]{:S(2)}) collective-permute-start(bf16[368,384]{1,0:T(8,128)(2,1)S(1)} %get-tuple-element.94), channel_id=1, source_target_pairs={{0,3},{1,2},{2,1},{3,0},{4,7},{5,6},{6,5},{7,4},{8,11},{9,10},{10,... | collective-permute-start | bytes 847880 | tf_op jit(solution)/shard_map/ppermute | solution.py:34
  139.7 27.2 %collective-permute-start.40 = (bf16[368,384]{1,0:T(8,128)(2,1)S(1)}, bf16[368,384]{1,0:T(8,128)(2,1)S(1)}, u32[]{:S(2)}, u32[]{:S(2)}) collective-permute-start(bf16[368,384]{1,0:T(8,128)(2,1)S(1)} %get-tuple-element.104), channel_id=1, source_target_pairs={{0,1},{1,0},{2,3},{3,2},{4,5},{5,4},{6,7},{7,6},{8,9},{9,8},{10,11... | collective-permute-start | bytes 847880 | tf_op jit(solution)/shard_map/ppermute | solution.py:34
  140.5 14.9 %collective-permute-start.41 = (bf16[880,128]{1,0:T(8,128)(2,1)S(1)}, bf16[880,128]{1,0:T(8,128)(2,1)S(1)}, u32[]{:S(2)}, u32[]{:S(2)}) collective-permute-start(bf16[880,128]{1,0:T(8,128)(2,1)S(1)} %get-tuple-element.105), channel_id=1, source_target_pairs={{0,4},{4,0},{8,12},{12,8},{1,5},{5,1},{9,13},{13,9},{2,6},{6,2},{1... | collective-permute-start | bytes 675848 | tf_op jit(solution)/shard_map/ppermute | solution.py:34
  144.1 16.1 %collective-permute-start.42 = (bf16[880,128]{1,0:T(8,128)(2,1)S(1)}, bf16[880,128]{1,0:T(8,128)(2,1)S(1)}, u32[]{:S(2)}, u32[]{:S(2)}) collective-permute-start(bf16[880,128]{1,0:T(8,128)(2,1)S(1)} %get-tuple-element.106), channel_id=1, source_target_pairs={{0,8},{4,12},{8,0},{12,4},{1,9},{5,13},{9,1},{13,5},{2,10},{6,14},... | collective-permute-start | bytes 675848 | tf_op jit(solution)/shard_map/ppermute | solution.py:34
  149.9 15.8 %collective-permute-start.43 = (bf16[880,128]{1,0:T(8,128)(2,1)S(1)}, bf16[880,128]{1,0:T(8,128)(2,1)S(1)}, u32[]{:S(2)}, u32[]{:S(2)}) collective-permute-start(bf16[880,128]{1,0:T(8,128)(2,1)S(1)} %last_kernels.1), channel_id=1, source_target_pairs={{0,12},{4,8},{8,4},{12,0},{1,13},{5,9},{9,5},{13,1},{2,14},{6,10},... | collective-permute-start | bytes 675848 | tf_op jit(solution)/shard_map/ppermute | solution.py:34
  155.1 18.3 %collective-permute-start.37 = (bf16[320,384]{1,0:T(8,128)(2,1)S(1)}, bf16[320,384]{1,0:T(8,128)(2,1)S(1)}, u32[]{:S(2)}, u32[]{:S(2)}) collective-permute-start(bf16[320,384]{1,0:T(8,128)(2,1)S(1)} %get-tuple-element.101), channel_id=1, source_target_pairs={{0,2},{1,3},{2,0},{3,1},{4,6},{5,7},{6,4},{7,5},{8,10},{9,11},{10,... | collective-permute-start | bytes 737288 | tf_op jit(solution)/shard_map/ppermute | solution.py:34
  155.5 16.4 %collective-permute-start.39 = (bf16[320,384]{1,0:T(8,128)(2,1)S(1)}, bf16[320,384]{1,0:T(8,128)(2,1)S(1)}, u32[]{:S(2)}, u32[]{:S(2)}) collective-permute-start(bf16[320,384]{1,0:T(8,128)(2,1)S(1)} %get-tuple-element.103), channel_id=1, source_target_pairs={{0,1},{1,0},{2,3},{3,2},{4,5},{5,4},{6,7},{7,6},{8,9},{9,8},{10,11... | collective-permute-start | bytes 737288 | tf_op jit(solution)/shard_map/ppermute | solution.py:34
  160.2 13.3 %collective-permute-start.38 = (bf16[320,384]{1,0:T(8,128)(2,1)S(1)}, bf16[320,384]{1,0:T(8,128)(2,1)S(1)}, u32[]{:S(2)}, u32[]{:S(2)}) collective-permute-start(bf16[320,384]{1,0:T(8,128)(2,1)S(1)} %get-tuple-element.102), channel_id=1, source_target_pairs={{0,3},{1,2},{2,1},{3,0},{4,7},{5,6},{6,5},{7,4},{8,11},{9,10},{10,... | collective-permute-start | bytes 737288 | tf_op jit(solution)/shard_map/ppermute | solution.py:34
  165.7 5.0 %collective-permute-start.36 = (bf16[4,16,1024]{2,1,0:T(8,128)(2,1)S(1)}, bf16[4,16,1024]{2,1,0:T(8,128)(2,1)S(1)}, u32[]{:S(2)}, u32[]{:S(2)}) collective-permute-start(bf16[4,16,1024]{2,1,0:T(8,128)(2,1)S(1)} %outputs_send.1), channel_id=1, source_target_pairs={{0,16},{16,0},{1,17},{17,1},{2,18},{18,2},{3,19},{19,3},{4,20},{20... | collective-permute-start | bytes 393224 | tf_op jit(solution)/shard_map/ppermute | solution.py:34
  166.9 8.1 %collective-permute-start.44 = (bf16[64,896]{1,0:T(8,128)(2,1)S(1)}, bf16[64,896]{1,0:T(8,128)(2,1)S(1)}, u32[]{:S(2)}, u32[]{:S(2)}) collective-permute-start(bf16[64,896]{1,0:T(8,128)(2,1)S(1)} %get-tuple-element.110), channel_id=1, source_target_pairs={{0,2},{1,3},{2,0},{3,1},{4,6},{5,7},{6,4},{7,5},{8,10},{9,11},{10,... | collective-permute-start | bytes 344072 | tf_op jit(solution)/shard_map/ppermute | solution.py:34
  171.9 4.4 %copy-start.1 = (bf16[4,64,2,1024]{3,2,1,0:T(2,128)(2,1)S(1)}, bf16[4,64,2,1024]{3,2,1,0:T(2,128)(2,1)}, u32[]{:S(2)}) copy-start(bf16[4,64,2,1024]{3,2,1,0:T(2,128)(2,1)} %param.17) | copy-start | bytes 3145732

commit v5 on v4

--- a/solution.py
+++ b/solution.py
@@ -382,7 +382,8 @@
             struct((2, *own.shape), BF16),
             (token,),
         )
-        column = [near] + [swap(near, "dp", k) for k in (1, 2, 3)]
+        column = {k: swap(near, "dp", k) for k in (3, 2, 1)}
+        column = [near, column[1], column[2], column[3]]
         first = call(join_kernel, "join_columns", column[:2], struct((2, *near.shape), BF16))
         column = [first, *column[2:]]
         across = [swap(part, "mp", 1) for part in column]
@@ -614,7 +615,7 @@
 
 
 def all_acts(acts, place):
-    return jnp.concatenate([a[:, place].reshape(4 * IMG, OUT) for a in acts], 0)
+    return jnp.concatenate([a[:, place].reshape(-1, OUT) for a in acts], 0)
 
 
 def all_grads(grads):
@@ -649,8 +650,9 @@
     return matrix, (token,)
 
 
-def fc_forward_kernel(a0, a1, a2, a3, weight, own, *sends):
-    rows = jnp.concatenate([all_acts((a0, a1, a2, a3), p) for p in range(9)], 1)
+def fc_forward_kernel(*refs):
+    acts, (weight, own, *sends) = refs[:8], refs[8:]
+    rows = jnp.concatenate([all_acts(acts, p) for p in range(9)], 1)
     for n in range(weight.shape[1] // 256):
         here = slice(n * 256, (n + 1) * 256)
         term = jnp.dot(rows, weight[:, here], preferred_element_type=F32)
@@ -718,7 +720,9 @@
         chunks[k][9] = small
 
 
-def fc_matrix_kernel(a0, a1, a2, a3, g0, g1, g2, g3, out, bias, token, part, sent):
+def fc_matrix_kernel(*refs):
+    acts, refs = refs[:8], refs[8:]
+    g0, g1, g2, g3, out, bias, token, part, sent = refs
     token[...] = jnp.zeros(token.shape, F32)
     grads = all_grads((g0, g1, g2, g3))
 
@@ -726,7 +730,7 @@
         return pltpu.make_async_copy(part.at[p % 3], out.at[pl.ds(p * 256, 256)], sent.at[p % 3])
 
     for p in range(9):
-        rows = all_acts((a0, a1, a2, a3), p).T
+        rows = all_acts(acts, p).T
         if p >= 3:
             copy(p - 3).wait()
         part[p % 3] = jnp.dot(rows, grads, preferred_element_type=F32)
@@ -769,9 +773,9 @@
         out[pl.ds(1 - s, 1), here] = other[pl.ds(4 * s + n, 1), :]
 
 
-def fc_section(pooled, near, far, params, weight, bias, stitch, cot, sel, s, d, m):
+def fc_section(pooled, near, far, params, own_weight, bias, stitch, cot, sel, s, d, m):
     count = lax.axis_size("dp")
-    hid = weight.shape[2]
+    hid = own_weight.shape[1]
     plane = struct((9, IMG, OUT), BF16)
     block = struct((4, IMG, hid), BF16)
     token = struct((8, 128), F32)
@@ -782,12 +786,17 @@
     chunks[:2] = call(
         partial(stitch_kernel, 0), "stitch_near", [sel, pooled, near, params], [plane] * 2, chunks[2:3]
     )
-    own_weight, after = load_matrix(weight, sel, s, chunks[:1])
     if count == 4:
-        moved = [chunks[0]] + [swap(chunks[k], "dp", k) for k in (1, 2, 3)]
-        own_acts = call(join_kernel, "join_acts", moved, struct((4, 9, IMG, OUT), BF16), after)
-        far_acts = swap(own_acts, "mp", 2)
-        acts = [own_acts, swap(own_acts, "mp", 1), far_acts, swap(far_acts, "mp", 1)]
+        def over_mp(acts):
+            far = swap(acts, "mp", 2)
+            return [acts, swap(acts, "mp", 1), far, swap(far, "mp", 1)]
+
+        two = struct((2, 9, IMG, OUT), BF16)
+        moved = [swap(chunks[2], "dp", 2), swap(chunks[3], "dp", 3)]
+        far_acts = call(join_kernel, "join_acts_far", moved, two)
+        moved = [chunks[0], swap(chunks[1], "dp", 1)]
+        near_acts = call(join_kernel, "join_acts_near", moved, two, (far_acts,))
+        acts = [a for pair in zip(over_mp(near_acts), over_mp(far_acts)) for a in pair]
         pre, *sends = call(
             fc_forward_kernel,
             "fc_forward",
@@ -919,7 +928,8 @@
     far3, far2, token = pack_maps(by_row, sel, 3)
     kernel, params, early = gather_kernels(conv_weight, conv_bias, conv_stitch, sel, s, m, token)
     cot = lax.dynamic_slice_in_dim(cotangent, d * IMG, IMG, 1).transpose(2, 0, 1, 3)
-    near1, near0, token = pack_maps(by_row, sel, 1, (token, early, cot))
+    matrix, loaded = load_matrix(fc_weight, sel, s, (token,))
+    near1, near0, token = pack_maps(by_row, sel, 1, (token, early, cot, *loaded))
     wires = [near0, swap(near1, "mp", 1), swap(far2, "mp", 2), swap(far3, "mp", 3)]
 
     taps = kernel.reshape(3, 3, 4 * BLK, OUT)
@@ -940,7 +950,7 @@
     near = swap(near, "section", 1)
 
     back, outputs, matrix_gradient, fc_stitch_sum = fc_section(
-        pooled, near, far, params, fc_weight, fc_bias, fc_stitch, cot, sel, s, d, m
+        pooled, near, far, params, matrix, fc_bias, fc_stitch, cot, sel, s, d, m
     )
     slope = call(
         slope_kernel,

time: 176 us -> 176 us (level)
  local copies, waits for them, and re-layouts: 0.26 us -> 2.45 us
    unnamed x9 -> x15, local copies, waits for them, and re-layouts: 0.07 us -> 2.27 us
    ppermute x45 -> x48, starting transfers between devices: 42.4 us -> 40.7 us  [swap(): return lax.ppermute(value, axis, [(i, i ^ bit) for i in range(count)])]
    ppermute x45 -> x48, waiting for transfers between devices: 68.3 us -> 67.4 us  [swap(): return lax.ppermute(value, axis, [(i, i ^ bit) for i in range(count)])]
    pallas_call x33 -> x34, Pallas kernels: 32.9 us -> 32.7 us  [call(): pl.pallas_call(kernel, in_specs=specs + [VMEM] * len(after), out_specs=ou...]
  transfers between devices with their start and end apart: 45 -> 48, of which waited for: 21 -> 23; matrix products, arithmetic and copies ran while one was open for 2% -> 2% of each run, Pallas kernels for 18% -> 18%
where the time goes in v5:
time: 176 us
  waiting for transfers between devices  67.4 us (38%)
  Pallas kernels  44.6 us (25%)
  starting transfers between devices  40.7 us (23%)
  matrix products  18.6 us (11%)
  local copies, waits for them, and re-layouts  2.45 us (1%)
    ppermute x48, waiting for transfers between devices, swap(): return lax.ppermute(value, axis, [(i, i ^ bit) for i in range(count)])  67.4 us
    ppermute x48, starting transfers between devices, swap(): return lax.ppermute(value, axis, [(i, i ^ bit) for i in range(count)])  40.7 us
    pallas_call x34, Pallas kernels, call(): pl.pallas_call(kernel, in_specs=specs + [VMEM] * len(after), out_specs=ou...  32.7 us
    conv_general_dilated x4, matrix products, conv(): lax.conv_general_dilated(maps, taps, (1, 1), (rows, (1, 1)), dimension_nu...  18.6 us
    pallas_call x2, Pallas kernels, pack_maps(): pl.pallas_call(partial(pack_kernel, len(after)), grid_spec=pltpu.Prefetch...  6.99 us
    pallas_call x3, Pallas kernels, place_grad(): pl.pallas_call(partial(place_grad_kernel, chunk, ks), in_specs=in_specs,...  4.89 us
  transfers between devices with their start and end apart: 48, of which 23 were waited for; matrix products, arithmetic and copies ran while one was open for 2% of the time, Pallas kernels for 18%

profile of v5, /device:TPU:8, one launch (start us, length us, event | category | flops | bytes accessed | tf_op | source)
XLA Modules:
  0.0 175.7 jit_solution(4740446748704725837)
XLA Ops:
  1.5 1.6 own_kernels.1.refs_0_
  3.0 1.6 collective-permute-start
  4.6 3.6 %pack_maps.2 = (bf16[688,384]{1,0:T(8,128)(2,1)S(1)}, bf16[688,384]{1,0:T(8,128)(2,1)}, f32[8,128]{1,0:T(8,128)S(1)}) custom-call(s32[7]{0:T(128)S(1)} %pad_add_fusion.sel.refs_0_, bf16[4,5408,96]{2,1,0:T(8,128)(2,1)} %bitcast.54), custom_call_target="tpu_custom_call" | custom-call | flops 1 | bytes 1 | tf_op jit(solution)/shard_map/pack_maps/pallas_call | solution.py:206
  8.8 3.0 %collective-permute-start.5 = (bf16[2,64,896]{2,1,0:T(8,128)(2,1)S(1)}, bf16[2,64,896]{2,1,0:T(8,128)(2,1)S(1)}, u32[]{:S(2)}, u32[]{:S(2)}) collective-permute-start(bf16[2,64,896]{2,1,0:T(8,128)(2,1)S(1)} %join_kernels.1.refs_1_.refs_0_), channel_id=1, source_target_pairs={{0,8},{4,12},{8,0},{12,4},{1,9},{5,13},{9,1},{13,5},{2,10},{6,14},... | collective-permute-start | bytes 688136 | tf_op jit(solution)/shard_map/ppermute | solution.py:34
  11.9 2.9 %load_matrix.1 = (bf16[2304,1024]{1,0:T(8,128)(2,1)S(1)}, f32[8,128]{1,0:T(8,128)S(1)}) custom-call(s32[7]{0:T(128)S(1)} %pad_add_fusion.sel.refs_0_, bf16[2,2304,1024]{2,1,0:T(8,128)(2,1)} %refs_1_.1, f32[8,128]{1,0:T(8,128)S(1)} %get-tuple-element.62.refs_2_.refs_0_), custom_call_target="tpu_custom_call" | custom-call | flops 1 | bytes 1 | tf_op jit(solution)/shard_map/load_matrix/pallas_call | solution.py:84
  14.8 2.2 %copy-done.2 = bf16[2304,1024]{1,0:T(8,128)(2,1)} copy-done((bf16[2304,1024]{1,0:T(8,128)(2,1)}, bf16[2304,1024]{1,0:T(8,128)(2,1)S(1)}, u32[]{:S(2)}) %copy-start.2) | copy-done | bytes 4718616
  17.2 3.4 %pack_maps.3 = (bf16[688,384]{1,0:T(8,128)(2,1)S(1)}, bf16[688,384]{1,0:T(8,128)(2,1)S(1)}, f32[8,128]{1,0:T(8,128)}) custom-call(s32[7]{0:T(128)S(1)} %pad_add_fusion.sel.refs_0_, bf16[4,5408,96]{2,1,0:T(8,128)(2,1)} %bitcast.55, f32[8,128]{1,0:T(8,128)S(1)} %get-tuple-element.62.refs_2_.refs_0_, bf16[2,64,896]{2,1,0:T(8,128)(2,1)S(1)} %join_kernels.1.refs_1_.refs_0_, ...), custom_call_target="tpu_custom_call" | custom-call | flops 1 | bytes 1 | tf_op jit(solution)/shard_map/pack_maps/pallas_call | solution.py:206
  20.6 1.6 collective-permute-start.1
  22.8 11.8 %collective-permute-done.6.refs_3_ = bf16[2,64,896]{2,1,0:T(8,128)(2,1)S(1)} collective-permute-done((bf16[2,64,896]{2,1,0:T(8,128)(2,1)S(1)}, bf16[2,64,896]{2,1,0:T(8,128)(2,1)S(1)}, u32[]{:S(2)}, u32[]{:S(2)}) %collective-permute-start.6) | collective-permute-done | bytes 229408 | tf_op jit(solution)/shard_map/ppermute | solution.py:34
  35.2 1.4 unpack_maps.1
  36.7 1.4 kernels.1
  38.0 5.6 %fusion.refs_1_ = f32[13,13,16,256]{3,2,1,0:T(8,128)S(1)} fusion(bf16[13,13,16,384]{3,2,1,0:T(8,128)(2,1)S(1)} %bitcast.40, bf16[3,3,384,256]{3,2,1,0:T(8,128)(2,1)S(1)} %bitcast.47), kind=kOutput, calls=%fused_computation.5 | convolution fusion | flops 4306501632 | bytes 6615040 | tf_op jit(solution)/shard_map/conv_general_dilated | solution.py:899
  43.7 1.6 pool.1
  45.3 1.6 collective-permute-start.11
  48.0 4.0 %collective-permute-done.11.refs_2_.refs_8_ = bf16[2,9,16,256]{3,2,1,0:T(8,128)(2,1)S(1)} collective-permute-done((bf16[2,9,16,256]{3,2,1,0:T(8,128)(2,1)S(1)}, bf16[2,9,16,256]{3,2,1,0:T(8,128)(2,1)S(1)}, u32[]{:S(2)}, u32[]{:S(2)}) %collective-permute-start.11) | collective-permute-done | bytes 147488 | tf_op jit(solution)/shard_map/ppermute | solution.py:34
  53.3 1.0 collective-permute-done.10.refs_2_.refs_7_
  54.9 2.9 %collective-permute-start.12 = (bf16[9,16,256]{2,1,0:T(8,128)(2,1)S(1)}, bf16[9,16,256]{2,1,0:T(8,128)(2,1)S(1)}, u32[]{:S(2)}, u32[]{:S(2)}) collective-permute-start(bf16[9,16,256]{2,1,0:T(8,128)(2,1)S(1)} %get-tuple-element.74), channel_id=1, source_target_pairs={{0,4},{4,0},{8,12},{12,8},{1,5},{5,1},{9,13},{13,9},{2,6},{6,2},{1... | collective-permute-start | bytes 221192 | tf_op jit(solution)/shard_map/ppermute | solution.py:34
  58.2 1.8 %collective-permute-done.14.refs_1_ = bf16[9,16,256]{2,1,0:T(8,128)(2,1)S(1)} collective-permute-done((bf16[9,16,256]{2,1,0:T(8,128)(2,1)S(1)}, bf16[9,16,256]{2,1,0:T(8,128)(2,1)S(1)}, u32[]{:S(2)}, u32[]{:S(2)}) %collective-permute-start.14) | collective-permute-done | bytes 73760 | tf_op jit(solution)/shard_map/ppermute | solution.py:34
  60.8 1.5 collective-permute-start.18
  62.8 2.9 %collective-permute-done.17.refs_4_ = bf16[2,9,16,256]{3,2,1,0:T(8,128)(2,1)S(1)} collective-permute-done((bf16[2,9,16,256]{3,2,1,0:T(8,128)(2,1)S(1)}, bf16[2,9,16,256]{3,2,1,0:T(8,128)(2,1)S(1)}, u32[]{:S(2)}, u32[]{:S(2)}) %collective-permute-start.17) | collective-permute-done | bytes 147488 | tf_op jit(solution)/shard_map/ppermute | solution.py:34
  65.7 1.6 collective-permute-done.18.refs_5_
  67.3 1.3 collective-permute-done.20.refs_7_
  68.7 1.4 fc_forward.1
  70.1 1.7 collective-permute-start.21
  71.8 1.4 collective-permute-start.22
  73.7 3.4 %collective-permute-done.21.refs_2_ = bf16[4,16,1024]{2,1,0:T(8,128)(2,1)S(1)} collective-permute-done((bf16[4,16,1024]{2,1,0:T(8,128)(2,1)S(1)}, bf16[4,16,1024]{2,1,0:T(8,128)(2,1)S(1)}, u32[]{:S(2)}, u32[]{:S(2)}) %collective-permute-start.21) | collective-permute-done | bytes 131104 | tf_op jit(solution)/shard_map/ppermute | solution.py:34
  77.1 5.4 %collective-permute-done.22.refs_3_ = bf16[4,16,1024]{2,1,0:T(8,128)(2,1)S(1)} collective-permute-done((bf16[4,16,1024]{2,1,0:T(8,128)(2,1)S(1)}, bf16[4,16,1024]{2,1,0:T(8,128)(2,1)S(1)}, u32[]{:S(2)}, u32[]{:S(2)}) %collective-permute-start.22) | collective-permute-done | bytes 131104 | tf_op jit(solution)/shard_map/ppermute | solution.py:34
  82.6 2.8 %collective-permute-done.23.refs_4_ = bf16[4,16,1024]{2,1,0:T(8,128)(2,1)S(1)} collective-permute-done((bf16[4,16,1024]{2,1,0:T(8,128)(2,1)S(1)}, bf16[4,16,1024]{2,1,0:T(8,128)(2,1)S(1)}, u32[]{:S(2)}, u32[]{:S(2)}) %collective-permute-start.23) | collective-permute-done | bytes 131104 | tf_op jit(solution)/shard_map/ppermute | solution.py:34
  85.4 0.9 fc_active.1
  86.4 3.0 %collective-permute-start.25 = (bf16[4,16,1024]{2,1,0:T(8,128)(2,1)S(1)}, bf16[4,16,1024]{2,1,0:T(8,128)(2,1)S(1)}, u32[]{:S(2)}, u32[]{:S(2)}) collective-permute-start(bf16[4,16,1024]{2,1,0:T(8,128)(2,1)S(1)} %get-tuple-element.83.refs_0_.refs_8_), channel_id=1, source_target_pairs={{0,8},{4,12},{8,0},{12,4},{1,9},{5,13},{9,1},{13,5},{2,10},{6,14},... | collective-permute-start | bytes 393224 | tf_op jit(solution)/shard_map/ppermute | solution.py:34
  89.3 2.8 %collective-permute-done.24.refs_1_.refs_9_ = bf16[4,16,1024]{2,1,0:T(8,128)(2,1)S(1)} collective-permute-done((bf16[4,16,1024]{2,1,0:T(8,128)(2,1)S(1)}, bf16[4,16,1024]{2,1,0:T(8,128)(2,1)S(1)}, u32[]{:S(2)}, u32[]{:S(2)}) %collective-permute-start.24) | collective-permute-done | bytes 131104 | tf_op jit(solution)/shard_map/ppermute | solution.py:34
  92.2 2.5 %collective-permute-done.25.refs_2_.refs_10_ = bf16[4,16,1024]{2,1,0:T(8,128)(2,1)S(1)} collective-permute-done((bf16[4,16,1024]{2,1,0:T(8,128)(2,1)S(1)}, bf16[4,16,1024]{2,1,0:T(8,128)(2,1)S(1)}, u32[]{:S(2)}, u32[]{:S(2)}) %collective-permute-start.25) | collective-permute-done | bytes 131104 | tf_op jit(solution)/shard_map/ppermute | solution.py:34
  94.7 1.7 fc_rows_near.1
  96.5 1.7 collective-permute-start.30
  98.7 3.6 %collective-permute-done.30.refs_0_.refs_11_ = bf16[4,16,1024]{2,1,0:T(8,128)(2,1)S(1)} collective-permute-done((bf16[4,16,1024]{2,1,0:T(8,128)(2,1)S(1)}, bf16[4,16,1024]{2,1,0:T(8,128)(2,1)S(1)}, u32[]{:S(2)}, u32[]{:S(2)}) %collective-permute-start.30) | collective-permute-done | bytes 131104 | tf_op jit(solution)/shard_map/ppermute | solution.py:34
  102.4 1.5 fc_rows_far.1
  104.0 1.8 %collective-permute-done.27.refs_2_ = bf16[3,9,16,256]{3,2,1,0:T(8,128)(2,1)S(1)} collective-permute-done((bf16[3,9,16,256]{3,2,1,0:T(8,128)(2,1)S(1)}, bf16[3,9,16,256]{3,2,1,0:T(8,128)(2,1)S(1)}, u32[]{:S(2)}, u32[]{:S(2)}) %collective-permute-start.27) | collective-permute-done | bytes 221216 | tf_op jit(solution)/shard_map/ppermute | solution.py:34
  105.9 1.7 collective-permute-start.28
  107.7 1.3 collective-permute-start.29
  109.5 3.9 %collective-permute-done.32.refs_2_ = bf16[1,9,16,256]{3,2,1,0:T(8,128)(2,1)S(1)} collective-permute-done((bf16[1,9,16,256]{3,2,1,0:T(8,128)(2,1)S(1)}, bf16[1,9,16,256]{3,2,1,0:T(8,128)(2,1)S(1)}, u32[]{:S(2)}, u32[]{:S(2)}) %collective-permute-start.32) | collective-permute-done | bytes 73760 | tf_op jit(solution)/shard_map/ppermute | solution.py:34
  113.5 1.6 collective-permute-start.34
  115.1 1.0 collective-permute-start.33
  116.1 3.4 %collective-permute-done.33.refs_2_ = bf16[10,16,256]{2,1,0:T(8,128)(2,1)S(1)} collective-permute-done((bf16[10,16,256]{2,1,0:T(8,128)(2,1)S(1)}, bf16[10,16,256]{2,1,0:T(8,128)(2,1)S(1)}, u32[]{:S(2)}, u32[]{:S(2)}) %collective-permute-start.33) | collective-permute-done | bytes 81952 | tf_op jit(solution)/shard_map/ppermute | solution.py:34
  120.0 2.1 %slope.1.refs_5_ = f32[169,16,256]{2,1,0:T(8,128)S(1)} custom-call(s32[7]{0:T(128)S(1)} %pad_add_fusion.sel.refs_0_, f32[13,13,16,256]{3,2,1,0:T(8,128)S(1)} %fusion.refs_1_, f32[8,256]{1,0:T(8,128)S(1)} %get-tuple-element.69.refs_2_.refs_3_.refs_9_, bf16[3,10,16,256]{3,2,1,0:T(8,128)(2,1)S(1)} %join_near.1.refs_3_.refs_1_), custom_call_target="tpu_custom_call" | custom-call | flops 1 | bytes 1 | tf_op jit(solution)/shard_map/slope/pallas_call | solution.py:84
  122.1 1.9 %collective-permute-done.35.refs_4_ = bf16[10,16,256]{2,1,0:T(8,128)(2,1)S(1)} collective-permute-done((bf16[10,16,256]{2,1,0:T(8,128)(2,1)S(1)}, bf16[10,16,256]{2,1,0:T(8,128)(2,1)S(1)}, u32[]{:S(2)}, u32[]{:S(2)}) %collective-permute-start.35) | collective-permute-done | bytes 81952 | tf_op jit(solution)/shard_map/ppermute | solution.py:34
  124.0 1.2 conv_gradient.1
  125.2 3.8 %convolution_convert_fusion = bf16[7,13,16,384]{3,2,1,0:T(8,128)(2,1)S(1)} fusion(bf16[13,13,16,256]{3,2,1,0:T(8,128)(2,1)S(1)} %bitcast.50, bf16[3,3,384,256]{3,2,1,0:T(8,128)(2,1)S(1)} %bitcast.48), kind=kOutput, calls=%fused_computation | convolution fusion | flops 2328397824 | bytes 4272128 | tf_op jit(solution)/shard_map/conv_general_dilated | solution.py:899
  128.9 1.0 pack_grad.2
  130.0 6.1 %fusion.1 = f32[3,3,384,256]{3,2,1,0:T(8,128)S(1)} fusion(bf16[13,13,16,384]{3,2,1,0:T(8,128)(2,1)S(1)} %pass_on.1, bf16[13,13,16,256]{3,2,1,0:T(8,128)(2,1)S(1)} %bitcast.51), kind=kOutput, calls=%fused_computation.6 | convolution fusion | flops 4306501632 | bytes 7000064 | tf_op jit(solution)/shard_map/conv_general_dilated | solution.py:899
  136.1 1.1 split_kernels.1
  137.8 1.3 collective-permute-start.37
  140.0 3.5 %collective-permute-start.44 = (bf16[880,128]{1,0:T(8,128)(2,1)S(1)}, bf16[880,128]{1,0:T(8,128)(2,1)S(1)}, u32[]{:S(2)}, u32[]{:S(2)}) collective-permute-start(bf16[880,128]{1,0:T(8,128)(2,1)S(1)} %get-tuple-element.105), channel_id=1, source_target_pairs={{0,4},{4,0},{8,12},{12,8},{1,5},{5,1},{9,13},{13,9},{2,6},{6,2},{1... | collective-permute-start | bytes 675848 | tf_op jit(solution)/shard_map/ppermute | solution.py:34
  143.5 5.2 %fc_matrix.1 = (f32[2304,1024]{1,0:T(8,128)}, f32[1,1024]{1,0:T(1,128)}, f32[8,128]{1,0:T(8,128)S(1)}) custom-call(bf16[2,9,16,256]{3,2,1,0:T(8,128)(2,1)S(1)} %join_acts_near.1.refs_0_, bf16[2,9,16,256]{3,2,1,0:T(8,128)(2,1)S(1)} %join_acts_far.1.refs_2_.refs_1_, bf16[2,9,16,256]{3,2,1,0:T(8,128)(2,1)S(1)} %collective-permute-done.15.refs_2_, ...), custom_call_target="tpu_custom_call" | custom-call | flops 1 | bytes 1 | tf_op jit(solution)/shard_map/fc_matrix/pallas_call | solution.py:84
  148.7 1.6 collective-permute-start.46
  150.3 3.2 %convolution_convert_fusion.1 = bf16[6,13,16,384]{3,2,1,0:T(8,128)(2,1)S(1)} fusion(bf16[13,13,16,256]{3,2,1,0:T(8,128)(2,1)S(1)} %bitcast.52, bf16[3,3,384,256]{3,2,1,0:T(8,128)(2,1)S(1)} %bitcast.49), kind=kOutput, calls=%fused_computation.1 | convolution fusion | flops 1979142144 | bytes 4112384 | tf_op jit(solution)/shard_map/conv_general_dilated | solution.py:899
  153.5 1.0 pack_grad.3
  155.1 3.2 %collective-permute-done.45.refs_3_ = bf16[880,128]{1,0:T(8,128)(2,1)S(1)} collective-permute-done((bf16[880,128]{1,0:T(8,128)(2,1)S(1)}, bf16[880,128]{1,0:T(8,128)(2,1)S(1)}, u32[]{:S(2)}, u32[]{:S(2)}) %collective-permute-start.45) | collective-permute-done | bytes 225312 | tf_op jit(solution)/shard_map/ppermute | solution.py:34
  158.3 6.8 %collective-permute-done.46.refs_4_ = bf16[880,128]{1,0:T(8,128)(2,1)S(1)} collective-permute-done((bf16[880,128]{1,0:T(8,128)(2,1)S(1)}, bf16[880,128]{1,0:T(8,128)(2,1)S(1)}, u32[]{:S(2)}, u32[]{:S(2)}) %collective-permute-start.46) | collective-permute-done | bytes 225312 | tf_op jit(solution)/shard_map/ppermute | solution.py:34
  166.9 1.2 stitch_sums.1
  168.1 1.8 %place_grad.3.refs_2_ = bf16[4,2704,96]{2,1,0:T(8,128)(2,1)} custom-call(s32[7]{0:T(128)S(1)} %pad_add_fusion.sel.refs_0_, bf16[368,384]{1,0:T(8,128)(2,1)S(1)} %get-tuple-element.95.refs_1_.refs_0_, bf16[368,384]{1,0:T(8,128)(2,1)S(1)} %collective-permute-done.43.refs_1_, bf16[368,384]{1,0:T(8,128)(2,1)S(1)} %collective-permute-done.36.refs_2_, ...), custom_call_target="tpu_custom_call" | custom-call | flops 1 | bytes 1 | tf_op jit(solution)/shard_map/place_grad/pallas_call | solution.py:285
  170.1 1.2 outputs.1
  171.3 1.5 place_grad.4.refs_2_
  172.9 1.5 place_grad.5
  174.4 1.3 finish_kernels.1
  (94 shorter events, 13.8 us)
Async XLA Ops:
  0.6 16.4 %copy-start = (bf16[4,64,2,1024]{3,2,1,0:T(2,128)(2,1)S(1)}, bf16[4,64,2,1024]{3,2,1,0:T(2,128)(2,1)}, u32[]{:S(2)}) copy-start(bf16[4,64,2,1024]{3,2,1,0:T(2,128)(2,1)} %param.17) | copy-start | bytes 3145732
  3.0 5.7 %collective-permute-start = (bf16[64,896]{1,0:T(8,128)(2,1)S(1)}, bf16[64,896]{1,0:T(8,128)(2,1)S(1)}, u32[]{:S(2)}, u32[]{:S(2)}) collective-permute-start(bf16[64,896]{1,0:T(8,128)(2,1)S(1)} %own_kernels.1.refs_0_), channel_id=1, source_target_pairs={{0,2},{1,3},{2,0},{3,1},{4,6},{5,7},{6,4},{7,5},{8,10},{9,11},{10,... | collective-permute-start | bytes 344072 | tf_op jit(solution)/shard_map/ppermute | solution.py:34
  8.2 26.5 %collective-permute-start.2 = (bf16[688,384]{1,0:T(8,128)(2,1)}, bf16[688,384]{1,0:T(8,128)(2,1)S(1)}, u32[]{:S(2)}, u32[]{:S(2)}) collective-permute-start(bf16[688,384]{1,0:T(8,128)(2,1)} %get-tuple-element.66), channel_id=1, source_target_pairs={{0,2},{1,3},{2,0},{3,1},{4,6},{5,7},{6,4},{7,5},{8,10},{9,11},{10,... | collective-permute-start | bytes 1585160 | tf_op jit(solution)/shard_map/ppermute | solution.py:34
  8.8 13.5 %collective-permute-start.4 = (bf16[2,64,896]{2,1,0:T(8,128)(2,1)S(1)}, bf16[2,64,896]{2,1,0:T(8,128)(2,1)S(1)}, u32[]{:S(2)}, u32[]{:S(2)}) collective-permute-start(bf16[2,64,896]{2,1,0:T(8,128)(2,1)S(1)} %join_kernels.1.refs_1_.refs_0_), channel_id=1, source_target_pairs={{0,4},{4,0},{8,12},{12,8},{1,5},{5,1},{9,13},{13,9},{2,6},{6,2},{1... | collective-permute-start | bytes 688136 | tf_op jit(solution)/shard_map/ppermute | solution.py:34
  8.8 13.9 %collective-permute-start.5 = (bf16[2,64,896]{2,1,0:T(8,128)(2,1)S(1)}, bf16[2,64,896]{2,1,0:T(8,128)(2,1)S(1)}, u32[]{:S(2)}, u32[]{:S(2)}) collective-permute-start(bf16[2,64,896]{2,1,0:T(8,128)(2,1)S(1)} %join_kernels.1.refs_1_.refs_0_), channel_id=1, source_target_pairs={{0,8},{4,12},{8,0},{12,4},{1,9},{5,13},{9,1},{13,5},{2,10},{6,14},... | collective-permute-start | bytes 688136 | tf_op jit(solution)/shard_map/ppermute | solution.py:34
  11.9 23.3 %collective-permute-start.3 = (bf16[688,384]{1,0:T(8,128)(2,1)S(1)}, bf16[688,384]{1,0:T(8,128)(2,1)S(1)}, u32[]{:S(2)}, u32[]{:S(2)}) collective-permute-start(bf16[688,384]{1,0:T(8,128)(2,1)S(1)} %get-tuple-element.67), channel_id=1, source_target_pairs={{0,3},{1,2},{2,1},{3,0},{4,7},{5,6},{6,5},{7,4},{8,11},{9,10},{10,... | collective-permute-start | bytes 1585160 | tf_op jit(solution)/shard_map/ppermute | solution.py:34
  14.8 2.2 %copy-start.2 = (bf16[2304,1024]{1,0:T(8,128)(2,1)}, bf16[2304,1024]{1,0:T(8,128)(2,1)S(1)}, u32[]{:S(2)}) copy-start(bf16[2304,1024]{1,0:T(8,128)(2,1)S(1)} %get-tuple-element.76.refs_8_.refs_3_.refs_1_) | copy-start | bytes 14155780
  20.6 14.6 %collective-permute-start.1 = (bf16[688,384]{1,0:T(8,128)(2,1)S(1)}, bf16[688,384]{1,0:T(8,128)(2,1)S(1)}, u32[]{:S(2)}, u32[]{:S(2)}) collective-permute-start(bf16[688,384]{1,0:T(8,128)(2,1)S(1)} %get-tuple-element.65), channel_id=1, source_target_pairs={{0,1},{1,0},{2,3},{3,2},{4,5},{5,4},{6,7},{7,6},{8,9},{9,8},{10,11... | collective-permute-start | bytes 1585160 | tf_op jit(solution)/shard_map/ppermute | solution.py:34
  22.2 12.4 %collective-permute-start.6 = (bf16[2,64,896]{2,1,0:T(8,128)(2,1)S(1)}, bf16[2,64,896]{2,1,0:T(8,128)(2,1)S(1)}, u32[]{:S(2)}, u32[]{:S(2)}) collective-permute-start(bf16[2,64,896]{2,1,0:T(8,128)(2,1)S(1)} %join_kernels.1.refs_1_.refs_0_), channel_id=1, source_target_pairs={{0,12},{4,8},{8,4},{12,0},{1,13},{5,9},{9,5},{13,1},{2,14},{6,10},... | collective-permute-start | bytes 688136 | tf_op jit(solution)/shard_map/ppermute | solution.py:34
  22.7 13.9 %collective-permute-start.7 = (bf16[2,2,64,896]{3,2,1,0:T(8,128)(2,1)S(1)}, bf16[2,2,64,896]{3,2,1,0:T(8,128)(2,1)S(1)}, u32[]{:S(2)}, u32[]{:S(2)}) collective-permute-start(bf16[2,2,64,896]{3,2,1,0:T(8,128)(2,1)S(1)} %join_columns.1.refs_1_), channel_id=1, source_target_pairs={{0,1},{1,0},{2,3},{3,2},{4,5},{5,4},{6,7},{7,6},{8,9},{9,8},{10,11... | collective-permute-start | bytes 1376264 | tf_op jit(solution)/shard_map/ppermute | solution.py:34
  34.7 2.0 %collective-permute-start.8 = (bf16[2,64,896]{2,1,0:T(8,128)(2,1)S(1)}, bf16[2,64,896]{2,1,0:T(8,128)(2,1)S(1)}, u32[]{:S(2)}, u32[]{:S(2)}) collective-permute-start(bf16[2,64,896]{2,1,0:T(8,128)(2,1)S(1)} %collective-permute-done.5.refs_2_), channel_id=1, source_target_pairs={{0,1},{1,0},{2,3},{3,2},{4,5},{5,4},{6,7},{7,6},{8,9},{9,8},{10,11... | collective-permute-start | bytes 688136 | tf_op jit(solution)/shard_map/ppermute | solution.py:34
  34.7 2.0 %collective-permute-start.9 = (bf16[2,64,896]{2,1,0:T(8,128)(2,1)S(1)}, bf16[2,64,896]{2,1,0:T(8,128)(2,1)S(1)}, u32[]{:S(2)}, u32[]{:S(2)}) collective-permute-start(bf16[2,64,896]{2,1,0:T(8,128)(2,1)S(1)} %collective-permute-done.6.refs_3_), channel_id=1, source_target_pairs={{0,1},{1,0},{2,3},{3,2},{4,5},{5,4},{6,7},{7,6},{8,9},{9,8},{10,11... | collective-permute-start | bytes 688136 | tf_op jit(solution)/shard_map/ppermute | solution.py:34
  38.0 30.7 %slice-start = ((s8[4718592]{0:T(1024)(128)(4,1)}), s8[4194304]{0:T(1024)(128)(4,1)S(1)}, s32[]{:S(2)}) async-start(s8[4718592]{0:T(1024)(128)(4,1)} %bitcast.38), calls=%async_computation | async-start | bytes 8388608
  38.0 30.7 %slice-start.1 = ((s8[4718592]{0:T(1024)(128)(4,1)}), s8[524288]{0:T(1024)(128)(4,1)S(1)}, s32[]{:S(2)}) async-start(s8[4718592]{0:T(1024)(128)(4,1)} %bitcast.38), calls=%async_computation.1 | async-start | bytes 1048576
  45.3 6.8 %collective-permute-start.11 = (bf16[2,9,16,256]{3,2,1,0:T(8,128)(2,1)S(1)}, bf16[2,9,16,256]{3,2,1,0:T(8,128)(2,1)S(1)}, u32[]{:S(2)}, u32[]{:S(2)}) collective-permute-start(bf16[2,9,16,256]{3,2,1,0:T(8,128)(2,1)S(1)} %get-tuple-element.71), channel_id=1, source_target_pairs={{0,16},{16,0},{1,17},{17,1},{2,18},{18,2},{3,19},{19,3},{4,20},{20... | collective-permute-start | bytes 442376 | tf_op jit(solution)/shard_map/ppermute | solution.py:34
  47.4 6.8 %collective-permute-start.10 = (bf16[2,9,16,256]{3,2,1,0:T(8,128)(2,1)S(1)}, bf16[2,9,16,256]{3,2,1,0:T(8,128)(2,1)S(1)}, u32[]{:S(2)}, u32[]{:S(2)}) collective-permute-start(bf16[2,9,16,256]{3,2,1,0:T(8,128)(2,1)S(1)} %pool_near.1), channel_id=1, source_target_pairs={{0,16},{16,0},{1,17},{17,1},{2,18},{18,2},{3,19},{19,3},{4,20},{20... | collective-permute-start | bytes 442376 | tf_op jit(solution)/shard_map/ppermute | solution.py:34
  52.7 5.5 %collective-permute-start.13 = (bf16[9,16,256]{2,1,0:T(8,128)(2,1)S(1)}, bf16[9,16,256]{2,1,0:T(8,128)(2,1)S(1)}, u32[]{:S(2)}, u32[]{:S(2)}) collective-permute-start(bf16[9,16,256]{2,1,0:T(8,128)(2,1)S(1)} %get-tuple-element.72.refs_4_), channel_id=1, source_target_pairs={{0,8},{4,12},{8,0},{12,4},{1,9},{5,13},{9,1},{13,5},{2,10},{6,14},... | collective-permute-start | bytes 221192 | tf_op jit(solution)/shard_map/ppermute | solution.py:34
  52.7 7.2 %collective-permute-start.14 = (bf16[9,16,256]{2,1,0:T(8,128)(2,1)S(1)}, bf16[9,16,256]{2,1,0:T(8,128)(2,1)S(1)}, u32[]{:S(2)}, u32[]{:S(2)}) collective-permute-start(bf16[9,16,256]{2,1,0:T(8,128)(2,1)S(1)} %get-tuple-element.75), channel_id=1, source_target_pairs={{0,12},{4,8},{8,4},{12,0},{1,13},{5,9},{9,5},{13,1},{2,14},{6,10},... | collective-permute-start | bytes 221192 | tf_op jit(solution)/shard_map/ppermute | solution.py:34
  54.9 5.3 %collective-permute-start.12 = (bf16[9,16,256]{2,1,0:T(8,128)(2,1)S(1)}, bf16[9,16,256]{2,1,0:T(8,128)(2,1)S(1)}, u32[]{:S(2)}, u32[]{:S(2)}) collective-permute-start(bf16[9,16,256]{2,1,0:T(8,128)(2,1)S(1)} %get-tuple-element.74), channel_id=1, source_target_pairs={{0,4},{4,0},{8,12},{12,8},{1,5},{5,1},{9,13},{13,9},{2,6},{6,2},{1... | collective-permute-start | bytes 221192 | tf_op jit(solution)/shard_map/ppermute | solution.py:34
  60.2 5.5 %collective-permute-start.17 = (bf16[2,9,16,256]{3,2,1,0:T(8,128)(2,1)S(1)}, bf16[2,9,16,256]{3,2,1,0:T(8,128)(2,1)S(1)}, u32[]{:S(2)}, u32[]{:S(2)}) collective-permute-start(bf16[2,9,16,256]{3,2,1,0:T(8,128)(2,1)S(1)} %join_acts_near.1.refs_0_), channel_id=1, source_target_pairs={{0,2},{1,3},{2,0},{3,1},{4,6},{5,7},{6,4},{7,5},{8,10},{9,11},{10,... | collective-permute-start | bytes 442376 | tf_op jit(solution)/shard_map/ppermute | solution.py:34
  60.8 6.5 %collective-permute-start.18 = (bf16[2,9,16,256]{3,2,1,0:T(8,128)(2,1)S(1)}, bf16[2,9,16,256]{3,2,1,0:T(8,128)(2,1)S(1)}, u32[]{:S(2)}, u32[]{:S(2)}) collective-permute-start(bf16[2,9,16,256]{3,2,1,0:T(8,128)(2,1)S(1)} %join_acts_far.1.refs_2_.refs_1_), channel_id=1, source_target_pairs={{0,2},{1,3},{2,0},{3,1},{4,6},{5,7},{6,4},{7,5},{8,10},{9,11},{10,... | collective-permute-start | bytes 442376 | tf_op jit(solution)/shard_map/ppermute | solution.py:34
  62.3 5.0 %collective-permute-start.15 = (bf16[2,9,16,256]{3,2,1,0:T(8,128)(2,1)S(1)}, bf16[2,9,16,256]{3,2,1,0:T(8,128)(2,1)S(1)}, u32[]{:S(2)}, u32[]{:S(2)}) collective-permute-start(bf16[2,9,16,256]{3,2,1,0:T(8,128)(2,1)S(1)} %join_acts_near.1.refs_0_), channel_id=1, source_target_pairs={{0,1},{1,0},{2,3},{3,2},{4,5},{5,4},{6,7},{7,6},{8,9},{9,8},{10,11... | collective-permute-start | bytes 442376 | tf_op jit(solution)/shard_map/ppermute | solution.py:34
  62.3 5.0 %collective-permute-start.16 = (bf16[2,9,16,256]{3,2,1,0:T(8,128)(2,1)S(1)}, bf16[2,9,16,256]{3,2,1,0:T(8,128)(2,1)S(1)}, u32[]{:S(2)}, u32[]{:S(2)}) collective-permute-start(bf16[2,9,16,256]{3,2,1,0:T(8,128)(2,1)S(1)} %join_acts_far.1.refs_2_.refs_1_), channel_id=1, source_target_pairs={{0,1},{1,0},{2,3},{3,2},{4,5},{5,4},{6,7},{7,6},{8,9},{9,8},{10,11... | collective-permute-start | bytes 442376 | tf_op jit(solution)/shard_map/ppermute | solution.py:34
  65.7 1.6 collective-permute-start.19
  67.3 1.4 collective-permute-start.20
  68.7 16.7 %copy-start.3 = (f32[2,2,1024]{2,1,0:T(2,128)S(1)}, f32[2,2,1024]{2,1,0:T(2,128)}, u32[]{:S(2)}) copy-start(f32[2,2,1024]{2,1,0:T(2,128)} %refs_3_.3) | copy-start | bytes 49156
  68.7 16.7 %copy-start.4 = (f32[2,1024]{1,0:T(2,128)S(1)}, f32[2,1024]{1,0:T(2,128)}, u32[]{:S(2)}) copy-start(f32[2,1024]{1,0:T(2,128)} %refs_5_.1) | copy-start | bytes 24580
  70.1 7.0 %collective-permute-start.21 = (bf16[4,16,1024]{2,1,0:T(8,128)(2,1)S(1)}, bf16[4,16,1024]{2,1,0:T(8,128)(2,1)S(1)}, u32[]{:S(2)}, u32[]{:S(2)}) collective-permute-start(bf16[4,16,1024]{2,1,0:T(8,128)(2,1)S(1)} %get-tuple-element.78), channel_id=1, source_target_pairs={{0,4},{4,0},{8,12},{12,8},{1,5},{5,1},{9,13},{13,9},{2,6},{6,2},{1... | collective-permute-start | bytes 393224 | tf_op jit(solution)/shard_map/ppermute | solution.py:34
  71.8 10.7 %collective-permute-start.22 = (bf16[4,16,1024]{2,1,0:T(8,128)(2,1)S(1)}, bf16[4,16,1024]{2,1,0:T(8,128)(2,1)S(1)}, u32[]{:S(2)}, u32[]{:S(2)}) collective-permute-start(bf16[4,16,1024]{2,1,0:T(8,128)(2,1)S(1)} %get-tuple-element.79), channel_id=1, source_target_pairs={{0,8},{4,12},{8,0},{12,4},{1,9},{5,13},{9,1},{13,5},{2,10},{6,14},... | collective-permute-start | bytes 393224 | tf_op jit(solution)/shard_map/ppermute | solution.py:34
  73.2 12.1 %collective-permute-start.23 = (bf16[4,16,1024]{2,1,0:T(8,128)(2,1)S(1)}, bf16[4,16,1024]{2,1,0:T(8,128)(2,1)S(1)}, u32[]{:S(2)}, u32[]{:S(2)}) collective-permute-start(bf16[4,16,1024]{2,1,0:T(8,128)(2,1)S(1)} %get-tuple-element.80), channel_id=1, source_target_pairs={{0,12},{4,8},{8,4},{12,0},{1,13},{5,9},{9,5},{13,1},{2,14},{6,10},... | collective-permute-start | bytes 393224 | tf_op jit(solution)/shard_map/ppermute | solution.py:34
  86.3 5.9 %collective-permute-start.24 = (bf16[4,16,1024]{2,1,0:T(8,128)(2,1)S(1)}, bf16[4,16,1024]{2,1,0:T(8,128)(2,1)S(1)}, u32[]{:S(2)}, u32[]{:S(2)}) collective-permute-start(bf16[4,16,1024]{2,1,0:T(8,128)(2,1)S(1)} %get-tuple-element.83.refs_0_.refs_8_), channel_id=1, source_target_pairs={{0,4},{4,0},{8,12},{12,8},{1,5},{5,1},{9,13},{13,9},{2,6},{6,2},{1... | collective-permute-start | bytes 393224 | tf_op jit(solution)/shard_map/ppermute | solution.py:34
  86.4 8.4 %collective-permute-start.25 = (bf16[4,16,1024]{2,1,0:T(8,128)(2,1)S(1)}, bf16[4,16,1024]{2,1,0:T(8,128)(2,1)S(1)}, u32[]{:S(2)}, u32[]{:S(2)}) collective-permute-start(bf16[4,16,1024]{2,1,0:T(8,128)(2,1)S(1)} %get-tuple-element.83.refs_0_.refs_8_), channel_id=1, source_target_pairs={{0,8},{4,12},{8,0},{12,4},{1,9},{5,13},{9,1},{13,5},{2,10},{6,14},... | collective-permute-start | bytes 393224 | tf_op jit(solution)/shard_map/ppermute | solution.py:34
  96.4 1.9 %collective-permute-start.26 = (bf16[2,3,9,16,256]{4,3,2,1,0:T(8,128)(2,1)S(1)}, bf16[2,3,9,16,256]{4,3,2,1,0:T(8,128)(2,1)S(1)}, u32[]{:S(2)}, u32[]{:S(2)}) collective-permute-start(bf16[2,3,9,16,256]{4,3,2,1,0:T(8,128)(2,1)S(1)} %get-tuple-element.85), channel_id=1, source_target_pairs={{0,1},{1,0},{2,3},{3,2},{4,5},{5,4},{6,7},{7,6},{8,9},{9,8},{10,11... | collective-permute-start | bytes 1327112 | tf_op jit(solution)/shard_map/ppermute | solution.py:34
  96.5 5.9 %collective-permute-start.30 = (bf16[4,16,1024]{2,1,0:T(8,128)(2,1)S(1)}, bf16[4,16,1024]{2,1,0:T(8,128)(2,1)S(1)}, u32[]{:S(2)}, u32[]{:S(2)}) collective-permute-start(bf16[4,16,1024]{2,1,0:T(8,128)(2,1)S(1)} %collective-permute-done.25.refs_2_.refs_10_), channel_id=1, source_target_pairs={{0,4},{4,0},{8,12},{12,8},{1,5},{5,1},{9,13},{13,9},{2,6},{6,2},{1... | collective-permute-start | bytes 393224 | tf_op jit(solution)/shard_map/ppermute | solution.py:34
  98.3 7.5 %collective-permute-start.27 = (bf16[3,9,16,256]{3,2,1,0:T(8,128)(2,1)S(1)}, bf16[3,9,16,256]{3,2,1,0:T(8,128)(2,1)S(1)}, u32[]{:S(2)}, u32[]{:S(2)}) collective-permute-start(bf16[3,9,16,256]{3,2,1,0:T(8,128)(2,1)S(1)} %cross_near.1.refs_2_), channel_id=1, source_target_pairs={{0,2},{1,3},{2,0},{3,1},{4,6},{5,7},{6,4},{7,5},{8,10},{9,11},{10,... | collective-permute-start | bytes 663560 | tf_op jit(solution)/shard_map/ppermute | solution.py:34
  103.9 5.1 %collective-permute-start.31 = (bf16[2,1,9,16,256]{4,3,2,1,0:T(8,128)(2,1)S(1)}, bf16[2,1,9,16,256]{4,3,2,1,0:T(8,128)(2,1)S(1)}, u32[]{:S(2)}, u32[]{:S(2)}) collective-permute-start(bf16[2,1,9,16,256]{4,3,2,1,0:T(8,128)(2,1)S(1)} %get-tuple-element.91), channel_id=1, source_target_pairs={{0,1},{1,0},{2,3},{3,2},{4,5},{5,4},{6,7},{7,6},{8,9},{9,8},{10,11... | collective-permute-start | bytes 442376 | tf_op jit(solution)/shard_map/ppermute | solution.py:34
  105.9 7.5 %collective-permute-start.28 = (bf16[10,16,256]{2,1,0:T(8,128)(2,1)S(1)}, bf16[10,16,256]{2,1,0:T(8,128)(2,1)S(1)}, u32[]{:S(2)}, u32[]{:S(2)}) collective-permute-start(bf16[10,16,256]{2,1,0:T(8,128)(2,1)S(1)} %get-tuple-element.88), channel_id=1, source_target_pairs={{0,4},{4,0},{8,12},{12,8},{1,5},{5,1},{9,13},{13,9},{2,6},{6,2},{1... | collective-permute-start | bytes 245768 | tf_op jit(solution)/shard_map/ppermute | solution.py:34
  107.7 5.8 %collective-permute-start.29 = (bf16[10,16,256]{2,1,0:T(8,128)(2,1)S(1)}, bf16[10,16,256]{2,1,0:T(8,128)(2,1)S(1)}, u32[]{:S(2)}, u32[]{:S(2)}) collective-permute-start(bf16[10,16,256]{2,1,0:T(8,128)(2,1)S(1)} %get-tuple-element.89), channel_id=1, source_target_pairs={{0,8},{4,12},{8,0},{12,4},{1,9},{5,13},{9,1},{13,5},{2,10},{6,14},... | collective-permute-start | bytes 245768 | tf_op jit(solution)/shard_map/ppermute | solution.py:34
  109.0 4.4 %collective-permute-start.32 = (bf16[1,9,16,256]{3,2,1,0:T(8,128)(2,1)S(1)}, bf16[1,9,16,256]{3,2,1,0:T(8,128)(2,1)S(1)}, u32[]{:S(2)}, u32[]{:S(2)}) collective-permute-start(bf16[1,9,16,256]{3,2,1,0:T(8,128)(2,1)S(1)} %cross_far.1), channel_id=1, source_target_pairs={{0,2},{1,3},{2,0},{3,1},{4,6},{5,7},{6,4},{7,5},{8,10},{9,11},{10,... | collective-permute-start | bytes 221192 | tf_op jit(solution)/shard_map/ppermute | solution.py:34
  113.5 10.5 %collective-permute-start.34 = (bf16[3,10,16,256]{3,2,1,0:T(8,128)(2,1)S(1)}, bf16[3,10,16,256]{3,2,1,0:T(8,128)(2,1)S(1)}, u32[]{:S(2)}, u32[]{:S(2)}) collective-permute-start(bf16[3,10,16,256]{3,2,1,0:T(8,128)(2,1)S(1)} %join_near.1.refs_3_.refs_1_), channel_id=1, source_target_pairs={{0,16},{16,0},{1,17},{17,1},{2,18},{18,2},{3,19},{19,3},{4,20},{20... | collective-permute-start | bytes 737288 | tf_op jit(solution)/shard_map/ppermute | solution.py:34
  115.1 4.4 %collective-permute-start.33 = (bf16[10,16,256]{2,1,0:T(8,128)(2,1)S(1)}, bf16[10,16,256]{2,1,0:T(8,128)(2,1)S(1)}, u32[]{:S(2)}, u32[]{:S(2)}) collective-permute-start(bf16[10,16,256]{2,1,0:T(8,128)(2,1)S(1)} %home_far.1.refs_3_), channel_id=1, source_target_pairs={{0,12},{4,8},{8,4},{12,0},{1,13},{5,9},{9,5},{13,1},{2,14},{6,10},... | collective-permute-start | bytes 245768 | tf_op jit(solution)/shard_map/ppermute | solution.py:34
  119.5 4.4 %collective-permute-start.35 = (bf16[10,16,256]{2,1,0:T(8,128)(2,1)S(1)}, bf16[10,16,256]{2,1,0:T(8,128)(2,1)S(1)}, u32[]{:S(2)}, u32[]{:S(2)}) collective-permute-start(bf16[10,16,256]{2,1,0:T(8,128)(2,1)S(1)} %collective-permute-done.33.refs_2_), channel_id=1, source_target_pairs={{0,16},{16,0},{1,17},{17,1},{2,18},{18,2},{3,19},{19,3},{4,20},{20... | collective-permute-start | bytes 245768 | tf_op jit(solution)/shard_map/ppermute | solution.py:34
  137.2 2.5 %collective-permute-start.38 = (bf16[3520,128]{1,0:T(8,128)(2,1)S(1)}, bf16[3520,128]{1,0:T(8,128)(2,1)S(1)}, u32[]{:S(2)}, u32[]{:S(2)}) collective-permute-start(bf16[3520,128]{1,0:T(8,128)(2,1)S(1)} %get-tuple-element.98), channel_id=1, source_target_pairs={{0,1},{1,0},{2,3},{3,2},{4,5},{5,4},{6,7},{7,6},{8,9},{9,8},{10,11... | collective-permute-start | bytes 2703368 | tf_op jit(solution)/shard_map/ppermute | solution.py:34
  137.3 11.4 %collective-permute-start.36 = (bf16[368,384]{1,0:T(8,128)(2,1)S(1)}, bf16[368,384]{1,0:T(8,128)(2,1)S(1)}, u32[]{:S(2)}, u32[]{:S(2)}) collective-permute-start(bf16[368,384]{1,0:T(8,128)(2,1)S(1)} %get-tuple-element.93), channel_id=1, source_target_pairs={{0,2},{1,3},{2,0},{3,1},{4,6},{5,7},{6,4},{7,5},{8,10},{9,11},{10,... | collective-permute-start | bytes 847880 | tf_op jit(solution)/shard_map/ppermute | solution.py:34
  137.8 15.7 %collective-permute-start.37 = (bf16[368,384]{1,0:T(8,128)(2,1)S(1)}, bf16[368,384]{1,0:T(8,128)(2,1)S(1)}, u32[]{:S(2)}, u32[]{:S(2)}) collective-permute-start(bf16[368,384]{1,0:T(8,128)(2,1)S(1)} %get-tuple-element.94), channel_id=1, source_target_pairs={{0,3},{1,2},{2,1},{3,0},{4,7},{5,6},{6,5},{7,4},{8,11},{9,10},{10,... | collective-permute-start | bytes 847880 | tf_op jit(solution)/shard_map/ppermute | solution.py:34
  139.2 27.2 %collective-permute-start.43 = (bf16[368,384]{1,0:T(8,128)(2,1)S(1)}, bf16[368,384]{1,0:T(8,128)(2,1)S(1)}, u32[]{:S(2)}, u32[]{:S(2)}) collective-permute-start(bf16[368,384]{1,0:T(8,128)(2,1)S(1)} %get-tuple-element.104), channel_id=1, source_target_pairs={{0,1},{1,0},{2,3},{3,2},{4,5},{5,4},{6,7},{7,6},{8,9},{9,8},{10,11... | collective-permute-start | bytes 847880 | tf_op jit(solution)/shard_map/ppermute | solution.py:34
  140.0 15.1 %collective-permute-start.44 = (bf16[880,128]{1,0:T(8,128)(2,1)S(1)}, bf16[880,128]{1,0:T(8,128)(2,1)S(1)}, u32[]{:S(2)}, u32[]{:S(2)}) collective-permute-start(bf16[880,128]{1,0:T(8,128)(2,1)S(1)} %get-tuple-element.105), channel_id=1, source_target_pairs={{0,4},{4,0},{8,12},{12,8},{1,5},{5,1},{9,13},{13,9},{2,6},{6,2},{1... | collective-permute-start | bytes 675848 | tf_op jit(solution)/shard_map/ppermute | solution.py:34
  143.5 14.8 %collective-permute-start.45 = (bf16[880,128]{1,0:T(8,128)(2,1)S(1)}, bf16[880,128]{1,0:T(8,128)(2,1)S(1)}, u32[]{:S(2)}, u32[]{:S(2)}) collective-permute-start(bf16[880,128]{1,0:T(8,128)(2,1)S(1)} %get-tuple-element.106), channel_id=1, source_target_pairs={{0,8},{4,12},{8,0},{12,4},{1,9},{5,13},{9,1},{13,5},{2,10},{6,14},... | collective-permute-start | bytes 675848 | tf_op jit(solution)/shard_map/ppermute | solution.py:34
  148.7 16.4 %collective-permute-start.46 = (bf16[880,128]{1,0:T(8,128)(2,1)S(1)}, bf16[880,128]{1,0:T(8,128)(2,1)S(1)}, u32[]{:S(2)}, u32[]{:S(2)}) collective-permute-start(bf16[880,128]{1,0:T(8,128)(2,1)S(1)} %last_kernels.1), channel_id=1, source_target_pairs={{0,12},{4,8},{8,4},{12,0},{1,13},{5,9},{9,5},{13,1},{2,14},{6,10},... | collective-permute-start | bytes 675848 | tf_op jit(solution)/shard_map/ppermute | solution.py:34
  154.6 18.3 %collective-permute-start.40 = (bf16[320,384]{1,0:T(8,128)(2,1)S(1)}, bf16[320,384]{1,0:T(8,128)(2,1)S(1)}, u32[]{:S(2)}, u32[]{:S(2)}) collective-permute-start(bf16[320,384]{1,0:T(8,128)(2,1)S(1)} %get-tuple-element.101), channel_id=1, source_target_pairs={{0,2},{1,3},{2,0},{3,1},{4,6},{5,7},{6,4},{7,5},{8,10},{9,11},{10,... | collective-permute-start | bytes 737288 | tf_op jit(solution)/shard_map/ppermute | solution.py:34
  155.1 16.2 %collective-permute-start.42 = (bf16[320,384]{1,0:T(8,128)(2,1)S(1)}, bf16[320,384]{1,0:T(8,128)(2,1)S(1)}, u32[]{:S(2)}, u32[]{:S(2)}) collective-permute-start(bf16[320,384]{1,0:T(8,128)(2,1)S(1)} %get-tuple-element.103), channel_id=1, source_target_pairs={{0,1},{1,0},{2,3},{3,2},{4,5},{5,4},{6,7},{7,6},{8,9},{9,8},{10,11... | collective-permute-start | bytes 737288 | tf_op jit(solution)/shard_map/ppermute | solution.py:34
  158.3 14.5 %collective-permute-start.41 = (bf16[320,384]{1,0:T(8,128)(2,1)S(1)}, bf16[320,384]{1,0:T(8,128)(2,1)S(1)}, u32[]{:S(2)}, u32[]{:S(2)}) collective-permute-start(bf16[320,384]{1,0:T(8,128)(2,1)S(1)} %get-tuple-element.102), channel_id=1, source_target_pairs={{0,3},{1,2},{2,1},{3,0},{4,7},{5,6},{6,5},{7,4},{8,11},{9,10},{10,... | collective-permute-start | bytes 737288 | tf_op jit(solution)/shard_map/ppermute | solution.py:34
  165.1 5.0 %collective-permute-start.39 = (bf16[4,16,1024]{2,1,0:T(8,128)(2,1)S(1)}, bf16[4,16,1024]{2,1,0:T(8,128)(2,1)S(1)}, u32[]{:S(2)}, u32[]{:S(2)}) collective-permute-start(bf16[4,16,1024]{2,1,0:T(8,128)(2,1)S(1)} %outputs_send.1), channel_id=1, source_target_pairs={{0,16},{16,0},{1,17},{17,1},{2,18},{18,2},{3,19},{19,3},{4,20},{20... | collective-permute-start | bytes 393224 | tf_op jit(solution)/shard_map/ppermute | solution.py:34
  166.4 8.0 %collective-permute-start.47 = (bf16[64,896]{1,0:T(8,128)(2,1)S(1)}, bf16[64,896]{1,0:T(8,128)(2,1)S(1)}, u32[]{:S(2)}, u32[]{:S(2)}) collective-permute-start(bf16[64,896]{1,0:T(8,128)(2,1)S(1)} %get-tuple-element.110), channel_id=1, source_target_pairs={{0,2},{1,3},{2,0},{3,1},{4,6},{5,7},{6,4},{7,5},{8,10},{9,11},{10,... | collective-permute-start | bytes 344072 | tf_op jit(solution)/shard_map/ppermute | solution.py:34
  171.3 4.4 %copy-start.1 = (bf16[4,64,2,1024]{3,2,1,0:T(2,128)(2,1)S(1)}, bf16[4,64,2,1024]{3,2,1,0:T(2,128)(2,1)}, u32[]{:S(2)}) copy-start(bf16[4,64,2,1024]{3,2,1,0:T(2,128)(2,1)} %param.17) | copy-start | bytes 3145732

commit v6 on v5

--- a/solution.py
+++ b/solution.py
@@ -824,8 +824,6 @@
         grads = gather4(pre_grad)
         ten = struct((10, IMG, OUT), BF16)
 
-        marks = []
-
         def home(ks, name, after=()):
             shape = (2, len(ks), 9, IMG, OUT)
             keep, send = call(
@@ -839,12 +837,11 @@
             crossing = call(cross_kernel, "cross_" + name, [keep, arrived], struct(shape[1:], BF16))
             crossed = swap(crossing, "mp", 2)
             inputs = [keep, arrived, crossed, sums]
-            marks.append(crossing)
             return call(home_kernel, "home_" + name, inputs, [ten] * len(ks))
 
         chunks = home((0, 1, 2), "near")
         moved = [chunks[0], swap(chunks[1], "dp", 1), swap(chunks[2], "dp", 2)]
-        (chunk,) = home((3,), "far", marks[:1])
+        (chunk,) = home((3,), "far")
         def matrix_gradient(after, grads=tuple(grads)):
             return call(
                 fc_matrix_kernel,

time: 176 us -> 176 us (level)
  no operation moved by 1% of the time
where the time goes in v6:
time: 176 us
  waiting for transfers between devices  67.4 us (38%)
  Pallas kernels  44.6 us (25%)
  starting transfers between devices  40.7 us (23%)
  matrix products  18.6 us (11%)
  local copies, waits for them, and re-layouts  2.45 us (1%)
    ppermute x48, waiting for transfers between devices, swap(): return lax.ppermute(value, axis, [(i, i ^ bit) for i in range(count)])  67.4 us
    ppermute x48, starting transfers between devices, swap(): return lax.ppermute(value, axis, [(i, i ^ bit) for i in range(count)])  40.7 us
    pallas_call x34, Pallas kernels, call(): pl.pallas_call(kernel, in_specs=specs + [VMEM] * len(after), out_specs=ou...  32.7 us
    conv_general_dilated x4, matrix products, conv(): lax.conv_general_dilated(maps, taps, (1, 1), (rows, (1, 1)), dimension_nu...  18.6 us
    pallas_call x2, Pallas kernels, pack_maps(): pl.pallas_call(partial(pack_kernel, len(after)), grid_spec=pltpu.Prefetch...  6.99 us
    pallas_call x3, Pallas kernels, place_grad(): pl.pallas_call(partial(place_grad_kernel, chunk, ks), in_specs=in_specs,...  4.89 us
  transfers between devices with their start and end apart: 48, of which 23 were waited for; matrix products, arithmetic and copies ran while one was open for 2% of the time, Pallas kernels for 18%

profile of v6, /device:TPU:8, one launch (start us, length us, event | category | flops | bytes accessed | tf_op | source)
XLA Modules:
  0.0 175.7 jit_solution(18093288878046630112)
XLA Ops:
  1.5 1.6 own_kernels.1.refs_0_
  3.0 1.6 collective-permute-start
  4.6 3.6 %pack_maps.2 = (bf16[688,384]{1,0:T(8,128)(2,1)S(1)}, bf16[688,384]{1,0:T(8,128)(2,1)}, f32[8,128]{1,0:T(8,128)S(1)}) custom-call(s32[7]{0:T(128)S(1)} %pad_add_fusion.sel.refs_0_, bf16[4,5408,96]{2,1,0:T(8,128)(2,1)} %bitcast.54), custom_call_target="tpu_custom_call" | custom-call | flops 1 | bytes 1 | tf_op jit(solution)/shard_map/pack_maps/pallas_call | solution.py:206
  8.8 3.0 %collective-permute-start.5 = (bf16[2,64,896]{2,1,0:T(8,128)(2,1)S(1)}, bf16[2,64,896]{2,1,0:T(8,128)(2,1)S(1)}, u32[]{:S(2)}, u32[]{:S(2)}) collective-permute-start(bf16[2,64,896]{2,1,0:T(8,128)(2,1)S(1)} %join_kernels.1.refs_1_.refs_0_), channel_id=1, source_target_pairs={{0,8},{4,12},{8,0},{12,4},{1,9},{5,13},{9,1},{13,5},{2,10},{6,14},... | collective-permute-start | bytes 688136 | tf_op jit(solution)/shard_map/ppermute | solution.py:34
  11.9 2.9 %load_matrix.1 = (bf16[2304,1024]{1,0:T(8,128)(2,1)S(1)}, f32[8,128]{1,0:T(8,128)S(1)}) custom-call(s32[7]{0:T(128)S(1)} %pad_add_fusion.sel.refs_0_, bf16[2,2304,1024]{2,1,0:T(8,128)(2,1)} %refs_1_.1, f32[8,128]{1,0:T(8,128)S(1)} %get-tuple-element.62.refs_2_.refs_0_), custom_call_target="tpu_custom_call" | custom-call | flops 1 | bytes 1 | tf_op jit(solution)/shard_map/load_matrix/pallas_call | solution.py:84
  14.8 2.2 %copy-done.2 = bf16[2304,1024]{1,0:T(8,128)(2,1)} copy-done((bf16[2304,1024]{1,0:T(8,128)(2,1)}, bf16[2304,1024]{1,0:T(8,128)(2,1)S(1)}, u32[]{:S(2)}) %copy-start.2) | copy-done | bytes 4718616
  17.2 3.4 %pack_maps.3 = (bf16[688,384]{1,0:T(8,128)(2,1)S(1)}, bf16[688,384]{1,0:T(8,128)(2,1)S(1)}, f32[8,128]{1,0:T(8,128)}) custom-call(s32[7]{0:T(128)S(1)} %pad_add_fusion.sel.refs_0_, bf16[4,5408,96]{2,1,0:T(8,128)(2,1)} %bitcast.55, f32[8,128]{1,0:T(8,128)S(1)} %get-tuple-element.62.refs_2_.refs_0_, bf16[2,64,896]{2,1,0:T(8,128)(2,1)S(1)} %join_kernels.1.refs_1_.refs_0_, ...), custom_call_target="tpu_custom_call" | custom-call | flops 1 | bytes 1 | tf_op jit(solution)/shard_map/pack_maps/pallas_call | solution.py:206
  20.6 1.6 collective-permute-start.1
  22.8 11.8 %collective-permute-done.6.refs_3_ = bf16[2,64,896]{2,1,0:T(8,128)(2,1)S(1)} collective-permute-done((bf16[2,64,896]{2,1,0:T(8,128)(2,1)S(1)}, bf16[2,64,896]{2,1,0:T(8,128)(2,1)S(1)}, u32[]{:S(2)}, u32[]{:S(2)}) %collective-permute-start.6) | collective-permute-done | bytes 229408 | tf_op jit(solution)/shard_map/ppermute | solution.py:34
  35.2 1.4 unpack_maps.1
  36.7 1.4 kernels.1
  38.0 5.6 %fusion.refs_1_ = f32[13,13,16,256]{3,2,1,0:T(8,128)S(1)} fusion(bf16[13,13,16,384]{3,2,1,0:T(8,128)(2,1)S(1)} %bitcast.40, bf16[3,3,384,256]{3,2,1,0:T(8,128)(2,1)S(1)} %bitcast.47), kind=kOutput, calls=%fused_computation.5 | convolution fusion | flops 4306501632 | bytes 6615040 | tf_op jit(solution)/shard_map/conv_general_dilated | solution.py:896
  43.7 1.6 pool.1
  45.3 1.6 collective-permute-start.11
  48.0 4.0 %collective-permute-done.11.refs_2_.refs_8_ = bf16[2,9,16,256]{3,2,1,0:T(8,128)(2,1)S(1)} collective-permute-done((bf16[2,9,16,256]{3,2,1,0:T(8,128)(2,1)S(1)}, bf16[2,9,16,256]{3,2,1,0:T(8,128)(2,1)S(1)}, u32[]{:S(2)}, u32[]{:S(2)}) %collective-permute-start.11) | collective-permute-done | bytes 147488 | tf_op jit(solution)/shard_map/ppermute | solution.py:34
  53.3 1.0 collective-permute-done.10.refs_2_.refs_7_
  54.9 2.9 %collective-permute-start.12 = (bf16[9,16,256]{2,1,0:T(8,128)(2,1)S(1)}, bf16[9,16,256]{2,1,0:T(8,128)(2,1)S(1)}, u32[]{:S(2)}, u32[]{:S(2)}) collective-permute-start(bf16[9,16,256]{2,1,0:T(8,128)(2,1)S(1)} %get-tuple-element.74), channel_id=1, source_target_pairs={{0,4},{4,0},{8,12},{12,8},{1,5},{5,1},{9,13},{13,9},{2,6},{6,2},{1... | collective-permute-start | bytes 221192 | tf_op jit(solution)/shard_map/ppermute | solution.py:34
  58.2 1.8 %collective-permute-done.14.refs_1_ = bf16[9,16,256]{2,1,0:T(8,128)(2,1)S(1)} collective-permute-done((bf16[9,16,256]{2,1,0:T(8,128)(2,1)S(1)}, bf16[9,16,256]{2,1,0:T(8,128)(2,1)S(1)}, u32[]{:S(2)}, u32[]{:S(2)}) %collective-permute-start.14) | collective-permute-done | bytes 73760 | tf_op jit(solution)/shard_map/ppermute | solution.py:34
  60.8 1.5 collective-permute-start.18
  62.8 2.9 %collective-permute-done.17.refs_4_ = bf16[2,9,16,256]{3,2,1,0:T(8,128)(2,1)S(1)} collective-permute-done((bf16[2,9,16,256]{3,2,1,0:T(8,128)(2,1)S(1)}, bf16[2,9,16,256]{3,2,1,0:T(8,128)(2,1)S(1)}, u32[]{:S(2)}, u32[]{:S(2)}) %collective-permute-start.17) | collective-permute-done | bytes 147488 | tf_op jit(solution)/shard_map/ppermute | solution.py:34
  65.7 1.6 collective-permute-done.18.refs_5_
  67.3 1.3 collective-permute-done.20.refs_7_
  68.7 1.4 fc_forward.1
  70.1 1.7 collective-permute-start.21
  71.8 1.4 collective-permute-start.22
  73.7 3.4 %collective-permute-done.21.refs_2_ = bf16[4,16,1024]{2,1,0:T(8,128)(2,1)S(1)} collective-permute-done((bf16[4,16,1024]{2,1,0:T(8,128)(2,1)S(1)}, bf16[4,16,1024]{2,1,0:T(8,128)(2,1)S(1)}, u32[]{:S(2)}, u32[]{:S(2)}) %collective-permute-start.21) | collective-permute-done | bytes 131104 | tf_op jit(solution)/shard_map/ppermute | solution.py:34
  77.1 5.4 %collective-permute-done.22.refs_3_ = bf16[4,16,1024]{2,1,0:T(8,128)(2,1)S(1)} collective-permute-done((bf16[4,16,1024]{2,1,0:T(8,128)(2,1)S(1)}, bf16[4,16,1024]{2,1,0:T(8,128)(2,1)S(1)}, u32[]{:S(2)}, u32[]{:S(2)}) %collective-permute-start.22) | collective-permute-done | bytes 131104 | tf_op jit(solution)/shard_map/ppermute | solution.py:34
  82.6 2.8 %collective-permute-done.23.refs_4_ = bf16[4,16,1024]{2,1,0:T(8,128)(2,1)S(1)} collective-permute-done((bf16[4,16,1024]{2,1,0:T(8,128)(2,1)S(1)}, bf16[4,16,1024]{2,1,0:T(8,128)(2,1)S(1)}, u32[]{:S(2)}, u32[]{:S(2)}) %collective-permute-start.23) | collective-permute-done | bytes 131104 | tf_op jit(solution)/shard_map/ppermute | solution.py:34
  85.4 0.9 fc_active.1
  86.4 3.0 %collective-permute-start.25 = (bf16[4,16,1024]{2,1,0:T(8,128)(2,1)S(1)}, bf16[4,16,1024]{2,1,0:T(8,128)(2,1)S(1)}, u32[]{:S(2)}, u32[]{:S(2)}) collective-permute-start(bf16[4,16,1024]{2,1,0:T(8,128)(2,1)S(1)} %get-tuple-element.83.refs_0_.refs_8_), channel_id=1, source_target_pairs={{0,8},{4,12},{8,0},{12,4},{1,9},{5,13},{9,1},{13,5},{2,10},{6,14},... | collective-permute-start | bytes 393224 | tf_op jit(solution)/shard_map/ppermute | solution.py:34
  89.3 2.8 %collective-permute-done.24.refs_1_.refs_9_ = bf16[4,16,1024]{2,1,0:T(8,128)(2,1)S(1)} collective-permute-done((bf16[4,16,1024]{2,1,0:T(8,128)(2,1)S(1)}, bf16[4,16,1024]{2,1,0:T(8,128)(2,1)S(1)}, u32[]{:S(2)}, u32[]{:S(2)}) %collective-permute-start.24) | collective-permute-done | bytes 131104 | tf_op jit(solution)/shard_map/ppermute | solution.py:34
  92.2 2.5 %collective-permute-done.25.refs_2_.refs_10_ = bf16[4,16,1024]{2,1,0:T(8,128)(2,1)S(1)} collective-permute-done((bf16[4,16,1024]{2,1,0:T(8,128)(2,1)S(1)}, bf16[4,16,1024]{2,1,0:T(8,128)(2,1)S(1)}, u32[]{:S(2)}, u32[]{:S(2)}) %collective-permute-start.25) | collective-permute-done | bytes 131104 | tf_op jit(solution)/shard_map/ppermute | solution.py:34
  94.7 1.7 fc_rows_near.1
  96.5 1.7 collective-permute-start.30
  98.7 3.6 %collective-permute-done.30.refs_0_.refs_11_ = bf16[4,16,1024]{2,1,0:T(8,128)(2,1)S(1)} collective-permute-done((bf16[4,16,1024]{2,1,0:T(8,128)(2,1)S(1)}, bf16[4,16,1024]{2,1,0:T(8,128)(2,1)S(1)}, u32[]{:S(2)}, u32[]{:S(2)}) %collective-permute-start.30) | collective-permute-done | bytes 131104 | tf_op jit(solution)/shard_map/ppermute | solution.py:34
  102.4 1.5 fc_rows_far.1
  104.0 1.8 %collective-permute-done.27.refs_2_ = bf16[3,9,16,256]{3,2,1,0:T(8,128)(2,1)S(1)} collective-permute-done((bf16[3,9,16,256]{3,2,1,0:T(8,128)(2,1)S(1)}, bf16[3,9,16,256]{3,2,1,0:T(8,128)(2,1)S(1)}, u32[]{:S(2)}, u32[]{:S(2)}) %collective-permute-start.27) | collective-permute-done | bytes 221216 | tf_op jit(solution)/shard_map/ppermute | solution.py:34
  105.9 1.7 collective-permute-start.28
  107.7 1.3 collective-permute-start.29
  109.5 3.9 %collective-permute-done.32.refs_2_ = bf16[1,9,16,256]{3,2,1,0:T(8,128)(2,1)S(1)} collective-permute-done((bf16[1,9,16,256]{3,2,1,0:T(8,128)(2,1)S(1)}, bf16[1,9,16,256]{3,2,1,0:T(8,128)(2,1)S(1)}, u32[]{:S(2)}, u32[]{:S(2)}) %collective-permute-start.32) | collective-permute-done | bytes 73760 | tf_op jit(solution)/shard_map/ppermute | solution.py:34
  113.5 1.6 collective-permute-start.34
  115.1 1.0 collective-permute-start.33
  116.1 3.4 %collective-permute-done.33.refs_2_ = bf16[10,16,256]{2,1,0:T(8,128)(2,1)S(1)} collective-permute-done((bf16[10,16,256]{2,1,0:T(8,128)(2,1)S(1)}, bf16[10,16,256]{2,1,0:T(8,128)(2,1)S(1)}, u32[]{:S(2)}, u32[]{:S(2)}) %collective-permute-start.33) | collective-permute-done | bytes 81952 | tf_op jit(solution)/shard_map/ppermute | solution.py:34
  120.0 2.1 %slope.1.refs_5_ = f32[169,16,256]{2,1,0:T(8,128)S(1)} custom-call(s32[7]{0:T(128)S(1)} %pad_add_fusion.sel.refs_0_, f32[13,13,16,256]{3,2,1,0:T(8,128)S(1)} %fusion.refs_1_, f32[8,256]{1,0:T(8,128)S(1)} %get-tuple-element.69.refs_2_.refs_3_.refs_9_, bf16[3,10,16,256]{3,2,1,0:T(8,128)(2,1)S(1)} %join_near.1.refs_3_.refs_1_), custom_call_target="tpu_custom_call" | custom-call | flops 1 | bytes 1 | tf_op jit(solution)/shard_map/slope/pallas_call | solution.py:84
  122.1 1.9 %collective-permute-done.35.refs_4_ = bf16[10,16,256]{2,1,0:T(8,128)(2,1)S(1)} collective-permute-done((bf16[10,16,256]{2,1,0:T(8,128)(2,1)S(1)}, bf16[10,16,256]{2,1,0:T(8,128)(2,1)S(1)}, u32[]{:S(2)}, u32[]{:S(2)}) %collective-permute-start.35) | collective-permute-done | bytes 81952 | tf_op jit(solution)/shard_map/ppermute | solution.py:34
  124.0 1.2 conv_gradient.1
  125.2 3.8 %convolution_convert_fusion = bf16[7,13,16,384]{3,2,1,0:T(8,128)(2,1)S(1)} fusion(bf16[13,13,16,256]{3,2,1,0:T(8,128)(2,1)S(1)} %bitcast.50, bf16[3,3,384,256]{3,2,1,0:T(8,128)(2,1)S(1)} %bitcast.48), kind=kOutput, calls=%fused_computation | convolution fusion | flops 2328397824 | bytes 4272128 | tf_op jit(solution)/shard_map/conv_general_dilated | solution.py:896
  128.9 1.0 pack_grad.2
  130.0 6.1 %fusion.1 = f32[3,3,384,256]{3,2,1,0:T(8,128)S(1)} fusion(bf16[13,13,16,384]{3,2,1,0:T(8,128)(2,1)S(1)} %pass_on.1, bf16[13,13,16,256]{3,2,1,0:T(8,128)(2,1)S(1)} %bitcast.51), kind=kOutput, calls=%fused_computation.6 | convolution fusion | flops 4306501632 | bytes 7000064 | tf_op jit(solution)/shard_map/conv_general_dilated | solution.py:896
  136.1 1.1 split_kernels.1
  137.8 1.3 collective-permute-start.37
  140.0 3.5 %collective-permute-start.44 = (bf16[880,128]{1,0:T(8,128)(2,1)S(1)}, bf16[880,128]{1,0:T(8,128)(2,1)S(1)}, u32[]{:S(2)}, u32[]{:S(2)}) collective-permute-start(bf16[880,128]{1,0:T(8,128)(2,1)S(1)} %get-tuple-element.105), channel_id=1, source_target_pairs={{0,4},{4,0},{8,12},{12,8},{1,5},{5,1},{9,13},{13,9},{2,6},{6,2},{1... | collective-permute-start | bytes 675848 | tf_op jit(solution)/shard_map/ppermute | solution.py:34
  143.5 5.2 %fc_matrix.1 = (f32[2304,1024]{1,0:T(8,128)}, f32[1,1024]{1,0:T(1,128)}, f32[8,128]{1,0:T(8,128)S(1)}) custom-call(bf16[2,9,16,256]{3,2,1,0:T(8,128)(2,1)S(1)} %join_acts_near.1.refs_0_, bf16[2,9,16,256]{3,2,1,0:T(8,128)(2,1)S(1)} %join_acts_far.1.refs_2_.refs_1_, bf16[2,9,16,256]{3,2,1,0:T(8,128)(2,1)S(1)} %collective-permute-done.15.refs_2_, ...), custom_call_target="tpu_custom_call" | custom-call | flops 1 | bytes 1 | tf_op jit(solution)/shard_map/fc_matrix/pallas_call | solution.py:84
  148.7 1.6 collective-permute-start.46
  150.3 3.2 %convolution_convert_fusion.1 = bf16[6,13,16,384]{3,2,1,0:T(8,128)(2,1)S(1)} fusion(bf16[13,13,16,256]{3,2,1,0:T(8,128)(2,1)S(1)} %bitcast.52, bf16[3,3,384,256]{3,2,1,0:T(8,128)(2,1)S(1)} %bitcast.49), kind=kOutput, calls=%fused_computation.1 | convolution fusion | flops 1979142144 | bytes 4112384 | tf_op jit(solution)/shard_map/conv_general_dilated | solution.py:896
  153.5 1.0 pack_grad.3
  155.1 3.2 %collective-permute-done.45.refs_3_ = bf16[880,128]{1,0:T(8,128)(2,1)S(1)} collective-permute-done((bf16[880,128]{1,0:T(8,128)(2,1)S(1)}, bf16[880,128]{1,0:T(8,128)(2,1)S(1)}, u32[]{:S(2)}, u32[]{:S(2)}) %collective-permute-start.45) | collective-permute-done | bytes 225312 | tf_op jit(solution)/shard_map/ppermute | solution.py:34
  158.3 6.8 %collective-permute-done.46.refs_4_ = bf16[880,128]{1,0:T(8,128)(2,1)S(1)} collective-permute-done((bf16[880,128]{1,0:T(8,128)(2,1)S(1)}, bf16[880,128]{1,0:T(8,128)(2,1)S(1)}, u32[]{:S(2)}, u32[]{:S(2)}) %collective-permute-start.46) | collective-permute-done | bytes 225312 | tf_op jit(solution)/shard_map/ppermute | solution.py:34
  166.9 1.2 stitch_sums.1
  168.1 1.8 %place_grad.3.refs_2_ = bf16[4,2704,96]{2,1,0:T(8,128)(2,1)} custom-call(s32[7]{0:T(128)S(1)} %pad_add_fusion.sel.refs_0_, bf16[368,384]{1,0:T(8,128)(2,1)S(1)} %get-tuple-element.95.refs_1_.refs_0_, bf16[368,384]{1,0:T(8,128)(2,1)S(1)} %collective-permute-done.43.refs_1_, bf16[368,384]{1,0:T(8,128)(2,1)S(1)} %collective-permute-done.36.refs_2_, ...), custom_call_target="tpu_custom_call" | custom-call | flops 1 | bytes 1 | tf_op jit(solution)/shard_map/place_grad/pallas_call | solution.py:285
  170.1 1.2 outputs.1
  171.3 1.5 place_grad.4.refs_2_
  172.9 1.5 place_grad.5
  174.4 1.3 finish_kernels.1
  (94 shorter events, 13.8 us)
Async XLA Ops:
  0.6 16.4 %copy-start = (bf16[4,64,2,1024]{3,2,1,0:T(2,128)(2,1)S(1)}, bf16[4,64,2,1024]{3,2,1,0:T(2,128)(2,1)}, u32[]{:S(2)}) copy-start(bf16[4,64,2,1024]{3,2,1,0:T(2,128)(2,1)} %param.17) | copy-start | bytes 3145732
  3.0 5.7 %collective-permute-start = (bf16[64,896]{1,0:T(8,128)(2,1)S(1)}, bf16[64,896]{1,0:T(8,128)(2,1)S(1)}, u32[]{:S(2)}, u32[]{:S(2)}) collective-permute-start(bf16[64,896]{1,0:T(8,128)(2,1)S(1)} %own_kernels.1.refs_0_), channel_id=1, source_target_pairs={{0,2},{1,3},{2,0},{3,1},{4,6},{5,7},{6,4},{7,5},{8,10},{9,11},{10,... | collective-permute-start | bytes 344072 | tf_op jit(solution)/shard_map/ppermute | solution.py:34
  8.2 26.5 %collective-permute-start.2 = (bf16[688,384]{1,0:T(8,128)(2,1)}, bf16[688,384]{1,0:T(8,128)(2,1)S(1)}, u32[]{:S(2)}, u32[]{:S(2)}) collective-permute-start(bf16[688,384]{1,0:T(8,128)(2,1)} %get-tuple-element.66), channel_id=1, source_target_pairs={{0,2},{1,3},{2,0},{3,1},{4,6},{5,7},{6,4},{7,5},{8,10},{9,11},{10,... | collective-permute-start | bytes 1585160 | tf_op jit(solution)/shard_map/ppermute | solution.py:34
  8.8 13.5 %collective-permute-start.4 = (bf16[2,64,896]{2,1,0:T(8,128)(2,1)S(1)}, bf16[2,64,896]{2,1,0:T(8,128)(2,1)S(1)}, u32[]{:S(2)}, u32[]{:S(2)}) collective-permute-start(bf16[2,64,896]{2,1,0:T(8,128)(2,1)S(1)} %join_kernels.1.refs_1_.refs_0_), channel_id=1, source_target_pairs={{0,4},{4,0},{8,12},{12,8},{1,5},{5,1},{9,13},{13,9},{2,6},{6,2},{1... | collective-permute-start | bytes 688136 | tf_op jit(solution)/shard_map/ppermute | solution.py:34
  8.8 13.9 %collective-permute-start.5 = (bf16[2,64,896]{2,1,0:T(8,128)(2,1)S(1)}, bf16[2,64,896]{2,1,0:T(8,128)(2,1)S(1)}, u32[]{:S(2)}, u32[]{:S(2)}) collective-permute-start(bf16[2,64,896]{2,1,0:T(8,128)(2,1)S(1)} %join_kernels.1.refs_1_.refs_0_), channel_id=1, source_target_pairs={{0,8},{4,12},{8,0},{12,4},{1,9},{5,13},{9,1},{13,5},{2,10},{6,14},... | collective-permute-start | bytes 688136 | tf_op jit(solution)/shard_map/ppermute | solution.py:34
  11.9 23.3 %collective-permute-start.3 = (bf16[688,384]{1,0:T(8,128)(2,1)S(1)}, bf16[688,384]{1,0:T(8,128)(2,1)S(1)}, u32[]{:S(2)}, u32[]{:S(2)}) collective-permute-start(bf16[688,384]{1,0:T(8,128)(2,1)S(1)} %get-tuple-element.67), channel_id=1, source_target_pairs={{0,3},{1,2},{2,1},{3,0},{4,7},{5,6},{6,5},{7,4},{8,11},{9,10},{10,... | collective-permute-start | bytes 1585160 | tf_op jit(solution)/shard_map/ppermute | solution.py:34
  14.8 2.2 %copy-start.2 = (bf16[2304,1024]{1,0:T(8,128)(2,1)}, bf16[2304,1024]{1,0:T(8,128)(2,1)S(1)}, u32[]{:S(2)}) copy-start(bf16[2304,1024]{1,0:T(8,128)(2,1)S(1)} %get-tuple-element.76.refs_8_.refs_3_.refs_1_) | copy-start | bytes 14155780
  20.6 14.6 %collective-permute-start.1 = (bf16[688,384]{1,0:T(8,128)(2,1)S(1)}, bf16[688,384]{1,0:T(8,128)(2,1)S(1)}, u32[]{:S(2)}, u32[]{:S(2)}) collective-permute-start(bf16[688,384]{1,0:T(8,128)(2,1)S(1)} %get-tuple-element.65), channel_id=1, source_target_pairs={{0,1},{1,0},{2,3},{3,2},{4,5},{5,4},{6,7},{7,6},{8,9},{9,8},{10,11... | collective-permute-start | bytes 1585160 | tf_op jit(solution)/shard_map/ppermute | solution.py:34
  22.2 12.4 %collective-permute-start.6 = (bf16[2,64,896]{2,1,0:T(8,128)(2,1)S(1)}, bf16[2,64,896]{2,1,0:T(8,128)(2,1)S(1)}, u32[]{:S(2)}, u32[]{:S(2)}) collective-permute-start(bf16[2,64,896]{2,1,0:T(8,128)(2,1)S(1)} %join_kernels.1.refs_1_.refs_0_), channel_id=1, source_target_pairs={{0,12},{4,8},{8,4},{12,0},{1,13},{5,9},{9,5},{13,1},{2,14},{6,10},... | collective-permute-start | bytes 688136 | tf_op jit(solution)/shard_map/ppermute | solution.py:34
  22.7 13.9 %collective-permute-start.7 = (bf16[2,2,64,896]{3,2,1,0:T(8,128)(2,1)S(1)}, bf16[2,2,64,896]{3,2,1,0:T(8,128)(2,1)S(1)}, u32[]{:S(2)}, u32[]{:S(2)}) collective-permute-start(bf16[2,2,64,896]{3,2,1,0:T(8,128)(2,1)S(1)} %join_columns.1.refs_1_), channel_id=1, source_target_pairs={{0,1},{1,0},{2,3},{3,2},{4,5},{5,4},{6,7},{7,6},{8,9},{9,8},{10,11... | collective-permute-start | bytes 1376264 | tf_op jit(solution)/shard_map/ppermute | solution.py:34
  34.7 2.0 %collective-permute-start.8 = (bf16[2,64,896]{2,1,0:T(8,128)(2,1)S(1)}, bf16[2,64,896]{2,1,0:T(8,128)(2,1)S(1)}, u32[]{:S(2)}, u32[]{:S(2)}) collective-permute-start(bf16[2,64,896]{2,1,0:T(8,128)(2,1)S(1)} %collective-permute-done.5.refs_2_), channel_id=1, source_target_pairs={{0,1},{1,0},{2,3},{3,2},{4,5},{5,4},{6,7},{7,6},{8,9},{9,8},{10,11... | collective-permute-start | bytes 688136 | tf_op jit(solution)/shard_map/ppermute | solution.py:34
  34.7 2.0 %collective-permute-start.9 = (bf16[2,64,896]{2,1,0:T(8,128)(2,1)S(1)}, bf16[2,64,896]{2,1,0:T(8,128)(2,1)S(1)}, u32[]{:S(2)}, u32[]{:S(2)}) collective-permute-start(bf16[2,64,896]{2,1,0:T(8,128)(2,1)S(1)} %collective-permute-done.6.refs_3_), channel_id=1, source_target_pairs={{0,1},{1,0},{2,3},{3,2},{4,5},{5,4},{6,7},{7,6},{8,9},{9,8},{10,11... | collective-permute-start | bytes 688136 | tf_op jit(solution)/shard_map/ppermute | solution.py:34
  38.0 30.7 %slice-start = ((s8[4718592]{0:T(1024)(128)(4,1)}), s8[4194304]{0:T(1024)(128)(4,1)S(1)}, s32[]{:S(2)}) async-start(s8[4718592]{0:T(1024)(128)(4,1)} %bitcast.38), calls=%async_computation | async-start | bytes 8388608
  38.0 30.7 %slice-start.1 = ((s8[4718592]{0:T(1024)(128)(4,1)}), s8[524288]{0:T(1024)(128)(4,1)S(1)}, s32[]{:S(2)}) async-start(s8[4718592]{0:T(1024)(128)(4,1)} %bitcast.38), calls=%async_computation.1 | async-start | bytes 1048576
  45.3 6.8 %collective-permute-start.11 = (bf16[2,9,16,256]{3,2,1,0:T(8,128)(2,1)S(1)}, bf16[2,9,16,256]{3,2,1,0:T(8,128)(2,1)S(1)}, u32[]{:S(2)}, u32[]{:S(2)}) collective-permute-start(bf16[2,9,16,256]{3,2,1,0:T(8,128)(2,1)S(1)} %get-tuple-element.71), channel_id=1, source_target_pairs={{0,16},{16,0},{1,17},{17,1},{2,18},{18,2},{3,19},{19,3},{4,20},{20... | collective-permute-start | bytes 442376 | tf_op jit(solution)/shard_map/ppermute | solution.py:34
  47.4 6.8 %collective-permute-start.10 = (bf16[2,9,16,256]{3,2,1,0:T(8,128)(2,1)S(1)}, bf16[2,9,16,256]{3,2,1,0:T(8,128)(2,1)S(1)}, u32[]{:S(2)}, u32[]{:S(2)}) collective-permute-start(bf16[2,9,16,256]{3,2,1,0:T(8,128)(2,1)S(1)} %pool_near.1), channel_id=1, source_target_pairs={{0,16},{16,0},{1,17},{17,1},{2,18},{18,2},{3,19},{19,3},{4,20},{20... | collective-permute-start | bytes 442376 | tf_op jit(solution)/shard_map/ppermute | solution.py:34
  52.7 5.5 %collective-permute-start.13 = (bf16[9,16,256]{2,1,0:T(8,128)(2,1)S(1)}, bf16[9,16,256]{2,1,0:T(8,128)(2,1)S(1)}, u32[]{:S(2)}, u32[]{:S(2)}) collective-permute-start(bf16[9,16,256]{2,1,0:T(8,128)(2,1)S(1)} %get-tuple-element.72.refs_4_), channel_id=1, source_target_pairs={{0,8},{4,12},{8,0},{12,4},{1,9},{5,13},{9,1},{13,5},{2,10},{6,14},... | collective-permute-start | bytes 221192 | tf_op jit(solution)/shard_map/ppermute | solution.py:34
  52.7 7.2 %collective-permute-start.14 = (bf16[9,16,256]{2,1,0:T(8,128)(2,1)S(1)}, bf16[9,16,256]{2,1,0:T(8,128)(2,1)S(1)}, u32[]{:S(2)}, u32[]{:S(2)}) collective-permute-start(bf16[9,16,256]{2,1,0:T(8,128)(2,1)S(1)} %get-tuple-element.75), channel_id=1, source_target_pairs={{0,12},{4,8},{8,4},{12,0},{1,13},{5,9},{9,5},{13,1},{2,14},{6,10},... | collective-permute-start | bytes 221192 | tf_op jit(solution)/shard_map/ppermute | solution.py:34
  54.9 5.3 %collective-permute-start.12 = (bf16[9,16,256]{2,1,0:T(8,128)(2,1)S(1)}, bf16[9,16,256]{2,1,0:T(8,128)(2,1)S(1)}, u32[]{:S(2)}, u32[]{:S(2)}) collective-permute-start(bf16[9,16,256]{2,1,0:T(8,128)(2,1)S(1)} %get-tuple-element.74), channel_id=1, source_target_pairs={{0,4},{4,0},{8,12},{12,8},{1,5},{5,1},{9,13},{13,9},{2,6},{6,2},{1... | collective-permute-start | bytes 221192 | tf_op jit(solution)/shard_map/ppermute | solution.py:34
  60.2 5.5 %collective-permute-start.17 = (bf16[2,9,16,256]{3,2,1,0:T(8,128)(2,1)S(1)}, bf16[2,9,16,256]{3,2,1,0:T(8,128)(2,1)S(1)}, u32[]{:S(2)}, u32[]{:S(2)}) collective-permute-start(bf16[2,9,16,256]{3,2,1,0:T(8,128)(2,1)S(1)} %join_acts_near.1.refs_0_), channel_id=1, source_target_pairs={{0,2},{1,3},{2,0},{3,1},{4,6},{5,7},{6,4},{7,5},{8,10},{9,11},{10,... | collective-permute-start | bytes 442376 | tf_op jit(solution)/shard_map/ppermute | solution.py:34
  60.8 6.5 %collective-permute-start.18 = (bf16[2,9,16,256]{3,2,1,0:T(8,128)(2,1)S(1)}, bf16[2,9,16,256]{3,2,1,0:T(8,128)(2,1)S(1)}, u32[]{:S(2)}, u32[]{:S(2)}) collective-permute-start(bf16[2,9,16,256]{3,2,1,0:T(8,128)(2,1)S(1)} %join_acts_far.1.refs_2_.refs_1_), channel_id=1, source_target_pairs={{0,2},{1,3},{2,0},{3,1},{4,6},{5,7},{6,4},{7,5},{8,10},{9,11},{10,... | collective-permute-start | bytes 442376 | tf_op jit(solution)/shard_map/ppermute | solution.py:34
  62.3 5.0 %collective-permute-start.15 = (bf16[2,9,16,256]{3,2,1,0:T(8,128)(2,1)S(1)}, bf16[2,9,16,256]{3,2,1,0:T(8,128)(2,1)S(1)}, u32[]{:S(2)}, u32[]{:S(2)}) collective-permute-start(bf16[2,9,16,256]{3,2,1,0:T(8,128)(2,1)S(1)} %join_acts_near.1.refs_0_), channel_id=1, source_target_pairs={{0,1},{1,0},{2,3},{3,2},{4,5},{5,4},{6,7},{7,6},{8,9},{9,8},{10,11... | collective-permute-start | bytes 442376 | tf_op jit(solution)/shard_map/ppermute | solution.py:34
  62.3 5.0 %collective-permute-start.16 = (bf16[2,9,16,256]{3,2,1,0:T(8,128)(2,1)S(1)}, bf16[2,9,16,256]{3,2,1,0:T(8,128)(2,1)S(1)}, u32[]{:S(2)}, u32[]{:S(2)}) collective-permute-start(bf16[2,9,16,256]{3,2,1,0:T(8,128)(2,1)S(1)} %join_acts_far.1.refs_2_.refs_1_), channel_id=1, source_target_pairs={{0,1},{1,0},{2,3},{3,2},{4,5},{5,4},{6,7},{7,6},{8,9},{9,8},{10,11... | collective-permute-start | bytes 442376 | tf_op jit(solution)/shard_map/ppermute | solution.py:34
  65.7 1.6 collective-permute-start.19
  67.3 1.4 collective-permute-start.20
  68.7 16.7 %copy-start.3 = (f32[2,2,1024]{2,1,0:T(2,128)S(1)}, f32[2,2,1024]{2,1,0:T(2,128)}, u32[]{:S(2)}) copy-start(f32[2,2,1024]{2,1,0:T(2,128)} %refs_3_.3) | copy-start | bytes 49156
  68.7 16.7 %copy-start.4 = (f32[2,1024]{1,0:T(2,128)S(1)}, f32[2,1024]{1,0:T(2,128)}, u32[]{:S(2)}) copy-start(f32[2,1024]{1,0:T(2,128)} %refs_5_.1) | copy-start | bytes 24580
  70.1 7.0 %collective-permute-start.21 = (bf16[4,16,1024]{2,1,0:T(8,128)(2,1)S(1)}, bf16[4,16,1024]{2,1,0:T(8,128)(2,1)S(1)}, u32[]{:S(2)}, u32[]{:S(2)}) collective-permute-start(bf16[4,16,1024]{2,1,0:T(8,128)(2,1)S(1)} %get-tuple-element.78), channel_id=1, source_target_pairs={{0,4},{4,0},{8,12},{12,8},{1,5},{5,1},{9,13},{13,9},{2,6},{6,2},{1... | collective-permute-start | bytes 393224 | tf_op jit(solution)/shard_map/ppermute | solution.py:34
  71.8 10.7 %collective-permute-start.22 = (bf16[4,16,1024]{2,1,0:T(8,128)(2,1)S(1)}, bf16[4,16,1024]{2,1,0:T(8,128)(2,1)S(1)}, u32[]{:S(2)}, u32[]{:S(2)}) collective-permute-start(bf16[4,16,1024]{2,1,0:T(8,128)(2,1)S(1)} %get-tuple-element.79), channel_id=1, source_target_pairs={{0,8},{4,12},{8,0},{12,4},{1,9},{5,13},{9,1},{13,5},{2,10},{6,14},... | collective-permute-start | bytes 393224 | tf_op jit(solution)/shard_map/ppermute | solution.py:34
  73.2 12.1 %collective-permute-start.23 = (bf16[4,16,1024]{2,1,0:T(8,128)(2,1)S(1)}, bf16[4,16,1024]{2,1,0:T(8,128)(2,1)S(1)}, u32[]{:S(2)}, u32[]{:S(2)}) collective-permute-start(bf16[4,16,1024]{2,1,0:T(8,128)(2,1)S(1)} %get-tuple-element.80), channel_id=1, source_target_pairs={{0,12},{4,8},{8,4},{12,0},{1,13},{5,9},{9,5},{13,1},{2,14},{6,10},... | collective-permute-start | bytes 393224 | tf_op jit(solution)/shard_map/ppermute | solution.py:34
  86.3 5.9 %collective-permute-start.24 = (bf16[4,16,1024]{2,1,0:T(8,128)(2,1)S(1)}, bf16[4,16,1024]{2,1,0:T(8,128)(2,1)S(1)}, u32[]{:S(2)}, u32[]{:S(2)}) collective-permute-start(bf16[4,16,1024]{2,1,0:T(8,128)(2,1)S(1)} %get-tuple-element.83.refs_0_.refs_8_), channel_id=1, source_target_pairs={{0,4},{4,0},{8,12},{12,8},{1,5},{5,1},{9,13},{13,9},{2,6},{6,2},{1... | collective-permute-start | bytes 393224 | tf_op jit(solution)/shard_map/ppermute | solution.py:34
  86.4 8.4 %collective-permute-start.25 = (bf16[4,16,1024]{2,1,0:T(8,128)(2,1)S(1)}, bf16[4,16,1024]{2,1,0:T(8,128)(2,1)S(1)}, u32[]{:S(2)}, u32[]{:S(2)}) collective-permute-start(bf16[4,16,1024]{2,1,0:T(8,128)(2,1)S(1)} %get-tuple-element.83.refs_0_.refs_8_), channel_id=1, source_target_pairs={{0,8},{4,12},{8,0},{12,4},{1,9},{5,13},{9,1},{13,5},{2,10},{6,14},... | collective-permute-start | bytes 393224 | tf_op jit(solution)/shard_map/ppermute | solution.py:34
  96.4 1.9 %collective-permute-start.26 = (bf16[2,3,9,16,256]{4,3,2,1,0:T(8,128)(2,1)S(1)}, bf16[2,3,9,16,256]{4,3,2,1,0:T(8,128)(2,1)S(1)}, u32[]{:S(2)}, u32[]{:S(2)}) collective-permute-start(bf16[2,3,9,16,256]{4,3,2,1,0:T(8,128)(2,1)S(1)} %get-tuple-element.85), channel_id=1, source_target_pairs={{0,1},{1,0},{2,3},{3,2},{4,5},{5,4},{6,7},{7,6},{8,9},{9,8},{10,11... | collective-permute-start | bytes 1327112 | tf_op jit(solution)/shard_map/ppermute | solution.py:34
  96.5 5.9 %collective-permute-start.30 = (bf16[4,16,1024]{2,1,0:T(8,128)(2,1)S(1)}, bf16[4,16,1024]{2,1,0:T(8,128)(2,1)S(1)}, u32[]{:S(2)}, u32[]{:S(2)}) collective-permute-start(bf16[4,16,1024]{2,1,0:T(8,128)(2,1)S(1)} %collective-permute-done.25.refs_2_.refs_10_), channel_id=1, source_target_pairs={{0,4},{4,0},{8,12},{12,8},{1,5},{5,1},{9,13},{13,9},{2,6},{6,2},{1... | collective-permute-start | bytes 393224 | tf_op jit(solution)/shard_map/ppermute | solution.py:34
  98.3 7.5 %collective-permute-start.27 = (bf16[3,9,16,256]{3,2,1,0:T(8,128)(2,1)S(1)}, bf16[3,9,16,256]{3,2,1,0:T(8,128)(2,1)S(1)}, u32[]{:S(2)}, u32[]{:S(2)}) collective-permute-start(bf16[3,9,16,256]{3,2,1,0:T(8,128)(2,1)S(1)} %cross_near.1), channel_id=1, source_target_pairs={{0,2},{1,3},{2,0},{3,1},{4,6},{5,7},{6,4},{7,5},{8,10},{9,11},{10,... | collective-permute-start | bytes 663560 | tf_op jit(solution)/shard_map/ppermute | solution.py:34
  103.9 5.1 %collective-permute-start.31 = (bf16[2,1,9,16,256]{4,3,2,1,0:T(8,128)(2,1)S(1)}, bf16[2,1,9,16,256]{4,3,2,1,0:T(8,128)(2,1)S(1)}, u32[]{:S(2)}, u32[]{:S(2)}) collective-permute-start(bf16[2,1,9,16,256]{4,3,2,1,0:T(8,128)(2,1)S(1)} %get-tuple-element.91), channel_id=1, source_target_pairs={{0,1},{1,0},{2,3},{3,2},{4,5},{5,4},{6,7},{7,6},{8,9},{9,8},{10,11... | collective-permute-start | bytes 442376 | tf_op jit(solution)/shard_map/ppermute | solution.py:34
  105.9 7.5 %collective-permute-start.28 = (bf16[10,16,256]{2,1,0:T(8,128)(2,1)S(1)}, bf16[10,16,256]{2,1,0:T(8,128)(2,1)S(1)}, u32[]{:S(2)}, u32[]{:S(2)}) collective-permute-start(bf16[10,16,256]{2,1,0:T(8,128)(2,1)S(1)} %get-tuple-element.88), channel_id=1, source_target_pairs={{0,4},{4,0},{8,12},{12,8},{1,5},{5,1},{9,13},{13,9},{2,6},{6,2},{1... | collective-permute-start | bytes 245768 | tf_op jit(solution)/shard_map/ppermute | solution.py:34
  107.7 5.8 %collective-permute-start.29 = (bf16[10,16,256]{2,1,0:T(8,128)(2,1)S(1)}, bf16[10,16,256]{2,1,0:T(8,128)(2,1)S(1)}, u32[]{:S(2)}, u32[]{:S(2)}) collective-permute-start(bf16[10,16,256]{2,1,0:T(8,128)(2,1)S(1)} %get-tuple-element.89), channel_id=1, source_target_pairs={{0,8},{4,12},{8,0},{12,4},{1,9},{5,13},{9,1},{13,5},{2,10},{6,14},... | collective-permute-start | bytes 245768 | tf_op jit(solution)/shard_map/ppermute | solution.py:34
  109.0 4.4 %collective-permute-start.32 = (bf16[1,9,16,256]{3,2,1,0:T(8,128)(2,1)S(1)}, bf16[1,9,16,256]{3,2,1,0:T(8,128)(2,1)S(1)}, u32[]{:S(2)}, u32[]{:S(2)}) collective-permute-start(bf16[1,9,16,256]{3,2,1,0:T(8,128)(2,1)S(1)} %cross_far.1), channel_id=1, source_target_pairs={{0,2},{1,3},{2,0},{3,1},{4,6},{5,7},{6,4},{7,5},{8,10},{9,11},{10,... | collective-permute-start | bytes 221192 | tf_op jit(solution)/shard_map/ppermute | solution.py:34
  113.5 10.5 %collective-permute-start.34 = (bf16[3,10,16,256]{3,2,1,0:T(8,128)(2,1)S(1)}, bf16[3,10,16,256]{3,2,1,0:T(8,128)(2,1)S(1)}, u32[]{:S(2)}, u32[]{:S(2)}) collective-permute-start(bf16[3,10,16,256]{3,2,1,0:T(8,128)(2,1)S(1)} %join_near.1.refs_3_.refs_1_), channel_id=1, source_target_pairs={{0,16},{16,0},{1,17},{17,1},{2,18},{18,2},{3,19},{19,3},{4,20},{20... | collective-permute-start | bytes 737288 | tf_op jit(solution)/shard_map/ppermute | solution.py:34
  115.1 4.4 %collective-permute-start.33 = (bf16[10,16,256]{2,1,0:T(8,128)(2,1)S(1)}, bf16[10,16,256]{2,1,0:T(8,128)(2,1)S(1)}, u32[]{:S(2)}, u32[]{:S(2)}) collective-permute-start(bf16[10,16,256]{2,1,0:T(8,128)(2,1)S(1)} %home_far.1.refs_3_), channel_id=1, source_target_pairs={{0,12},{4,8},{8,4},{12,0},{1,13},{5,9},{9,5},{13,1},{2,14},{6,10},... | collective-permute-start | bytes 245768 | tf_op jit(solution)/shard_map/ppermute | solution.py:34
  119.5 4.4 %collective-permute-start.35 = (bf16[10,16,256]{2,1,0:T(8,128)(2,1)S(1)}, bf16[10,16,256]{2,1,0:T(8,128)(2,1)S(1)}, u32[]{:S(2)}, u32[]{:S(2)}) collective-permute-start(bf16[10,16,256]{2,1,0:T(8,128)(2,1)S(1)} %collective-permute-done.33.refs_2_), channel_id=1, source_target_pairs={{0,16},{16,0},{1,17},{17,1},{2,18},{18,2},{3,19},{19,3},{4,20},{20... | collective-permute-start | bytes 245768 | tf_op jit(solution)/shard_map/ppermute | solution.py:34
  137.2 2.5 %collective-permute-start.38 = (bf16[3520,128]{1,0:T(8,128)(2,1)S(1)}, bf16[3520,128]{1,0:T(8,128)(2,1)S(1)}, u32[]{:S(2)}, u32[]{:S(2)}) collective-permute-start(bf16[3520,128]{1,0:T(8,128)(2,1)S(1)} %get-tuple-element.98), channel_id=1, source_target_pairs={{0,1},{1,0},{2,3},{3,2},{4,5},{5,4},{6,7},{7,6},{8,9},{9,8},{10,11... | collective-permute-start | bytes 2703368 | tf_op jit(solution)/shard_map/ppermute | solution.py:34
  137.3 11.4 %collective-permute-start.36 = (bf16[368,384]{1,0:T(8,128)(2,1)S(1)}, bf16[368,384]{1,0:T(8,128)(2,1)S(1)}, u32[]{:S(2)}, u32[]{:S(2)}) collective-permute-start(bf16[368,384]{1,0:T(8,128)(2,1)S(1)} %get-tuple-element.93), channel_id=1, source_target_pairs={{0,2},{1,3},{2,0},{3,1},{4,6},{5,7},{6,4},{7,5},{8,10},{9,11},{10,... | collective-permute-start | bytes 847880 | tf_op jit(solution)/shard_map/ppermute | solution.py:34
  137.8 15.7 %collective-permute-start.37 = (bf16[368,384]{1,0:T(8,128)(2,1)S(1)}, bf16[368,384]{1,0:T(8,128)(2,1)S(1)}, u32[]{:S(2)}, u32[]{:S(2)}) collective-permute-start(bf16[368,384]{1,0:T(8,128)(2,1)S(1)} %get-tuple-element.94), channel_id=1, source_target_pairs={{0,3},{1,2},{2,1},{3,0},{4,7},{5,6},{6,5},{7,4},{8,11},{9,10},{10,... | collective-permute-start | bytes 847880 | tf_op jit(solution)/shard_map/ppermute | solution.py:34
  139.2 27.2 %collective-permute-start.43 = (bf16[368,384]{1,0:T(8,128)(2,1)S(1)}, bf16[368,384]{1,0:T(8,128)(2,1)S(1)}, u32[]{:S(2)}, u32[]{:S(2)}) collective-permute-start(bf16[368,384]{1,0:T(8,128)(2,1)S(1)} %get-tuple-element.104), channel_id=1, source_target_pairs={{0,1},{1,0},{2,3},{3,2},{4,5},{5,4},{6,7},{7,6},{8,9},{9,8},{10,11... | collective-permute-start | bytes 847880 | tf_op jit(solution)/shard_map/ppermute | solution.py:34
  140.0 15.1 %collective-permute-start.44 = (bf16[880,128]{1,0:T(8,128)(2,1)S(1)}, bf16[880,128]{1,0:T(8,128)(2,1)S(1)}, u32[]{:S(2)}, u32[]{:S(2)}) collective-permute-start(bf16[880,128]{1,0:T(8,128)(2,1)S(1)} %get-tuple-element.105), channel_id=1, source_target_pairs={{0,4},{4,0},{8,12},{12,8},{1,5},{5,1},{9,13},{13,9},{2,6},{6,2},{1... | collective-permute-start | bytes 675848 | tf_op jit(solution)/shard_map/ppermute | solution.py:34
  143.5 14.8 %collective-permute-start.45 = (bf16[880,128]{1,0:T(8,128)(2,1)S(1)}, bf16[880,128]{1,0:T(8,128)(2,1)S(1)}, u32[]{:S(2)}, u32[]{:S(2)}) collective-permute-start(bf16[880,128]{1,0:T(8,128)(2,1)S(1)} %get-tuple-element.106), channel_id=1, source_target_pairs={{0,8},{4,12},{8,0},{12,4},{1,9},{5,13},{9,1},{13,5},{2,10},{6,14},... | collective-permute-start | bytes 675848 | tf_op jit(solution)/shard_map/ppermute | solution.py:34
  148.7 16.4 %collective-permute-start.46 = (bf16[880,128]{1,0:T(8,128)(2,1)S(1)}, bf16[880,128]{1,0:T(8,128)(2,1)S(1)}, u32[]{:S(2)}, u32[]{:S(2)}) collective-permute-start(bf16[880,128]{1,0:T(8,128)(2,1)S(1)} %last_kernels.1), channel_id=1, source_target_pairs={{0,12},{4,8},{8,4},{12,0},{1,13},{5,9},{9,5},{13,1},{2,14},{6,10},... | collective-permute-start | bytes 675848 | tf_op jit(solution)/shard_map/ppermute | solution.py:34
  154.6 18.3 %collective-permute-start.40 = (bf16[320,384]{1,0:T(8,128)(2,1)S(1)}, bf16[320,384]{1,0:T(8,128)(2,1)S(1)}, u32[]{:S(2)}, u32[]{:S(2)}) collective-permute-start(bf16[320,384]{1,0:T(8,128)(2,1)S(1)} %get-tuple-element.101), channel_id=1, source_target_pairs={{0,2},{1,3},{2,0},{3,1},{4,6},{5,7},{6,4},{7,5},{8,10},{9,11},{10,... | collective-permute-start | bytes 737288 | tf_op jit(solution)/shard_map/ppermute | solution.py:34
  155.1 16.2 %collective-permute-start.42 = (bf16[320,384]{1,0:T(8,128)(2,1)S(1)}, bf16[320,384]{1,0:T(8,128)(2,1)S(1)}, u32[]{:S(2)}, u32[]{:S(2)}) collective-permute-start(bf16[320,384]{1,0:T(8,128)(2,1)S(1)} %get-tuple-element.103), channel_id=1, source_target_pairs={{0,1},{1,0},{2,3},{3,2},{4,5},{5,4},{6,7},{7,6},{8,9},{9,8},{10,11... | collective-permute-start | bytes 737288 | tf_op jit(solution)/shard_map/ppermute | solution.py:34
  158.3 14.5 %collective-permute-start.41 = (bf16[320,384]{1,0:T(8,128)(2,1)S(1)}, bf16[320,384]{1,0:T(8,128)(2,1)S(1)}, u32[]{:S(2)}, u32[]{:S(2)}) collective-permute-start(bf16[320,384]{1,0:T(8,128)(2,1)S(1)} %get-tuple-element.102), channel_id=1, source_target_pairs={{0,3},{1,2},{2,1},{3,0},{4,7},{5,6},{6,5},{7,4},{8,11},{9,10},{10,... | collective-permute-start | bytes 737288 | tf_op jit(solution)/shard_map/ppermute | solution.py:34
  165.1 5.0 %collective-permute-start.39 = (bf16[4,16,1024]{2,1,0:T(8,128)(2,1)S(1)}, bf16[4,16,1024]{2,1,0:T(8,128)(2,1)S(1)}, u32[]{:S(2)}, u32[]{:S(2)}) collective-permute-start(bf16[4,16,1024]{2,1,0:T(8,128)(2,1)S(1)} %outputs_send.1), channel_id=1, source_target_pairs={{0,16},{16,0},{1,17},{17,1},{2,18},{18,2},{3,19},{19,3},{4,20},{20... | collective-permute-start | bytes 393224 | tf_op jit(solution)/shard_map/ppermute | solution.py:34
  166.4 8.0 %collective-permute-start.47 = (bf16[64,896]{1,0:T(8,128)(2,1)S(1)}, bf16[64,896]{1,0:T(8,128)(2,1)S(1)}, u32[]{:S(2)}, u32[]{:S(2)}) collective-permute-start(bf16[64,896]{1,0:T(8,128)(2,1)S(1)} %get-tuple-element.110), channel_id=1, source_target_pairs={{0,2},{1,3},{2,0},{3,1},{4,6},{5,7},{6,4},{7,5},{8,10},{9,11},{10,... | collective-permute-start | bytes 344072 | tf_op jit(solution)/shard_map/ppermute | solution.py:34
  171.3 4.4 %copy-start.1 = (bf16[4,64,2,1024]{3,2,1,0:T(2,128)(2,1)S(1)}, bf16[4,64,2,1024]{3,2,1,0:T(2,128)(2,1)}, u32[]{:S(2)}) copy-start(bf16[4,64,2,1024]{3,2,1,0:T(2,128)(2,1)} %param.17) | copy-start | bytes 3145732
